TPU v7x, 32 devices: a whole 2x2x4 slice. The times are simulated.
32 devices in a mesh: sec: 2 (over x), ep: 16 (over z, y, core).
Axes of the slice: x: 2, y: 2, z: 4, core: 2. Of those that a mesh axis runs over, the one named last changes fastest.
Arguments:
- queries: bfloat16 [32, 4, 32, 576], P(('sec', 'ep')), may hold values from -24 to 24, as said below
- new_latent: bfloat16 [32, 4, 576], P(('sec', 'ep')), may hold values from -5 to 5
- cache_latent: bfloat16 [32, 8192, 576], P(('sec', 'ep')), may hold values from -5 to 5
- cache_len: int32 [32], P(('sec', 'ep')), may hold values from 1 to 8192, 131072 in all
- route_ids: int32 [32, 4, 8], P(('sec', 'ep')), may hold values from 0 to 15, all different within a row; in each aligned block of 4 rows (0 to 3, 4 to 7, ..., all dimensions but the last counted through in order) at most 2 rows name the same one
- route_scores: float32 [32, 4, 8], P(('sec', 'ep')), may hold values from 0.02 to 1
- residual: bfloat16 [32, 4, 7168], P(('sec', 'ep')), may hold values from -6 to 6
- norm_gain: bfloat16 [7168], replicated, may hold values from 0.099609375 to 1.8984375
- w_uv: bfloat16 [32, 512, 128], P(('sec', 'ep')), may hold values from -0.25 to 0.25
- w_out: bfloat16 [32, 128, 7168], P(('sec', 'ep')), may hold values from -0.09375 to 0.09375
- w_gate: bfloat16 [16, 7168, 1024], P('ep', None, 'sec'), may hold values from -0.0625 to 0.0625
- w_up: bfloat16 [16, 7168, 1024], P('ep', None, 'sec'), may hold values from -0.0625 to 0.0625
- w_down: bfloat16 [16, 1024, 7168], P('ep', 'sec'), may hold values from -0.1875 to 0.1875
Outputs:
- mixed: bfloat16 [32, 4, 7168], P(('sec', 'ep'))
Inputs may be any that keep to these rules, and one draw needn't show every extreme that they name: `queries`: A few heads of some rows may have a query that is a multiple of that row's new latent entry. `route_ids`: each row and step names 8 different experts; over the 4 steps of one row no expert is named more than 2 times, and in some rows one expert is named exactly 2 times.
All inputs are finite; a program needn't handle non-finite values. No bound on the sum of `cache_len` on one device may be relied on, other than what follows from the above.
Results may differ from a plain program's by a relative error of at most 0.015.
Values may be sent and summed in bfloat16 or wider, within the bound.
No kernel may reach another device: no remote copies, remote signals or barrier semaphores. Data moves between devices by JAX's collectives and lax.ppermute only.
A program may use at most 128 MiB of HBM per device.

v0:
```python
import jax
import jax.numpy as jnp
from jax import lax
from jax.sharding import PartitionSpec as P

LAT = 512
ROPE = 64
VDIM = 128
STEPS = 4
BLK = 512
CAP = 2


def attend(query_rows, step_ids, cached_rows, new_keys, length):
    row_count = query_rows.shape[0]
    score_scale = (VDIM + ROPE) ** (-0.5)
    contract = (((1,), (1,)), ((), ()))

    def update(carried, key_rows, visible):
        running_max, denominator, summed = carried
        scores = (
            lax.dot_general(query_rows, key_rows, contract, preferred_element_type=jnp.float32)
            * score_scale
        )
        scores = jnp.where(visible, scores, -1e30)
        new_max = jnp.maximum(running_max, jnp.max(scores, axis=1, keepdims=True))
        factor = jnp.exp(running_max - new_max)
        weights = jnp.exp(scores - new_max)
        denominator = denominator * factor + jnp.sum(weights, axis=1, keepdims=True)
        summed = summed * factor + jnp.dot(
            weights.astype(jnp.bfloat16), key_rows[:, :LAT], preferred_element_type=jnp.float32
        )
        return (new_max, denominator, summed)

    start_state = (
        jnp.full((row_count, 1), -1e30, jnp.float32),
        jnp.zeros((row_count, 1), jnp.float32),
        jnp.zeros((row_count, LAT), jnp.float32),
    )
    block_total = (length + BLK - 1) // BLK

    def block_step(block_index, carried):
        key_rows = lax.dynamic_slice_in_dim(cached_rows, block_index * BLK, BLK, 0)
        positions = block_index * BLK + jnp.arange(BLK, dtype=jnp.int32)
        visible = (positions < length)[None, :]
        return update(carried, key_rows, visible)

    carried = lax.fori_loop(0, block_total, block_step, start_state)
    visible_new = jnp.arange(STEPS, dtype=jnp.int32)[None, :] <= step_ids[:, None]
    running_max, denominator, summed = update(carried, new_keys, visible_new)
    return (summed / denominator).astype(jnp.bfloat16)


def head_products(by_head, w_uv, w_out):
    source_count, step_count, local_heads, latent_width = by_head.shape
    row_count = source_count * step_count
    head_values = jnp.dot(
        by_head[:, :, 0].reshape(row_count, latent_width),
        w_uv[0],
        preferred_element_type=jnp.float32,
    ).astype(jnp.bfloat16)
    flat_out = w_out.reshape(local_heads * w_out.shape[1], w_out.shape[2])

    def term(first_row, row_total):
        return jnp.dot(head_values, flat_out, preferred_element_type=jnp.float32)

    return (term, step_count)


def per_device(
    queries,
    new_latent,
    cache_latent,
    cache_len,
    route_ids,
    route_scores,
    residual,
    norm_gain,
    w_uv,
    w_out,
    w_gate,
    w_up,
    w_down,
):
    head_count = queries.shape[2]
    width = residual.shape[2]
    n_sec = lax.axis_size("sec")
    n_ep = lax.axis_size("ep")
    query_rows = queries[0].reshape(STEPS * head_count, queries.shape[3])
    step_ids = jnp.repeat(jnp.arange(STEPS, dtype=jnp.int32), head_count)
    latent_out = attend(query_rows, step_ids, cache_latent[0], new_latent[0], cache_len[0])
    latent_out = latent_out.reshape(1, STEPS, head_count, LAT)
    by_head = lax.all_to_all(latent_out, ("sec", "ep"), split_axis=2, concat_axis=0, tiled=True)
    term, step_count = head_products(by_head, w_uv, w_out)
    attended = lax.psum_scatter(
        term(jnp.int32(0), step_count * lax.axis_size(("sec", "ep"))),
        ("sec", "ep"),
        scatter_dimension=0,
        tiled=True,
    )
    hidden = residual[0].astype(jnp.float32) + attended
    mean_square = jnp.mean(hidden * hidden, axis=-1, keepdims=True)
    normed = (hidden * lax.rsqrt(mean_square + 1e-06) * norm_gain.astype(jnp.float32)).astype(
        jnp.bfloat16
    )
    exp_local = w_gate.shape[0]
    experts = exp_local * n_ep
    slots = CAP
    ids_here = route_ids[0]
    scores_here = route_scores[0]
    matches = ids_here[:, :, None] == jnp.arange(experts, dtype=jnp.int32)[None, None, :]
    shares = scores_here / jnp.sum(scores_here, axis=1, keepdims=True) * 2.5
    coefficient = jnp.sum(jnp.where(matches, shares[:, :, None], 0.0), axis=1)
    routed = jnp.sum(matches.astype(jnp.int32), axis=1)
    earlier = jnp.cumsum(routed, axis=0) - routed
    placed = (routed.T[:, None, :] == 1) & (
        earlier.T[:, None, :] == jnp.arange(slots, dtype=jnp.int32)[None, :, None]
    )
    slot_table = placed.astype(jnp.float32).reshape(experts * slots, STEPS)
    weight_table = (
        (placed.astype(jnp.float32) * coefficient.T[:, None, :]).reshape(experts * slots, STEPS).T
    )
    outgoing = jnp.dot(
        slot_table.astype(jnp.bfloat16), normed, preferred_element_type=jnp.float32
    ).astype(jnp.bfloat16)
    outgoing = outgoing.reshape(n_ep, exp_local, slots, width)
    copies = jnp.broadcast_to(outgoing[None], (n_sec,) + outgoing.shape).reshape(
        (n_sec * n_ep,) + outgoing.shape[1:]
    )
    received = lax.all_to_all(copies, ("sec", "ep"), split_axis=0, concat_axis=0, tiled=True)
    rows_in = received[:, 0].reshape(-1, width)
    gate_value = jnp.dot(rows_in, w_gate[0], preferred_element_type=jnp.float32)
    up_value = jnp.dot(rows_in, w_up[0], preferred_element_type=jnp.float32)
    activated = (jax.nn.silu(gate_value) * up_value).astype(jnp.bfloat16)
    product = jnp.dot(activated, w_down[0], preferred_element_type=jnp.float32)
    outputs = [product.reshape(received.shape[0], slots, width)]
    partial_value = jnp.stack(outputs, axis=1)
    returned = lax.all_to_all(
        partial_value.astype(jnp.bfloat16), ("sec", "ep"), split_axis=0, concat_axis=0, tiled=True
    ).astype(partial_value.dtype)
    expert_out = jnp.sum(returned.reshape(n_sec, experts, slots, width), axis=0).astype(
        jnp.bfloat16
    )
    mixture = jnp.dot(
        weight_table,
        expert_out.reshape(experts * slots, width).astype(jnp.float32),
        precision=lax.Precision.HIGHEST,
        preferred_element_type=jnp.float32,
    )
    return (hidden + mixture).astype(jnp.bfloat16)[None]


def solution(mesh):
    placed = (
        P(("sec", "ep"), None, None, None),
        P(("sec", "ep"), None, None),
        P(("sec", "ep"), None, None),
        P(("sec", "ep")),
        P(("sec", "ep"), None, None),
        P(("sec", "ep"), None, None),
        P(("sec", "ep"), None, None),
        P(),
        P(("sec", "ep"), None, None),
        P(("sec", "ep"), None, None),
        P("ep", None, "sec"),
        P("ep", None, "sec"),
        P("ep", "sec", None),
    )
    return jax.shard_map(
        per_device,
        mesh=mesh,
        in_specs=placed,
        out_specs=P(("sec", "ep"), None, None),
        check_vma=False,
    )
```

profile of v0, /device:TPU:0, one launch (start us, length us, event | category | flops | bytes accessed | tf_op | source)
XLA Modules:
  0.0 319.9 jit_solution(6619711028290416372)
XLA Ops:
  7.4 14.1 %copy.40 = bf16[1,8192,576]{2,1,0:T(8,128)(2,1)} copy(bf16[1,8192,576]{1,2,0:T(8,128)(2,1)} %param.17) | data formatting | bytes 18874368 | tf_op args[2]
  21.6 57.8 %while.14 = (s32[]{:T(128)}, f32[128,1]{0,1:T(1,128)S(1)}, f32[128,1]{0,1:T(1,128)S(1)}, f32[128,512]{1,0:T(8,128)S(1)}, s32[]{:T(128)}, /*index=5*/s32[]{:T(128...) while((s32[]{:T(128)}, f32[128,1]{0,1:T(1,128)S(1)}, ...), condition=%wide.region_3.4_spmd, body=%wide.region_0.3_spmd.sunk | while | flops 143197568 | bytes 2647219 | solution.py:48
  29.5 1.4 fusion.65
  33.1 1.4 fusion.65
  36.7 1.4 fusion.65
  40.3 1.4 fusion.65
  43.9 1.4 fusion.65
  47.5 1.4 fusion.65
  51.1 1.4 fusion.65
  58.4 1.4 fusion.65
  65.6 1.4 fusion.65
  72.8 1.4 fusion.65
  80.1 14.4 %all_to_all.25 = bf16[1,4,32,512]{3,1,0,2:T(4,128)(2,1)S(1)} all-to-all(bf16[1,4,32,512]{3,1,0,2:T(4,128)(2,1)S(1)} %copy.41), channel_id=1, replica_groups=mesh['sec'=2,'ep'=16] {'sec','ep'}, dimensions={2} | all-to-all | bytes 262144 | tf_op jit(solution)/shard_map/all_to_all | solution.py:93
  94.5 2.6 fusion.19
  97.9 136.2 %all-reduce.3.cloned.1.call-done = f32[128,7168]{1,0:T(8,128)} async-done(((f32[128,7168]{1,0:T(8,128)}), f32[128,7168]{1,0:T(8,128)}) %all-reduce.3.cloned.1.call-update) | async-done | bytes 3670032
  237.2 28.0 %all_to_all.26 = bf16[32,1,2,7168]{3,2,1,0:T(2,128)(2,1)} all-to-all(bf16[32,1,2,7168]{3,2,1,0:T(2,128)(2,1)S(1)} %bitcast.117), channel_id=1, replica_groups=mesh['sec'=2,'ep'=16] {'sec','ep'}, dimensions={0} | all-to-all | bytes 1835008 | tf_op jit(solution)/shard_map/all_to_all | solution.py:130
  265.2 2.5 reshape_squeeze.11
  267.7 4.5 %fusion.17 = f32[64,512]{1,0:T(8,128)S(1)} fusion(bf16[64,7168]{1,0:T(8,128)(2,1)S(1)} %reshape_squeeze.11, bf16[1,7168,512]{2,1,0:T(8,128)(2,1)} %param.25), kind=kOutput, calls=%fused_computation.26 | convolution fusion | flops 469762048 | bytes 8388608 | tf_op jit(solution)/shard_map/dot_general | solution.py:132
  272.1 4.5 %fusion.26 = bf16[64,512]{1,0:T(8,128)(2,1)S(1)} fusion(bf16[64,7168]{1,0:T(8,128)(2,1)S(1)} %reshape_squeeze.11, bf16[1,7168,512]{2,1,0:T(8,128)(2,1)} %param.26, f32[64,512]{1,0:T(8,128)S(1)} %fusion.17), kind=kOutput, calls=%fused_computation.34 | convolution fusion | flops 469958656 | bytes 8454144 | tf_op jit(solution)/shard_map/dot_general | solution.py:133
  276.6 4.5 %fusion.10 = bf16[32,1,2,7168]{3,0,2,1:T(8,128)(2,1)S(1)} fusion(bf16[1,512,7168]{2,1,0:T(8,128)(2,1)} %param.27, bf16[32,2,512]{2,1,0:T(2,128)(2,1)S(1)} %dot_general.42), kind=kOutput, calls=%fused_computation.17 | convolution fusion | flops 470220800 | bytes 8323072 | tf_op jit(solution)/shard_map/dot_general | solution.py:135
  281.1 1.9 copy.48
  283.0 2.6 all-to-all-start.2
  286.0 24.0 %all-to-all-done.2 = bf16[32,1,2,7168]{3,2,1,0:T(2,128)(2,1)S(1)} async-done(((bf16[32,1,2,7168]{3,2,1,0:T(2,128)(2,1)}), bf16[32,1,2,7168]{3,2,1,0:T(2,128)(2,1)S(1)}, u32[]{:S(2)}, u32[]{:S(2)}) %all-to-all-start.2) | async-done | bytes 917536 | tf_op jit(solution)/shard_map/all_to_all | solution.py:138
  311.1 1.9 fusion.13
  (158 shorter events, 48.6 us)
Async XLA Ops:
  6.5 88.0 %copy-start = (bf16[1,128,7168]{2,1,0:T(8,128)(2,1)S(1)}, bf16[1,128,7168]{2,1,0:T(8,128)(2,1)}, u32[]{:S(2)}) copy-start(bf16[1,128,7168]{2,1,0:T(8,128)(2,1)} %param.24) | copy-start | bytes 5505028
  6.5 227.6 %all-reduce.3.cloned.1.call-start = ((), (), s32[]{:S(2)}) async-start(), calls=%async_computation.3 | async-start | bytes 7340032
  7.3 14.2 %copy-start.1 = (bf16[1,4,32,576]{3,2,1,0:T(8,128)(2,1)S(1)}, bf16[1,4,32,576]{3,2,1,0:T(8,128)(2,1)}, u32[]{:S(2)}) copy-start(bf16[1,4,32,576]{3,2,1,0:T(8,128)(2,1)} %param.15) | copy-start | bytes 442372
  21.5 58.0 %copy-start.7 = (bf16[1,4,576]{2,1,0:T(4,128)(2,1)S(1)}, bf16[1,4,576]{2,1,0:T(4,128)(2,1)}, u32[]{:S(2)}) copy-start(bf16[1,4,576]{2,1,0:T(4,128)(2,1)} %param.16) | copy-start | bytes 13828
  21.5 73.0 %copy-start.3 = (bf16[1,512,128]{2,1,0:T(8,128)(2,1)S(1)}, bf16[1,512,128]{2,1,0:T(8,128)(2,1)}, u32[]{:S(2)}) copy-start(bf16[1,512,128]{2,1,0:T(8,128)(2,1)} %param.23) | copy-start | bytes 393220
  79.3 17.8 %copy-start.5 = (s32[1,4,8]{2,1,0:T(4,128)S(1)}, s32[1,4,8]{2,1,0:T(4,128)}, u32[]{:S(2)}) copy-start(s32[1,4,8]{2,1,0:T(4,128)} %param.19) | copy-start | bytes 388
  79.3 18.4 %copy-start.4 = (bf16[7168]{0:T(1024)(128)(2,1)S(1)}, bf16[7168]{0:T(1024)(128)(2,1)}, u32[]{:S(2)}) copy-start(bf16[7168]{0:T(1024)(128)(2,1)} %param.22) | copy-start | bytes 43012
  79.4 154.7 %copy-start.2 = (bf16[1,4,7168]{2,1,0:T(4,128)(2,1)S(1)}, bf16[1,4,7168]{2,1,0:T(4,128)(2,1)}, u32[]{:S(2)}) copy-start(bf16[1,4,7168]{2,1,0:T(4,128)(2,1)} %param.21) | copy-start | bytes 172036
  276.6 9.0 %copy-start.6 = (f32[1,4,8]{2,1,0:T(4,128)S(1)}, f32[1,4,8]{2,1,0:T(4,128)}, u32[]{:S(2)}) copy-start(f32[1,4,8]{2,1,0:T(4,128)} %param.20) | copy-start | bytes 388
  283.0 27.0 %all-to-all-start.2 = ((bf16[32,1,2,7168]{3,2,1,0:T(2,128)(2,1)}), bf16[32,1,2,7168]{3,2,1,0:T(2,128)(2,1)S(1)}, u32[]{:S(2)}, u32[]{:S(2)}) async-start(bf16[32,1,2,7168]{3,2,1,0:T(2,128)(2,1)} %copy.48), calls=%async_computation.2 | async-start | bytes 1835008 | tf_op jit(solution)/shard_map/all_to_all | solution.py:138
Sparse Core Ops, SparseCore 0:
  97.3 136.7 all-reduce.2
where the time goes:
time: 323 us; the launch traced here: 320 us
  waiting for transfers between devices  160 us (50%)
  matrix products  64.3 us (20%)
  blocking collectives  42.4 us (13%)
  local copies, waits for them, and re-layouts  20.1 us (6%)
  other arithmetic  15.1 us (5%)
  between operations  14.5 us (4%)
    unnamed x2, waiting for transfers between devices  136 us
    all_to_all x1, blocking collectives, per_device(): lax.all_to_all(copies, ('sec', 'ep'), split_axis=0, concat_axis=0, tiled=...  28 us
    all_to_all x1, waiting for transfers between devices, per_device(): lax.all_to_all(partial_value.astype(jnp.bfloat16), ('sec', 'ep'), split_a...  24 us
    dot_general x17, matrix products, update(): lax.dot_general(query_rows, key_rows, contract, preferred_element_type=jn...  23.3 us
    dot_general x17, matrix products, update(): jnp.dot(weights.astype(jnp.bfloat16), key_rows[:, :LAT], preferred_elemen...  21.8 us
    all_to_all x1, blocking collectives, per_device(): lax.all_to_all(latent_out, ('sec', 'ep'), split_axis=2, concat_axis=0, ti...  14.4 us
    unnamed x17, local copies, waits for them, and re-layouts  14.2 us
    lt x16, other arithmetic, block_step(): visible = (positions < length)[None, :]  10.5 us
  transfers between devices with their start and end apart: 2, of which 2 were waited for; matrix products, arithmetic and copies ran while one was open for 0% of the time, Pallas kernels for 0%

commit v1 on v0

v1 whole, which is shorter than its diff:
```python
import functools
import math

import jax
import jax.numpy as jnp
from jax import lax
from jax.experimental import pallas as pl
from jax.experimental.pallas import tpu as pltpu
from jax.sharding import PartitionSpec as P

LAT = 512
ROPE = 64
VDIM = 128
STEPS = 4
TOPK = 8
BLK = 2048
SPAN = 8
AXES = ("sec", "ep")
NT = (((1,), (1,)), ((), ()))
BF = jnp.bfloat16
F32 = jnp.float32
VMEM_LIMIT = 16 * 1024 * 1024


def device_of(plane, place, n):
    return (place >> 2) * (n // 2) + plane * 4 + (place & 3)


def plane_groups(n):
    return [[device_of(b, p, n) for p in range(SPAN)] for b in range(n // SPAN)]


def line_groups(n):
    return [[device_of(b, p, n) for b in range(n // SPAN)] for p in range(SPAN)]


def chip_groups(n):
    return [[device_of(b, 2 * q + c, n) for q in range(4)] for b in range(n // SPAN) for c in range(2)]


def exchange(x, groups):
    return lax.all_to_all(x, AXES, 0, 0, axis_index_groups=groups, tiled=True)


def swap_core(x, n):
    return lax.ppermute(x, AXES, [(d, d ^ 1) for d in range(n)])


def iota2(shape, axis):
    return lax.broadcasted_iota(jnp.int32, shape, axis)


def one_hot(columns, count):
    return (iota2(columns.shape, 1) == columns).astype(BF)


def pick(matrix, rows):
    return jnp.dot(matrix, rows, preferred_element_type=F32)


def attend_kernel(n, len_ref, q_ref, new_ref, keys_ref, out_ref, m_ref, l_ref, acc_ref):
    rows = q_ref.shape[0]
    heads = rows // STEPS
    factor_base2 = (VDIM + ROPE) ** (-0.5) * math.log2(math.e)
    i = pl.program_id(0)
    length = len_ref[0]
    blk = keys_ref.shape[1]

    @pl.when(i == 0)
    def _():
        new = new_ref[...]
        s = lax.dot_general(q_ref[...], new, NT, preferred_element_type=F32)
        step = iota2(s.shape, 0) // heads
        s = jnp.where(iota2(s.shape, 1) <= step, s, -1e30)
        m = jnp.max(s, axis=1, keepdims=True)
        p = jnp.exp2((s - m) * factor_base2)
        m_ref[...] = m
        l_ref[...] = jnp.sum(p, axis=1, keepdims=True)
        acc_ref[...] = jnp.dot(p.astype(BF), new[:, :LAT], preferred_element_type=F32)

    def update(masked):
        keys = keys_ref[...]
        s = jnp.dot(q_ref[...], keys, preferred_element_type=F32)
        if masked:
            s = jnp.where(iota2(s.shape, 1) < length - i * blk, s, -1e30)
        m_old = m_ref[...]
        m = jnp.maximum(m_old, jnp.max(s, axis=1, keepdims=True))
        factor = jnp.exp2((m_old - m) * factor_base2)
        p = jnp.exp2((s - m) * factor_base2)
        m_ref[...] = m
        l_ref[...] = l_ref[...] * factor + jnp.sum(p, axis=1, keepdims=True)
        acc_ref[...] = acc_ref[...] * factor + lax.dot_general(
            p.astype(BF), keys[:LAT], NT, preferred_element_type=F32
        )

    pl.when((i + 1) * blk <= length)(functools.partial(update, False))
    pl.when((i * blk < length) & ((i + 1) * blk > length))(functools.partial(update, True))

    @pl.when(i == pl.num_programs(0) - 1)
    def _():
        out = (acc_ref[...] / l_ref[...]).astype(BF)
        r = iota2((rows, rows), 0)
        out_ref[...] = pick(one_hot((r % STEPS) * heads + r // STEPS, rows), out).astype(BF)


def attend(n, length, q, new, keys):
    rows, width = q.shape
    cached = keys.shape[1]
    blk = min(BLK, cached)

    def block(i, len_ref):
        return (0, jnp.minimum(i, (len_ref[0] - 1) // blk))

    def whole(i, len_ref):
        return (0, 0)

    return pl.pallas_call(
        functools.partial(attend_kernel, n),
        grid_spec=pltpu.PrefetchScalarGridSpec(
            num_scalar_prefetch=1,
            grid=(cached // blk,),
            in_specs=[
                pl.BlockSpec(q.shape, whole),
                pl.BlockSpec(new.shape, whole),
                pl.BlockSpec((width, blk), block),
            ],
            out_specs=pl.BlockSpec((rows, LAT), whole),
            scratch_shapes=[
                pltpu.VMEM((rows, 1), F32),
                pltpu.VMEM((rows, 1), F32),
                pltpu.VMEM((rows, LAT), F32),
            ],
        ),
        out_shape=jax.ShapeDtypeStruct((rows, LAT), BF),
        compiler_params=pltpu.CompilerParams(vmem_limit_bytes=58 * 1024 * 1024),
        cost_estimate=pl.CostEstimate(
            flops=2 * rows * cached * (width + LAT),
            bytes_accessed=2 * cached * width,
            transcendentals=rows * cached,
        ),
        name="attend",
    )(length, q, new, keys)


def values_kernel(n, latents_ref, uv_ref, out_ref):
    values = jnp.dot(latents_ref[...], uv_ref[...], preferred_element_type=F32).astype(BF)
    for p in range(SPAN):
        out_ref[p] = values


def project_kernel(n, values_ref, weights_ref, out_ref):
    planes = n // SPAN
    group = 4 * STEPS
    total = jnp.zeros((n * STEPS, weights_ref.shape[2]), F32)
    for p in range(SPAN):
        total += jnp.dot(values_ref[p], weights_ref[p, :VDIM], preferred_element_type=F32)
    total = total.astype(BF)
    for b in range(planes):
        for top in range(2):
            start = (top * planes + b) * group
            out_ref[b, top * group : (top + 1) * group] = total[start : start + group]


def expert_kernel(n, me_ref, here_ref, there_ref, gain_ref, routes_ref, gate_ref, up_ref, down_ref, near_ref, far_ref):
    planes = n // SPAN
    rows = n * STEPS
    me = me_ref[0]
    core = me % 2
    expert = me_ref[1]
    part = here_ref.shape[2]
    width = gate_ref.shape[0]
    gate = jnp.zeros((rows, gate_ref.shape[1]), F32)
    up = jnp.zeros((rows, up_ref.shape[1]), F32)
    square = jnp.zeros((rows, 1), F32)
    for ref, side in ((here_ref, core), (there_ref, 1 - core)):
        for q in range(4):
            start = pl.multiple_of((2 * q + side) * part, part)
            x = ref[q].astype(F32)
            square += jnp.sum(x * x, axis=1, keepdims=True)
            scaled = (x * gain_ref[:, pl.ds(start, part)].astype(F32)).astype(BF)
            gate += jnp.dot(scaled, gate_ref[pl.ds(start, part)], preferred_element_type=F32)
            up += jnp.dot(scaled, up_ref[pl.ds(start, part)], preferred_element_type=F32)
    norm = lax.rsqrt(square / width + 1e-06)
    gate = gate * norm
    act = (gate * jax.nn.sigmoid(gate) * (up * norm)).astype(BF)
    r = iota2((rows, rows), 0)
    c, q = r // (rows // 2), (r // (planes * STEPS)) % 4
    k, step = (r // STEPS) % planes, r % STEPS
    order = one_hot((k * SPAN + 2 * q + (c ^ core)) * STEPS + step, rows)
    act = pick(order, act).astype(BF)
    routes = pick(order, routes_ref[...])
    scores = routes[:, TOPK : 2 * TOPK] + routes[:, 2 * TOPK : 3 * TOPK]
    chosen = jnp.where(routes[:, :TOPK] == expert.astype(F32), scores, 0.0)
    coef = jnp.sum(chosen, axis=1, keepdims=True) / jnp.sum(scores, axis=1, keepdims=True) * 2.5
    for p in range(SPAN):
        out = jnp.dot(act, down_ref[:, p * part : (p + 1) * part], preferred_element_type=F32) * coef
        near_ref[:, p * part : (p + 1) * part] = out[: rows // 2].astype(BF)
        far_ref[:, p * part : (p + 1) * part] = out[rows // 2 :].astype(BF)


def single(kernel, n, out_shape, scalars, arrays, name, flops):
    return pl.pallas_call(
        functools.partial(kernel, n),
        in_specs=[pl.BlockSpec(memory_space=pltpu.SMEM)] * len(scalars)
        + [pl.BlockSpec(memory_space=pltpu.VMEM)] * len(arrays),
        out_shape=out_shape,
        compiler_params=pltpu.CompilerParams(vmem_limit_bytes=VMEM_LIMIT),
        cost_estimate=pl.CostEstimate(
            flops=flops, bytes_accessed=sum(2 * a.size for a in arrays), transcendentals=0
        ),
        name=name,
    )(*scalars, *arrays)


def per_device(
    queries,
    new_latent,
    cache_latent,
    cache_len,
    route_ids,
    route_scores,
    residual,
    norm_gain,
    w_uv,
    w_out,
    w_gate,
    w_up,
    w_down,
):
    n_ep = lax.axis_size("ep")
    n = lax.axis_size("sec") * n_ep
    planes = n // SPAN
    heads = queries.shape[2]
    width = residual.shape[2]
    part = width // SPAN
    rows = n * STEPS
    me = lax.axis_index(AXES).astype(jnp.int32)
    everyone, planes_of, lines, chips = None, plane_groups(n), line_groups(n), chip_groups(n)

    with jax.named_scope("share_weights"):
        high = route_scores[0].astype(BF)
        low = (route_scores[0] - high.astype(F32)).astype(BF)
        routes = jnp.concatenate([route_ids[0].astype(BF), high, low], axis=1)
        routes = jnp.pad(routes, ((0, 0), (0, part - 3 * TOPK)))
        by_part = jnp.concatenate(
            [
                w_out[0].reshape(VDIM, SPAN, part),
                residual[0].reshape(STEPS, SPAN, part),
                jnp.broadcast_to(routes[:, None], (STEPS, SPAN, part)),
                jnp.zeros((16 - 2 * STEPS, SPAN, part), BF),
            ],
            axis=0,
        )
        shared = exchange(jnp.swapaxes(by_part, 0, 1), planes_of)

    with jax.named_scope("attention"):
        latents = attend(
            n,
            cache_len,
            queries[0].reshape(STEPS * heads, queries.shape[3]),
            new_latent[0],
            jnp.swapaxes(cache_latent[0], 0, 1),
        )

    with jax.named_scope("to_heads"):
        latents = exchange(latents.reshape(n, STEPS, LAT), everyone)
        values = single(
            values_kernel,
            n,
            jax.ShapeDtypeStruct((SPAN, rows, VDIM), BF),
            [],
            [latents.reshape(rows, LAT), w_uv[0]],
            "head_values",
            2 * rows * LAT * VDIM,
        )
        values = exchange(values, planes_of)

    with jax.named_scope("project"):
        parts = single(
            project_kernel,
            n,
            jax.ShapeDtypeStruct((planes, SPAN * STEPS, part), BF),
            [],
            [values, shared],
            "project",
            2 * rows * SPAN * VDIM * part,
        )
        parts = exchange(parts, lines)
        own = shared[:, VDIM : VDIM + STEPS].reshape(SPAN * STEPS, part)
        hidden = (jnp.sum(parts.astype(F32), axis=0) + own.astype(F32)).astype(BF)
        routes = shared[:, VDIM + STEPS : VDIM + 2 * STEPS, :128].reshape(SPAN * STEPS, 128)

    with jax.named_scope("spread_hidden"):
        along = jnp.concatenate([hidden, routes], axis=1)
        along = exchange(jnp.broadcast_to(along[None], (planes,) + along.shape), lines)
        along = along.reshape(rows, part + 128)
        routes = along[:, part:]
        here = exchange(jnp.broadcast_to(along[None, :, :part], (4, rows, part)), chips)
        there = swap_core(here, n)

    with jax.named_scope("experts"):
        near, far = single(
            expert_kernel,
            n,
            [jax.ShapeDtypeStruct((rows // 2, width), BF)] * 2,
            [jnp.stack([me, me % n_ep])],
            [here, there, norm_gain.reshape(1, width), routes, w_gate[0], w_up[0], w_down[0]],
            "experts",
            6 * rows * width * w_gate.shape[2],
        )

    with jax.named_scope("own_hidden"):
        core = me % 2
        plane, place = (me // 4) % planes, (me // (n // 2)) * 4 + me % 4
        start = (plane * SPAN + place) * STEPS
        own = [lax.dynamic_slice_in_dim(x, start, STEPS, axis=1) for x in (here, there)]
        own = [jnp.where(core == c, own[0], own[1]) for c in range(2)]
        own = jnp.stack(own, axis=1).reshape(SPAN, STEPS, part)
        own = jnp.swapaxes(own, 0, 1).reshape(STEPS, width)

    with jax.named_scope("collect"):
        total = (near.astype(F32) + swap_core(far, n).astype(F32)).astype(BF)
        total = exchange(total.reshape(4, planes * STEPS, width), chips)
        total = jnp.sum(total.astype(F32), axis=0).astype(BF)
        total = exchange(total.reshape(planes, STEPS, width), lines)
        result = jnp.sum(total.astype(F32), axis=0) + own.astype(F32)
        return result.astype(BF)[None]


def solution(mesh):
    placed = (
        P(("sec", "ep"), None, None, None),
        P(("sec", "ep"), None, None),
        P(("sec", "ep"), None, None),
        P(("sec", "ep")),
        P(("sec", "ep"), None, None),
        P(("sec", "ep"), None, None),
        P(("sec", "ep"), None, None),
        P(),
        P(("sec", "ep"), None, None),
        P(("sec", "ep"), None, None),
        P("ep", None, "sec"),
        P("ep", None, "sec"),
        P("ep", "sec", None),
    )
    return jax.shard_map(
        per_device,
        mesh=mesh,
        in_specs=placed,
        out_specs=P(("sec", "ep"), None, None),
        check_vma=False,
    )
```

time: 323 us -> 153 us (0.47)
  waiting for transfers between devices: 160 us -> 24.9 us
  matrix products: 64.3 us -> 0 us
  blocking collectives: 42.4 us -> 68.1 us
  starting transfers between devices: 2.64 us -> 21.2 us
  Pallas kernels: 0 us -> 14.4 us
  between operations: 14.5 us -> 0.89 us
  other arithmetic: 15.1 us -> 4.89 us
    unnamed x2 -> x0, waiting for transfers between devices: 136 us -> none
    dot_general x40 -> x0, matrix products: 64.3 us -> none  [the longest x17 23.3 us: update(): lax.dot_general(query_rows, key_rows, contract, preferred_element_type=jn...]
    all_to_all x2 -> x4, blocking collectives: 42.4 us -> 68.1 us  [exchange(): return lax.all_to_all(x, AXES, 0, 0, axis_index_groups=groups, tiled=True)]
    all_to_all x1 -> x4, starting transfers between devices: 2.63 us -> 21 us  [exchange(): return lax.all_to_all(x, AXES, 0, 0, axis_index_groups=groups, tiled=True)]
    pallas_call x0 -> x4, Pallas kernels: none -> 14.4 us  [the longest x1 7.86 us: attend(): pl.pallas_call(functools.partial(attend_kernel, n), grid_spec=pltpu.Prefe...]
    lt x16 -> x0, other arithmetic: 10.5 us -> none  [block_step(): visible = (positions < length)[None, :]]
    ppermute x0 -> x2, waiting for transfers between devices: none -> 4.68 us  [swap_core(): return lax.ppermute(x, AXES, [(d, d ^ 1) for d in range(n)])]
    all_to_all x1 -> x4, waiting for transfers between devices: 24 us -> 20.2 us  [exchange(): return lax.all_to_all(x, AXES, 0, 0, axis_index_groups=groups, tiled=True)]
  transfers between devices with their start and end apart: 2 -> 6, of which waited for: 2 -> 6; matrix products, arithmetic and copies ran while one was open for 0% -> 6% of each run, Pallas kernels for 0% -> 0%
where the time goes in v1:
time: 153 us; the launch traced here: 152 us
  blocking collectives  68.1 us (45%)
  waiting for transfers between devices  24.9 us (16%)
  starting transfers between devices  21.2 us (14%)
  local copies, waits for them, and re-layouts  18 us (12%)
  Pallas kernels  14.4 us (9%)
  other arithmetic  4.89 us (3%)
    all_to_all x4, blocking collectives, exchange(): return lax.all_to_all(x, AXES, 0, 0, axis_index_groups=groups, tiled=True)  68.1 us
    all_to_all x4, starting transfers between devices, exchange(): return lax.all_to_all(x, AXES, 0, 0, axis_index_groups=groups, tiled=True)  21 us
    all_to_all x4, waiting for transfers between devices, exchange(): return lax.all_to_all(x, AXES, 0, 0, axis_index_groups=groups, tiled=True)  20.2 us
    unnamed x17, local copies, waits for them, and re-layouts  12.6 us
    pallas_call x1, Pallas kernels, attend(): pl.pallas_call(functools.partial(attend_kernel, n), grid_spec=pltpu.Prefe...  7.86 us
    pallas_call x3, Pallas kernels, single(): pl.pallas_call(functools.partial(kernel, n), in_specs=[pl.BlockSpec(memor...  6.52 us
    ppermute x2, waiting for transfers between devices, swap_core(): return lax.ppermute(x, AXES, [(d, d ^ 1) for d in range(n)])  4.68 us
    transpose x1, other arithmetic, per_device(): shared = exchange(jnp.swapaxes(by_part, 0, 1), planes_of)  3.39 us
  transfers between devices with their start and end apart: 6, of which 6 were waited for; matrix products, arithmetic and copies ran while one was open for 6% of the time, Pallas kernels for 0%

profile of v1, /device:TPU:0, one launch (start us, length us, event | category | flops | bytes accessed | tf_op | source)
XLA Modules:
  0.0 152.3 jit_solution(10943398232105532857)
XLA Ops:
  0.7 7.9 %attend.1 = bf16[128,512]{1,0:T(8,128)(2,1)} custom-call(s32[1]{0:T(128)S(6)} %copy.20.len_ref, bf16[128,576]{1,0:T(8,128)(2,1)} %bitcast.49, bf16[4,576]{1,0:T(4,128)(2,1)} %bitcast.52, bf16[576,8192]{1,0:T(8,128)(2,1)} %bitcast.43), custom_call_target="tpu_custom_call" | custom-call | flops 2281701376 | bytes 9437184 | tf_op jit(solution)/shard_map/attention/attend/pallas_call | solution.py:117
  8.5 1.6 %reshape.54 = bf16[32,4,512]{2,1,0:T(4,128)(2,1)} reshape(bf16[128,512]{1,0:T(8,128)(2,1)} %attend.1) | data formatting | bytes 262144 | tf_op jit(solution)/shard_map/to_heads/reshape | solution.py:266
  10.1 8.8 %all-to-all-start = ((bf16[32,4,512]{2,1,0:T(4,128)(2,1)}), bf16[32,4,512]{2,1,0:T(4,128)(2,1)S(1)}, u32[]{:S(2)}, u32[]{:S(2)}) async-start(bf16[32,4,512]{2,1,0:T(4,128)(2,1)} %reshape.54), calls=%async_computation | async-start | bytes 262144 | tf_op jit(solution)/shard_map/to_heads/all_to_all | solution.py:42
  19.0 3.3 %copy.17 = bf16[1,128,7168]{1,2,0:T(8,128)(2,1)S(1)} copy(bf16[1,128,7168]{2,1,0:T(8,128)(2,1)} %param.22) | data formatting | bytes 3670016 | tf_op args[9]
  22.3 2.7 %copy.18 = bf16[128,8,896]{2,0,1:T(8,128)(2,1)} copy(bf16[128,8,896]{0,2,1:T(8,128)(2,1)S(1)} %bitcast.44) | data formatting | bytes 3670016 | tf_op jit(solution)/shard_map/share_weights/reshape;share_weights/squeeze | solution.py:247
  25.1 2.0 %all-to-all-done = bf16[32,4,512]{2,1,0:T(4,128)(2,1)S(1)} async-done(((bf16[32,4,512]{2,1,0:T(4,128)(2,1)}), bf16[32,4,512]{2,1,0:T(4,128)(2,1)S(1)}, u32[]{:S(2)}, u32[]{:S(2)}) %all-to-all-start) | async-done | bytes 131104 | tf_op jit(solution)/shard_map/to_heads/all_to_all | solution.py:42
  28.1 3.4 %all-to-all-start.1 = ((bf16[8,128,128]{2,1,0:T(8,128)(2,1)}), bf16[8,128,128]{2,1,0:T(8,128)(2,1)S(1)}, u32[]{:S(2)}, u32[]{:S(2)}) async-start(bf16[8,128,128]{2,1,0:T(8,128)(2,1)} %head_values.1), calls=%async_computation.1 | async-start | bytes 524288 | tf_op jit(solution)/shard_map/to_heads/all_to_all | solution.py:42
  31.6 3.4 %maximum_bitcast_fusion = bf16[8,144,896]{2,1,0:T(8,128)(2,1)} fusion(bf16[4,8,896]{2,0,1:T(4,128)(2,1)S(1)} %broadcast_in_dim.8, bf16[4,8,896]{2,0,1:T(4,128)(2,1)S(1)} %bitcast.50, bf16[128,8,896]{2,0,1:T(8,128)(2,1)} %copy.18, bf16[144]{0:T(256)(128)(2,1)S(1)} %pad.12.clone), kind=kLoop, calls=%fused_computation | loop fusion | flops 8257536 | bytes 4014368 | tf_op jit(solution)/shard_map/share_weights/transpose | solution.py:254
  34.9 2.6 %all-to-all-done.1.values_ref = bf16[8,128,128]{2,1,0:T(8,128)(2,1)S(1)} async-done(((bf16[8,128,128]{2,1,0:T(8,128)(2,1)}), bf16[8,128,128]{2,1,0:T(8,128)(2,1)S(1)}, u32[]{:S(2)}, u32[]{:S(2)}) %all-to-all-start.1) | async-done | bytes 262176 | tf_op jit(solution)/shard_map/to_heads/all_to_all | solution.py:42
  37.5 29.3 %all_to_all.40.weights_ref = bf16[8,144,896]{2,1,0:T(8,128)(2,1)S(1)} all-to-all(bf16[8,144,896]{2,1,0:T(8,128)(2,1)} %maximum_bitcast_fusion), channel_id=1, replica_groups={{0,1,2,3,16,17,18,19},{4,5,6,7,20,21,22,23},{8,9,10,11,24,25,26,27},{12..., dimensions={0} | all-to-all | bytes 4128768 | tf_op jit(solution)/shard_map/share_weights/all_to_all | solution.py:42
  66.8 1.3 project.1
  68.1 3.4 %all-to-all-start.3 = ((bf16[4,32,896]{2,1,0:T(8,128)(2,1)}), bf16[4,32,896]{2,1,0:T(8,128)(2,1)S(1)}, u32[]{:S(2)}, u32[]{:S(2)}) async-start(bf16[4,32,896]{2,1,0:T(8,128)(2,1)} %project.1), calls=%async_computation.3 | async-start | bytes 458752 | tf_op jit(solution)/shard_map/project/all_to_all | solution.py:42
  71.6 8.2 %all-to-all-done.3 = bf16[4,32,896]{2,1,0:T(8,128)(2,1)S(1)} async-done(((bf16[4,32,896]{2,1,0:T(8,128)(2,1)}), bf16[4,32,896]{2,1,0:T(8,128)(2,1)S(1)}, u32[]{:S(2)}, u32[]{:S(2)}) %all-to-all-start.3) | async-done | bytes 229408 | tf_op jit(solution)/shard_map/project/all_to_all | solution.py:42
  79.9 10.7 %all_to_all.41 = bf16[4,32,1024]{2,1,0:T(8,128)(2,1)S(1)} all-to-all(bf16[4,32,1024]{2,1,0:T(8,128)(2,1)S(1)} %broadcast_in_dim.10), channel_id=1, replica_groups={{0,4,8,12},{1,5,9,13},{2,6,10,14},{3,7,11,15},{16,20,24,28},{17,21,25,2..., dimensions={0} | all-to-all | bytes 524288 | tf_op jit(solution)/shard_map/spread_hidden/all_to_all | solution.py:42
  90.7 12.3 %all_to_all.42.here_ref = bf16[4,128,896]{2,1,0:T(8,128)(2,1)S(1)} all-to-all(bf16[4,128,896]{2,1,0:T(8,128)(2,1)S(1)} %broadcast_in_dim.11), channel_id=1, replica_groups={{0,2,16,18},{1,3,17,19},{4,6,20,22},{5,7,21,23},{8,10,24,26},{9,11,25,2..., dimensions={0} | all-to-all | bytes 1835008 | tf_op jit(solution)/shard_map/spread_hidden/all_to_all | solution.py:42
  103.2 2.3 %collective-permute-done.there_ref = bf16[4,128,896]{2,1,0:T(8,128)(2,1)S(1)} collective-permute-done((bf16[4,128,896]{2,1,0:T(8,128)(2,1)S(1)}, bf16[4,128,896]{2,1,0:T(8,128)(2,1)S(1)}, u32[]{:S(2)}, u32[]{:S(2)}) %collective-permute-start) | collective-permute-done | bytes 917536 | tf_op jit(solution)/shard_map/spread_hidden/ppermute | solution.py:46
  105.5 3.1 %copy-done = bf16[1,7168,512]{2,1,0:T(8,128)(2,1)S(1)} copy-done((bf16[1,7168,512]{2,1,0:T(8,128)(2,1)S(1)}, bf16[1,7168,512]{2,1,0:T(8,128)(2,1)}, u32[]{:S(2)}) %copy-start) | copy-done | bytes 7340056
  108.6 3.1 %copy-done.1 = bf16[1,7168,512]{2,1,0:T(8,128)(2,1)S(1)} copy-done((bf16[1,7168,512]{2,1,0:T(8,128)(2,1)S(1)}, bf16[1,7168,512]{2,1,0:T(8,128)(2,1)}, u32[]{:S(2)}) %copy-start.1) | copy-done | bytes 7340056
  111.7 3.1 %copy-done.2 = bf16[1,512,7168]{2,1,0:T(8,128)(2,1)S(1)} copy-done((bf16[1,512,7168]{2,1,0:T(8,128)(2,1)S(1)}, bf16[1,512,7168]{2,1,0:T(8,128)(2,1)}, u32[]{:S(2)}) %copy-start.2) | copy-done | bytes 7340056
  114.8 4.3 %experts.1 = (bf16[64,7168]{1,0:T(8,128)(2,1)S(1)}, bf16[64,7168]{1,0:T(8,128)(2,1)S(1)}) custom-call(s32[2]{0:T(128)S(1)} %pad_add_fusion.me_ref, bf16[4,128,896]{2,1,0:T(8,128)(2,1)S(1)} %all_to_all.42.here_ref, bf16[4,128,896]{2,1,0:T(8,128)(2,1)S(1)} %collective-permute-done.there_ref, bf16[1,7168]{1,0:T(2,128)(2,1)S(1)} %reshape.58.gain_ref, ...), custom_call_target="tpu_custom_call" | custom-call | flops 2818572288 | bytes 23902208 | tf_op jit(solution)/shard_map/experts/experts/pallas_call | solution.py:202
  119.3 2.3 %collective-permute-done.1 = bf16[64,7168]{1,0:T(8,128)(2,1)S(1)} collective-permute-done((bf16[64,7168]{1,0:T(8,128)(2,1)S(1)}, bf16[64,7168]{1,0:T(8,128)(2,1)S(1)}, u32[]{:S(2)}, u32[]{:S(2)}) %collective-permute-start.1) | collective-permute-done | bytes 917536 | tf_op jit(solution)/shard_map/collect/ppermute | solution.py:46
  121.8 15.7 %all_to_all.43 = bf16[4,16,7168]{2,1,0:T(8,128)(2,1)S(1)} all-to-all(bf16[4,16,7168]{2,1,0:T(8,128)(2,1)S(1)} %bitcast.45), channel_id=1, replica_groups={{0,2,16,18},{1,3,17,19},{4,6,20,22},{5,7,21,23},{8,10,24,26},{9,11,25,2..., dimensions={0} | all-to-all | bytes 1835008 | tf_op jit(solution)/shard_map/collect/all_to_all | solution.py:42
  138.6 5.3 %all-to-all-start.7 = ((bf16[4,4,7168]{2,1,0:T(4,128)(2,1)}), bf16[4,4,7168]{2,1,0:T(4,128)(2,1)S(1)}, u32[]{:S(2)}, u32[]{:S(2)}) async-start(bf16[4,4,7168]{2,1,0:T(4,128)(2,1)} %reshape.60), calls=%async_computation.7 | async-start | bytes 458752 | tf_op jit(solution)/shard_map/collect/all_to_all | solution.py:42
  144.1 7.5 %all-to-all-done.7 = bf16[4,4,7168]{2,1,0:T(4,128)(2,1)S(1)} async-done(((bf16[4,4,7168]{2,1,0:T(4,128)(2,1)}), bf16[4,4,7168]{2,1,0:T(4,128)(2,1)S(1)}, u32[]{:S(2)}, u32[]{:S(2)}) %all-to-all-start.7) | async-done | bytes 229408 | tf_op jit(solution)/shard_map/collect/all_to_all | solution.py:42
  (43 shorter events, 3.7 us)
Async XLA Ops:
  0.7 18.3 %copy-start.7 = (f32[1,4,8]{2,1,0:T(4,128)S(1)}, f32[1,4,8]{2,1,0:T(4,128)}, u32[]{:S(2)}) copy-start(f32[1,4,8]{2,1,0:T(4,128)} %param.18) | copy-start | bytes 388
  10.1 17.1 %all-to-all-start = ((bf16[32,4,512]{2,1,0:T(4,128)(2,1)}), bf16[32,4,512]{2,1,0:T(4,128)(2,1)S(1)}, u32[]{:S(2)}, u32[]{:S(2)}) async-start(bf16[32,4,512]{2,1,0:T(4,128)(2,1)} %reshape.54), calls=%async_computation | async-start | bytes 262144 | tf_op jit(solution)/shard_map/to_heads/all_to_all | solution.py:42
  22.3 2.8 %copy-start.6 = (s32[1,4,8]{2,1,0:T(4,128)S(1)}, s32[1,4,8]{2,1,0:T(4,128)}, u32[]{:S(2)}) copy-start(s32[1,4,8]{2,1,0:T(4,128)} %param.17) | copy-start | bytes 388
  22.3 4.9 %copy-start.3 = (bf16[1,512,128]{2,1,0:T(8,128)(2,1)S(1)}, bf16[1,512,128]{2,1,0:T(8,128)(2,1)}, u32[]{:S(2)}) copy-start(bf16[1,512,128]{2,1,0:T(8,128)(2,1)} %param.21) | copy-start | bytes 393220
  22.3 9.2 %copy-start.4 = (bf16[1,4,7168]{2,1,0:T(4,128)(2,1)S(1)}, bf16[1,4,7168]{2,1,0:T(4,128)(2,1)}, u32[]{:S(2)}) copy-start(bf16[1,4,7168]{2,1,0:T(4,128)(2,1)} %param.19) | copy-start | bytes 172036
  28.1 9.4 %all-to-all-start.1 = ((bf16[8,128,128]{2,1,0:T(8,128)(2,1)}), bf16[8,128,128]{2,1,0:T(8,128)(2,1)S(1)}, u32[]{:S(2)}, u32[]{:S(2)}) async-start(bf16[8,128,128]{2,1,0:T(8,128)(2,1)} %head_values.1), calls=%async_computation.1 | async-start | bytes 524288 | tf_op jit(solution)/shard_map/to_heads/all_to_all | solution.py:42
  68.1 11.7 %all-to-all-start.3 = ((bf16[4,32,896]{2,1,0:T(8,128)(2,1)}), bf16[4,32,896]{2,1,0:T(8,128)(2,1)S(1)}, u32[]{:S(2)}, u32[]{:S(2)}) async-start(bf16[4,32,896]{2,1,0:T(8,128)(2,1)} %project.1), calls=%async_computation.3 | async-start | bytes 458752 | tf_op jit(solution)/shard_map/project/all_to_all | solution.py:42
  79.9 23.1 %copy-start.5 = (bf16[7168]{0:T(1024)(128)(2,1)S(1)}, bf16[7168]{0:T(1024)(128)(2,1)}, u32[]{:S(2)}) copy-start(bf16[7168]{0:T(1024)(128)(2,1)} %param.20) | copy-start | bytes 43012
  103.0 2.5 %collective-permute-start = (bf16[4,128,896]{2,1,0:T(8,128)(2,1)S(1)}, bf16[4,128,896]{2,1,0:T(8,128)(2,1)S(1)}, u32[]{:S(2)}, u32[]{:S(2)}) collective-permute-start(bf16[4,128,896]{2,1,0:T(8,128)(2,1)S(1)} %all_to_all.42.here_ref), channel_id=1, source_target_pairs={{0,1},{1,0},{2,3},{3,2},{4,5},{5,4},{6,7},{7,6},{8,9},{9,8},{10,11... | collective-permute-start | bytes 2752520 | tf_op jit(solution)/shard_map/spread_hidden/ppermute | solution.py:46
  105.5 3.1 %copy-start = (bf16[1,7168,512]{2,1,0:T(8,128)(2,1)S(1)}, bf16[1,7168,512]{2,1,0:T(8,128)(2,1)}, u32[]{:S(2)}) copy-start(bf16[1,7168,512]{2,1,0:T(8,128)(2,1)} %param.23) | copy-start | bytes 22020100
  108.6 3.1 %copy-start.1 = (bf16[1,7168,512]{2,1,0:T(8,128)(2,1)S(1)}, bf16[1,7168,512]{2,1,0:T(8,128)(2,1)}, u32[]{:S(2)}) copy-start(bf16[1,7168,512]{2,1,0:T(8,128)(2,1)} %param.24) | copy-start | bytes 22020100
  111.7 3.1 %copy-start.2 = (bf16[1,512,7168]{2,1,0:T(8,128)(2,1)S(1)}, bf16[1,512,7168]{2,1,0:T(8,128)(2,1)}, u32[]{:S(2)}) copy-start(bf16[1,512,7168]{2,1,0:T(8,128)(2,1)} %param.25) | copy-start | bytes 22020100
  119.1 2.5 %collective-permute-start.1 = (bf16[64,7168]{1,0:T(8,128)(2,1)S(1)}, bf16[64,7168]{1,0:T(8,128)(2,1)S(1)}, u32[]{:S(2)}, u32[]{:S(2)}) collective-permute-start(bf16[64,7168]{1,0:T(8,128)(2,1)S(1)} %get-tuple-element.8), channel_id=1, source_target_pairs={{0,1},{1,0},{2,3},{3,2},{4,5},{5,4},{6,7},{7,6},{8,9},{9,8},{10,11... | collective-permute-start | bytes 2752520 | tf_op jit(solution)/shard_map/collect/ppermute | solution.py:46
  138.6 12.9 %all-to-all-start.7 = ((bf16[4,4,7168]{2,1,0:T(4,128)(2,1)}), bf16[4,4,7168]{2,1,0:T(4,128)(2,1)S(1)}, u32[]{:S(2)}, u32[]{:S(2)}) async-start(bf16[4,4,7168]{2,1,0:T(4,128)(2,1)} %reshape.60), calls=%async_computation.7 | async-start | bytes 458752 | tf_op jit(solution)/shard_map/collect/all_to_all | solution.py:42

commit v2 on v1

v2 whole, which is shorter than its diff:
```python
import functools
import math

import jax
import jax.numpy as jnp
from jax import lax
from jax.experimental import pallas as pl
from jax.experimental.pallas import tpu as pltpu
from jax.sharding import PartitionSpec as P

LAT = 512
ROPE = 64
VDIM = 128
STEPS = 4
TOPK = 8
BLK = 2048
SPAN = 8
AXES = ("sec", "ep")
NT = (((1,), (1,)), ((), ()))
BF = jnp.bfloat16
F32 = jnp.float32
VMEM_LIMIT = 16 * 1024 * 1024


def mask_of(n, q=0, c=0, k=0):
    return (q >> 1) * (n // 2) + k * 4 + (q & 1) * 2 + c


def swap(x, n, **differ):
    mask = mask_of(n, **differ)
    return lax.ppermute(x, AXES, [(d, d ^ mask) for d in range(n)])


def iota2(shape, axis):
    return lax.broadcasted_iota(jnp.int32, shape, axis)


def one_hot(columns, count):
    return (iota2(columns.shape, 1) == columns).astype(BF)


def pick(matrix, rows):
    return jnp.dot(matrix, rows, preferred_element_type=F32)


def attend_kernel(n, len_ref, q_ref, new_ref, keys_ref, out_ref, m_ref, l_ref, acc_ref):
    rows = q_ref.shape[0]
    heads = rows // STEPS
    factor_base2 = (VDIM + ROPE) ** (-0.5) * math.log2(math.e)
    i = pl.program_id(0)
    length = len_ref[0]
    blk = keys_ref.shape[1]

    @pl.when(i == 0)
    def _():
        new = new_ref[...]
        s = lax.dot_general(q_ref[...], new, NT, preferred_element_type=F32)
        step = iota2(s.shape, 0) // heads
        s = jnp.where(iota2(s.shape, 1) <= step, s, -1e30)
        m = jnp.max(s, axis=1, keepdims=True)
        p = jnp.exp2((s - m) * factor_base2)
        m_ref[...] = m
        l_ref[...] = jnp.sum(p, axis=1, keepdims=True)
        acc_ref[...] = jnp.dot(p.astype(BF), new[:, :LAT], preferred_element_type=F32)

    def update(masked):
        keys = keys_ref[...]
        s = jnp.dot(q_ref[...], keys, preferred_element_type=F32)
        if masked:
            s = jnp.where(iota2(s.shape, 1) < length - i * blk, s, -1e30)
        m_old = m_ref[...]
        m = jnp.maximum(m_old, jnp.max(s, axis=1, keepdims=True))
        factor = jnp.exp2((m_old - m) * factor_base2)
        p = jnp.exp2((s - m) * factor_base2)
        m_ref[...] = m
        l_ref[...] = l_ref[...] * factor + jnp.sum(p, axis=1, keepdims=True)
        acc_ref[...] = acc_ref[...] * factor + lax.dot_general(
            p.astype(BF), keys[:LAT], NT, preferred_element_type=F32
        )

    pl.when((i + 1) * blk <= length)(functools.partial(update, False))
    pl.when((i * blk < length) & ((i + 1) * blk > length))(functools.partial(update, True))

    @pl.when(i == pl.num_programs(0) - 1)
    def _():
        out = (acc_ref[...] / l_ref[...]).astype(BF)
        r = iota2((rows, rows), 0)
        moved = pick(one_hot((r % STEPS) * heads + r // STEPS, rows), out)
        out_ref[...] = moved.reshape(out_ref.shape).astype(BF)


def attend(n, length, q, new, keys):
    rows, width = q.shape
    cached = keys.shape[1]
    blk = min(BLK, cached)

    def block(i, len_ref):
        return (0, jnp.minimum(i, (len_ref[0] - 1) // blk))

    def whole(i, len_ref):
        return (0, 0)

    return pl.pallas_call(
        functools.partial(attend_kernel, n),
        grid_spec=pltpu.PrefetchScalarGridSpec(
            num_scalar_prefetch=1,
            grid=(cached // blk,),
            in_specs=[
                pl.BlockSpec(q.shape, whole),
                pl.BlockSpec(new.shape, whole),
                pl.BlockSpec((width, blk), block),
            ],
            out_specs=pl.BlockSpec((rows // STEPS, STEPS, LAT), lambda i, len_ref: (0, 0, 0)),
            scratch_shapes=[
                pltpu.VMEM((rows, 1), F32),
                pltpu.VMEM((rows, 1), F32),
                pltpu.VMEM((rows, LAT), F32),
            ],
        ),
        out_shape=jax.ShapeDtypeStruct((rows // STEPS, STEPS, LAT), BF),
        compiler_params=pltpu.CompilerParams(vmem_limit_bytes=56 * 1024 * 1024),
        cost_estimate=pl.CostEstimate(
            flops=2 * rows * cached * (width + LAT),
            bytes_accessed=2 * cached * width,
            transcendentals=rows * cached,
        ),
        name="attend",
    )(length, q, new, keys)


def values_kernel(n, latents_ref, uv_ref, *refs):
    out_ref = refs[-1]
    out_ref[...] = jnp.dot(latents_ref[...], uv_ref[...], preferred_element_type=F32).astype(BF)


def project_kernel(n, me_ref, *refs):
    values, weights, (keep_ref, give_ref, total_ref) = refs[:4], refs[4:8], refs[8:]
    planes = n // SPAN
    rows = n * STEPS
    group = 4 * STEPS
    me = me_ref[0]
    core, plane = me % 2, (me // 4) % planes
    part = keep_ref.shape[1]
    carried = jnp.concatenate([weights[q][VDIM:] for q in range(4)], axis=0)
    extra = carried.shape[0] // 4
    r = iota2((rows, 4 * extra), 0)
    differ = (r // STEPS) ^ me
    q = (differ // (n // 2)) * 2 + (differ // 2) % 2
    same = (differ % 2 == 0) & ((differ // 4) % planes == 0)
    total = pick(one_hot(jnp.where(same, q * extra + r % STEPS, -1), 4 * extra), carried)
    for q in range(4):
        total += jnp.dot(values[q][...], weights[q][:VDIM], preferred_element_type=F32)
    total_ref[...] = total
    for k in range(planes):
        for top in range(2):
            start = pl.multiple_of((top * planes + (plane ^ k)) * group, group)
            block = total_ref[pl.ds(start, group)]
            here = pl.ds((2 * k + top) * group, group)
            keep_ref[here] = jnp.where(core == 0, block[:, :part], block[:, part:])
            give_ref[here] = jnp.where(core == 0, block[:, part:], block[:, :part]).astype(BF)


def expert_kernel(n, me_ref, *refs):
    blocks, refs = refs[:8], refs[8:]
    gain_ref, gate_hbm, up_hbm, down_hbm, near_ref, far_ref, own_ref = refs[:7]
    gate_ref, up_ref, down_ref, gate_sem, up_sem, down_sem = refs[7:]
    planes = n // SPAN
    rows = n * STEPS
    me = me_ref[0]
    core, chip = me % 2, (me // (n // 2)) * 2 + (me // 2) % 2
    place = chip * 2 + core
    expert = me_ref[1]
    width = gate_ref.shape[0]
    part = width // SPAN

    starts = [
        pl.multiple_of(((chip ^ (i % 4)) * 2 + (core ^ (i // 4))) * part, part) for i in range(SPAN)
    ]
    copies = []
    for i in range(SPAN):
        here = pl.ds(starts[i], part)
        copies.append(
            (
                pltpu.make_async_copy(gate_hbm.at[here], gate_ref.at[here], gate_sem.at[i]),
                pltpu.make_async_copy(up_hbm.at[here], up_ref.at[here], up_sem.at[i]),
            )
        )
    downs = []
    for i in range(SPAN):
        here = (slice(None), pl.ds(i * part, part))
        downs.append(
            pltpu.make_async_copy(down_hbm.at[here], down_ref.at[here], down_sem.at[i])
        )
    for pair in copies:
        for copy in pair:
            copy.start()
    for copy in downs:
        copy.start()

    gate = jnp.zeros((rows, gate_ref.shape[1]), F32)
    up = jnp.zeros((rows, up_ref.shape[1]), F32)
    square = jnp.zeros((rows, 1), F32)
    r = iota2((own_ref.shape[0], rows), 0)
    mine = one_hot(jnp.where(r < STEPS, place * STEPS + r, -1), rows)
    for i in range(SPAN):
        here = pl.ds(starts[i], part)
        raw = blocks[i][:, :part]
        x = raw.astype(F32)
        square += jnp.sum(x * x, axis=1, keepdims=True)
        scaled = (x * gain_ref[:, here].astype(F32)).astype(BF)
        own_ref[:, here] = pick(mine, raw).astype(BF)
        copies[i][0].wait()
        gate += jnp.dot(scaled, gate_ref[here], preferred_element_type=F32)
        copies[i][1].wait()
        up += jnp.dot(scaled, up_ref[here], preferred_element_type=F32)
    norm = lax.rsqrt(square / width + 1e-06)
    gate = gate * norm
    act = (gate * jax.nn.sigmoid(gate) * (up * norm)).astype(BF)
    r = iota2((rows, rows), 0)
    c, q = r // (rows // 2), (r // (planes * STEPS)) % 4
    k, step = (r // STEPS) % planes, r % STEPS
    order = one_hot((k * SPAN + (place ^ (2 * q + c))) * STEPS + step, rows)
    act = pick(order, act).astype(BF)
    routes = pick(order, blocks[0][:, part:] + blocks[4][:, part:])
    scores = routes[:, TOPK : 2 * TOPK] + routes[:, 2 * TOPK : 3 * TOPK]
    chosen = jnp.where(routes[:, :TOPK] == expert.astype(F32), scores, 0.0)
    coef = jnp.sum(chosen, axis=1, keepdims=True) / jnp.sum(scores, axis=1, keepdims=True) * 2.5
    for p in range(SPAN):
        here = slice(p * part, (p + 1) * part)
        downs[p].wait()
        out = jnp.dot(act, down_ref[:, here], preferred_element_type=F32) * coef
        near_ref[:, here] = out[: rows // 2].astype(BF)
        far_ref[:, here] = out[rows // 2 :].astype(BF)


def run_experts(n, scalars, blocks, gain, w_gate, w_up, w_down):
    rows = n * STEPS
    width, units = w_gate.shape
    half = jax.ShapeDtypeStruct((rows // 2, width), BF)
    return pl.pallas_call(
        functools.partial(expert_kernel, n),
        in_specs=[pl.BlockSpec(memory_space=pltpu.SMEM)]
        + [pl.BlockSpec(memory_space=pltpu.VMEM)] * (len(blocks) + 1)
        + [pl.BlockSpec(memory_space=pl.ANY)] * 3,
        out_shape=[half, half, jax.ShapeDtypeStruct((16, width), BF)],
        scratch_shapes=[
            pltpu.VMEM((width, units), BF),
            pltpu.VMEM((width, units), BF),
            pltpu.VMEM((units, width), BF),
            pltpu.SemaphoreType.DMA((SPAN,)),
            pltpu.SemaphoreType.DMA((SPAN,)),
            pltpu.SemaphoreType.DMA((SPAN,)),
        ],
        compiler_params=pltpu.CompilerParams(vmem_limit_bytes=36 * 1024 * 1024),
        cost_estimate=pl.CostEstimate(
            flops=6 * rows * width * units,
            bytes_accessed=6 * width * units,
            transcendentals=rows * units,
        ),
        name="experts",
    )(scalars, *blocks, gain, w_gate, w_up, w_down)


def single(kernel, n, out_shape, scalars, arrays, name, flops, scratch=(), awaited=()):
    return pl.pallas_call(
        functools.partial(kernel, n),
        in_specs=[pl.BlockSpec(memory_space=pltpu.SMEM)] * len(scalars)
        + [pl.BlockSpec(memory_space=pltpu.VMEM)] * len(arrays)
        + [pl.BlockSpec(memory_space=pl.ANY)] * len(awaited),
        out_shape=out_shape,
        scratch_shapes=scratch,
        compiler_params=pltpu.CompilerParams(vmem_limit_bytes=VMEM_LIMIT),
        cost_estimate=pl.CostEstimate(
            flops=flops, bytes_accessed=sum(2 * a.size for a in arrays), transcendentals=0
        ),
        name=name,
    )(*scalars, *arrays, *awaited)


def per_device(
    queries,
    new_latent,
    cache_latent,
    cache_len,
    route_ids,
    route_scores,
    residual,
    norm_gain,
    w_uv,
    w_out,
    w_gate,
    w_up,
    w_down,
):
    n_ep = lax.axis_size("ep")
    n = lax.axis_size("sec") * n_ep
    planes = n // SPAN
    heads = queries.shape[2]
    width = residual.shape[2]
    part = width // SPAN
    rows = n * STEPS
    me = lax.axis_index(AXES).astype(jnp.int32)
    scalars = jnp.stack([me, me % n_ep])
    chip = (me // (n // 2)) * 2 + (me // 2) % 2

    with jax.named_scope("share_weights"):
        high = route_scores[0].astype(BF)
        low = (route_scores[0] - high.astype(F32)).astype(BF)
        routes = jnp.concatenate([route_ids[0].astype(BF), high, low], axis=1)
        routes = jnp.pad(routes, ((0, 16 - 2 * STEPS), (0, 2 * part - 3 * TOPK)))
        weights = []
        for q in range(4):
            start = (chip ^ q) * 2 * part
            piece = jnp.concatenate(
                [
                    lax.dynamic_slice(w_out[0], (0, start), (VDIM, 2 * part)),
                    lax.dynamic_slice(residual[0], (0, start), (STEPS, 2 * part)),
                    routes,
                ],
                axis=0,
            )
            weights.append(piece if q == 0 else swap(piece, n, q=q))

    with jax.named_scope("attention"):
        latents = attend(
            n,
            cache_len,
            queries[0].reshape(STEPS * heads, queries.shape[3]),
            new_latent[0],
            jnp.swapaxes(cache_latent[0], 0, 1),
        )

    with jax.named_scope("to_heads"):
        latents = lax.all_to_all(latents, AXES, 0, 0, tiled=True)
        values = single(
            values_kernel,
            n,
            jax.ShapeDtypeStruct((rows, VDIM), BF),
            [],
            [latents.reshape(rows, LAT), w_uv[0]],
            "head_values",
            2 * rows * LAT * VDIM,
            awaited=weights[1:],
        )
        values = [values] + [swap(values, n, q=q) for q in range(1, 4)]

    with jax.named_scope("project"):
        keep, give = single(
            project_kernel,
            n,
            [jax.ShapeDtypeStruct((rows, part), F32), jax.ShapeDtypeStruct((rows, part), BF)],
            [scalars],
            values + weights,
            "project",
            4 * rows * 4 * VDIM * part,
            [pltpu.VMEM((rows, 2 * part), F32)],
        )
        total = keep + swap(give, n, c=1).astype(F32)
        total = total.reshape(planes, SPAN * STEPS, part)
        hidden = total[0]
        for k in range(1, planes):
            hidden = hidden + swap(total[k].astype(BF), n, k=k).astype(F32)
        hidden = hidden.astype(BF)

    with jax.named_scope("spread_hidden"):
        routes = jnp.stack([w[VDIM + STEPS : VDIM + 2 * STEPS, :128] for w in weights])
        routes = routes[chip ^ jnp.arange(4)]
        routes = jnp.stack([jnp.where(me % 2 == c, routes, 0) for c in range(2)], axis=1)
        along = jnp.concatenate([hidden, routes.reshape(SPAN * STEPS, 128)], axis=1)
        along = jnp.concatenate([along] + [swap(along, n, k=k) for k in range(1, planes)], axis=0)
        blocks = [along] + [swap(along[:, :part], n, q=q) for q in range(1, 4)]
        blocks = blocks + [swap(x, n, c=1) for x in blocks]

    with jax.named_scope("experts"):
        near, far, own = run_experts(
            n, scalars, blocks, norm_gain.reshape(1, width), w_gate[0], w_up[0], w_down[0]
        )

    with jax.named_scope("collect"):
        total = near.astype(F32) + swap(far, n, c=1).astype(F32)
        total = total.reshape(4, planes * STEPS, width)
        kept = total[0]
        for q in range(1, 4):
            kept = kept + swap(total[q].astype(BF), n, q=q).astype(F32)
        kept = kept.reshape(planes, STEPS, width)
        result = kept[0] + own[:STEPS].astype(F32)
        for k in range(1, planes):
            result = result + swap(kept[k].astype(BF), n, k=k).astype(F32)
        return result.astype(BF)[None]


def solution(mesh):
    placed = (
        P(("sec", "ep"), None, None, None),
        P(("sec", "ep"), None, None),
        P(("sec", "ep"), None, None),
        P(("sec", "ep")),
        P(("sec", "ep"), None, None),
        P(("sec", "ep"), None, None),
        P(("sec", "ep"), None, None),
        P(),
        P(("sec", "ep"), None, None),
        P(("sec", "ep"), None, None),
        P("ep", None, "sec"),
        P("ep", None, "sec"),
        P("ep", "sec", None),
    )
    return jax.shard_map(
        per_device,
        mesh=mesh,
        in_specs=placed,
        out_specs=P(("sec", "ep"), None, None),
        check_vma=False,
    )
```

time: 153 us -> 133 us (0.87)
  blocking collectives: 68.1 us -> 0 us
  waiting for transfers between devices: 24.9 us -> 65.2 us
  starting transfers between devices: 21.2 us -> 37.4 us
  local copies, waits for them, and re-layouts: 18 us -> 7.21 us
  Pallas kernels: 14.4 us -> 19.8 us
  other arithmetic: 4.89 us -> 2.35 us
    all_to_all x4 -> x0, blocking collectives: 68.1 us -> none  [exchange(): return lax.all_to_all(x, AXES, 0, 0, axis_index_groups=groups, tiled=True)]
    ppermute x2 -> x27, waiting for transfers between devices: 4.68 us -> 62 us  [swap(): return lax.ppermute(x, AXES, [(d, d ^ mask) for d in range(n)])]
    ppermute x2 -> x27, starting transfers between devices: 0.21 us -> 26.8 us  [swap(): return lax.ppermute(x, AXES, [(d, d ^ mask) for d in range(n)])]
    all_to_all x4 -> x1, waiting for transfers between devices: 20.2 us -> 3.15 us  [per_device(): latents = lax.all_to_all(latents, AXES, 0, 0, tiled=True)]
    pallas_call x0 -> x1, Pallas kernels: none -> 11.8 us  [run_experts(): pl.pallas_call(functools.partial(expert_kernel, n), in_specs=[pl.BlockSpe...]
    all_to_all x4 -> x1, starting transfers between devices: 21 us -> 10.6 us  [per_device(): latents = lax.all_to_all(latents, AXES, 0, 0, tiled=True)]
    unnamed x17 -> x16, local copies, waits for them, and re-layouts: 12.6 us -> 6.19 us
    pallas_call x3 -> x2, Pallas kernels: 6.52 us -> 1.61 us  [single(): pl.pallas_call(functools.partial(kernel, n), in_specs=[pl.BlockSpec(memor...]
  transfers between devices with their start and end apart: 6 -> 28, of which waited for: 6 -> 23; matrix products, arithmetic and copies ran while one was open for 6% -> 2% of each run, Pallas kernels for 0% -> 0%
where the time goes in v2:
time: 133 us
  waiting for transfers between devices  65.2 us (49%)
  starting transfers between devices  37.4 us (28%)
  Pallas kernels  19.8 us (15%)
  local copies, waits for them, and re-layouts  7.21 us (5%)
  other arithmetic  2.35 us (2%)
    ppermute x27, waiting for transfers between devices, swap(): return lax.ppermute(x, AXES, [(d, d ^ mask) for d in range(n)])  62 us
    ppermute x27, starting transfers between devices, swap(): return lax.ppermute(x, AXES, [(d, d ^ mask) for d in range(n)])  26.8 us
    pallas_call x1, Pallas kernels, run_experts(): pl.pallas_call(functools.partial(expert_kernel, n), in_specs=[pl.BlockSpe...  11.8 us
    all_to_all x1, starting transfers between devices, per_device(): latents = lax.all_to_all(latents, AXES, 0, 0, tiled=True)  10.6 us
    pallas_call x1, Pallas kernels, attend(): pl.pallas_call(functools.partial(attend_kernel, n), grid_spec=pltpu.Prefe...  6.39 us
    unnamed x16, local copies, waits for them, and re-layouts  6.19 us
    all_to_all x1, waiting for transfers between devices, per_device(): latents = lax.all_to_all(latents, AXES, 0, 0, tiled=True)  3.15 us
  transfers between devices with their start and end apart: 28, of which 23 were waited for; matrix products, arithmetic and copies ran while one was open for 2% of the time, Pallas kernels for 0%

profile of v2, /device:TPU:0, one launch (start us, length us, event | category | flops | bytes accessed | tf_op | source)
XLA Modules:
  0.0 133.0 jit_solution(16297362125844286550)
XLA Ops:
  0.7 6.4 %attend.1 = bf16[32,4,512]{2,1,0:T(4,128)(2,1)} custom-call(s32[1]{0:T(128)S(6)} %copy.15.len_ref, bf16[128,576]{1,0:T(8,128)(2,1)} %bitcast.57, bf16[4,576]{1,0:T(4,128)(2,1)} %bitcast.60, bf16[576,8192]{1,0:T(8,128)(2,1)} %bitcast.55), custom_call_target="tpu_custom_call" | custom-call | flops 2281701376 | bytes 9437184 | tf_op jit(solution)/shard_map/attention/attend/pallas_call | solution.py:103
  7.1 10.6 %all-to-all-start = ((bf16[32,4,512]{2,1,0:T(4,128)(2,1)}), bf16[32,4,512]{2,1,0:T(4,128)(2,1)S(1)}, u32[]{:S(2)}, u32[]{:S(2)}) async-start(bf16[32,4,512]{2,1,0:T(4,128)(2,1)} %attend.1), calls=%async_computation | async-start | bytes 262144 | tf_op jit(solution)/shard_map/to_heads/all_to_all | solution.py:334
  19.1 1.6 %collective-permute-start.1 = (bf16[144,1792]{1,0:T(8,128)(2,1)}, bf16[144,1792]{1,0:T(8,128)(2,1)S(1)}, u32[]{:S(2)}, u32[]{:S(2)}) collective-permute-start(bf16[144,1792]{1,0:T(8,128)(2,1)} %get-tuple-element.37), channel_id=1, source_target_pairs={{0,16},{1,17},{2,18},{3,19},{4,20},{5,21},{6,22},{7,23},{8,24},{9,... | collective-permute-start | bytes 1548296 | tf_op jit(solution)/shard_map/share_weights/ppermute | solution.py:31
  22.7 3.2 %all-to-all-done = bf16[32,4,512]{2,1,0:T(4,128)(2,1)S(1)} async-done(((bf16[32,4,512]{2,1,0:T(4,128)(2,1)}), bf16[32,4,512]{2,1,0:T(4,128)(2,1)S(1)}, u32[]{:S(2)}, u32[]{:S(2)}) %all-to-all-start) | async-done | bytes 131104 | tf_op jit(solution)/shard_map/to_heads/all_to_all | solution.py:334
  25.9 8.6 %collective-permute-done.1.refs_1_.refs_6_ = bf16[144,1792]{1,0:T(8,128)(2,1)S(1)} collective-permute-done((bf16[144,1792]{1,0:T(8,128)(2,1)}, bf16[144,1792]{1,0:T(8,128)(2,1)S(1)}, u32[]{:S(2)}, u32[]{:S(2)}) %collective-permute-start.1) | collective-permute-done | bytes 516128 | tf_op jit(solution)/shard_map/share_weights/ppermute | solution.py:31
  34.5 11.6 %collective-permute-done.2.refs_2_.refs_7_ = bf16[144,1792]{1,0:T(8,128)(2,1)S(1)} collective-permute-done((bf16[144,1792]{1,0:T(8,128)(2,1)S(1)}, bf16[144,1792]{1,0:T(8,128)(2,1)S(1)}, u32[]{:S(2)}, u32[]{:S(2)}) %collective-permute-start.2) | collective-permute-done | bytes 516128 | tf_op jit(solution)/shard_map/share_weights/ppermute | solution.py:31
  57.4 2.3 %collective-permute-start.9 = (bf16[32,896]{1,0:T(8,128)(2,1)S(1)}, bf16[32,896]{1,0:T(8,128)(2,1)S(1)}, u32[]{:S(2)}, u32[]{:S(2)}) collective-permute-start(bf16[32,896]{1,0:T(8,128)(2,1)S(1)} %get-tuple-element.34), channel_id=1, source_target_pairs={{0,12},{1,13},{2,14},{3,15},{4,8},{5,9},{6,10},{7,11},{8,4},{9,5},... | collective-permute-start | bytes 172040 | tf_op jit(solution)/shard_map/project/ppermute | solution.py:31
  60.2 3.7 %collective-permute-done.9 = bf16[32,896]{1,0:T(8,128)(2,1)S(1)} collective-permute-done((bf16[32,896]{1,0:T(8,128)(2,1)S(1)}, bf16[32,896]{1,0:T(8,128)(2,1)S(1)}, u32[]{:S(2)}, u32[]{:S(2)}) %collective-permute-start.9) | collective-permute-done | bytes 57376 | tf_op jit(solution)/shard_map/project/ppermute | solution.py:31
  63.9 1.9 %collective-permute-done.8 = bf16[32,896]{1,0:T(8,128)(2,1)S(1)} collective-permute-done((bf16[32,896]{1,0:T(8,128)(2,1)S(1)}, bf16[32,896]{1,0:T(8,128)(2,1)S(1)}, u32[]{:S(2)}, u32[]{:S(2)}) %collective-permute-start.8) | collective-permute-done | bytes 57376 | tf_op jit(solution)/shard_map/project/ppermute | solution.py:31
  65.8 2.5 %collective-permute-start.12 = (bf16[32,1024]{1,0:T(8,128)(2,1)S(1)}, bf16[32,1024]{1,0:T(8,128)(2,1)S(1)}, u32[]{:S(2)}, u32[]{:S(2)}) collective-permute-start(bf16[32,1024]{1,0:T(8,128)(2,1)S(1)} %pad_maximum_fusion.5), channel_id=1, source_target_pairs={{0,12},{1,13},{2,14},{3,15},{4,8},{5,9},{6,10},{7,11},{8,4},{9,5},... | collective-permute-start | bytes 196616 | tf_op jit(solution)/shard_map/spread_hidden/ppermute | solution.py:31
  68.4 2.0 %collective-permute-start.10 = (bf16[32,1024]{1,0:T(8,128)(2,1)S(1)}, bf16[32,1024]{1,0:T(8,128)(2,1)S(1)}, u32[]{:S(2)}, u32[]{:S(2)}) collective-permute-start(bf16[32,1024]{1,0:T(8,128)(2,1)S(1)} %pad_maximum_fusion.5), channel_id=1, source_target_pairs={{0,4},{1,5},{2,6},{3,7},{4,0},{5,1},{6,2},{7,3},{8,12},{9,13},{10,... | collective-permute-start | bytes 196616 | tf_op jit(solution)/shard_map/spread_hidden/ppermute | solution.py:31
  70.3 2.4 %collective-permute-done.12 = bf16[32,1024]{1,0:T(8,128)(2,1)S(1)} collective-permute-done((bf16[32,1024]{1,0:T(8,128)(2,1)S(1)}, bf16[32,1024]{1,0:T(8,128)(2,1)S(1)}, u32[]{:S(2)}, u32[]{:S(2)}) %collective-permute-start.12) | collective-permute-done | bytes 65568 | tf_op jit(solution)/shard_map/spread_hidden/ppermute | solution.py:31
  72.7 1.7 %collective-permute-done.11 = bf16[32,1024]{1,0:T(8,128)(2,1)S(1)} collective-permute-done((bf16[32,1024]{1,0:T(8,128)(2,1)S(1)}, bf16[32,1024]{1,0:T(8,128)(2,1)S(1)}, u32[]{:S(2)}, u32[]{:S(2)}) %collective-permute-start.11) | collective-permute-done | bytes 65568 | tf_op jit(solution)/shard_map/spread_hidden/ppermute | solution.py:31
  74.5 2.3 %collective-permute-start.15 = (bf16[128,896]{1,0:T(8,128)(2,1)S(1)}, bf16[128,896]{1,0:T(8,128)(2,1)S(1)}, u32[]{:S(2)}, u32[]{:S(2)}) collective-permute-start(bf16[128,896]{1,0:T(8,128)(2,1)S(1)} %slice.105), channel_id=1, source_target_pairs={{0,18},{1,19},{2,16},{3,17},{4,22},{5,23},{6,20},{7,21},{8,26},{9,... | collective-permute-start | bytes 688136 | tf_op jit(solution)/shard_map/spread_hidden/ppermute | solution.py:31
  78.0 6.0 %collective-permute-done.15.refs_3_ = bf16[128,896]{1,0:T(8,128)(2,1)S(1)} collective-permute-done((bf16[128,896]{1,0:T(8,128)(2,1)S(1)}, bf16[128,896]{1,0:T(8,128)(2,1)S(1)}, u32[]{:S(2)}, u32[]{:S(2)}) %collective-permute-start.15) | collective-permute-done | bytes 229408 | tf_op jit(solution)/shard_map/spread_hidden/ppermute | solution.py:31
  84.0 3.5 %collective-permute-done.14.refs_2_ = bf16[128,896]{1,0:T(8,128)(2,1)S(1)} collective-permute-done((bf16[128,896]{1,0:T(8,128)(2,1)S(1)}, bf16[128,896]{1,0:T(8,128)(2,1)S(1)}, u32[]{:S(2)}, u32[]{:S(2)}) %collective-permute-start.14) | collective-permute-done | bytes 229408 | tf_op jit(solution)/shard_map/spread_hidden/ppermute | solution.py:31
  89.4 3.1 %copy-done = bf16[1,7168,512]{2,1,0:T(8,128)(2,1)S(1)} copy-done((bf16[1,7168,512]{2,1,0:T(8,128)(2,1)S(1)}, bf16[1,7168,512]{2,1,0:T(8,128)(2,1)}, u32[]{:S(2)}) %copy-start) | copy-done | bytes 7340056
  92.5 3.1 %copy-done.1 = bf16[1,7168,512]{2,1,0:T(8,128)(2,1)S(1)} copy-done((bf16[1,7168,512]{2,1,0:T(8,128)(2,1)S(1)}, bf16[1,7168,512]{2,1,0:T(8,128)(2,1)}, u32[]{:S(2)}) %copy-start.1) | copy-done | bytes 7340056
  95.5 11.8 %experts.1 = (bf16[64,7168]{1,0:T(8,128)(2,1)S(1)}, bf16[64,7168]{1,0:T(8,128)(2,1)S(1)}, bf16[16,7168]{1,0:T(8,128)(2,1)S(1)}) custom-call(s32[2]{0:T(128)S(1)} %pad_add_fusion.me_ref, bf16[128,1024]{1,0:T(8,128)(2,1)S(1)} %pad_maximum_fusion.4.refs_0_, bf16[128,896]{1,0:T(8,128)(2,1)S(1)} %collective-permute-done.13.refs_1_, ...), custom_call_target="tpu_custom_call" | custom-call | flops 2818572288 | bytes 22020096 | tf_op jit(solution)/shard_map/experts/experts/pallas_call | solution.py:240
  107.6 2.3 %collective-permute-done.20 = bf16[64,7168]{1,0:T(8,128)(2,1)S(1)} collective-permute-done((bf16[64,7168]{1,0:T(8,128)(2,1)S(1)}, bf16[64,7168]{1,0:T(8,128)(2,1)S(1)}, u32[]{:S(2)}, u32[]{:S(2)}) %collective-permute-start.20) | collective-permute-done | bytes 917536 | tf_op jit(solution)/shard_map/collect/ppermute | solution.py:31
  111.4 1.7 %collective-permute-start.23 = (bf16[16,7168]{1,0:T(8,128)(2,1)S(1)}, bf16[16,7168]{1,0:T(8,128)(2,1)S(1)}, u32[]{:S(2)}, u32[]{:S(2)}) collective-permute-start(bf16[16,7168]{1,0:T(8,128)(2,1)S(1)} %get-tuple-element.28), channel_id=1, source_target_pairs={{0,18},{1,19},{2,16},{3,17},{4,22},{5,23},{6,20},{7,21},{8,26},{9,... | collective-permute-start | bytes 688136 | tf_op jit(solution)/shard_map/collect/ppermute | solution.py:31
  113.7 9.1 %collective-permute-done.21 = bf16[16,7168]{1,0:T(8,128)(2,1)S(1)} collective-permute-done((bf16[16,7168]{1,0:T(8,128)(2,1)S(1)}, bf16[16,7168]{1,0:T(8,128)(2,1)S(1)}, u32[]{:S(2)}, u32[]{:S(2)}) %collective-permute-start.21) | collective-permute-done | bytes 229408 | tf_op jit(solution)/shard_map/collect/ppermute | solution.py:31
  125.9 2.0 %collective-permute-start.25 = (bf16[4,7168]{1,0:T(4,128)(2,1)S(1)}, bf16[4,7168]{1,0:T(4,128)(2,1)S(1)}, u32[]{:S(2)}, u32[]{:S(2)}) collective-permute-start(bf16[4,7168]{1,0:T(4,128)(2,1)S(1)} %get-tuple-element.32), channel_id=1, source_target_pairs={{0,8},{1,9},{2,10},{3,11},{4,12},{5,13},{6,14},{7,15},{8,0},{9,1},... | collective-permute-start | bytes 172040 | tf_op jit(solution)/shard_map/collect/ppermute | solution.py:31
  130.5 1.7 %collective-permute-done.25 = bf16[4,7168]{1,0:T(4,128)(2,1)S(1)} collective-permute-done((bf16[4,7168]{1,0:T(4,128)(2,1)S(1)}, bf16[4,7168]{1,0:T(4,128)(2,1)S(1)}, u32[]{:S(2)}, u32[]{:S(2)}) %collective-permute-start.25) | collective-permute-done | bytes 57376 | tf_op jit(solution)/shard_map/collect/ppermute | solution.py:31
  (83 shorter events, 27.0 us)
Async XLA Ops:
  7.1 18.8 %all-to-all-start = ((bf16[32,4,512]{2,1,0:T(4,128)(2,1)}), bf16[32,4,512]{2,1,0:T(4,128)(2,1)S(1)}, u32[]{:S(2)}, u32[]{:S(2)}) async-start(bf16[32,4,512]{2,1,0:T(4,128)(2,1)} %attend.1), calls=%async_computation | async-start | bytes 262144 | tf_op jit(solution)/shard_map/to_heads/all_to_all | solution.py:334
  19.1 15.3 %collective-permute-start.1 = (bf16[144,1792]{1,0:T(8,128)(2,1)}, bf16[144,1792]{1,0:T(8,128)(2,1)S(1)}, u32[]{:S(2)}, u32[]{:S(2)}) collective-permute-start(bf16[144,1792]{1,0:T(8,128)(2,1)} %get-tuple-element.37), channel_id=1, source_target_pairs={{0,16},{1,17},{2,18},{3,19},{4,20},{5,21},{6,22},{7,23},{8,24},{9,... | collective-permute-start | bytes 1548296 | tf_op jit(solution)/shard_map/share_weights/ppermute | solution.py:31
  20.7 25.3 %collective-permute-start.2 = (bf16[144,1792]{1,0:T(8,128)(2,1)S(1)}, bf16[144,1792]{1,0:T(8,128)(2,1)S(1)}, u32[]{:S(2)}, u32[]{:S(2)}) collective-permute-start(bf16[144,1792]{1,0:T(8,128)(2,1)S(1)} %get-tuple-element.38), channel_id=1, source_target_pairs={{0,18},{1,19},{2,16},{3,17},{4,22},{5,23},{6,20},{7,21},{8,26},{9,... | collective-permute-start | bytes 1548296 | tf_op jit(solution)/shard_map/share_weights/ppermute | solution.py:31
  22.2 24.6 %collective-permute-start = (bf16[144,1792]{1,0:T(8,128)(2,1)S(1)}, bf16[144,1792]{1,0:T(8,128)(2,1)S(1)}, u32[]{:S(2)}, u32[]{:S(2)}) collective-permute-start(bf16[144,1792]{1,0:T(8,128)(2,1)S(1)} %get-tuple-element.39), channel_id=1, source_target_pairs={{0,2},{1,3},{2,0},{3,1},{4,6},{5,7},{6,4},{7,5},{8,10},{9,11},{10,... | collective-permute-start | bytes 1548296 | tf_op jit(solution)/shard_map/share_weights/ppermute | solution.py:31
  47.0 4.9 %collective-permute-start.5 = (bf16[128,128]{1,0:T(8,128)(2,1)S(1)}, bf16[128,128]{1,0:T(8,128)(2,1)S(1)}, u32[]{:S(2)}, u32[]{:S(2)}) collective-permute-start(bf16[128,128]{1,0:T(8,128)(2,1)S(1)} %head_values.1.refs_0_), channel_id=1, source_target_pairs={{0,18},{1,19},{2,16},{3,17},{4,22},{5,23},{6,20},{7,21},{8,26},{9,... | collective-permute-start | bytes 98312 | tf_op jit(solution)/shard_map/to_heads/ppermute | solution.py:31
  48.3 3.9 %collective-permute-start.4 = (bf16[128,128]{1,0:T(8,128)(2,1)S(1)}, bf16[128,128]{1,0:T(8,128)(2,1)S(1)}, u32[]{:S(2)}, u32[]{:S(2)}) collective-permute-start(bf16[128,128]{1,0:T(8,128)(2,1)S(1)} %head_values.1.refs_0_), channel_id=1, source_target_pairs={{0,16},{1,17},{2,18},{3,19},{4,20},{5,21},{6,22},{7,23},{8,24},{9,... | collective-permute-start | bytes 98312 | tf_op jit(solution)/shard_map/to_heads/ppermute | solution.py:31
  48.9 3.9 %collective-permute-start.3 = (bf16[128,128]{1,0:T(8,128)(2,1)S(1)}, bf16[128,128]{1,0:T(8,128)(2,1)S(1)}, u32[]{:S(2)}, u32[]{:S(2)}) collective-permute-start(bf16[128,128]{1,0:T(8,128)(2,1)S(1)} %head_values.1.refs_0_), channel_id=1, source_target_pairs={{0,2},{1,3},{2,0},{3,1},{4,6},{5,7},{6,4},{7,5},{8,10},{9,11},{10,... | collective-permute-start | bytes 98312 | tf_op jit(solution)/shard_map/to_heads/ppermute | solution.py:31
  55.9 4.2 %collective-permute-start.7 = (bf16[32,896]{1,0:T(8,128)(2,1)S(1)}, bf16[32,896]{1,0:T(8,128)(2,1)S(1)}, u32[]{:S(2)}, u32[]{:S(2)}) collective-permute-start(bf16[32,896]{1,0:T(8,128)(2,1)S(1)} %get-tuple-element.33), channel_id=1, source_target_pairs={{0,4},{1,5},{2,6},{3,7},{4,0},{5,1},{6,2},{7,3},{8,12},{9,13},{10,... | collective-permute-start | bytes 172040 | tf_op jit(solution)/shard_map/project/ppermute | solution.py:31
  57.4 6.5 %collective-permute-start.9 = (bf16[32,896]{1,0:T(8,128)(2,1)S(1)}, bf16[32,896]{1,0:T(8,128)(2,1)S(1)}, u32[]{:S(2)}, u32[]{:S(2)}) collective-permute-start(bf16[32,896]{1,0:T(8,128)(2,1)S(1)} %get-tuple-element.34), channel_id=1, source_target_pairs={{0,12},{1,13},{2,14},{3,15},{4,8},{5,9},{6,10},{7,11},{8,4},{9,5},... | collective-permute-start | bytes 172040 | tf_op jit(solution)/shard_map/project/ppermute | solution.py:31
  59.7 6.1 %collective-permute-start.8 = (bf16[32,896]{1,0:T(8,128)(2,1)S(1)}, bf16[32,896]{1,0:T(8,128)(2,1)S(1)}, u32[]{:S(2)}, u32[]{:S(2)}) collective-permute-start(bf16[32,896]{1,0:T(8,128)(2,1)S(1)} %get-tuple-element.35), channel_id=1, source_target_pairs={{0,8},{1,9},{2,10},{3,11},{4,12},{5,13},{6,14},{7,15},{8,0},{9,1},... | collective-permute-start | bytes 172040 | tf_op jit(solution)/shard_map/project/ppermute | solution.py:31
  65.8 6.9 %collective-permute-start.12 = (bf16[32,1024]{1,0:T(8,128)(2,1)S(1)}, bf16[32,1024]{1,0:T(8,128)(2,1)S(1)}, u32[]{:S(2)}, u32[]{:S(2)}) collective-permute-start(bf16[32,1024]{1,0:T(8,128)(2,1)S(1)} %pad_maximum_fusion.5), channel_id=1, source_target_pairs={{0,12},{1,13},{2,14},{3,15},{4,8},{5,9},{6,10},{7,11},{8,4},{9,5},... | collective-permute-start | bytes 196616 | tf_op jit(solution)/shard_map/spread_hidden/ppermute | solution.py:31
  68.3 6.1 %collective-permute-start.11 = (bf16[32,1024]{1,0:T(8,128)(2,1)S(1)}, bf16[32,1024]{1,0:T(8,128)(2,1)S(1)}, u32[]{:S(2)}, u32[]{:S(2)}) collective-permute-start(bf16[32,1024]{1,0:T(8,128)(2,1)S(1)} %pad_maximum_fusion.5), channel_id=1, source_target_pairs={{0,8},{1,9},{2,10},{3,11},{4,12},{5,13},{6,14},{7,15},{8,0},{9,1},... | collective-permute-start | bytes 196616 | tf_op jit(solution)/shard_map/spread_hidden/ppermute | solution.py:31
  68.4 6.1 %collective-permute-start.10 = (bf16[32,1024]{1,0:T(8,128)(2,1)S(1)}, bf16[32,1024]{1,0:T(8,128)(2,1)S(1)}, u32[]{:S(2)}, u32[]{:S(2)}) collective-permute-start(bf16[32,1024]{1,0:T(8,128)(2,1)S(1)} %pad_maximum_fusion.5), channel_id=1, source_target_pairs={{0,4},{1,5},{2,6},{3,7},{4,0},{5,1},{6,2},{7,3},{8,12},{9,13},{10,... | collective-permute-start | bytes 196616 | tf_op jit(solution)/shard_map/spread_hidden/ppermute | solution.py:31
  74.5 9.5 %collective-permute-start.15 = (bf16[128,896]{1,0:T(8,128)(2,1)S(1)}, bf16[128,896]{1,0:T(8,128)(2,1)S(1)}, u32[]{:S(2)}, u32[]{:S(2)}) collective-permute-start(bf16[128,896]{1,0:T(8,128)(2,1)S(1)} %slice.105), channel_id=1, source_target_pairs={{0,18},{1,19},{2,16},{3,17},{4,22},{5,23},{6,20},{7,21},{8,26},{9,... | collective-permute-start | bytes 688136 | tf_op jit(solution)/shard_map/spread_hidden/ppermute | solution.py:31
  76.8 10.8 %collective-permute-start.14 = (bf16[128,896]{1,0:T(8,128)(2,1)S(1)}, bf16[128,896]{1,0:T(8,128)(2,1)S(1)}, u32[]{:S(2)}, u32[]{:S(2)}) collective-permute-start(bf16[128,896]{1,0:T(8,128)(2,1)S(1)} %slice.105), channel_id=1, source_target_pairs={{0,16},{1,17},{2,18},{3,19},{4,20},{5,21},{6,22},{7,23},{8,24},{9,... | collective-permute-start | bytes 688136 | tf_op jit(solution)/shard_map/spread_hidden/ppermute | solution.py:31
  77.5 10.1 %collective-permute-start.13 = (bf16[128,896]{1,0:T(8,128)(2,1)S(1)}, bf16[128,896]{1,0:T(8,128)(2,1)S(1)}, u32[]{:S(2)}, u32[]{:S(2)}) collective-permute-start(bf16[128,896]{1,0:T(8,128)(2,1)S(1)} %slice.105), channel_id=1, source_target_pairs={{0,2},{1,3},{2,0},{3,1},{4,6},{5,7},{6,4},{7,5},{8,10},{9,11},{10,... | collective-permute-start | bytes 688136 | tf_op jit(solution)/shard_map/spread_hidden/ppermute | solution.py:31
  78.0 10.1 %collective-permute-start.16 = (bf16[128,1024]{1,0:T(8,128)(2,1)S(1)}, bf16[128,1024]{1,0:T(8,128)(2,1)S(1)}, u32[]{:S(2)}, u32[]{:S(2)}) collective-permute-start(bf16[128,1024]{1,0:T(8,128)(2,1)S(1)} %pad_maximum_fusion.4.refs_0_), channel_id=1, source_target_pairs={{0,1},{1,0},{2,3},{3,2},{4,5},{5,4},{6,7},{7,6},{8,9},{9,8},{10,11... | collective-permute-start | bytes 786440 | tf_op jit(solution)/shard_map/spread_hidden/ppermute | solution.py:31
  84.0 4.1 %collective-permute-start.19 = (bf16[128,896]{1,0:T(8,128)(2,1)S(1)}, bf16[128,896]{1,0:T(8,128)(2,1)S(1)}, u32[]{:S(2)}, u32[]{:S(2)}) collective-permute-start(bf16[128,896]{1,0:T(8,128)(2,1)S(1)} %collective-permute-done.15.refs_3_), channel_id=1, source_target_pairs={{0,1},{1,0},{2,3},{3,2},{4,5},{5,4},{6,7},{7,6},{8,9},{9,8},{10,11... | collective-permute-start | bytes 688136 | tf_op jit(solution)/shard_map/spread_hidden/ppermute | solution.py:31
  110.2 12.7 %collective-permute-start.21 = (bf16[16,7168]{1,0:T(8,128)(2,1)S(1)}, bf16[16,7168]{1,0:T(8,128)(2,1)S(1)}, u32[]{:S(2)}, u32[]{:S(2)}) collective-permute-start(bf16[16,7168]{1,0:T(8,128)(2,1)S(1)} %get-tuple-element.27), channel_id=1, source_target_pairs={{0,2},{1,3},{2,0},{3,1},{4,6},{5,7},{6,4},{7,5},{8,10},{9,11},{10,... | collective-permute-start | bytes 688136 | tf_op jit(solution)/shard_map/collect/ppermute | solution.py:31
  111.4 11.5 %collective-permute-start.23 = (bf16[16,7168]{1,0:T(8,128)(2,1)S(1)}, bf16[16,7168]{1,0:T(8,128)(2,1)S(1)}, u32[]{:S(2)}, u32[]{:S(2)}) collective-permute-start(bf16[16,7168]{1,0:T(8,128)(2,1)S(1)} %get-tuple-element.28), channel_id=1, source_target_pairs={{0,18},{1,19},{2,16},{3,17},{4,22},{5,23},{6,20},{7,21},{8,26},{9,... | collective-permute-start | bytes 688136 | tf_op jit(solution)/shard_map/collect/ppermute | solution.py:31
  113.0 11.1 %collective-permute-start.22 = (bf16[16,7168]{1,0:T(8,128)(2,1)S(1)}, bf16[16,7168]{1,0:T(8,128)(2,1)S(1)}, u32[]{:S(2)}, u32[]{:S(2)}) collective-permute-start(bf16[16,7168]{1,0:T(8,128)(2,1)S(1)} %get-tuple-element.29), channel_id=1, source_target_pairs={{0,16},{1,17},{2,18},{3,19},{4,20},{5,21},{6,22},{7,23},{8,24},{9,... | collective-permute-start | bytes 688136 | tf_op jit(solution)/shard_map/collect/ppermute | solution.py:31
  124.3 5.0 %collective-permute-start.24 = (bf16[4,7168]{1,0:T(4,128)(2,1)S(1)}, bf16[4,7168]{1,0:T(4,128)(2,1)S(1)}, u32[]{:S(2)}, u32[]{:S(2)}) collective-permute-start(bf16[4,7168]{1,0:T(4,128)(2,1)S(1)} %get-tuple-element.30), channel_id=1, source_target_pairs={{0,4},{1,5},{2,6},{3,7},{4,0},{5,1},{6,2},{7,3},{8,12},{9,13},{10,... | collective-permute-start | bytes 172040 | tf_op jit(solution)/shard_map/collect/ppermute | solution.py:31
  124.4 6.1 %collective-permute-start.26 = (bf16[4,7168]{1,0:T(4,128)(2,1)S(1)}, bf16[4,7168]{1,0:T(4,128)(2,1)S(1)}, u32[]{:S(2)}, u32[]{:S(2)}) collective-permute-start(bf16[4,7168]{1,0:T(4,128)(2,1)S(1)} %get-tuple-element.31), channel_id=1, source_target_pairs={{0,12},{1,13},{2,14},{3,15},{4,8},{5,9},{6,10},{7,11},{8,4},{9,5},... | collective-permute-start | bytes 172040 | tf_op jit(solution)/shard_map/collect/ppermute | solution.py:31
  125.9 6.4 %collective-permute-start.25 = (bf16[4,7168]{1,0:T(4,128)(2,1)S(1)}, bf16[4,7168]{1,0:T(4,128)(2,1)S(1)}, u32[]{:S(2)}, u32[]{:S(2)}) collective-permute-start(bf16[4,7168]{1,0:T(4,128)(2,1)S(1)} %get-tuple-element.32), channel_id=1, source_target_pairs={{0,8},{1,9},{2,10},{3,11},{4,12},{5,13},{6,14},{7,15},{8,0},{9,1},... | collective-permute-start | bytes 172040 | tf_op jit(solution)/shard_map/collect/ppermute | solution.py:31
  (12 other events, 144.7 us)

commit v3 on v1

v3 whole, which is shorter than its diff:
```python
import functools
import math

import jax
import jax.numpy as jnp
from jax import lax
from jax.experimental import pallas as pl
from jax.experimental.pallas import tpu as pltpu
from jax.sharding import PartitionSpec as P

LAT = 512
ROPE = 64
VDIM = 128
STEPS = 4
TOPK = 8
BLK = 2048
SPAN = 8
AXES = ("sec", "ep")
NT = (((1,), (1,)), ((), ()))
BF = jnp.bfloat16
F32 = jnp.float32
VMEM_LIMIT = 16 * 1024 * 1024


def mask_of(n, q=0, c=0, k=0):
    return (q >> 1) * (n // 2) + k * 4 + (q & 1) * 2 + c


def swap(x, n, **differ):
    mask = mask_of(n, **differ)
    return lax.ppermute(x, AXES, [(d, d ^ mask) for d in range(n)])


def iota2(shape, axis):
    return lax.broadcasted_iota(jnp.int32, shape, axis)


def one_hot(columns, count):
    return (iota2(columns.shape, 1) == columns).astype(BF)


def pick(matrix, rows):
    return jnp.dot(matrix, rows, preferred_element_type=F32)


def attend_kernel(n, len_ref, q_ref, new_ref, keys_ref, out_ref, m_ref, l_ref, acc_ref):
    rows = q_ref.shape[0]
    heads = rows // STEPS
    factor_base2 = (VDIM + ROPE) ** (-0.5) * math.log2(math.e)
    i = pl.program_id(0)
    length = len_ref[0]
    blk = keys_ref.shape[1]

    @pl.when(i == 0)
    def _():
        new = new_ref[...]
        s = lax.dot_general(q_ref[...], new, NT, preferred_element_type=F32)
        step = iota2(s.shape, 0) // heads
        s = jnp.where(iota2(s.shape, 1) <= step, s, -1e30)
        m = jnp.max(s, axis=1, keepdims=True)
        p = jnp.exp2((s - m) * factor_base2)
        m_ref[...] = m
        l_ref[...] = jnp.sum(p, axis=1, keepdims=True)
        acc_ref[...] = jnp.dot(p.astype(BF), new[:, :LAT], preferred_element_type=F32)

    def update(masked):
        keys = keys_ref[...]
        s = jnp.dot(q_ref[...], keys, preferred_element_type=F32)
        if masked:
            s = jnp.where(iota2(s.shape, 1) < length - i * blk, s, -1e30)
        m_old = m_ref[...]
        m = jnp.maximum(m_old, jnp.max(s, axis=1, keepdims=True))
        factor = jnp.exp2((m_old - m) * factor_base2)
        p = jnp.exp2((s - m) * factor_base2)
        m_ref[...] = m
        l_ref[...] = l_ref[...] * factor + jnp.sum(p, axis=1, keepdims=True)
        acc_ref[...] = acc_ref[...] * factor + lax.dot_general(
            p.astype(BF), keys[:LAT], NT, preferred_element_type=F32
        )

    pl.when((i + 1) * blk <= length)(functools.partial(update, False))
    pl.when((i * blk < length) & ((i + 1) * blk > length))(functools.partial(update, True))

    @pl.when(i == pl.num_programs(0) - 1)
    def _():
        out = (acc_ref[...] / l_ref[...]).astype(BF)
        r = iota2((rows, rows), 0)
        moved = pick(one_hot((r % STEPS) * heads + r // STEPS, rows), out)
        out_ref[...] = moved.reshape(out_ref.shape).astype(BF)


def attend(n, length, q, new, keys):
    rows, width = q.shape
    cached = keys.shape[1]
    blk = min(BLK, cached)

    def block(i, len_ref):
        return (0, jnp.minimum(i, (len_ref[0] - 1) // blk))

    def whole(i, len_ref):
        return (0, 0)

    return pl.pallas_call(
        functools.partial(attend_kernel, n),
        grid_spec=pltpu.PrefetchScalarGridSpec(
            num_scalar_prefetch=1,
            grid=(cached // blk,),
            in_specs=[
                pl.BlockSpec(q.shape, whole),
                pl.BlockSpec(new.shape, whole),
                pl.BlockSpec((width, blk), block),
            ],
            out_specs=pl.BlockSpec((rows // STEPS, STEPS, LAT), lambda i, len_ref: (0, 0, 0)),
            scratch_shapes=[
                pltpu.VMEM((rows, 1), F32),
                pltpu.VMEM((rows, 1), F32),
                pltpu.VMEM((rows, LAT), F32),
            ],
        ),
        out_shape=jax.ShapeDtypeStruct((rows // STEPS, STEPS, LAT), BF),
        compiler_params=pltpu.CompilerParams(vmem_limit_bytes=56 * 1024 * 1024),
        cost_estimate=pl.CostEstimate(
            flops=2 * rows * cached * (width + LAT),
            bytes_accessed=2 * cached * width,
            transcendentals=rows * cached,
        ),
        name="attend",
    )(length, q, new, keys)


def partner_order(n, me, rows):
    planes = n // SPAN
    r = iota2((rows, rows), 0)
    c, q = r // (rows // 2), (r // (planes * STEPS)) % 4
    k, step = (r // STEPS) % planes, r % STEPS
    return me ^ ((q >> 1) * (n // 2) + k * 4 + (q & 1) * 2 + c), step


def heads_kernel(n, me_ref, latents_ref, uv_ref, out_ref, near_ref, far_ref):
    rows = n * STEPS
    values = jnp.dot(latents_ref[...], uv_ref[...], preferred_element_type=F32).astype(BF)
    device, step = partner_order(n, me_ref[0], rows)
    values = pick(one_hot(device * STEPS + step, rows), values).astype(BF)
    part = out_ref.shape[1] // SPAN
    for p in range(SPAN):
        here = slice(p * part, (p + 1) * part)
        out = jnp.dot(values, out_ref[:, here], preferred_element_type=F32)
        near_ref[:, here] = out[: rows // 2]
        far_ref[:, here] = out[rows // 2 :].astype(BF)


def norm_kernel(n, *refs):
    parts, (residual_ref, gain_ref, routes_ref, hidden_ref, out_ref) = refs[:-5], refs[-5:]
    hidden = residual_ref[...].astype(F32)
    for ref in parts:
        hidden += ref[...].astype(F32)
    hidden_ref[...] = hidden
    width = hidden.shape[1]
    mean_square = jnp.sum(hidden * hidden, axis=1, keepdims=True) / width
    normed = hidden * lax.rsqrt(mean_square + 1e-06) * gain_ref[...].astype(F32)
    out_ref[:, :width] = normed.astype(BF)
    out_ref[:, width:] = routes_ref[...]


def load_kernel(n, *refs):
    sources, targets, sem = refs[1:4], refs[5:8], refs[8]
    copies = [pltpu.make_async_copy(refs[0], refs[4], sem.at[12])]
    for i in range(3):
        step = sources[i].shape[0] // 4
        for j in range(4):
            here = pl.ds(j * step, step)
            copies.append(
                pltpu.make_async_copy(sources[i].at[here], targets[i].at[here], sem.at[4 * i + j])
            )
    for copy in copies:
        copy.start()
    for copy in copies:
        copy.wait()


def load(n, passed, arrays):
    return pl.pallas_call(
        functools.partial(load_kernel, n),
        in_specs=[pl.BlockSpec(memory_space=pltpu.VMEM)] + [pl.BlockSpec(memory_space=pl.ANY)] * 3,
        out_specs=[pl.BlockSpec(memory_space=pltpu.VMEM)] * 4,
        out_shape=[jax.ShapeDtypeStruct(a.shape, a.dtype) for a in [passed] + arrays],
        scratch_shapes=[pltpu.SemaphoreType.DMA((13,))],
        compiler_params=pltpu.CompilerParams(vmem_limit_bytes=26 * 1024 * 1024),
        cost_estimate=pl.CostEstimate(
            flops=0, bytes_accessed=sum(4 * a.size for a in arrays), transcendentals=0
        ),
        name="load_experts",
    )(passed, *arrays)


def expert_kernel(n, expert_ref, *refs):
    blocks, (gate_ref, up_ref, down_ref, near_ref, far_ref) = refs[:8], refs[8:]
    rows = n * STEPS
    width, units = gate_ref.shape
    part = width // SPAN
    gate = jnp.zeros((rows, units), F32)
    up = jnp.zeros((rows, units), F32)
    for p in range(SPAN):
        here = slice(p * part, (p + 1) * part)
        x = jnp.concatenate([ref[:, here] for ref in blocks], axis=0)
        gate += jnp.dot(x, gate_ref[here], preferred_element_type=F32)
        up += jnp.dot(x, up_ref[here], preferred_element_type=F32)
    act = (gate * jax.nn.sigmoid(gate) * up).astype(BF)
    routes = jnp.concatenate([ref[:, width:] for ref in blocks], axis=0).astype(F32)
    scores = routes[:, TOPK : 2 * TOPK] + routes[:, 2 * TOPK : 3 * TOPK]
    chosen = jnp.where(routes[:, :TOPK] == expert_ref[0].astype(F32), scores, 0.0)
    coef = jnp.sum(chosen, axis=1, keepdims=True) / jnp.sum(scores, axis=1, keepdims=True) * 2.5
    for p in range(SPAN):
        here = slice(p * part, (p + 1) * part)
        out = jnp.dot(act, down_ref[:, here], preferred_element_type=F32) * coef
        near_ref[:, here] = out[: rows // 2]
        far_ref[:, here] = out[rows // 2 :].astype(BF)


def single(kernel, n, out_shape, scalars, arrays, name, flops):
    return pl.pallas_call(
        functools.partial(kernel, n),
        in_specs=[pl.BlockSpec(memory_space=pltpu.SMEM)] * len(scalars)
        + [pl.BlockSpec(memory_space=pltpu.VMEM)] * len(arrays),
        out_shape=out_shape,
        compiler_params=pltpu.CompilerParams(vmem_limit_bytes=VMEM_LIMIT),
        cost_estimate=pl.CostEstimate(
            flops=flops, bytes_accessed=sum(2 * a.size for a in arrays), transcendentals=0
        ),
        name=name,
    )(*scalars, *arrays)


def reduce_rows(near, far, n):
    planes = n // SPAN
    width = near.shape[1]
    total = (near + swap(far, n, c=1).astype(F32)).reshape(4, planes * STEPS, width)
    kept = total[0]
    for q in range(1, 4):
        kept = kept + swap(total[q].astype(BF), n, q=q).astype(F32)
    kept = kept.reshape(planes, STEPS, width)
    return [kept[0]] + [swap(kept[k].astype(BF), n, k=k) for k in range(1, planes)]


def per_device(
    queries,
    new_latent,
    cache_latent,
    cache_len,
    route_ids,
    route_scores,
    residual,
    norm_gain,
    w_uv,
    w_out,
    w_gate,
    w_up,
    w_down,
):
    n_ep = lax.axis_size("ep")
    n = lax.axis_size("sec") * n_ep
    planes = n // SPAN
    heads = queries.shape[2]
    width = residual.shape[2]
    rows = n * STEPS
    me = lax.axis_index(AXES).astype(jnp.int32)

    with jax.named_scope("attention"):
        latents = attend(
            n,
            cache_len,
            queries[0].reshape(STEPS * heads, queries.shape[3]),
            new_latent[0],
            jnp.swapaxes(cache_latent[0], 0, 1),
        )

    with jax.named_scope("heads"):
        latents = lax.all_to_all(latents, AXES, 0, 0, tiled=True)
        near, far = single(
            heads_kernel,
            n,
            [jax.ShapeDtypeStruct((rows // 2, width), dtype) for dtype in (F32, BF)],
            [me.reshape(1)],
            [latents.reshape(rows, LAT), w_uv[0], w_out[0]],
            "heads",
            2 * rows * VDIM * (LAT + width),
        )
        parts = reduce_rows(near, far, n)

    with jax.named_scope("norm"):
        high = route_scores[0].astype(BF)
        low = (route_scores[0] - high.astype(F32)).astype(BF)
        routes = jnp.concatenate([route_ids[0].astype(BF), high, low], axis=1)
        routes = jnp.pad(routes, ((0, 0), (0, 128 - 3 * TOPK)))
        hidden, normed = single(
            norm_kernel,
            n,
            [
                jax.ShapeDtypeStruct((STEPS, width), F32),
                jax.ShapeDtypeStruct((STEPS, width + 128), BF),
            ],
            [],
            parts + [residual[0], norm_gain.reshape(1, width), routes],
            "norm",
            8 * STEPS * width,
        )

    with jax.named_scope("spread"):
        along = jnp.concatenate([normed] + [swap(normed, n, k=k) for k in range(1, planes)], axis=0)
        blocks = [along] + [swap(along, n, q=q) for q in range(1, 4)]
        along, *weights = load(n, along, [w_gate[0], w_up[0], w_down[0]])
        blocks = blocks + [swap(x, n, c=1) for x in [along] + blocks[1:]]

    with jax.named_scope("experts"):
        near, far = single(
            expert_kernel,
            n,
            [jax.ShapeDtypeStruct((rows // 2, width), dtype) for dtype in (F32, BF)],
            [(me % n_ep).reshape(1)],
            blocks + weights,
            "experts",
            6 * rows * width * w_gate.shape[2],
        )

    with jax.named_scope("collect"):
        result = hidden
        for term in reduce_rows(near, far, n):
            result = result + term.astype(F32)
        return result.astype(BF)[None]


def solution(mesh):
    placed = (
        P(("sec", "ep"), None, None, None),
        P(("sec", "ep"), None, None),
        P(("sec", "ep"), None, None),
        P(("sec", "ep")),
        P(("sec", "ep"), None, None),
        P(("sec", "ep"), None, None),
        P(("sec", "ep"), None, None),
        P(),
        P(("sec", "ep"), None, None),
        P(("sec", "ep"), None, None),
        P("ep", None, "sec"),
        P("ep", None, "sec"),
        P("ep", "sec", None),
    )
    return jax.shard_map(
        per_device,
        mesh=mesh,
        in_specs=placed,
        out_specs=P(("sec", "ep"), None, None),
        check_vma=False,
    )
```

time: 153 us -> 121 us (0.79)
  blocking collectives: 68.1 us -> 0 us
  waiting for transfers between devices: 24.9 us -> 46.1 us
  starting transfers between devices: 21.2 us -> 32.6 us
  Pallas kernels: 14.4 us -> 20.4 us
  other arithmetic: 4.89 us -> 1.58 us
    all_to_all x4 -> x0, blocking collectives: 68.1 us -> none  [exchange(): return lax.all_to_all(x, AXES, 0, 0, axis_index_groups=groups, tiled=True)]
    ppermute x2 -> x24, waiting for transfers between devices: 4.68 us -> 37.9 us  [swap(): return lax.ppermute(x, AXES, [(d, d ^ mask) for d in range(n)])]
    ppermute x2 -> x24, starting transfers between devices: 0.21 us -> 24.7 us  [swap(): return lax.ppermute(x, AXES, [(d, d ^ mask) for d in range(n)])]
    all_to_all x4 -> x1, starting transfers between devices: 21 us -> 7.93 us  [per_device(): latents = lax.all_to_all(latents, AXES, 0, 0, tiled=True)]
    all_to_all x4 -> x1, waiting for transfers between devices: 20.2 us -> 8.22 us  [per_device(): latents = lax.all_to_all(latents, AXES, 0, 0, tiled=True)]
    pallas_call x0 -> x1, Pallas kernels: none -> 7.71 us  [load(): pl.pallas_call(functools.partial(load_kernel, n), in_specs=[pl.BlockSpec(...]
    unnamed x17 -> x24, local copies, waits for them, and re-layouts: 12.6 us -> 18.1 us
    transpose x1 -> x0, other arithmetic: 3.39 us -> none  [per_device(): shared = exchange(jnp.swapaxes(by_part, 0, 1), planes_of)]
  transfers between devices with their start and end apart: 6 -> 25, of which waited for: 6 -> 18; matrix products, arithmetic and copies ran while one was open for 6% -> 0% of each run, Pallas kernels for 0% -> 6%
where the time goes in v3:
time: 121 us; the launch traced here: 120 us
  waiting for transfers between devices  46.1 us (38%)
  starting transfers between devices  32.6 us (27%)
  Pallas kernels  20.4 us (17%)
  local copies, waits for them, and re-layouts  18.4 us (15%)
  other arithmetic  1.58 us (1%)
    ppermute x24, waiting for transfers between devices, swap(): return lax.ppermute(x, AXES, [(d, d ^ mask) for d in range(n)])  37.9 us
    ppermute x24, starting transfers between devices, swap(): return lax.ppermute(x, AXES, [(d, d ^ mask) for d in range(n)])  24.7 us
    unnamed x24, local copies, waits for them, and re-layouts  18.1 us
    all_to_all x1, waiting for transfers between devices, per_device(): latents = lax.all_to_all(latents, AXES, 0, 0, tiled=True)  8.22 us
    pallas_call x1, Pallas kernels, attend(): pl.pallas_call(functools.partial(attend_kernel, n), grid_spec=pltpu.Prefe...  8 us
    all_to_all x1, starting transfers between devices, per_device(): latents = lax.all_to_all(latents, AXES, 0, 0, tiled=True)  7.93 us
    pallas_call x1, Pallas kernels, load(): pl.pallas_call(functools.partial(load_kernel, n), in_specs=[pl.BlockSpec(...  7.71 us
    pallas_call x3, Pallas kernels, single(): pl.pallas_call(functools.partial(kernel, n), in_specs=[pl.BlockSpec(memor...  4.71 us
  transfers between devices with their start and end apart: 25, of which 18 were waited for; matrix products, arithmetic and copies ran while one was open for 0% of the time, Pallas kernels for 6%

profile of v3, /device:TPU:0, one launch (start us, length us, event | category | flops | bytes accessed | tf_op | source)
XLA Modules:
  0.0 120.1 jit_solution(16887898880830988192)
XLA Ops:
  0.7 8.0 %attend.1 = bf16[32,4,512]{2,1,0:T(4,128)(2,1)} custom-call(s32[1]{0:T(128)S(6)} %copy.14.len_ref, bf16[128,576]{1,0:T(8,128)(2,1)} %bitcast.30, bf16[4,576]{1,0:T(4,128)(2,1)} %bitcast.31, bf16[576,8192]{1,0:T(8,128)(2,1)} %bitcast.26), custom_call_target="tpu_custom_call" | custom-call | flops 2281701376 | bytes 9437184 | tf_op jit(solution)/shard_map/attention/attend/pallas_call | solution.py:103
  8.7 7.9 %all-to-all-start = ((bf16[32,4,512]{2,1,0:T(4,128)(2,1)}), bf16[32,4,512]{2,1,0:T(4,128)(2,1)S(1)}, u32[]{:S(2)}, u32[]{:S(2)}) async-start(bf16[32,4,512]{2,1,0:T(4,128)(2,1)} %attend.1), calls=%async_computation | async-start | bytes 262144 | tf_op jit(solution)/shard_map/heads/all_to_all | solution.py:278
  16.6 8.2 %all-to-all-done = bf16[32,4,512]{2,1,0:T(4,128)(2,1)S(1)} async-done(((bf16[32,4,512]{2,1,0:T(4,128)(2,1)}), bf16[32,4,512]{2,1,0:T(4,128)(2,1)S(1)}, u32[]{:S(2)}, u32[]{:S(2)}) %all-to-all-start) | async-done | bytes 131104 | tf_op jit(solution)/shard_map/heads/all_to_all | solution.py:278
  26.1 2.2 %collective-permute-done = bf16[64,7168]{1,0:T(8,128)(2,1)S(1)} collective-permute-done((bf16[64,7168]{1,0:T(8,128)(2,1)S(1)}, bf16[64,7168]{1,0:T(8,128)(2,1)S(1)}, u32[]{:S(2)}, u32[]{:S(2)}) %collective-permute-start) | collective-permute-done | bytes 917536 | tf_op jit(solution)/shard_map/heads/ppermute | solution.py:31
  29.2 1.7 %collective-permute-start.3 = (bf16[16,7168]{1,0:T(8,128)(2,1)S(1)}, bf16[16,7168]{1,0:T(8,128)(2,1)S(1)}, u32[]{:S(2)}, u32[]{:S(2)}) collective-permute-start(bf16[16,7168]{1,0:T(8,128)(2,1)S(1)} %get-tuple-element.39), channel_id=1, source_target_pairs={{0,18},{1,19},{2,16},{3,17},{4,22},{5,23},{6,20},{7,21},{8,26},{9,... | collective-permute-start | bytes 688136 | tf_op jit(solution)/shard_map/heads/ppermute | solution.py:31
  32.3 9.1 %collective-permute-done.1 = bf16[16,7168]{1,0:T(8,128)(2,1)S(1)} collective-permute-done((bf16[16,7168]{1,0:T(8,128)(2,1)S(1)}, bf16[16,7168]{1,0:T(8,128)(2,1)S(1)}, u32[]{:S(2)}, u32[]{:S(2)}) %collective-permute-start.1) | collective-permute-done | bytes 229408 | tf_op jit(solution)/shard_map/heads/ppermute | solution.py:31
  44.3 2.9 %collective-permute-start.4 = (bf16[4,7168]{1,0:T(4,128)(2,1)S(1)}, bf16[4,7168]{1,0:T(4,128)(2,1)S(1)}, u32[]{:S(2)}, u32[]{:S(2)}) collective-permute-start(bf16[4,7168]{1,0:T(4,128)(2,1)S(1)} %get-tuple-element.46), channel_id=1, source_target_pairs={{0,4},{1,5},{2,6},{3,7},{4,0},{5,1},{6,2},{7,3},{8,12},{9,13},{10,... | collective-permute-start | bytes 172040 | tf_op jit(solution)/shard_map/heads/ppermute | solution.py:31
  50.4 1.8 %collective-permute-start.9 = (bf16[4,7296]{1,0:T(4,128)(2,1)S(1)}, bf16[4,7296]{1,0:T(4,128)(2,1)S(1)}, u32[]{:S(2)}, u32[]{:S(2)}) collective-permute-start(bf16[4,7296]{1,0:T(4,128)(2,1)S(1)} %get-tuple-element.18), channel_id=1, source_target_pairs={{0,12},{1,13},{2,14},{3,15},{4,8},{5,9},{6,10},{7,11},{8,4},{9,5},... | collective-permute-start | bytes 175112 | tf_op jit(solution)/shard_map/spread/ppermute | solution.py:31
  53.2 1.6 %collective-permute-start.7 = (bf16[4,7296]{1,0:T(4,128)(2,1)S(1)}, bf16[4,7296]{1,0:T(4,128)(2,1)S(1)}, u32[]{:S(2)}, u32[]{:S(2)}) collective-permute-start(bf16[4,7296]{1,0:T(4,128)(2,1)S(1)} %get-tuple-element.18), channel_id=1, source_target_pairs={{0,4},{1,5},{2,6},{3,7},{4,0},{5,1},{6,2},{7,3},{8,12},{9,13},{10,... | collective-permute-start | bytes 175112 | tf_op jit(solution)/shard_map/spread/ppermute | solution.py:31
  54.8 2.3 %collective-permute-done.9 = bf16[4,7296]{1,0:T(4,128)(2,1)S(1)} collective-permute-done((bf16[4,7296]{1,0:T(4,128)(2,1)S(1)}, bf16[4,7296]{1,0:T(4,128)(2,1)S(1)}, u32[]{:S(2)}, u32[]{:S(2)}) %collective-permute-start.9) | collective-permute-done | bytes 58400 | tf_op jit(solution)/shard_map/spread/ppermute | solution.py:31
  61.8 7.7 %load_experts.1 = (bf16[16,7296]{1,0:T(8,128)(2,1)S(1)}, bf16[7168,512]{1,0:T(8,128)(2,1)S(1)}, bf16[7168,512]{1,0:T(8,128)(2,1)S(1)}, bf16[512,7168]{1,0:T(8,128)(2,1)S(1)}) custom-call(bf16[16,7296]{1,0:T(8,128)(2,1)S(1)} %pad_maximum_fusion.refs_0_, bf16[7168,512]{1,0:T(8,128)(2,1)} %bitcast.27, bf16[7168,512]{1,0:T(8,128)(2,1)} %bitcast.28, ...), custom_call_target="tpu_custom_call" | custom-call | bytes 44040192 | tf_op jit(solution)/shard_map/spread/load_experts/pallas_call | solution.py:182
  69.5 2.9 %copy-done = bf16[7168,512]{1,0:T(8,128)(2,1)} copy-done((bf16[7168,512]{1,0:T(8,128)(2,1)}, bf16[7168,512]{1,0:T(8,128)(2,1)S(1)}, u32[]{:S(2)}) %copy-start) | copy-done | bytes 7340056
  72.4 3.0 %copy-done.2 = bf16[7168,512]{1,0:T(8,128)(2,1)} copy-done((bf16[7168,512]{1,0:T(8,128)(2,1)}, bf16[7168,512]{1,0:T(8,128)(2,1)S(1)}, u32[]{:S(2)}) %copy-start.2) | copy-done | bytes 7340056
  75.4 3.0 %copy-done.4 = bf16[512,7168]{1,0:T(8,128)(2,1)} copy-done((bf16[512,7168]{1,0:T(8,128)(2,1)}, bf16[512,7168]{1,0:T(8,128)(2,1)S(1)}, u32[]{:S(2)}) %copy-start.4) | copy-done | bytes 7340056
  80.9 3.1 %copy-done.1 = bf16[7168,512]{1,0:T(8,128)(2,1)S(1)} copy-done((bf16[7168,512]{1,0:T(8,128)(2,1)S(1)}, bf16[7168,512]{1,0:T(8,128)(2,1)}, u32[]{:S(2)}) %copy-start.1) | copy-done | bytes 7340056
  83.9 3.1 %copy-done.3 = bf16[7168,512]{1,0:T(8,128)(2,1)S(1)} copy-done((bf16[7168,512]{1,0:T(8,128)(2,1)S(1)}, bf16[7168,512]{1,0:T(8,128)(2,1)}, u32[]{:S(2)}) %copy-start.3) | copy-done | bytes 7340056
  87.0 3.1 %copy-done.5 = bf16[512,7168]{1,0:T(8,128)(2,1)S(1)} copy-done((bf16[512,7168]{1,0:T(8,128)(2,1)S(1)}, bf16[512,7168]{1,0:T(8,128)(2,1)}, u32[]{:S(2)}) %copy-start.5) | copy-done | bytes 7340056
  90.1 3.6 %experts.1 = (f32[64,7168]{1,0:T(8,128)S(1)}, bf16[64,7168]{1,0:T(8,128)(2,1)S(1)}) custom-call(s32[1]{0:T(128)} %bitcast.10.expert_ref, bf16[16,7296]{1,0:T(8,128)(2,1)S(1)} %pad_maximum_fusion.refs_0_, bf16[16,7296]{1,0:T(8,128)(2,1)S(1)} %collective-permute-done.10.refs_1_, bf16[16,7296]{1,0:T(8,128)(2,1)S(1)} %collective-permute-done.11.refs_2_, ...), custom_call_target="tpu_custom_call" | custom-call | flops 2818572288 | bytes 23887872 | tf_op jit(solution)/shard_map/experts/experts/pallas_call | solution.py:221
  94.0 2.3 %collective-permute-done.17 = bf16[64,7168]{1,0:T(8,128)(2,1)S(1)} collective-permute-done((bf16[64,7168]{1,0:T(8,128)(2,1)S(1)}, bf16[64,7168]{1,0:T(8,128)(2,1)S(1)}, u32[]{:S(2)}, u32[]{:S(2)}) %collective-permute-start.17) | collective-permute-done | bytes 917536 | tf_op jit(solution)/shard_map/collect/ppermute | solution.py:31
  97.8 1.8 %collective-permute-start.20 = (bf16[16,7168]{1,0:T(8,128)(2,1)S(1)}, bf16[16,7168]{1,0:T(8,128)(2,1)S(1)}, u32[]{:S(2)}, u32[]{:S(2)}) collective-permute-start(bf16[16,7168]{1,0:T(8,128)(2,1)S(1)} %get-tuple-element.36), channel_id=1, source_target_pairs={{0,18},{1,19},{2,16},{3,17},{4,22},{5,23},{6,20},{7,21},{8,26},{9,... | collective-permute-start | bytes 688136 | tf_op jit(solution)/shard_map/collect/ppermute | solution.py:31
  100.1 9.1 %collective-permute-done.18 = bf16[16,7168]{1,0:T(8,128)(2,1)S(1)} collective-permute-done((bf16[16,7168]{1,0:T(8,128)(2,1)S(1)}, bf16[16,7168]{1,0:T(8,128)(2,1)S(1)}, u32[]{:S(2)}, u32[]{:S(2)}) %collective-permute-start.18) | collective-permute-done | bytes 229408 | tf_op jit(solution)/shard_map/collect/ppermute | solution.py:31
  111.6 1.7 %collective-permute-start.23 = (bf16[4,7168]{1,0:T(4,128)(2,1)S(1)}, bf16[4,7168]{1,0:T(4,128)(2,1)S(1)}, u32[]{:S(2)}, u32[]{:S(2)}) collective-permute-start(bf16[4,7168]{1,0:T(4,128)(2,1)S(1)} %get-tuple-element.42), channel_id=1, source_target_pairs={{0,12},{1,13},{2,14},{3,15},{4,8},{5,9},{6,10},{7,11},{8,4},{9,5},... | collective-permute-start | bytes 172040 | tf_op jit(solution)/shard_map/collect/ppermute | solution.py:31
  114.9 2.7 %collective-permute-done.23 = bf16[4,7168]{1,0:T(4,128)(2,1)S(1)} collective-permute-done((bf16[4,7168]{1,0:T(4,128)(2,1)S(1)}, bf16[4,7168]{1,0:T(4,128)(2,1)S(1)}, u32[]{:S(2)}, u32[]{:S(2)}) %collective-permute-start.23) | collective-permute-done | bytes 57376 | tf_op jit(solution)/shard_map/collect/ppermute | solution.py:31
  117.6 1.8 %collective-permute-done.22 = bf16[4,7168]{1,0:T(4,128)(2,1)S(1)} collective-permute-done((bf16[4,7168]{1,0:T(4,128)(2,1)S(1)}, bf16[4,7168]{1,0:T(4,128)(2,1)S(1)}, u32[]{:S(2)}, u32[]{:S(2)}) %collective-permute-start.22) | collective-permute-done | bytes 57376 | tf_op jit(solution)/shard_map/collect/ppermute | solution.py:31
  (71 shorter events, 24.6 us)
Async XLA Ops:
  8.7 16.2 %all-to-all-start = ((bf16[32,4,512]{2,1,0:T(4,128)(2,1)}), bf16[32,4,512]{2,1,0:T(4,128)(2,1)S(1)}, u32[]{:S(2)}, u32[]{:S(2)}) async-start(bf16[32,4,512]{2,1,0:T(4,128)(2,1)} %attend.1), calls=%async_computation | async-start | bytes 262144 | tf_op jit(solution)/shard_map/heads/all_to_all | solution.py:278
  25.8 2.5 %collective-permute-start = (bf16[64,7168]{1,0:T(8,128)(2,1)S(1)}, bf16[64,7168]{1,0:T(8,128)(2,1)S(1)}, u32[]{:S(2)}, u32[]{:S(2)}) collective-permute-start(bf16[64,7168]{1,0:T(8,128)(2,1)S(1)} %get-tuple-element.16), channel_id=1, source_target_pairs={{0,1},{1,0},{2,3},{3,2},{4,5},{5,4},{6,7},{7,6},{8,9},{9,8},{10,11... | collective-permute-start | bytes 2752520 | tf_op jit(solution)/shard_map/heads/ppermute | solution.py:31
  28.6 12.7 %collective-permute-start.1 = (bf16[16,7168]{1,0:T(8,128)(2,1)S(1)}, bf16[16,7168]{1,0:T(8,128)(2,1)S(1)}, u32[]{:S(2)}, u32[]{:S(2)}) collective-permute-start(bf16[16,7168]{1,0:T(8,128)(2,1)S(1)} %get-tuple-element.38), channel_id=1, source_target_pairs={{0,2},{1,3},{2,0},{3,1},{4,6},{5,7},{6,4},{7,5},{8,10},{9,11},{10,... | collective-permute-start | bytes 688136 | tf_op jit(solution)/shard_map/heads/ppermute | solution.py:31
  29.2 12.2 %collective-permute-start.3 = (bf16[16,7168]{1,0:T(8,128)(2,1)S(1)}, bf16[16,7168]{1,0:T(8,128)(2,1)S(1)}, u32[]{:S(2)}, u32[]{:S(2)}) collective-permute-start(bf16[16,7168]{1,0:T(8,128)(2,1)S(1)} %get-tuple-element.39), channel_id=1, source_target_pairs={{0,18},{1,19},{2,16},{3,17},{4,22},{5,23},{6,20},{7,21},{8,26},{9,... | collective-permute-start | bytes 688136 | tf_op jit(solution)/shard_map/heads/ppermute | solution.py:31
  30.9 11.7 %collective-permute-start.2 = (bf16[16,7168]{1,0:T(8,128)(2,1)S(1)}, bf16[16,7168]{1,0:T(8,128)(2,1)S(1)}, u32[]{:S(2)}, u32[]{:S(2)}) collective-permute-start(bf16[16,7168]{1,0:T(8,128)(2,1)S(1)} %get-tuple-element.40), channel_id=1, source_target_pairs={{0,16},{1,17},{2,18},{3,19},{4,20},{5,21},{6,22},{7,23},{8,24},{9,... | collective-permute-start | bytes 688136 | tf_op jit(solution)/shard_map/heads/ppermute | solution.py:31
  42.8 6.2 %collective-permute-start.6 = (bf16[4,7168]{1,0:T(4,128)(2,1)S(1)}, bf16[4,7168]{1,0:T(4,128)(2,1)S(1)}, u32[]{:S(2)}, u32[]{:S(2)}) collective-permute-start(bf16[4,7168]{1,0:T(4,128)(2,1)S(1)} %get-tuple-element.44), channel_id=1, source_target_pairs={{0,12},{1,13},{2,14},{3,15},{4,8},{5,9},{6,10},{7,11},{8,4},{9,5},... | collective-permute-start | bytes 172040 | tf_op jit(solution)/shard_map/heads/ppermute | solution.py:31
  44.1 6.1 %collective-permute-start.5 = (bf16[4,7168]{1,0:T(4,128)(2,1)S(1)}, bf16[4,7168]{1,0:T(4,128)(2,1)S(1)}, u32[]{:S(2)}, u32[]{:S(2)}) collective-permute-start(bf16[4,7168]{1,0:T(4,128)(2,1)S(1)} %get-tuple-element.45), channel_id=1, source_target_pairs={{0,8},{1,9},{2,10},{3,11},{4,12},{5,13},{6,14},{7,15},{8,0},{9,1},... | collective-permute-start | bytes 172040 | tf_op jit(solution)/shard_map/heads/ppermute | solution.py:31
  44.3 5.8 %collective-permute-start.4 = (bf16[4,7168]{1,0:T(4,128)(2,1)S(1)}, bf16[4,7168]{1,0:T(4,128)(2,1)S(1)}, u32[]{:S(2)}, u32[]{:S(2)}) collective-permute-start(bf16[4,7168]{1,0:T(4,128)(2,1)S(1)} %get-tuple-element.46), channel_id=1, source_target_pairs={{0,4},{1,5},{2,6},{3,7},{4,0},{5,1},{6,2},{7,3},{8,12},{9,13},{10,... | collective-permute-start | bytes 172040 | tf_op jit(solution)/shard_map/heads/ppermute | solution.py:31
  50.4 6.8 %collective-permute-start.9 = (bf16[4,7296]{1,0:T(4,128)(2,1)S(1)}, bf16[4,7296]{1,0:T(4,128)(2,1)S(1)}, u32[]{:S(2)}, u32[]{:S(2)}) collective-permute-start(bf16[4,7296]{1,0:T(4,128)(2,1)S(1)} %get-tuple-element.18), channel_id=1, source_target_pairs={{0,12},{1,13},{2,14},{3,15},{4,8},{5,9},{6,10},{7,11},{8,4},{9,5},... | collective-permute-start | bytes 175112 | tf_op jit(solution)/shard_map/spread/ppermute | solution.py:31
  52.1 5.9 %collective-permute-start.8 = (bf16[4,7296]{1,0:T(4,128)(2,1)S(1)}, bf16[4,7296]{1,0:T(4,128)(2,1)S(1)}, u32[]{:S(2)}, u32[]{:S(2)}) collective-permute-start(bf16[4,7296]{1,0:T(4,128)(2,1)S(1)} %get-tuple-element.18), channel_id=1, source_target_pairs={{0,8},{1,9},{2,10},{3,11},{4,12},{5,13},{6,14},{7,15},{8,0},{9,1},... | collective-permute-start | bytes 175112 | tf_op jit(solution)/shard_map/spread/ppermute | solution.py:31
  53.2 4.9 %collective-permute-start.7 = (bf16[4,7296]{1,0:T(4,128)(2,1)S(1)}, bf16[4,7296]{1,0:T(4,128)(2,1)S(1)}, u32[]{:S(2)}, u32[]{:S(2)}) collective-permute-start(bf16[4,7296]{1,0:T(4,128)(2,1)S(1)} %get-tuple-element.18), channel_id=1, source_target_pairs={{0,4},{1,5},{2,6},{3,7},{4,0},{5,1},{6,2},{7,3},{8,12},{9,13},{10,... | collective-permute-start | bytes 175112 | tf_op jit(solution)/shard_map/spread/ppermute | solution.py:31
  58.2 20.1 %collective-permute-start.12 = (bf16[16,7296]{1,0:T(8,128)(2,1)S(1)}, bf16[16,7296]{1,0:T(8,128)(2,1)S(1)}, u32[]{:S(2)}, u32[]{:S(2)}) collective-permute-start(bf16[16,7296]{1,0:T(8,128)(2,1)S(1)} %pad_maximum_fusion.refs_0_), channel_id=1, source_target_pairs={{0,18},{1,19},{2,16},{3,17},{4,22},{5,23},{6,20},{7,21},{8,26},{9,... | collective-permute-start | bytes 700424 | tf_op jit(solution)/shard_map/spread/ppermute | solution.py:31
  59.5 19.4 %collective-permute-start.11 = (bf16[16,7296]{1,0:T(8,128)(2,1)S(1)}, bf16[16,7296]{1,0:T(8,128)(2,1)S(1)}, u32[]{:S(2)}, u32[]{:S(2)}) collective-permute-start(bf16[16,7296]{1,0:T(8,128)(2,1)S(1)} %pad_maximum_fusion.refs_0_), channel_id=1, source_target_pairs={{0,16},{1,17},{2,18},{3,19},{4,20},{5,21},{6,22},{7,23},{8,24},{9,... | collective-permute-start | bytes 700424 | tf_op jit(solution)/shard_map/spread/ppermute | solution.py:31
  60.9 18.0 %collective-permute-start.10 = (bf16[16,7296]{1,0:T(8,128)(2,1)S(1)}, bf16[16,7296]{1,0:T(8,128)(2,1)S(1)}, u32[]{:S(2)}, u32[]{:S(2)}) collective-permute-start(bf16[16,7296]{1,0:T(8,128)(2,1)S(1)} %pad_maximum_fusion.refs_0_), channel_id=1, source_target_pairs={{0,2},{1,3},{2,0},{3,1},{4,6},{5,7},{6,4},{7,5},{8,10},{9,11},{10,... | collective-permute-start | bytes 700424 | tf_op jit(solution)/shard_map/spread/ppermute | solution.py:31
  78.4 1.8 %collective-permute-start.16 = (bf16[16,7296]{1,0:T(8,128)(2,1)S(1)}, bf16[16,7296]{1,0:T(8,128)(2,1)S(1)}, u32[]{:S(2)}, u32[]{:S(2)}) collective-permute-start(bf16[16,7296]{1,0:T(8,128)(2,1)S(1)} %collective-permute-done.12.refs_3_), channel_id=1, source_target_pairs={{0,1},{1,0},{2,3},{3,2},{4,5},{5,4},{6,7},{7,6},{8,9},{9,8},{10,11... | collective-permute-start | bytes 700424 | tf_op jit(solution)/shard_map/spread/ppermute | solution.py:31
  78.9 1.6 %collective-permute-start.15 = (bf16[16,7296]{1,0:T(8,128)(2,1)S(1)}, bf16[16,7296]{1,0:T(8,128)(2,1)S(1)}, u32[]{:S(2)}, u32[]{:S(2)}) collective-permute-start(bf16[16,7296]{1,0:T(8,128)(2,1)S(1)} %collective-permute-done.11.refs_2_), channel_id=1, source_target_pairs={{0,1},{1,0},{2,3},{3,2},{4,5},{5,4},{6,7},{7,6},{8,9},{9,8},{10,11... | collective-permute-start | bytes 700424 | tf_op jit(solution)/shard_map/spread/ppermute | solution.py:31
  78.9 1.9 %collective-permute-start.14 = (bf16[16,7296]{1,0:T(8,128)(2,1)S(1)}, bf16[16,7296]{1,0:T(8,128)(2,1)S(1)}, u32[]{:S(2)}, u32[]{:S(2)}) collective-permute-start(bf16[16,7296]{1,0:T(8,128)(2,1)S(1)} %collective-permute-done.10.refs_1_), channel_id=1, source_target_pairs={{0,1},{1,0},{2,3},{3,2},{4,5},{5,4},{6,7},{7,6},{8,9},{9,8},{10,11... | collective-permute-start | bytes 700424 | tf_op jit(solution)/shard_map/spread/ppermute | solution.py:31
  93.7 2.5 %collective-permute-start.17 = (bf16[64,7168]{1,0:T(8,128)(2,1)S(1)}, bf16[64,7168]{1,0:T(8,128)(2,1)S(1)}, u32[]{:S(2)}, u32[]{:S(2)}) collective-permute-start(bf16[64,7168]{1,0:T(8,128)(2,1)S(1)} %get-tuple-element.24), channel_id=1, source_target_pairs={{0,1},{1,0},{2,3},{3,2},{4,5},{5,4},{6,7},{7,6},{8,9},{9,8},{10,11... | collective-permute-start | bytes 2752520 | tf_op jit(solution)/shard_map/collect/ppermute | solution.py:31
  96.5 12.7 %collective-permute-start.18 = (bf16[16,7168]{1,0:T(8,128)(2,1)S(1)}, bf16[16,7168]{1,0:T(8,128)(2,1)S(1)}, u32[]{:S(2)}, u32[]{:S(2)}) collective-permute-start(bf16[16,7168]{1,0:T(8,128)(2,1)S(1)} %get-tuple-element.35), channel_id=1, source_target_pairs={{0,2},{1,3},{2,0},{3,1},{4,6},{5,7},{6,4},{7,5},{8,10},{9,11},{10,... | collective-permute-start | bytes 688136 | tf_op jit(solution)/shard_map/collect/ppermute | solution.py:31
  97.8 11.4 %collective-permute-start.20 = (bf16[16,7168]{1,0:T(8,128)(2,1)S(1)}, bf16[16,7168]{1,0:T(8,128)(2,1)S(1)}, u32[]{:S(2)}, u32[]{:S(2)}) collective-permute-start(bf16[16,7168]{1,0:T(8,128)(2,1)S(1)} %get-tuple-element.36), channel_id=1, source_target_pairs={{0,18},{1,19},{2,16},{3,17},{4,22},{5,23},{6,20},{7,21},{8,26},{9,... | collective-permute-start | bytes 688136 | tf_op jit(solution)/shard_map/collect/ppermute | solution.py:31
  99.5 10.9 %collective-permute-start.19 = (bf16[16,7168]{1,0:T(8,128)(2,1)S(1)}, bf16[16,7168]{1,0:T(8,128)(2,1)S(1)}, u32[]{:S(2)}, u32[]{:S(2)}) collective-permute-start(bf16[16,7168]{1,0:T(8,128)(2,1)S(1)} %get-tuple-element.37), channel_id=1, source_target_pairs={{0,16},{1,17},{2,18},{3,19},{4,20},{5,21},{6,22},{7,23},{8,24},{9,... | collective-permute-start | bytes 688136 | tf_op jit(solution)/shard_map/collect/ppermute | solution.py:31
  110.6 4.3 %collective-permute-start.21 = (bf16[4,7168]{1,0:T(4,128)(2,1)S(1)}, bf16[4,7168]{1,0:T(4,128)(2,1)S(1)}, u32[]{:S(2)}, u32[]{:S(2)}) collective-permute-start(bf16[4,7168]{1,0:T(4,128)(2,1)S(1)} %get-tuple-element.41), channel_id=1, source_target_pairs={{0,4},{1,5},{2,6},{3,7},{4,0},{5,1},{6,2},{7,3},{8,12},{9,13},{10,... | collective-permute-start | bytes 172040 | tf_op jit(solution)/shard_map/collect/ppermute | solution.py:31
  111.6 6.0 %collective-permute-start.23 = (bf16[4,7168]{1,0:T(4,128)(2,1)S(1)}, bf16[4,7168]{1,0:T(4,128)(2,1)S(1)}, u32[]{:S(2)}, u32[]{:S(2)}) collective-permute-start(bf16[4,7168]{1,0:T(4,128)(2,1)S(1)} %get-tuple-element.42), channel_id=1, source_target_pairs={{0,12},{1,13},{2,14},{3,15},{4,8},{5,9},{6,10},{7,11},{8,4},{9,5},... | collective-permute-start | bytes 172040 | tf_op jit(solution)/shard_map/collect/ppermute | solution.py:31
  113.3 6.0 %collective-permute-start.22 = (bf16[4,7168]{1,0:T(4,128)(2,1)S(1)}, bf16[4,7168]{1,0:T(4,128)(2,1)S(1)}, u32[]{:S(2)}, u32[]{:S(2)}) collective-permute-start(bf16[4,7168]{1,0:T(4,128)(2,1)S(1)} %get-tuple-element.43), channel_id=1, source_target_pairs={{0,8},{1,9},{2,10},{3,11},{4,12},{5,13},{6,14},{7,15},{8,0},{9,1},... | collective-permute-start | bytes 172040 | tf_op jit(solution)/shard_map/collect/ppermute | solution.py:31
  (13 other events, 101.2 us)

commit v4 on v3

--- a/solution.py
+++ b/solution.py
@@ -43,28 +43,51 @@
     return jnp.dot(matrix, rows, preferred_element_type=F32)
 
 
-def attend_kernel(n, len_ref, q_ref, new_ref, keys_ref, out_ref, m_ref, l_ref, acc_ref):
+def attend_kernel(n, len_ref, q_hbm, new_hbm, keys_hbm, out_ref, q_ref, new_ref, keys_ref, m_ref, l_ref, acc_ref, small_sem, sem):
     rows = q_ref.shape[0]
     heads = rows // STEPS
     factor_base2 = (VDIM + ROPE) ** (-0.5) * math.log2(math.e)
-    i = pl.program_id(0)
     length = len_ref[0]
-    blk = keys_ref.shape[1]
-
-    @pl.when(i == 0)
-    def _():
-        new = new_ref[...]
-        s = lax.dot_general(q_ref[...], new, NT, preferred_element_type=F32)
-        step = iota2(s.shape, 0) // heads
-        s = jnp.where(iota2(s.shape, 1) <= step, s, -1e30)
-        m = jnp.max(s, axis=1, keepdims=True)
-        p = jnp.exp2((s - m) * factor_base2)
-        m_ref[...] = m
-        l_ref[...] = jnp.sum(p, axis=1, keepdims=True)
-        acc_ref[...] = jnp.dot(p.astype(BF), new[:, :LAT], preferred_element_type=F32)
-
-    def update(masked):
-        keys = keys_ref[...]
+    blk = min(BLK, keys_ref.shape[1])
+
+    def block_at(i):
+        return pl.ds(pl.multiple_of(i * blk, blk), blk)
+
+    def block_copy(i):
+        return pltpu.make_async_copy(
+            keys_hbm.at[:, block_at(i)], keys_ref.at[:, block_at(i)], sem.at[i]
+        )
+
+    def start(i):
+        @pl.when(i * blk < length)
+        def _():
+            block_copy(i).start()
+
+    q_copy = pltpu.make_async_copy(q_hbm, q_ref, small_sem.at[0])
+    new_copy = pltpu.make_async_copy(new_hbm, new_ref, small_sem.at[1])
+    q_copy.start()
+    new_copy.start()
+    start(0)
+    start(1)
+    r = iota2((rows, rows), 0)
+    order = one_hot((r % STEPS) * heads + r // STEPS, rows)
+    q_copy.wait()
+    new_copy.wait()
+
+    new = new_ref[...]
+    s = lax.dot_general(q_ref[...], new, NT, preferred_element_type=F32)
+    step = iota2(s.shape, 0) // heads
+    s = jnp.where(iota2(s.shape, 1) <= step, s, -1e30)
+    m = jnp.max(s, axis=1, keepdims=True)
+    p = jnp.exp2((s - m) * factor_base2)
+    m_ref[...] = m
+    l_ref[...] = jnp.sum(p, axis=1, keepdims=True)
+    acc_ref[...] = jnp.dot(p.astype(BF), new[:, :LAT], preferred_element_type=F32)
+
+    def update(i, masked):
+        start(i + 2)
+        block_copy(i).wait()
+        keys = keys_ref[:, block_at(i)]
         s = jnp.dot(q_ref[...], keys, preferred_element_type=F32)
         if masked:
             s = jnp.where(iota2(s.shape, 1) < length - i * blk, s, -1e30)
@@ -78,45 +101,39 @@
             p.astype(BF), keys[:LAT], NT, preferred_element_type=F32
         )
 
-    pl.when((i + 1) * blk <= length)(functools.partial(update, False))
-    pl.when((i * blk < length) & ((i + 1) * blk > length))(functools.partial(update, True))
-
-    @pl.when(i == pl.num_programs(0) - 1)
+    full = length // blk
+
+    @pl.loop(0, full)
+    def _(i):
+        update(i, False)
+
+    @pl.when(full * blk < length)
     def _():
-        out = (acc_ref[...] / l_ref[...]).astype(BF)
-        r = iota2((rows, rows), 0)
-        moved = pick(one_hot((r % STEPS) * heads + r // STEPS, rows), out)
-        out_ref[...] = moved.reshape(out_ref.shape).astype(BF)
+        update(full, True)
+
+    out = (acc_ref[...] / l_ref[...]).astype(BF)
+    out_ref[...] = pick(order, out).reshape(out_ref.shape).astype(BF)
 
 
 def attend(n, length, q, new, keys):
     rows, width = q.shape
     cached = keys.shape[1]
-    blk = min(BLK, cached)
-
-    def block(i, len_ref):
-        return (0, jnp.minimum(i, (len_ref[0] - 1) // blk))
-
-    def whole(i, len_ref):
-        return (0, 0)
-
+    blocks = cached // min(BLK, cached)
     return pl.pallas_call(
         functools.partial(attend_kernel, n),
-        grid_spec=pltpu.PrefetchScalarGridSpec(
-            num_scalar_prefetch=1,
-            grid=(cached // blk,),
-            in_specs=[
-                pl.BlockSpec(q.shape, whole),
-                pl.BlockSpec(new.shape, whole),
-                pl.BlockSpec((width, blk), block),
-            ],
-            out_specs=pl.BlockSpec((rows // STEPS, STEPS, LAT), lambda i, len_ref: (0, 0, 0)),
-            scratch_shapes=[
-                pltpu.VMEM((rows, 1), F32),
-                pltpu.VMEM((rows, 1), F32),
-                pltpu.VMEM((rows, LAT), F32),
-            ],
-        ),
+        in_specs=[pl.BlockSpec(memory_space=pltpu.SMEM)]
+        + [pl.BlockSpec(memory_space=pl.ANY)] * 3,
+        out_specs=pl.BlockSpec(memory_space=pltpu.VMEM),
+        scratch_shapes=[
+            pltpu.VMEM(q.shape, BF),
+            pltpu.VMEM(new.shape, BF),
+            pltpu.VMEM(keys.shape, BF),
+            pltpu.VMEM((rows, 1), F32),
+            pltpu.VMEM((rows, 1), F32),
+            pltpu.VMEM((rows, LAT), F32),
+            pltpu.SemaphoreType.DMA((2,)),
+            pltpu.SemaphoreType.DMA((blocks,)),
+        ],
         out_shape=jax.ShapeDtypeStruct((rows // STEPS, STEPS, LAT), BF),
         compiler_params=pltpu.CompilerParams(vmem_limit_bytes=56 * 1024 * 1024),
         cost_estimate=pl.CostEstimate(
@@ -185,7 +202,7 @@
         out_specs=[pl.BlockSpec(memory_space=pltpu.VMEM)] * 4,
         out_shape=[jax.ShapeDtypeStruct(a.shape, a.dtype) for a in [passed] + arrays],
         scratch_shapes=[pltpu.SemaphoreType.DMA((13,))],
-        compiler_params=pltpu.CompilerParams(vmem_limit_bytes=26 * 1024 * 1024),
+        compiler_params=pltpu.CompilerParams(vmem_limit_bytes=36 * 1024 * 1024),
         cost_estimate=pl.CostEstimate(
             flops=0, bytes_accessed=sum(4 * a.size for a in arrays), transcendentals=0
         ),
@@ -193,7 +210,7 @@
     )(passed, *arrays)
 
 
-def expert_kernel(n, expert_ref, *refs):
+def expert_kernel(n, me_ref, *refs, n_ep):
     blocks, (gate_ref, up_ref, down_ref, near_ref, far_ref) = refs[:8], refs[8:]
     rows = n * STEPS
     width, units = gate_ref.shape
@@ -208,7 +225,7 @@
     act = (gate * jax.nn.sigmoid(gate) * up).astype(BF)
     routes = jnp.concatenate([ref[:, width:] for ref in blocks], axis=0).astype(F32)
     scores = routes[:, TOPK : 2 * TOPK] + routes[:, 2 * TOPK : 3 * TOPK]
-    chosen = jnp.where(routes[:, :TOPK] == expert_ref[0].astype(F32), scores, 0.0)
+    chosen = jnp.where(routes[:, :TOPK] == (me_ref[0] % n_ep).astype(F32), scores, 0.0)
     coef = jnp.sum(chosen, axis=1, keepdims=True) / jnp.sum(scores, axis=1, keepdims=True) * 2.5
     for p in range(SPAN):
         here = slice(p * part, (p + 1) * part)
@@ -263,7 +280,7 @@
     heads = queries.shape[2]
     width = residual.shape[2]
     rows = n * STEPS
-    me = lax.axis_index(AXES).astype(jnp.int32)
+    me_one = lax.axis_index(AXES).astype(jnp.int32).reshape(1)
 
     with jax.named_scope("attention"):
         latents = attend(
@@ -280,7 +297,7 @@
             heads_kernel,
             n,
             [jax.ShapeDtypeStruct((rows // 2, width), dtype) for dtype in (F32, BF)],
-            [me.reshape(1)],
+            [me_one],
             [latents.reshape(rows, LAT), w_uv[0], w_out[0]],
             "heads",
             2 * rows * VDIM * (LAT + width),
@@ -313,10 +330,10 @@
 
     with jax.named_scope("experts"):
         near, far = single(
-            expert_kernel,
+            functools.partial(expert_kernel, n_ep=n_ep),
             n,
             [jax.ShapeDtypeStruct((rows // 2, width), dtype) for dtype in (F32, BF)],
-            [(me % n_ep).reshape(1)],
+            [me_one],
             blocks + weights,
             "experts",
             6 * rows * width * w_gate.shape[2],

time: 121 us -> 108 us (0.89)
  local copies, waits for them, and re-layouts: 18.4 us -> 3.41 us
  starting transfers between devices: 32.6 us -> 35.7 us
    unnamed x24 -> x14, local copies, waits for them, and re-layouts: 18.1 us -> 3.11 us
    pallas_call x1, Pallas kernels: 8 us -> 4.57 us  [attend(): pl.pallas_call(functools.partial(attend_kernel, n), in_specs=[pl.BlockSpe...]
    all_to_all x1, starting transfers between devices: 7.93 us -> 11 us  [per_device(): latents = lax.all_to_all(latents, AXES, 0, 0, tiled=True)]
    pallas_call x1, Pallas kernels: 7.71 us -> 10.6 us  [load(): pl.pallas_call(functools.partial(load_kernel, n), in_specs=[pl.BlockSpec(...]
  transfers between devices with their start and end apart: 25 -> 25, of which waited for: 18 -> 18; matrix products, arithmetic and copies ran while one was open for 0% -> 0% of each run, Pallas kernels for 6% -> 10%
where the time goes in v4:
time: 108 us
  waiting for transfers between devices  46.1 us (43%)
  starting transfers between devices  35.7 us (33%)
  Pallas kernels  19.9 us (18%)
  local copies, waits for them, and re-layouts  3.41 us (3%)
  other arithmetic  1.58 us (1%)
    ppermute x24, waiting for transfers between devices, swap(): return lax.ppermute(x, AXES, [(d, d ^ mask) for d in range(n)])  37.9 us
    ppermute x24, starting transfers between devices, swap(): return lax.ppermute(x, AXES, [(d, d ^ mask) for d in range(n)])  24.7 us
    all_to_all x1, starting transfers between devices, per_device(): latents = lax.all_to_all(latents, AXES, 0, 0, tiled=True)  11 us
    pallas_call x1, Pallas kernels, load(): pl.pallas_call(functools.partial(load_kernel, n), in_specs=[pl.BlockSpec(...  10.6 us
    all_to_all x1, waiting for transfers between devices, per_device(): latents = lax.all_to_all(latents, AXES, 0, 0, tiled=True)  8.22 us
    pallas_call x3, Pallas kernels, single(): pl.pallas_call(functools.partial(kernel, n), in_specs=[pl.BlockSpec(memor...  4.74 us
    pallas_call x1, Pallas kernels, attend(): pl.pallas_call(functools.partial(attend_kernel, n), in_specs=[pl.BlockSpe...  4.57 us
    unnamed x14, local copies, waits for them, and re-layouts  3.11 us
  transfers between devices with their start and end apart: 25, of which 18 were waited for; matrix products, arithmetic and copies ran while one was open for 0% of the time, Pallas kernels for 10%

profile of v4, /device:TPU:0, one launch (start us, length us, event | category | flops | bytes accessed | tf_op | source)
XLA Modules:
  0.0 107.7 jit_solution(22560079357506122)
XLA Ops:
  0.7 4.6 %attend.1 = bf16[32,4,512]{2,1,0:T(4,128)(2,1)} custom-call(s32[1]{0:T(128)S(6)} %copy.14.len_ref, bf16[128,576]{1,0:T(8,128)(2,1)} %bitcast.29, bf16[4,576]{1,0:T(4,128)(2,1)} %bitcast.30, bf16[576,8192]{1,0:T(8,128)(2,1)} %bitcast.25), custom_call_target="tpu_custom_call" | custom-call | flops 2281701376 | bytes 9437184 | tf_op jit(solution)/shard_map/attention/attend/pallas_call | solution.py:122
  5.3 11.0 %all-to-all-start = ((bf16[32,4,512]{2,1,0:T(4,128)(2,1)}), bf16[32,4,512]{2,1,0:T(4,128)(2,1)S(1)}, u32[]{:S(2)}, u32[]{:S(2)}) async-start(bf16[32,4,512]{2,1,0:T(4,128)(2,1)} %attend.1), calls=%async_computation | async-start | bytes 262144 | tf_op jit(solution)/shard_map/heads/all_to_all | solution.py:295
  16.3 8.2 %all-to-all-done = bf16[32,4,512]{2,1,0:T(4,128)(2,1)S(1)} async-done(((bf16[32,4,512]{2,1,0:T(4,128)(2,1)}), bf16[32,4,512]{2,1,0:T(4,128)(2,1)S(1)}, u32[]{:S(2)}, u32[]{:S(2)}) %all-to-all-start) | async-done | bytes 131104 | tf_op jit(solution)/shard_map/heads/all_to_all | solution.py:295
  25.8 2.2 %collective-permute-done = bf16[64,7168]{1,0:T(8,128)(2,1)S(1)} collective-permute-done((bf16[64,7168]{1,0:T(8,128)(2,1)S(1)}, bf16[64,7168]{1,0:T(8,128)(2,1)S(1)}, u32[]{:S(2)}, u32[]{:S(2)}) %collective-permute-start) | collective-permute-done | bytes 917536 | tf_op jit(solution)/shard_map/heads/ppermute | solution.py:31
  28.9 1.7 %collective-permute-start.3 = (bf16[16,7168]{1,0:T(8,128)(2,1)S(1)}, bf16[16,7168]{1,0:T(8,128)(2,1)S(1)}, u32[]{:S(2)}, u32[]{:S(2)}) collective-permute-start(bf16[16,7168]{1,0:T(8,128)(2,1)S(1)} %get-tuple-element.39), channel_id=1, source_target_pairs={{0,18},{1,19},{2,16},{3,17},{4,22},{5,23},{6,20},{7,21},{8,26},{9,... | collective-permute-start | bytes 688136 | tf_op jit(solution)/shard_map/heads/ppermute | solution.py:31
  30.6 1.3 %collective-permute-start.2 = (bf16[16,7168]{1,0:T(8,128)(2,1)S(1)}, bf16[16,7168]{1,0:T(8,128)(2,1)S(1)}, u32[]{:S(2)}, u32[]{:S(2)}) collective-permute-start(bf16[16,7168]{1,0:T(8,128)(2,1)S(1)} %get-tuple-element.40), channel_id=1, source_target_pairs={{0,16},{1,17},{2,18},{3,19},{4,20},{5,21},{6,22},{7,23},{8,24},{9,... | collective-permute-start | bytes 688136 | tf_op jit(solution)/shard_map/heads/ppermute | solution.py:31
  31.9 9.1 %collective-permute-done.1 = bf16[16,7168]{1,0:T(8,128)(2,1)S(1)} collective-permute-done((bf16[16,7168]{1,0:T(8,128)(2,1)S(1)}, bf16[16,7168]{1,0:T(8,128)(2,1)S(1)}, u32[]{:S(2)}, u32[]{:S(2)}) %collective-permute-start.1) | collective-permute-done | bytes 229408 | tf_op jit(solution)/shard_map/heads/ppermute | solution.py:31
  42.5 1.3 %collective-permute-start.6 = (bf16[4,7168]{1,0:T(4,128)(2,1)S(1)}, bf16[4,7168]{1,0:T(4,128)(2,1)S(1)}, u32[]{:S(2)}, u32[]{:S(2)}) collective-permute-start(bf16[4,7168]{1,0:T(4,128)(2,1)S(1)} %get-tuple-element.44), channel_id=1, source_target_pairs={{0,12},{1,13},{2,14},{3,15},{4,8},{5,9},{6,10},{7,11},{8,4},{9,5},... | collective-permute-start | bytes 172040 | tf_op jit(solution)/shard_map/heads/ppermute | solution.py:31
  44.0 2.9 %collective-permute-start.4 = (bf16[4,7168]{1,0:T(4,128)(2,1)S(1)}, bf16[4,7168]{1,0:T(4,128)(2,1)S(1)}, u32[]{:S(2)}, u32[]{:S(2)}) collective-permute-start(bf16[4,7168]{1,0:T(4,128)(2,1)S(1)} %get-tuple-element.46), channel_id=1, source_target_pairs={{0,4},{1,5},{2,6},{3,7},{4,0},{5,1},{6,2},{7,3},{8,12},{9,13},{10,... | collective-permute-start | bytes 172040 | tf_op jit(solution)/shard_map/heads/ppermute | solution.py:31
  47.0 1.6 %collective-permute-done.6.refs_3_ = bf16[4,7168]{1,0:T(4,128)(2,1)S(1)} collective-permute-done((bf16[4,7168]{1,0:T(4,128)(2,1)S(1)}, bf16[4,7168]{1,0:T(4,128)(2,1)S(1)}, u32[]{:S(2)}, u32[]{:S(2)}) %collective-permute-start.6) | collective-permute-done | bytes 57376 | tf_op jit(solution)/shard_map/heads/ppermute | solution.py:31
  50.0 1.8 %collective-permute-start.9 = (bf16[4,7296]{1,0:T(4,128)(2,1)S(1)}, bf16[4,7296]{1,0:T(4,128)(2,1)S(1)}, u32[]{:S(2)}, u32[]{:S(2)}) collective-permute-start(bf16[4,7296]{1,0:T(4,128)(2,1)S(1)} %get-tuple-element.18), channel_id=1, source_target_pairs={{0,12},{1,13},{2,14},{3,15},{4,8},{5,9},{6,10},{7,11},{8,4},{9,5},... | collective-permute-start | bytes 175112 | tf_op jit(solution)/shard_map/spread/ppermute | solution.py:31
  52.8 1.7 %collective-permute-start.7 = (bf16[4,7296]{1,0:T(4,128)(2,1)S(1)}, bf16[4,7296]{1,0:T(4,128)(2,1)S(1)}, u32[]{:S(2)}, u32[]{:S(2)}) collective-permute-start(bf16[4,7296]{1,0:T(4,128)(2,1)S(1)} %get-tuple-element.18), channel_id=1, source_target_pairs={{0,4},{1,5},{2,6},{3,7},{4,0},{5,1},{6,2},{7,3},{8,12},{9,13},{10,... | collective-permute-start | bytes 175112 | tf_op jit(solution)/shard_map/spread/ppermute | solution.py:31
  54.5 2.3 %collective-permute-done.9 = bf16[4,7296]{1,0:T(4,128)(2,1)S(1)} collective-permute-done((bf16[4,7296]{1,0:T(4,128)(2,1)S(1)}, bf16[4,7296]{1,0:T(4,128)(2,1)S(1)}, u32[]{:S(2)}, u32[]{:S(2)}) %collective-permute-start.9) | collective-permute-done | bytes 58400 | tf_op jit(solution)/shard_map/spread/ppermute | solution.py:31
  57.9 1.3 %collective-permute-start.12 = (bf16[16,7296]{1,0:T(8,128)(2,1)S(1)}, bf16[16,7296]{1,0:T(8,128)(2,1)S(1)}, u32[]{:S(2)}, u32[]{:S(2)}) collective-permute-start(bf16[16,7296]{1,0:T(8,128)(2,1)S(1)} %pad_maximum_fusion.refs_0_), channel_id=1, source_target_pairs={{0,18},{1,19},{2,16},{3,17},{4,22},{5,23},{6,20},{7,21},{8,26},{9,... | collective-permute-start | bytes 700424 | tf_op jit(solution)/shard_map/spread/ppermute | solution.py:31
  59.2 1.4 %collective-permute-start.11 = (bf16[16,7296]{1,0:T(8,128)(2,1)S(1)}, bf16[16,7296]{1,0:T(8,128)(2,1)S(1)}, u32[]{:S(2)}, u32[]{:S(2)}) collective-permute-start(bf16[16,7296]{1,0:T(8,128)(2,1)S(1)} %pad_maximum_fusion.refs_0_), channel_id=1, source_target_pairs={{0,16},{1,17},{2,18},{3,19},{4,20},{5,21},{6,22},{7,23},{8,24},{9,... | collective-permute-start | bytes 700424 | tf_op jit(solution)/shard_map/spread/ppermute | solution.py:31
  61.4 10.6 %load_experts.1 = (bf16[16,7296]{1,0:T(8,128)(2,1)S(1)}, bf16[7168,512]{1,0:T(8,128)(2,1)S(1)}, bf16[7168,512]{1,0:T(8,128)(2,1)S(1)}, bf16[512,7168]{1,0:T(8,128)(2,1)}) custom-call(bf16[16,7296]{1,0:T(8,128)(2,1)S(1)} %pad_maximum_fusion.refs_0_, bf16[7168,512]{1,0:T(8,128)(2,1)} %bitcast.26, bf16[7168,512]{1,0:T(8,128)(2,1)} %bitcast.27, ...), custom_call_target="tpu_custom_call" | custom-call | bytes 44040192 | tf_op jit(solution)/shard_map/spread/load_experts/pallas_call | solution.py:199
  74.6 3.1 %copy-done = bf16[512,7168]{1,0:T(8,128)(2,1)S(1)} copy-done((bf16[512,7168]{1,0:T(8,128)(2,1)S(1)}, bf16[512,7168]{1,0:T(8,128)(2,1)}, u32[]{:S(2)}) %copy-start) | copy-done | bytes 7340056
  77.7 3.6 %experts.1 = (f32[64,7168]{1,0:T(8,128)S(1)}, bf16[64,7168]{1,0:T(8,128)(2,1)S(1)}) custom-call(s32[1]{0:T(128)} %bitcast.me_ref, bf16[16,7296]{1,0:T(8,128)(2,1)S(1)} %pad_maximum_fusion.refs_0_, bf16[16,7296]{1,0:T(8,128)(2,1)S(1)} %collective-permute-done.10.refs_1_, bf16[16,7296]{1,0:T(8,128)(2,1)S(1)} %collective-permute-done.11.refs_2_, ...), custom_call_target="tpu_custom_call" | custom-call | flops 2818572288 | bytes 23887872 | tf_op jit(solution)/shard_map/experts/experts/pallas_call | solution.py:238
  81.5 2.3 %collective-permute-done.17 = bf16[64,7168]{1,0:T(8,128)(2,1)S(1)} collective-permute-done((bf16[64,7168]{1,0:T(8,128)(2,1)S(1)}, bf16[64,7168]{1,0:T(8,128)(2,1)S(1)}, u32[]{:S(2)}, u32[]{:S(2)}) %collective-permute-start.17) | collective-permute-done | bytes 917536 | tf_op jit(solution)/shard_map/collect/ppermute | solution.py:31
  85.3 1.8 %collective-permute-start.20 = (bf16[16,7168]{1,0:T(8,128)(2,1)S(1)}, bf16[16,7168]{1,0:T(8,128)(2,1)S(1)}, u32[]{:S(2)}, u32[]{:S(2)}) collective-permute-start(bf16[16,7168]{1,0:T(8,128)(2,1)S(1)} %get-tuple-element.36), channel_id=1, source_target_pairs={{0,18},{1,19},{2,16},{3,17},{4,22},{5,23},{6,20},{7,21},{8,26},{9,... | collective-permute-start | bytes 688136 | tf_op jit(solution)/shard_map/collect/ppermute | solution.py:31
  87.7 9.1 %collective-permute-done.18 = bf16[16,7168]{1,0:T(8,128)(2,1)S(1)} collective-permute-done((bf16[16,7168]{1,0:T(8,128)(2,1)S(1)}, bf16[16,7168]{1,0:T(8,128)(2,1)S(1)}, u32[]{:S(2)}, u32[]{:S(2)}) %collective-permute-start.18) | collective-permute-done | bytes 229408 | tf_op jit(solution)/shard_map/collect/ppermute | solution.py:31
  99.2 1.7 %collective-permute-start.23 = (bf16[4,7168]{1,0:T(4,128)(2,1)S(1)}, bf16[4,7168]{1,0:T(4,128)(2,1)S(1)}, u32[]{:S(2)}, u32[]{:S(2)}) collective-permute-start(bf16[4,7168]{1,0:T(4,128)(2,1)S(1)} %get-tuple-element.42), channel_id=1, source_target_pairs={{0,12},{1,13},{2,14},{3,15},{4,8},{5,9},{6,10},{7,11},{8,4},{9,5},... | collective-permute-start | bytes 172040 | tf_op jit(solution)/shard_map/collect/ppermute | solution.py:31
  102.5 2.7 %collective-permute-done.23 = bf16[4,7168]{1,0:T(4,128)(2,1)S(1)} collective-permute-done((bf16[4,7168]{1,0:T(4,128)(2,1)S(1)}, bf16[4,7168]{1,0:T(4,128)(2,1)S(1)}, u32[]{:S(2)}, u32[]{:S(2)}) %collective-permute-start.23) | collective-permute-done | bytes 57376 | tf_op jit(solution)/shard_map/collect/ppermute | solution.py:31
  105.2 1.8 %collective-permute-done.22 = bf16[4,7168]{1,0:T(4,128)(2,1)S(1)} collective-permute-done((bf16[4,7168]{1,0:T(4,128)(2,1)S(1)}, bf16[4,7168]{1,0:T(4,128)(2,1)S(1)}, u32[]{:S(2)}, u32[]{:S(2)}) %collective-permute-start.22) | collective-permute-done | bytes 57376 | tf_op jit(solution)/shard_map/collect/ppermute | solution.py:31
  (61 shorter events, 17.8 us)
Async XLA Ops:
  5.3 19.2 %all-to-all-start = ((bf16[32,4,512]{2,1,0:T(4,128)(2,1)}), bf16[32,4,512]{2,1,0:T(4,128)(2,1)S(1)}, u32[]{:S(2)}, u32[]{:S(2)}) async-start(bf16[32,4,512]{2,1,0:T(4,128)(2,1)} %attend.1), calls=%async_computation | async-start | bytes 262144 | tf_op jit(solution)/shard_map/heads/all_to_all | solution.py:295
  25.5 2.5 %collective-permute-start = (bf16[64,7168]{1,0:T(8,128)(2,1)S(1)}, bf16[64,7168]{1,0:T(8,128)(2,1)S(1)}, u32[]{:S(2)}, u32[]{:S(2)}) collective-permute-start(bf16[64,7168]{1,0:T(8,128)(2,1)S(1)} %get-tuple-element.16), channel_id=1, source_target_pairs={{0,1},{1,0},{2,3},{3,2},{4,5},{5,4},{6,7},{7,6},{8,9},{9,8},{10,11... | collective-permute-start | bytes 2752520 | tf_op jit(solution)/shard_map/heads/ppermute | solution.py:31
  28.3 12.7 %collective-permute-start.1 = (bf16[16,7168]{1,0:T(8,128)(2,1)S(1)}, bf16[16,7168]{1,0:T(8,128)(2,1)S(1)}, u32[]{:S(2)}, u32[]{:S(2)}) collective-permute-start(bf16[16,7168]{1,0:T(8,128)(2,1)S(1)} %get-tuple-element.38), channel_id=1, source_target_pairs={{0,2},{1,3},{2,0},{3,1},{4,6},{5,7},{6,4},{7,5},{8,10},{9,11},{10,... | collective-permute-start | bytes 688136 | tf_op jit(solution)/shard_map/heads/ppermute | solution.py:31
  28.9 12.2 %collective-permute-start.3 = (bf16[16,7168]{1,0:T(8,128)(2,1)S(1)}, bf16[16,7168]{1,0:T(8,128)(2,1)S(1)}, u32[]{:S(2)}, u32[]{:S(2)}) collective-permute-start(bf16[16,7168]{1,0:T(8,128)(2,1)S(1)} %get-tuple-element.39), channel_id=1, source_target_pairs={{0,18},{1,19},{2,16},{3,17},{4,22},{5,23},{6,20},{7,21},{8,26},{9,... | collective-permute-start | bytes 688136 | tf_op jit(solution)/shard_map/heads/ppermute | solution.py:31
  30.6 11.7 %collective-permute-start.2 = (bf16[16,7168]{1,0:T(8,128)(2,1)S(1)}, bf16[16,7168]{1,0:T(8,128)(2,1)S(1)}, u32[]{:S(2)}, u32[]{:S(2)}) collective-permute-start(bf16[16,7168]{1,0:T(8,128)(2,1)S(1)} %get-tuple-element.40), channel_id=1, source_target_pairs={{0,16},{1,17},{2,18},{3,19},{4,20},{5,21},{6,22},{7,23},{8,24},{9,... | collective-permute-start | bytes 688136 | tf_op jit(solution)/shard_map/heads/ppermute | solution.py:31
  42.5 6.2 %collective-permute-start.6 = (bf16[4,7168]{1,0:T(4,128)(2,1)S(1)}, bf16[4,7168]{1,0:T(4,128)(2,1)S(1)}, u32[]{:S(2)}, u32[]{:S(2)}) collective-permute-start(bf16[4,7168]{1,0:T(4,128)(2,1)S(1)} %get-tuple-element.44), channel_id=1, source_target_pairs={{0,12},{1,13},{2,14},{3,15},{4,8},{5,9},{6,10},{7,11},{8,4},{9,5},... | collective-permute-start | bytes 172040 | tf_op jit(solution)/shard_map/heads/ppermute | solution.py:31
  43.7 6.1 %collective-permute-start.5 = (bf16[4,7168]{1,0:T(4,128)(2,1)S(1)}, bf16[4,7168]{1,0:T(4,128)(2,1)S(1)}, u32[]{:S(2)}, u32[]{:S(2)}) collective-permute-start(bf16[4,7168]{1,0:T(4,128)(2,1)S(1)} %get-tuple-element.45), channel_id=1, source_target_pairs={{0,8},{1,9},{2,10},{3,11},{4,12},{5,13},{6,14},{7,15},{8,0},{9,1},... | collective-permute-start | bytes 172040 | tf_op jit(solution)/shard_map/heads/ppermute | solution.py:31
  44.0 5.8 %collective-permute-start.4 = (bf16[4,7168]{1,0:T(4,128)(2,1)S(1)}, bf16[4,7168]{1,0:T(4,128)(2,1)S(1)}, u32[]{:S(2)}, u32[]{:S(2)}) collective-permute-start(bf16[4,7168]{1,0:T(4,128)(2,1)S(1)} %get-tuple-element.46), channel_id=1, source_target_pairs={{0,4},{1,5},{2,6},{3,7},{4,0},{5,1},{6,2},{7,3},{8,12},{9,13},{10,... | collective-permute-start | bytes 172040 | tf_op jit(solution)/shard_map/heads/ppermute | solution.py:31
  50.0 6.7 %collective-permute-start.9 = (bf16[4,7296]{1,0:T(4,128)(2,1)S(1)}, bf16[4,7296]{1,0:T(4,128)(2,1)S(1)}, u32[]{:S(2)}, u32[]{:S(2)}) collective-permute-start(bf16[4,7296]{1,0:T(4,128)(2,1)S(1)} %get-tuple-element.18), channel_id=1, source_target_pairs={{0,12},{1,13},{2,14},{3,15},{4,8},{5,9},{6,10},{7,11},{8,4},{9,5},... | collective-permute-start | bytes 175112 | tf_op jit(solution)/shard_map/spread/ppermute | solution.py:31
  51.8 5.9 %collective-permute-start.8 = (bf16[4,7296]{1,0:T(4,128)(2,1)S(1)}, bf16[4,7296]{1,0:T(4,128)(2,1)S(1)}, u32[]{:S(2)}, u32[]{:S(2)}) collective-permute-start(bf16[4,7296]{1,0:T(4,128)(2,1)S(1)} %get-tuple-element.18), channel_id=1, source_target_pairs={{0,8},{1,9},{2,10},{3,11},{4,12},{5,13},{6,14},{7,15},{8,0},{9,1},... | collective-permute-start | bytes 175112 | tf_op jit(solution)/shard_map/spread/ppermute | solution.py:31
  52.8 4.9 %collective-permute-start.7 = (bf16[4,7296]{1,0:T(4,128)(2,1)S(1)}, bf16[4,7296]{1,0:T(4,128)(2,1)S(1)}, u32[]{:S(2)}, u32[]{:S(2)}) collective-permute-start(bf16[4,7296]{1,0:T(4,128)(2,1)S(1)} %get-tuple-element.18), channel_id=1, source_target_pairs={{0,4},{1,5},{2,6},{3,7},{4,0},{5,1},{6,2},{7,3},{8,12},{9,13},{10,... | collective-permute-start | bytes 175112 | tf_op jit(solution)/shard_map/spread/ppermute | solution.py:31
  57.9 14.2 %collective-permute-start.12 = (bf16[16,7296]{1,0:T(8,128)(2,1)S(1)}, bf16[16,7296]{1,0:T(8,128)(2,1)S(1)}, u32[]{:S(2)}, u32[]{:S(2)}) collective-permute-start(bf16[16,7296]{1,0:T(8,128)(2,1)S(1)} %pad_maximum_fusion.refs_0_), channel_id=1, source_target_pairs={{0,18},{1,19},{2,16},{3,17},{4,22},{5,23},{6,20},{7,21},{8,26},{9,... | collective-permute-start | bytes 700424 | tf_op jit(solution)/shard_map/spread/ppermute | solution.py:31
  59.2 13.5 %collective-permute-start.11 = (bf16[16,7296]{1,0:T(8,128)(2,1)S(1)}, bf16[16,7296]{1,0:T(8,128)(2,1)S(1)}, u32[]{:S(2)}, u32[]{:S(2)}) collective-permute-start(bf16[16,7296]{1,0:T(8,128)(2,1)S(1)} %pad_maximum_fusion.refs_0_), channel_id=1, source_target_pairs={{0,16},{1,17},{2,18},{3,19},{4,20},{5,21},{6,22},{7,23},{8,24},{9,... | collective-permute-start | bytes 700424 | tf_op jit(solution)/shard_map/spread/ppermute | solution.py:31
  60.6 12.2 %collective-permute-start.10 = (bf16[16,7296]{1,0:T(8,128)(2,1)S(1)}, bf16[16,7296]{1,0:T(8,128)(2,1)S(1)}, u32[]{:S(2)}, u32[]{:S(2)}) collective-permute-start(bf16[16,7296]{1,0:T(8,128)(2,1)S(1)} %pad_maximum_fusion.refs_0_), channel_id=1, source_target_pairs={{0,2},{1,3},{2,0},{3,1},{4,6},{5,7},{6,4},{7,5},{8,10},{9,11},{10,... | collective-permute-start | bytes 700424 | tf_op jit(solution)/shard_map/spread/ppermute | solution.py:31
  72.1 1.8 %collective-permute-start.16 = (bf16[16,7296]{1,0:T(8,128)(2,1)S(1)}, bf16[16,7296]{1,0:T(8,128)(2,1)S(1)}, u32[]{:S(2)}, u32[]{:S(2)}) collective-permute-start(bf16[16,7296]{1,0:T(8,128)(2,1)S(1)} %collective-permute-done.12.refs_3_), channel_id=1, source_target_pairs={{0,1},{1,0},{2,3},{3,2},{4,5},{5,4},{6,7},{7,6},{8,9},{9,8},{10,11... | collective-permute-start | bytes 700424 | tf_op jit(solution)/shard_map/spread/ppermute | solution.py:31
  72.6 1.6 %collective-permute-start.15 = (bf16[16,7296]{1,0:T(8,128)(2,1)S(1)}, bf16[16,7296]{1,0:T(8,128)(2,1)S(1)}, u32[]{:S(2)}, u32[]{:S(2)}) collective-permute-start(bf16[16,7296]{1,0:T(8,128)(2,1)S(1)} %collective-permute-done.11.refs_2_), channel_id=1, source_target_pairs={{0,1},{1,0},{2,3},{3,2},{4,5},{5,4},{6,7},{7,6},{8,9},{9,8},{10,11... | collective-permute-start | bytes 700424 | tf_op jit(solution)/shard_map/spread/ppermute | solution.py:31
  72.7 1.9 %collective-permute-start.14 = (bf16[16,7296]{1,0:T(8,128)(2,1)S(1)}, bf16[16,7296]{1,0:T(8,128)(2,1)S(1)}, u32[]{:S(2)}, u32[]{:S(2)}) collective-permute-start(bf16[16,7296]{1,0:T(8,128)(2,1)S(1)} %collective-permute-done.10.refs_1_), channel_id=1, source_target_pairs={{0,1},{1,0},{2,3},{3,2},{4,5},{5,4},{6,7},{7,6},{8,9},{9,8},{10,11... | collective-permute-start | bytes 700424 | tf_op jit(solution)/shard_map/spread/ppermute | solution.py:31
  81.3 2.5 %collective-permute-start.17 = (bf16[64,7168]{1,0:T(8,128)(2,1)S(1)}, bf16[64,7168]{1,0:T(8,128)(2,1)S(1)}, u32[]{:S(2)}, u32[]{:S(2)}) collective-permute-start(bf16[64,7168]{1,0:T(8,128)(2,1)S(1)} %get-tuple-element.24), channel_id=1, source_target_pairs={{0,1},{1,0},{2,3},{3,2},{4,5},{5,4},{6,7},{7,6},{8,9},{9,8},{10,11... | collective-permute-start | bytes 2752520 | tf_op jit(solution)/shard_map/collect/ppermute | solution.py:31
  84.1 12.7 %collective-permute-start.18 = (bf16[16,7168]{1,0:T(8,128)(2,1)S(1)}, bf16[16,7168]{1,0:T(8,128)(2,1)S(1)}, u32[]{:S(2)}, u32[]{:S(2)}) collective-permute-start(bf16[16,7168]{1,0:T(8,128)(2,1)S(1)} %get-tuple-element.35), channel_id=1, source_target_pairs={{0,2},{1,3},{2,0},{3,1},{4,6},{5,7},{6,4},{7,5},{8,10},{9,11},{10,... | collective-permute-start | bytes 688136 | tf_op jit(solution)/shard_map/collect/ppermute | solution.py:31
  85.3 11.4 %collective-permute-start.20 = (bf16[16,7168]{1,0:T(8,128)(2,1)S(1)}, bf16[16,7168]{1,0:T(8,128)(2,1)S(1)}, u32[]{:S(2)}, u32[]{:S(2)}) collective-permute-start(bf16[16,7168]{1,0:T(8,128)(2,1)S(1)} %get-tuple-element.36), channel_id=1, source_target_pairs={{0,18},{1,19},{2,16},{3,17},{4,22},{5,23},{6,20},{7,21},{8,26},{9,... | collective-permute-start | bytes 688136 | tf_op jit(solution)/shard_map/collect/ppermute | solution.py:31
  87.1 10.9 %collective-permute-start.19 = (bf16[16,7168]{1,0:T(8,128)(2,1)S(1)}, bf16[16,7168]{1,0:T(8,128)(2,1)S(1)}, u32[]{:S(2)}, u32[]{:S(2)}) collective-permute-start(bf16[16,7168]{1,0:T(8,128)(2,1)S(1)} %get-tuple-element.37), channel_id=1, source_target_pairs={{0,16},{1,17},{2,18},{3,19},{4,20},{5,21},{6,22},{7,23},{8,24},{9,... | collective-permute-start | bytes 688136 | tf_op jit(solution)/shard_map/collect/ppermute | solution.py:31
  98.2 4.3 %collective-permute-start.21 = (bf16[4,7168]{1,0:T(4,128)(2,1)S(1)}, bf16[4,7168]{1,0:T(4,128)(2,1)S(1)}, u32[]{:S(2)}, u32[]{:S(2)}) collective-permute-start(bf16[4,7168]{1,0:T(4,128)(2,1)S(1)} %get-tuple-element.41), channel_id=1, source_target_pairs={{0,4},{1,5},{2,6},{3,7},{4,0},{5,1},{6,2},{7,3},{8,12},{9,13},{10,... | collective-permute-start | bytes 172040 | tf_op jit(solution)/shard_map/collect/ppermute | solution.py:31
  99.2 6.0 %collective-permute-start.23 = (bf16[4,7168]{1,0:T(4,128)(2,1)S(1)}, bf16[4,7168]{1,0:T(4,128)(2,1)S(1)}, u32[]{:S(2)}, u32[]{:S(2)}) collective-permute-start(bf16[4,7168]{1,0:T(4,128)(2,1)S(1)} %get-tuple-element.42), channel_id=1, source_target_pairs={{0,12},{1,13},{2,14},{3,15},{4,8},{5,9},{6,10},{7,11},{8,4},{9,5},... | collective-permute-start | bytes 172040 | tf_op jit(solution)/shard_map/collect/ppermute | solution.py:31
  100.9 6.1 %collective-permute-start.22 = (bf16[4,7168]{1,0:T(4,128)(2,1)S(1)}, bf16[4,7168]{1,0:T(4,128)(2,1)S(1)}, u32[]{:S(2)}, u32[]{:S(2)}) collective-permute-start(bf16[4,7168]{1,0:T(4,128)(2,1)S(1)} %get-tuple-element.43), channel_id=1, source_target_pairs={{0,8},{1,9},{2,10},{3,11},{4,12},{5,13},{6,14},{7,15},{8,0},{9,1},... | collective-permute-start | bytes 172040 | tf_op jit(solution)/shard_map/collect/ppermute | solution.py:31
  (8 other events, 85.6 us)

commit v5 on v4

--- a/solution.py
+++ b/solution.py
@@ -14,6 +14,7 @@
 STEPS = 4
 TOPK = 8
 BLK = 2048
+CHUNKS = 2
 SPAN = 8
 AXES = ("sec", "ep")
 NT = (((1,), (1,)), ((), ()))
@@ -153,7 +154,15 @@
     return me ^ ((q >> 1) * (n // 2) + k * 4 + (q & 1) * 2 + c), step
 
 
-def heads_kernel(n, me_ref, latents_ref, uv_ref, out_ref, near_ref, far_ref):
+def store_halves(out, p, near_refs, far_refs):
+    rows, part = out.shape
+    chunk, place = p // (SPAN // CHUNKS), p % (SPAN // CHUNKS)
+    here = slice(place * part, (place + 1) * part)
+    near_refs[chunk][:, here] = out[: rows // 2]
+    far_refs[chunk][:, here] = out[rows // 2 :].astype(BF)
+
+
+def heads_kernel(n, me_ref, latents_ref, uv_ref, out_ref, *refs):
     rows = n * STEPS
     values = jnp.dot(latents_ref[...], uv_ref[...], preferred_element_type=F32).astype(BF)
     device, step = partner_order(n, me_ref[0], rows)
@@ -162,27 +171,35 @@
     for p in range(SPAN):
         here = slice(p * part, (p + 1) * part)
         out = jnp.dot(values, out_ref[:, here], preferred_element_type=F32)
-        near_ref[:, here] = out[: rows // 2]
-        far_ref[:, here] = out[rows // 2 :].astype(BF)
+        store_halves(out, p, refs[:CHUNKS], refs[CHUNKS:])
 
 
 def norm_kernel(n, *refs):
-    parts, (residual_ref, gain_ref, routes_ref, hidden_ref, out_ref) = refs[:-5], refs[-5:]
-    hidden = residual_ref[...].astype(F32)
-    for ref in parts:
-        hidden += ref[...].astype(F32)
-    hidden_ref[...] = hidden
-    width = hidden.shape[1]
-    mean_square = jnp.sum(hidden * hidden, axis=1, keepdims=True) / width
-    normed = hidden * lax.rsqrt(mean_square + 1e-06) * gain_ref[...].astype(F32)
-    out_ref[:, :width] = normed.astype(BF)
-    out_ref[:, width:] = routes_ref[...]
+    planes = n // SPAN
+    parts, refs = refs[: planes * CHUNKS], refs[planes * CHUNKS :]
+    residual_ref, gain_ref, routes_ref, hidden_ref, out_refs = *refs[:4], refs[4:]
+    width = residual_ref.shape[1]
+    chunk = width // CHUNKS
+    square = 0.0
+    for c in range(CHUNKS):
+        here = slice(c * chunk, (c + 1) * chunk)
+        hidden = residual_ref[:, here].astype(F32)
+        for ref in parts[c * planes : (c + 1) * planes]:
+            hidden += ref[...].astype(F32)
+        hidden_ref[:, here] = hidden
+        square += jnp.sum(hidden * hidden, axis=1, keepdims=True)
+    factor = lax.rsqrt(square / width + 1e-06)
+    for c in range(CHUNKS):
+        here = slice(c * chunk, (c + 1) * chunk)
+        normed = hidden_ref[:, here] * factor * gain_ref[:, here].astype(F32)
+        out_refs[c][:, :chunk] = normed.astype(BF)
+    out_refs[-1][:, chunk:] = routes_ref[...]
 
 
 def load_kernel(n, *refs):
-    sources, targets, sem = refs[1:4], refs[5:8], refs[8]
-    copies = [pltpu.make_async_copy(refs[0], refs[4], sem.at[12])]
-    for i in range(3):
+    sources, targets, sem = refs[1:3], refs[4:6], refs[6]
+    copies = [pltpu.make_async_copy(refs[0], refs[3], sem.at[8])]
+    for i in range(2):
         step = sources[i].shape[0] // 4
         for j in range(4):
             here = pl.ds(j * step, step)
@@ -198,11 +215,11 @@
 def load(n, passed, arrays):
     return pl.pallas_call(
         functools.partial(load_kernel, n),
-        in_specs=[pl.BlockSpec(memory_space=pltpu.VMEM)] + [pl.BlockSpec(memory_space=pl.ANY)] * 3,
-        out_specs=[pl.BlockSpec(memory_space=pltpu.VMEM)] * 4,
+        in_specs=[pl.BlockSpec(memory_space=pltpu.VMEM)] + [pl.BlockSpec(memory_space=pl.ANY)] * 2,
+        out_specs=[pl.BlockSpec(memory_space=pltpu.VMEM)] * 3,
         out_shape=[jax.ShapeDtypeStruct(a.shape, a.dtype) for a in [passed] + arrays],
-        scratch_shapes=[pltpu.SemaphoreType.DMA((13,))],
-        compiler_params=pltpu.CompilerParams(vmem_limit_bytes=36 * 1024 * 1024),
+        scratch_shapes=[pltpu.SemaphoreType.DMA((9,))],
+        compiler_params=pltpu.CompilerParams(vmem_limit_bytes=44 * 1024 * 1024),
         cost_estimate=pl.CostEstimate(
             flops=0, bytes_accessed=sum(4 * a.size for a in arrays), transcendentals=0
         ),
@@ -210,28 +227,66 @@
     )(passed, *arrays)
 
 
-def expert_kernel(n, me_ref, *refs, n_ep):
-    blocks, (gate_ref, up_ref, down_ref, near_ref, far_ref) = refs[:8], refs[8:]
+def expert_kernel(n, n_ep, me_ref, *refs):
+    blocks, refs = refs[: 8 * CHUNKS], refs[8 * CHUNKS :]
+    gate_ref, up_ref, down_hbm, refs = *refs[:3], refs[3:]
+    near_refs, far_refs, down_ref, sem = refs[:CHUNKS], refs[CHUNKS : 2 * CHUNKS], *refs[2 * CHUNKS :]
     rows = n * STEPS
     width, units = gate_ref.shape
     part = width // SPAN
+    down_copies = []
+    for p in range(SPAN):
+        here = pl.ds(p * part, part)
+        down_copies.append(
+            pltpu.make_async_copy(down_hbm.at[:, here], down_ref.at[:, here], sem.at[p])
+        )
+    for copy in down_copies:
+        copy.start()
     gate = jnp.zeros((rows, units), F32)
     up = jnp.zeros((rows, units), F32)
     for p in range(SPAN):
+        chunk, place = p // (SPAN // CHUNKS), p % (SPAN // CHUNKS)
+        here = slice(place * part, (place + 1) * part)
+        x = jnp.concatenate([ref[:, here] for ref in blocks[8 * chunk : 8 * chunk + 8]], axis=0)
         here = slice(p * part, (p + 1) * part)
-        x = jnp.concatenate([ref[:, here] for ref in blocks], axis=0)
         gate += jnp.dot(x, gate_ref[here], preferred_element_type=F32)
         up += jnp.dot(x, up_ref[here], preferred_element_type=F32)
     act = (gate * jax.nn.sigmoid(gate) * up).astype(BF)
-    routes = jnp.concatenate([ref[:, width:] for ref in blocks], axis=0).astype(F32)
+    routes = [ref[:, width // CHUNKS :] for ref in blocks[-8:]]
+    routes = jnp.concatenate(routes, axis=0).astype(F32)
     scores = routes[:, TOPK : 2 * TOPK] + routes[:, 2 * TOPK : 3 * TOPK]
     chosen = jnp.where(routes[:, :TOPK] == (me_ref[0] % n_ep).astype(F32), scores, 0.0)
     coef = jnp.sum(chosen, axis=1, keepdims=True) / jnp.sum(scores, axis=1, keepdims=True) * 2.5
     for p in range(SPAN):
-        here = slice(p * part, (p + 1) * part)
-        out = jnp.dot(act, down_ref[:, here], preferred_element_type=F32) * coef
-        near_ref[:, here] = out[: rows // 2]
-        far_ref[:, here] = out[rows // 2 :].astype(BF)
+        down_copies[p].wait()
+        down = down_ref[:, p * part : (p + 1) * part]
+        out = jnp.dot(act, down, preferred_element_type=F32) * coef
+        store_halves(out, p, near_refs, far_refs)
+
+
+def halves(n, width):
+    shape = (n * STEPS // 2, width // CHUNKS)
+    return [jax.ShapeDtypeStruct(shape, dtype) for dtype in [F32] * CHUNKS + [BF] * CHUNKS]
+
+
+def run_experts(n, n_ep, me, blocks, gate, up, down):
+    rows = n * STEPS
+    units, width = down.shape
+    return pl.pallas_call(
+        functools.partial(expert_kernel, n, n_ep),
+        in_specs=[pl.BlockSpec(memory_space=pltpu.SMEM)]
+        + [pl.BlockSpec(memory_space=pltpu.VMEM)] * (len(blocks) + 2)
+        + [pl.BlockSpec(memory_space=pl.ANY)],
+        out_shape=halves(n, width),
+        scratch_shapes=[pltpu.VMEM(down.shape, BF), pltpu.SemaphoreType.DMA((SPAN,))],
+        compiler_params=pltpu.CompilerParams(vmem_limit_bytes=40 * 1024 * 1024),
+        cost_estimate=pl.CostEstimate(
+            flops=6 * rows * width * units,
+            bytes_accessed=6 * width * units,
+            transcendentals=rows * units,
+        ),
+        name="experts",
+    )(me, *blocks, gate, up, down)
 
 
 def single(kernel, n, out_shape, scalars, arrays, name, flops):
@@ -293,57 +348,56 @@
 
     with jax.named_scope("heads"):
         latents = lax.all_to_all(latents, AXES, 0, 0, tiled=True)
-        near, far = single(
+        out = single(
             heads_kernel,
             n,
-            [jax.ShapeDtypeStruct((rows // 2, width), dtype) for dtype in (F32, BF)],
+            halves(n, width),
             [me_one],
             [latents.reshape(rows, LAT), w_uv[0], w_out[0]],
             "heads",
             2 * rows * VDIM * (LAT + width),
         )
-        parts = reduce_rows(near, far, n)
+        parts = [reduce_rows(out[c], out[CHUNKS + c], n) for c in range(CHUNKS)]
 
     with jax.named_scope("norm"):
         high = route_scores[0].astype(BF)
         low = (route_scores[0] - high.astype(F32)).astype(BF)
         routes = jnp.concatenate([route_ids[0].astype(BF), high, low], axis=1)
         routes = jnp.pad(routes, ((0, 0), (0, 128 - 3 * TOPK)))
-        hidden, normed = single(
+        widths = [width // CHUNKS] * (CHUNKS - 1) + [width // CHUNKS + 128]
+        hidden, *normed = single(
             norm_kernel,
             n,
-            [
-                jax.ShapeDtypeStruct((STEPS, width), F32),
-                jax.ShapeDtypeStruct((STEPS, width + 128), BF),
-            ],
+            [jax.ShapeDtypeStruct((STEPS, width), F32)]
+            + [jax.ShapeDtypeStruct((STEPS, w), BF) for w in widths],
             [],
-            parts + [residual[0], norm_gain.reshape(1, width), routes],
+            sum(parts, []) + [residual[0], norm_gain.reshape(1, width), routes],
             "norm",
             8 * STEPS * width,
         )
 
     with jax.named_scope("spread"):
-        along = jnp.concatenate([normed] + [swap(normed, n, k=k) for k in range(1, planes)], axis=0)
-        blocks = [along] + [swap(along, n, q=q) for q in range(1, 4)]
-        along, *weights = load(n, along, [w_gate[0], w_up[0], w_down[0]])
-        blocks = blocks + [swap(x, n, c=1) for x in [along] + blocks[1:]]
+        blocks = []
+        for c in range(CHUNKS):
+            x = normed[c]
+            along = jnp.concatenate([x] + [swap(x, n, k=k) for k in range(1, planes)], axis=0)
+            others = [swap(along, n, q=q) for q in range(1, 4)]
+            if c == CHUNKS - 1:
+                along, gate, up = load(n, along, [w_gate[0], w_up[0]])
+            here = [along] + others
+            blocks += here + [swap(x, n, c=1) for x in here]
 
     with jax.named_scope("experts"):
-        near, far = single(
-            functools.partial(expert_kernel, n_ep=n_ep),
-            n,
-            [jax.ShapeDtypeStruct((rows // 2, width), dtype) for dtype in (F32, BF)],
-            [me_one],
-            blocks + weights,
-            "experts",
-            6 * rows * width * w_gate.shape[2],
-        )
+        out = run_experts(n, n_ep, me_one, blocks, gate, up, w_down[0])
 
     with jax.named_scope("collect"):
-        result = hidden
-        for term in reduce_rows(near, far, n):
-            result = result + term.astype(F32)
-        return result.astype(BF)[None]
+        results = []
+        for c in range(CHUNKS):
+            result = hidden[:, c * (width // CHUNKS) : (c + 1) * (width // CHUNKS)]
+            for term in reduce_rows(out[c], out[CHUNKS + c], n):
+                result = result + term.astype(F32)
+            results.append(result.astype(BF))
+        return jnp.concatenate(results, axis=1)[None]
 
 
 def solution(mesh):

time: 108 us -> 111 us (1.028)
  starting transfers between devices: 35.7 us -> 56.5 us
  waiting for transfers between devices: 46.1 us -> 26.8 us
  Pallas kernels: 19.9 us -> 24.5 us
  local copies, waits for them, and re-layouts: 3.41 us -> 0.35 us
    ppermute x24 -> x48, starting transfers between devices: 24.7 us -> 46.5 us  [swap(): return lax.ppermute(x, AXES, [(d, d ^ mask) for d in range(n)])]
    ppermute x24 -> x48, waiting for transfers between devices: 37.9 us -> 18.8 us  [swap(): return lax.ppermute(x, AXES, [(d, d ^ mask) for d in range(n)])]
    pallas_call x0 -> x1, Pallas kernels: none -> 9.07 us  [run_experts(): pl.pallas_call(functools.partial(expert_kernel, n, n_ep), in_specs=[pl.Bl...]
    pallas_call x3 -> x2, Pallas kernels: 4.74 us -> 1.08 us  [single(): pl.pallas_call(functools.partial(kernel, n), in_specs=[pl.BlockSpec(memor...]
    unnamed x14 -> x12, local copies, waits for them, and re-layouts: 3.11 us -> 0.03 us
    pallas_call x1, Pallas kernels: 10.6 us -> 8.35 us  [load(): pl.pallas_call(functools.partial(load_kernel, n), in_specs=[pl.BlockSpec(...]
    pallas_call x1, Pallas kernels: 4.57 us -> 5.98 us  [attend(): pl.pallas_call(functools.partial(attend_kernel, n), in_specs=[pl.BlockSpe...]
  transfers between devices with their start and end apart: 25 -> 49, of which waited for: 18 -> 21; matrix products, arithmetic and copies ran while one was open for 0% -> 1% of each run, Pallas kernels for 10% -> 8%
where the time goes in v5:
time: 111 us
  starting transfers between devices  56.5 us (51%)
  waiting for transfers between devices  26.8 us (24%)
  Pallas kernels  24.5 us (22%)
  other arithmetic  1.62 us (1%)
  between operations  1.13 us (1%)
    ppermute x48, starting transfers between devices, swap(): return lax.ppermute(x, AXES, [(d, d ^ mask) for d in range(n)])  46.5 us
    ppermute x48, waiting for transfers between devices, swap(): return lax.ppermute(x, AXES, [(d, d ^ mask) for d in range(n)])  18.8 us
    all_to_all x1, starting transfers between devices, per_device(): latents = lax.all_to_all(latents, AXES, 0, 0, tiled=True)  10 us
    pallas_call x1, Pallas kernels, run_experts(): pl.pallas_call(functools.partial(expert_kernel, n, n_ep), in_specs=[pl.Bl...  9.07 us
    pallas_call x1, Pallas kernels, load(): pl.pallas_call(functools.partial(load_kernel, n), in_specs=[pl.BlockSpec(...  8.35 us
    all_to_all x1, waiting for transfers between devices, per_device(): latents = lax.all_to_all(latents, AXES, 0, 0, tiled=True)  8.04 us
    pallas_call x1, Pallas kernels, attend(): pl.pallas_call(functools.partial(attend_kernel, n), in_specs=[pl.BlockSpe...  5.98 us
  transfers between devices with their start and end apart: 49, of which 21 were waited for; matrix products, arithmetic and copies ran while one was open for 1% of the time, Pallas kernels for 8%

profile of v5, /device:TPU:0, one launch (start us, length us, event | category | flops | bytes accessed | tf_op | source)
XLA Modules:
  0.0 110.9 jit_solution(9901652369022661409)
XLA Ops:
  0.8 6.0 %attend.1 = bf16[32,4,512]{2,1,0:T(4,128)(2,1)} custom-call(s32[1]{0:T(128)S(6)} %copy.14.len_ref, bf16[128,576]{1,0:T(8,128)(2,1)} %bitcast.29, bf16[4,576]{1,0:T(4,128)(2,1)} %bitcast.30, bf16[576,8192]{1,0:T(8,128)(2,1)} %bitcast.25), custom_call_target="tpu_custom_call" | custom-call | flops 2281701376 | bytes 9437184 | tf_op jit(solution)/shard_map/attention/attend/pallas_call | solution.py:123
  6.8 10.0 %all-to-all-start = ((bf16[32,4,512]{2,1,0:T(4,128)(2,1)}), bf16[32,4,512]{2,1,0:T(4,128)(2,1)S(1)}, u32[]{:S(2)}, u32[]{:S(2)}) async-start(bf16[32,4,512]{2,1,0:T(4,128)(2,1)} %attend.1), calls=%async_computation | async-start | bytes 262144 | tf_op jit(solution)/shard_map/heads/all_to_all | solution.py:350
  16.8 8.0 %all-to-all-done = bf16[32,4,512]{2,1,0:T(4,128)(2,1)S(1)} async-done(((bf16[32,4,512]{2,1,0:T(4,128)(2,1)}), bf16[32,4,512]{2,1,0:T(4,128)(2,1)S(1)}, u32[]{:S(2)}, u32[]{:S(2)}) %all-to-all-start) | async-done | bytes 131104 | tf_op jit(solution)/shard_map/heads/all_to_all | solution.py:350
  28.5 1.7 %collective-permute-start.3 = (bf16[16,3584]{1,0:T(8,128)(2,1)S(1)}, bf16[16,3584]{1,0:T(8,128)(2,1)S(1)}, u32[]{:S(2)}, u32[]{:S(2)}) collective-permute-start(bf16[16,3584]{1,0:T(8,128)(2,1)S(1)} %get-tuple-element.61), channel_id=1, source_target_pairs={{0,18},{1,19},{2,16},{3,17},{4,22},{5,23},{6,20},{7,21},{8,26},{9,... | collective-permute-start | bytes 344072 | tf_op jit(solution)/shard_map/heads/ppermute | solution.py:32
  32.2 1.7 %collective-permute-start.10 = (bf16[16,3584]{1,0:T(8,128)(2,1)S(1)}, bf16[16,3584]{1,0:T(8,128)(2,1)S(1)}, u32[]{:S(2)}, u32[]{:S(2)}) collective-permute-start(bf16[16,3584]{1,0:T(8,128)(2,1)S(1)} %get-tuple-element.58), channel_id=1, source_target_pairs={{0,18},{1,19},{2,16},{3,17},{4,22},{5,23},{6,20},{7,21},{8,26},{9,... | collective-permute-start | bytes 344072 | tf_op jit(solution)/shard_map/heads/ppermute | solution.py:32
  33.9 3.2 %collective-permute-done.1 = bf16[16,3584]{1,0:T(8,128)(2,1)S(1)} collective-permute-done((bf16[16,3584]{1,0:T(8,128)(2,1)S(1)}, bf16[16,3584]{1,0:T(8,128)(2,1)S(1)}, u32[]{:S(2)}, u32[]{:S(2)}) %collective-permute-start.1) | collective-permute-done | bytes 114720 | tf_op jit(solution)/shard_map/heads/ppermute | solution.py:32
  38.0 1.4 %collective-permute-start.6 = (bf16[4,3584]{1,0:T(4,128)(2,1)S(1)}, bf16[4,3584]{1,0:T(4,128)(2,1)S(1)}, u32[]{:S(2)}, u32[]{:S(2)}) collective-permute-start(bf16[4,3584]{1,0:T(4,128)(2,1)S(1)} %get-tuple-element.74), channel_id=1, source_target_pairs={{0,12},{1,13},{2,14},{3,15},{4,8},{5,9},{6,10},{7,11},{8,4},{9,5},... | collective-permute-start | bytes 86024 | tf_op jit(solution)/shard_map/heads/ppermute | solution.py:32
  40.6 1.8 %collective-permute-start.4 = (bf16[4,3584]{1,0:T(4,128)(2,1)S(1)}, bf16[4,3584]{1,0:T(4,128)(2,1)S(1)}, u32[]{:S(2)}, u32[]{:S(2)}) collective-permute-start(bf16[4,3584]{1,0:T(4,128)(2,1)S(1)} %get-tuple-element.76), channel_id=1, source_target_pairs={{0,4},{1,5},{2,6},{3,7},{4,0},{5,1},{6,2},{7,3},{8,12},{9,13},{10,... | collective-permute-start | bytes 86024 | tf_op jit(solution)/shard_map/heads/ppermute | solution.py:32
  42.6 1.4 %collective-permute-start.13 = (bf16[4,3584]{1,0:T(4,128)(2,1)S(1)}, bf16[4,3584]{1,0:T(4,128)(2,1)S(1)}, u32[]{:S(2)}, u32[]{:S(2)}) collective-permute-start(bf16[4,3584]{1,0:T(4,128)(2,1)S(1)} %get-tuple-element.71), channel_id=1, source_target_pairs={{0,12},{1,13},{2,14},{3,15},{4,8},{5,9},{6,10},{7,11},{8,4},{9,5},... | collective-permute-start | bytes 86024 | tf_op jit(solution)/shard_map/heads/ppermute | solution.py:32
  44.3 2.7 %collective-permute-start.11 = (bf16[4,3584]{1,0:T(4,128)(2,1)S(1)}, bf16[4,3584]{1,0:T(4,128)(2,1)S(1)}, u32[]{:S(2)}, u32[]{:S(2)}) collective-permute-start(bf16[4,3584]{1,0:T(4,128)(2,1)S(1)} %get-tuple-element.73), channel_id=1, source_target_pairs={{0,4},{1,5},{2,6},{3,7},{4,0},{5,1},{6,2},{7,3},{8,12},{9,13},{10,... | collective-permute-start | bytes 86024 | tf_op jit(solution)/shard_map/heads/ppermute | solution.py:32
  49.4 2.3 %collective-permute-start.16 = (bf16[4,3584]{1,0:T(4,128)(2,1)S(1)}, bf16[4,3584]{1,0:T(4,128)(2,1)S(1)}, u32[]{:S(2)}, u32[]{:S(2)}) collective-permute-start(bf16[4,3584]{1,0:T(4,128)(2,1)S(1)} %get-tuple-element.24), channel_id=1, source_target_pairs={{0,12},{1,13},{2,14},{3,15},{4,8},{5,9},{6,10},{7,11},{8,4},{9,5},... | collective-permute-start | bytes 86024 | tf_op jit(solution)/shard_map/spread/ppermute | solution.py:32
  53.8 2.2 %collective-permute-start.26 = (bf16[4,3712]{1,0:T(4,128)(2,1)S(1)}, bf16[4,3712]{1,0:T(4,128)(2,1)S(1)}, u32[]{:S(2)}, u32[]{:S(2)}) collective-permute-start(bf16[4,3712]{1,0:T(4,128)(2,1)S(1)} %get-tuple-element.25), channel_id=1, source_target_pairs={{0,12},{1,13},{2,14},{3,15},{4,8},{5,9},{6,10},{7,11},{8,4},{9,5},... | collective-permute-start | bytes 89096 | tf_op jit(solution)/shard_map/spread/ppermute | solution.py:32
  56.1 2.1 %collective-permute-start.24 = (bf16[4,3712]{1,0:T(4,128)(2,1)S(1)}, bf16[4,3712]{1,0:T(4,128)(2,1)S(1)}, u32[]{:S(2)}, u32[]{:S(2)}) collective-permute-start(bf16[4,3712]{1,0:T(4,128)(2,1)S(1)} %get-tuple-element.25), channel_id=1, source_target_pairs={{0,4},{1,5},{2,6},{3,7},{4,0},{5,1},{6,2},{7,3},{8,12},{9,13},{10,... | collective-permute-start | bytes 89096 | tf_op jit(solution)/shard_map/spread/ppermute | solution.py:32
  62.0 1.4 %collective-permute-start.29 = (bf16[16,3712]{1,0:T(8,128)(2,1)S(1)}, bf16[16,3712]{1,0:T(8,128)(2,1)S(1)}, u32[]{:S(2)}, u32[]{:S(2)}) collective-permute-start(bf16[16,3712]{1,0:T(8,128)(2,1)S(1)} %pad_maximum_fusion.refs_0_), channel_id=1, source_target_pairs={{0,18},{1,19},{2,16},{3,17},{4,22},{5,23},{6,20},{7,21},{8,26},{9,... | collective-permute-start | bytes 356360 | tf_op jit(solution)/shard_map/spread/ppermute | solution.py:32
  65.8 8.4 %load_experts.1 = (bf16[16,3712]{1,0:T(8,128)(2,1)S(1)}, bf16[7168,512]{1,0:T(8,128)(2,1)S(1)}, bf16[7168,512]{1,0:T(8,128)(2,1)}) custom-call(bf16[16,3712]{1,0:T(8,128)(2,1)S(1)} %pad_maximum_fusion.refs_0_, bf16[7168,512]{1,0:T(8,128)(2,1)} %bitcast.26, bf16[7168,512]{1,0:T(8,128)(2,1)} %bitcast.27), custom_call_target="tpu_custom_call" | custom-call | bytes 29360128 | tf_op jit(solution)/shard_map/spread/load_experts/pallas_call | solution.py:216
  77.1 9.1 %experts.1 = (f32[64,3584]{1,0:T(8,128)S(1)}, f32[64,3584]{1,0:T(8,128)S(1)}, bf16[64,3584]{1,0:T(8,128)(2,1)S(1)}, bf16[64,3584]{1,0:T(8,128)(2,1)S(1)}) custom-call(s32[1]{0:T(128)} %bitcast.me_ref, bf16[16,3584]{1,0:T(8,128)(2,1)S(1)} %pad_maximum_fusion.1.refs_0_, bf16[16,3584]{1,0:T(8,128)(2,1)S(1)} %collective-permute-done.17.refs_1_, ...), custom_call_target="tpu_custom_call" | custom-call | flops 2818572288 | bytes 22020096 | tf_op jit(solution)/shard_map/experts/experts/pallas_call | solution.py:275
  88.3 1.6 %collective-permute-start.35 = (bf16[16,3584]{1,0:T(8,128)(2,1)S(1)}, bf16[16,3584]{1,0:T(8,128)(2,1)S(1)}, u32[]{:S(2)}, u32[]{:S(2)}) collective-permute-start(bf16[16,3584]{1,0:T(8,128)(2,1)S(1)} %get-tuple-element.51), channel_id=1, source_target_pairs={{0,2},{1,3},{2,0},{3,1},{4,6},{5,7},{6,4},{7,5},{8,10},{9,11},{10,... | collective-permute-start | bytes 344072 | tf_op jit(solution)/shard_map/collect/ppermute | solution.py:32
  92.0 1.6 %collective-permute-start.42 = (bf16[16,3584]{1,0:T(8,128)(2,1)S(1)}, bf16[16,3584]{1,0:T(8,128)(2,1)S(1)}, u32[]{:S(2)}, u32[]{:S(2)}) collective-permute-start(bf16[16,3584]{1,0:T(8,128)(2,1)S(1)} %get-tuple-element.54), channel_id=1, source_target_pairs={{0,2},{1,3},{2,0},{3,1},{4,6},{5,7},{6,4},{7,5},{8,10},{9,11},{10,... | collective-permute-start | bytes 344072 | tf_op jit(solution)/shard_map/collect/ppermute | solution.py:32
  94.4 1.4 %collective-permute-done.35 = bf16[16,3584]{1,0:T(8,128)(2,1)S(1)} collective-permute-done((bf16[16,3584]{1,0:T(8,128)(2,1)S(1)}, bf16[16,3584]{1,0:T(8,128)(2,1)S(1)}, u32[]{:S(2)}, u32[]{:S(2)}) %collective-permute-start.35) | collective-permute-done | bytes 114720 | tf_op jit(solution)/shard_map/collect/ppermute | solution.py:32
  97.0 1.3 %collective-permute-done.36 = bf16[16,3584]{1,0:T(8,128)(2,1)S(1)} collective-permute-done((bf16[16,3584]{1,0:T(8,128)(2,1)S(1)}, bf16[16,3584]{1,0:T(8,128)(2,1)S(1)}, u32[]{:S(2)}, u32[]{:S(2)}) %collective-permute-start.36) | collective-permute-done | bytes 114720 | tf_op jit(solution)/shard_map/collect/ppermute | solution.py:32
  98.5 2.1 %collective-permute-start.40 = (bf16[4,3584]{1,0:T(4,128)(2,1)S(1)}, bf16[4,3584]{1,0:T(4,128)(2,1)S(1)}, u32[]{:S(2)}, u32[]{:S(2)}) collective-permute-start(bf16[4,3584]{1,0:T(4,128)(2,1)S(1)} %get-tuple-element.66), channel_id=1, source_target_pairs={{0,12},{1,13},{2,14},{3,15},{4,8},{5,9},{6,10},{7,11},{8,4},{9,5},... | collective-permute-start | bytes 86024 | tf_op jit(solution)/shard_map/collect/ppermute | solution.py:32
  103.1 2.1 %collective-permute-start.47 = (bf16[4,3584]{1,0:T(4,128)(2,1)S(1)}, bf16[4,3584]{1,0:T(4,128)(2,1)S(1)}, u32[]{:S(2)}, u32[]{:S(2)}) collective-permute-start(bf16[4,3584]{1,0:T(4,128)(2,1)S(1)} %get-tuple-element.69), channel_id=1, source_target_pairs={{0,12},{1,13},{2,14},{3,15},{4,8},{5,9},{6,10},{7,11},{8,4},{9,5},... | collective-permute-start | bytes 86024 | tf_op jit(solution)/shard_map/collect/ppermute | solution.py:32
  106.6 2.2 %collective-permute-done.47 = bf16[4,3584]{1,0:T(4,128)(2,1)S(1)} collective-permute-done((bf16[4,3584]{1,0:T(4,128)(2,1)S(1)}, bf16[4,3584]{1,0:T(4,128)(2,1)S(1)}, u32[]{:S(2)}, u32[]{:S(2)}) %collective-permute-start.47) | collective-permute-done | bytes 28704 | tf_op jit(solution)/shard_map/collect/ppermute | solution.py:32
  108.8 1.4 %collective-permute-done.46 = bf16[4,3584]{1,0:T(4,128)(2,1)S(1)} collective-permute-done((bf16[4,3584]{1,0:T(4,128)(2,1)S(1)}, bf16[4,3584]{1,0:T(4,128)(2,1)S(1)}, u32[]{:S(2)}, u32[]{:S(2)}) %collective-permute-start.46) | collective-permute-done | bytes 28704 | tf_op jit(solution)/shard_map/collect/ppermute | solution.py:32
  (118 shorter events, 32.7 us)
Async XLA Ops:
  6.8 18.1 %all-to-all-start = ((bf16[32,4,512]{2,1,0:T(4,128)(2,1)}), bf16[32,4,512]{2,1,0:T(4,128)(2,1)S(1)}, u32[]{:S(2)}, u32[]{:S(2)}) async-start(bf16[32,4,512]{2,1,0:T(4,128)(2,1)} %attend.1), calls=%async_computation | async-start | bytes 262144 | tf_op jit(solution)/shard_map/heads/all_to_all | solution.py:350
  27.9 9.2 %collective-permute-start.1 = (bf16[16,3584]{1,0:T(8,128)(2,1)S(1)}, bf16[16,3584]{1,0:T(8,128)(2,1)S(1)}, u32[]{:S(2)}, u32[]{:S(2)}) collective-permute-start(bf16[16,3584]{1,0:T(8,128)(2,1)S(1)} %get-tuple-element.60), channel_id=1, source_target_pairs={{0,2},{1,3},{2,0},{3,1},{4,6},{5,7},{6,4},{7,5},{8,10},{9,11},{10,... | collective-permute-start | bytes 344072 | tf_op jit(solution)/shard_map/heads/ppermute | solution.py:32
  28.5 9.4 %collective-permute-start.3 = (bf16[16,3584]{1,0:T(8,128)(2,1)S(1)}, bf16[16,3584]{1,0:T(8,128)(2,1)S(1)}, u32[]{:S(2)}, u32[]{:S(2)}) collective-permute-start(bf16[16,3584]{1,0:T(8,128)(2,1)S(1)} %get-tuple-element.61), channel_id=1, source_target_pairs={{0,18},{1,19},{2,16},{3,17},{4,22},{5,23},{6,20},{7,21},{8,26},{9,... | collective-permute-start | bytes 344072 | tf_op jit(solution)/shard_map/heads/ppermute | solution.py:32
  30.2 7.7 %collective-permute-start.2 = (bf16[16,3584]{1,0:T(8,128)(2,1)S(1)}, bf16[16,3584]{1,0:T(8,128)(2,1)S(1)}, u32[]{:S(2)}, u32[]{:S(2)}) collective-permute-start(bf16[16,3584]{1,0:T(8,128)(2,1)S(1)} %get-tuple-element.62), channel_id=1, source_target_pairs={{0,16},{1,17},{2,18},{3,19},{4,20},{5,21},{6,22},{7,23},{8,24},{9,... | collective-permute-start | bytes 344072 | tf_op jit(solution)/shard_map/heads/ppermute | solution.py:32
  31.6 9.0 %collective-permute-start.8 = (bf16[16,3584]{1,0:T(8,128)(2,1)S(1)}, bf16[16,3584]{1,0:T(8,128)(2,1)S(1)}, u32[]{:S(2)}, u32[]{:S(2)}) collective-permute-start(bf16[16,3584]{1,0:T(8,128)(2,1)S(1)} %get-tuple-element.57), channel_id=1, source_target_pairs={{0,2},{1,3},{2,0},{3,1},{4,6},{5,7},{6,4},{7,5},{8,10},{9,11},{10,... | collective-permute-start | bytes 344072 | tf_op jit(solution)/shard_map/heads/ppermute | solution.py:32
  32.2 10.3 %collective-permute-start.10 = (bf16[16,3584]{1,0:T(8,128)(2,1)S(1)}, bf16[16,3584]{1,0:T(8,128)(2,1)S(1)}, u32[]{:S(2)}, u32[]{:S(2)}) collective-permute-start(bf16[16,3584]{1,0:T(8,128)(2,1)S(1)} %get-tuple-element.58), channel_id=1, source_target_pairs={{0,18},{1,19},{2,16},{3,17},{4,22},{5,23},{6,20},{7,21},{8,26},{9,... | collective-permute-start | bytes 344072 | tf_op jit(solution)/shard_map/heads/ppermute | solution.py:32
  39.4 7.8 %collective-permute-start.5 = (bf16[4,3584]{1,0:T(4,128)(2,1)S(1)}, bf16[4,3584]{1,0:T(4,128)(2,1)S(1)}, u32[]{:S(2)}, u32[]{:S(2)}) collective-permute-start(bf16[4,3584]{1,0:T(4,128)(2,1)S(1)} %get-tuple-element.75), channel_id=1, source_target_pairs={{0,8},{1,9},{2,10},{3,11},{4,12},{5,13},{6,14},{7,15},{8,0},{9,1},... | collective-permute-start | bytes 86024 | tf_op jit(solution)/shard_map/heads/ppermute | solution.py:32
  40.6 6.5 %collective-permute-start.4 = (bf16[4,3584]{1,0:T(4,128)(2,1)S(1)}, bf16[4,3584]{1,0:T(4,128)(2,1)S(1)}, u32[]{:S(2)}, u32[]{:S(2)}) collective-permute-start(bf16[4,3584]{1,0:T(4,128)(2,1)S(1)} %get-tuple-element.76), channel_id=1, source_target_pairs={{0,4},{1,5},{2,6},{3,7},{4,0},{5,1},{6,2},{7,3},{8,12},{9,13},{10,... | collective-permute-start | bytes 86024 | tf_op jit(solution)/shard_map/heads/ppermute | solution.py:32
  49.4 6.7 %collective-permute-start.16 = (bf16[4,3584]{1,0:T(4,128)(2,1)S(1)}, bf16[4,3584]{1,0:T(4,128)(2,1)S(1)}, u32[]{:S(2)}, u32[]{:S(2)}) collective-permute-start(bf16[4,3584]{1,0:T(4,128)(2,1)S(1)} %get-tuple-element.24), channel_id=1, source_target_pairs={{0,12},{1,13},{2,14},{3,15},{4,8},{5,9},{6,10},{7,11},{8,4},{9,5},... | collective-permute-start | bytes 86024 | tf_op jit(solution)/shard_map/spread/ppermute | solution.py:32
  51.7 6.5 %collective-permute-start.15 = (bf16[4,3584]{1,0:T(4,128)(2,1)S(1)}, bf16[4,3584]{1,0:T(4,128)(2,1)S(1)}, u32[]{:S(2)}, u32[]{:S(2)}) collective-permute-start(bf16[4,3584]{1,0:T(4,128)(2,1)S(1)} %get-tuple-element.24), channel_id=1, source_target_pairs={{0,8},{1,9},{2,10},{3,11},{4,12},{5,13},{6,14},{7,15},{8,0},{9,1},... | collective-permute-start | bytes 86024 | tf_op jit(solution)/shard_map/spread/ppermute | solution.py:32
  58.4 6.9 %collective-permute-start.19 = (bf16[16,3584]{1,0:T(8,128)(2,1)S(1)}, bf16[16,3584]{1,0:T(8,128)(2,1)S(1)}, u32[]{:S(2)}, u32[]{:S(2)}) collective-permute-start(bf16[16,3584]{1,0:T(8,128)(2,1)S(1)} %pad_maximum_fusion.1.refs_0_), channel_id=1, source_target_pairs={{0,18},{1,19},{2,16},{3,17},{4,22},{5,23},{6,20},{7,21},{8,26},{9,... | collective-permute-start | bytes 344072 | tf_op jit(solution)/shard_map/spread/ppermute | solution.py:32
  59.5 14.7 %collective-permute-start.18 = (bf16[16,3584]{1,0:T(8,128)(2,1)S(1)}, bf16[16,3584]{1,0:T(8,128)(2,1)S(1)}, u32[]{:S(2)}, u32[]{:S(2)}) collective-permute-start(bf16[16,3584]{1,0:T(8,128)(2,1)S(1)} %pad_maximum_fusion.1.refs_0_), channel_id=1, source_target_pairs={{0,16},{1,17},{2,18},{3,19},{4,20},{5,21},{6,22},{7,23},{8,24},{9,... | collective-permute-start | bytes 344072 | tf_op jit(solution)/shard_map/spread/ppermute | solution.py:32
  60.8 13.4 %collective-permute-start.17 = (bf16[16,3584]{1,0:T(8,128)(2,1)S(1)}, bf16[16,3584]{1,0:T(8,128)(2,1)S(1)}, u32[]{:S(2)}, u32[]{:S(2)}) collective-permute-start(bf16[16,3584]{1,0:T(8,128)(2,1)S(1)} %pad_maximum_fusion.1.refs_0_), channel_id=1, source_target_pairs={{0,2},{1,3},{2,0},{3,1},{4,6},{5,7},{6,4},{7,5},{8,10},{9,11},{10,... | collective-permute-start | bytes 344072 | tf_op jit(solution)/shard_map/spread/ppermute | solution.py:32
  62.0 12.8 %collective-permute-start.29 = (bf16[16,3712]{1,0:T(8,128)(2,1)S(1)}, bf16[16,3712]{1,0:T(8,128)(2,1)S(1)}, u32[]{:S(2)}, u32[]{:S(2)}) collective-permute-start(bf16[16,3712]{1,0:T(8,128)(2,1)S(1)} %pad_maximum_fusion.refs_0_), channel_id=1, source_target_pairs={{0,18},{1,19},{2,16},{3,17},{4,22},{5,23},{6,20},{7,21},{8,26},{9,... | collective-permute-start | bytes 356360 | tf_op jit(solution)/shard_map/spread/ppermute | solution.py:32
  63.5 11.4 %collective-permute-start.28 = (bf16[16,3712]{1,0:T(8,128)(2,1)S(1)}, bf16[16,3712]{1,0:T(8,128)(2,1)S(1)}, u32[]{:S(2)}, u32[]{:S(2)}) collective-permute-start(bf16[16,3712]{1,0:T(8,128)(2,1)S(1)} %pad_maximum_fusion.refs_0_), channel_id=1, source_target_pairs={{0,16},{1,17},{2,18},{3,19},{4,20},{5,21},{6,22},{7,23},{8,24},{9,... | collective-permute-start | bytes 356360 | tf_op jit(solution)/shard_map/spread/ppermute | solution.py:32
  65.3 10.0 %collective-permute-start.27 = (bf16[16,3712]{1,0:T(8,128)(2,1)S(1)}, bf16[16,3712]{1,0:T(8,128)(2,1)S(1)}, u32[]{:S(2)}, u32[]{:S(2)}) collective-permute-start(bf16[16,3712]{1,0:T(8,128)(2,1)S(1)} %pad_maximum_fusion.refs_0_), channel_id=1, source_target_pairs={{0,2},{1,3},{2,0},{3,1},{4,6},{5,7},{6,4},{7,5},{8,10},{9,11},{10,... | collective-permute-start | bytes 356360 | tf_op jit(solution)/shard_map/spread/ppermute | solution.py:32
  88.3 7.6 %collective-permute-start.35 = (bf16[16,3584]{1,0:T(8,128)(2,1)S(1)}, bf16[16,3584]{1,0:T(8,128)(2,1)S(1)}, u32[]{:S(2)}, u32[]{:S(2)}) collective-permute-start(bf16[16,3584]{1,0:T(8,128)(2,1)S(1)} %get-tuple-element.51), channel_id=1, source_target_pairs={{0,2},{1,3},{2,0},{3,1},{4,6},{5,7},{6,4},{7,5},{8,10},{9,11},{10,... | collective-permute-start | bytes 344072 | tf_op jit(solution)/shard_map/collect/ppermute | solution.py:32
  89.8 7.2 %collective-permute-start.37 = (bf16[16,3584]{1,0:T(8,128)(2,1)S(1)}, bf16[16,3584]{1,0:T(8,128)(2,1)S(1)}, u32[]{:S(2)}, u32[]{:S(2)}) collective-permute-start(bf16[16,3584]{1,0:T(8,128)(2,1)S(1)} %get-tuple-element.52), channel_id=1, source_target_pairs={{0,18},{1,19},{2,16},{3,17},{4,22},{5,23},{6,20},{7,21},{8,26},{9,... | collective-permute-start | bytes 344072 | tf_op jit(solution)/shard_map/collect/ppermute | solution.py:32
  90.7 7.6 %collective-permute-start.36 = (bf16[16,3584]{1,0:T(8,128)(2,1)S(1)}, bf16[16,3584]{1,0:T(8,128)(2,1)S(1)}, u32[]{:S(2)}, u32[]{:S(2)}) collective-permute-start(bf16[16,3584]{1,0:T(8,128)(2,1)S(1)} %get-tuple-element.53), channel_id=1, source_target_pairs={{0,16},{1,17},{2,18},{3,19},{4,20},{5,21},{6,22},{7,23},{8,24},{9,... | collective-permute-start | bytes 344072 | tf_op jit(solution)/shard_map/collect/ppermute | solution.py:32
  92.0 8.7 %collective-permute-start.42 = (bf16[16,3584]{1,0:T(8,128)(2,1)S(1)}, bf16[16,3584]{1,0:T(8,128)(2,1)S(1)}, u32[]{:S(2)}, u32[]{:S(2)}) collective-permute-start(bf16[16,3584]{1,0:T(8,128)(2,1)S(1)} %get-tuple-element.54), channel_id=1, source_target_pairs={{0,2},{1,3},{2,0},{3,1},{4,6},{5,7},{6,4},{7,5},{8,10},{9,11},{10,... | collective-permute-start | bytes 344072 | tf_op jit(solution)/shard_map/collect/ppermute | solution.py:32
  93.5 8.4 %collective-permute-start.44 = (bf16[16,3584]{1,0:T(8,128)(2,1)S(1)}, bf16[16,3584]{1,0:T(8,128)(2,1)S(1)}, u32[]{:S(2)}, u32[]{:S(2)}) collective-permute-start(bf16[16,3584]{1,0:T(8,128)(2,1)S(1)} %get-tuple-element.55), channel_id=1, source_target_pairs={{0,18},{1,19},{2,16},{3,17},{4,22},{5,23},{6,20},{7,21},{8,26},{9,... | collective-permute-start | bytes 344072 | tf_op jit(solution)/shard_map/collect/ppermute | solution.py:32
  95.8 6.5 %collective-permute-start.43 = (bf16[16,3584]{1,0:T(8,128)(2,1)S(1)}, bf16[16,3584]{1,0:T(8,128)(2,1)S(1)}, u32[]{:S(2)}, u32[]{:S(2)}) collective-permute-start(bf16[16,3584]{1,0:T(8,128)(2,1)S(1)} %get-tuple-element.56), channel_id=1, source_target_pairs={{0,16},{1,17},{2,18},{3,19},{4,20},{5,21},{6,22},{7,23},{8,24},{9,... | collective-permute-start | bytes 344072 | tf_op jit(solution)/shard_map/collect/ppermute | solution.py:32
  98.4 6.8 %collective-permute-start.38 = (bf16[4,3584]{1,0:T(4,128)(2,1)S(1)}, bf16[4,3584]{1,0:T(4,128)(2,1)S(1)}, u32[]{:S(2)}, u32[]{:S(2)}) collective-permute-start(bf16[4,3584]{1,0:T(4,128)(2,1)S(1)} %get-tuple-element.65), channel_id=1, source_target_pairs={{0,4},{1,5},{2,6},{3,7},{4,0},{5,1},{6,2},{7,3},{8,12},{9,13},{10,... | collective-permute-start | bytes 86024 | tf_op jit(solution)/shard_map/collect/ppermute | solution.py:32
  98.5 7.4 %collective-permute-start.40 = (bf16[4,3584]{1,0:T(4,128)(2,1)S(1)}, bf16[4,3584]{1,0:T(4,128)(2,1)S(1)}, u32[]{:S(2)}, u32[]{:S(2)}) collective-permute-start(bf16[4,3584]{1,0:T(4,128)(2,1)S(1)} %get-tuple-element.66), channel_id=1, source_target_pairs={{0,12},{1,13},{2,14},{3,15},{4,8},{5,9},{6,10},{7,11},{8,4},{9,5},... | collective-permute-start | bytes 86024 | tf_op jit(solution)/shard_map/collect/ppermute | solution.py:32
  (31 other events, 285.8 us)

commit v6 on v4

--- a/solution.py
+++ b/solution.py
@@ -14,6 +14,8 @@
 STEPS = 4
 TOPK = 8
 BLK = 2048
+LOADS = 8
+SECOND_ORDER = [(c, j, i) for c in (0, 2) for j in range(2) for i in range(2)]
 SPAN = 8
 AXES = ("sec", "ep")
 NT = (((1,), (1,)), ((), ()))
@@ -179,15 +181,19 @@
     out_ref[:, width:] = routes_ref[...]
 
 
-def load_kernel(n, *refs):
-    sources, targets, sem = refs[1:4], refs[5:8], refs[8]
-    copies = [pltpu.make_async_copy(refs[0], refs[4], sem.at[12])]
-    for i in range(3):
-        step = sources[i].shape[0] // 4
-        for j in range(4):
-            here = pl.ds(j * step, step)
+def load_kernel(n, ranges, *refs):
+    count = len(ranges)
+    sources, targets, sem = refs[1 : 1 + count], refs[2 + count : 2 + 2 * count], refs[-1]
+    copies = [pltpu.make_async_copy(refs[0], refs[1 + count], sem.at[0])]
+    for source, target, (first, rows) in zip(sources, targets, ranges):
+        step = rows // LOADS
+        for j in range(LOADS):
             copies.append(
-                pltpu.make_async_copy(sources[i].at[here], targets[i].at[here], sem.at[4 * i + j])
+                pltpu.make_async_copy(
+                    source.at[pl.ds(first + j * step, step)],
+                    target.at[pl.ds(j * step, step)],
+                    sem.at[len(copies)],
+                )
             )
     for copy in copies:
         copy.start()
@@ -195,35 +201,47 @@
         copy.wait()
 
 
-def load(n, passed, arrays):
+def load(n, passed, arrays, ranges, limit):
+    shapes = [(rows, a.shape[1]) for a, (_, rows) in zip(arrays, ranges)]
     return pl.pallas_call(
-        functools.partial(load_kernel, n),
-        in_specs=[pl.BlockSpec(memory_space=pltpu.VMEM)] + [pl.BlockSpec(memory_space=pl.ANY)] * 3,
-        out_specs=[pl.BlockSpec(memory_space=pltpu.VMEM)] * 4,
-        out_shape=[jax.ShapeDtypeStruct(a.shape, a.dtype) for a in [passed] + arrays],
-        scratch_shapes=[pltpu.SemaphoreType.DMA((13,))],
-        compiler_params=pltpu.CompilerParams(vmem_limit_bytes=36 * 1024 * 1024),
+        functools.partial(load_kernel, n, ranges),
+        in_specs=[pl.BlockSpec(memory_space=pltpu.VMEM)]
+        + [pl.BlockSpec(memory_space=pl.ANY)] * len(arrays),
+        out_specs=[pl.BlockSpec(memory_space=pltpu.VMEM)] * (1 + len(arrays)),
+        out_shape=[jax.ShapeDtypeStruct(passed.shape, passed.dtype)]
+        + [jax.ShapeDtypeStruct(shape, BF) for shape in shapes],
+        scratch_shapes=[pltpu.SemaphoreType.DMA((1 + LOADS * len(arrays),))],
+        compiler_params=pltpu.CompilerParams(vmem_limit_bytes=limit * 1024 * 1024),
         cost_estimate=pl.CostEstimate(
-            flops=0, bytes_accessed=sum(4 * a.size for a in arrays), transcendentals=0
+            flops=0, bytes_accessed=sum(4 * r * c for r, c in shapes), transcendentals=0
         ),
-        name="load_experts",
+        name="load",
     )(passed, *arrays)
 
 
 def expert_kernel(n, me_ref, *refs, n_ep):
-    blocks, (gate_ref, up_ref, down_ref, near_ref, far_ref) = refs[:8], refs[8:]
+    firsts, seconds = refs[:4], refs[4:8]
+    gate_ref, first_up_ref, second_up_ref, down_ref, near_ref, far_ref = refs[8:]
     rows = n * STEPS
+    group = rows // 8
     width, units = gate_ref.shape
     part = width // SPAN
     gate = jnp.zeros((rows, units), F32)
     up = jnp.zeros((rows, units), F32)
     for p in range(SPAN):
-        here = slice(p * part, (p + 1) * part)
-        x = jnp.concatenate([ref[:, here] for ref in blocks], axis=0)
-        gate += jnp.dot(x, gate_ref[here], preferred_element_type=F32)
-        up += jnp.dot(x, up_ref[here], preferred_element_type=F32)
+        half, place = p // 4, p % 4
+        here = slice(place * part, (place + 1) * part)
+        if half == 0:
+            x = [ref[:, here] for ref in firsts]
+        else:
+            x = [seconds[c + i][j * group : (j + 1) * group, here] for c, j, i in SECOND_ORDER]
+        x = jnp.concatenate(x, axis=0)
+        up_part = (first_up_ref, second_up_ref)[half][here]
+        gate += jnp.dot(x, gate_ref[p * part : (p + 1) * part], preferred_element_type=F32)
+        up += jnp.dot(x, up_part, preferred_element_type=F32)
     act = (gate * jax.nn.sigmoid(gate) * up).astype(BF)
-    routes = jnp.concatenate([ref[:, width:] for ref in blocks], axis=0).astype(F32)
+    routes = [seconds[c + i][j * group : (j + 1) * group, width // 2 :] for c, j, i in SECOND_ORDER]
+    routes = jnp.concatenate(routes, axis=0).astype(F32)
     scores = routes[:, TOPK : 2 * TOPK] + routes[:, 2 * TOPK : 3 * TOPK]
     chosen = jnp.where(routes[:, :TOPK] == (me_ref[0] % n_ep).astype(F32), scores, 0.0)
     coef = jnp.sum(chosen, axis=1, keepdims=True) / jnp.sum(scores, axis=1, keepdims=True) * 2.5
@@ -248,15 +266,35 @@
     )(*scalars, *arrays)
 
 
-def reduce_rows(near, far, n):
+def reduce_rows(near, far, n, beside=lambda rows: rows):
     planes = n // SPAN
+    group = planes * STEPS
     width = near.shape[1]
-    total = (near + swap(far, n, c=1).astype(F32)).reshape(4, planes * STEPS, width)
-    kept = total[0]
-    for q in range(1, 4):
-        kept = kept + swap(total[q].astype(BF), n, q=q).astype(F32)
-    kept = kept.reshape(planes, STEPS, width)
+    total = (near + swap(far, n, c=1).astype(F32)).reshape(2, 2, group, width)
+    first, second = total[..., : width // 2], total[..., width // 2 :]
+    first_sent = swap(first[1].astype(BF), n, q=2)
+    second_sent = swap(second[:, 1].astype(BF), n, q=1)
+    kept = beside(first[0].reshape(2 * group, width // 2)).reshape(2, group, width // 2)
+    first = kept + first_sent.astype(F32)
+    second = second[:, 0] + second_sent.astype(F32)
+    first = first[0] + swap(first[1].astype(BF), n, q=1).astype(F32)
+    second = second[0] + swap(second[1].astype(BF), n, q=2).astype(F32)
+    kept = jnp.concatenate([first, second], axis=1).reshape(planes, STEPS, width)
     return [kept[0]] + [swap(kept[k].astype(BF), n, k=k) for k in range(1, planes)]
+
+
+def spread_rows(rows, n, width, beside):
+    planes = n // SPAN
+    along = jnp.concatenate([rows] + [swap(rows, n, k=k) for k in range(1, planes)], axis=0)
+    first, second = along[:, : width // 2], along[:, width // 2 :]
+    first = jnp.concatenate([first, swap(first, n, q=1)], axis=0)
+    second = jnp.concatenate([second, swap(second, n, q=2)], axis=0)
+    first_far, second_far = swap(first, n, q=2), swap(second, n, q=1)
+    first = beside(first)
+    firsts, seconds = [first, first_far], [second, second_far]
+    return (
+        firsts + [swap(x, n, c=1) for x in firsts] + seconds + [swap(x, n, c=1) for x in seconds]
+    )
 
 
 def per_device(
@@ -302,7 +340,16 @@
             "heads",
             2 * rows * VDIM * (LAT + width),
         )
-        parts = reduce_rows(near, far, n)
+        loaded = []
+
+        def load_first(rows):
+            rows, *arrays = load(
+                n, rows, [w_gate[0], w_up[0]], [(0, width), (0, width // 2)], 42
+            )
+            loaded.extend(arrays)
+            return rows
+
+        parts = reduce_rows(near, far, n, load_first)
 
     with jax.named_scope("norm"):
         high = route_scores[0].astype(BF)
@@ -323,10 +370,16 @@
         )
 
     with jax.named_scope("spread"):
-        along = jnp.concatenate([normed] + [swap(normed, n, k=k) for k in range(1, planes)], axis=0)
-        blocks = [along] + [swap(along, n, q=q) for q in range(1, 4)]
-        along, *weights = load(n, along, [w_gate[0], w_up[0], w_down[0]])
-        blocks = blocks + [swap(x, n, c=1) for x in [along] + blocks[1:]]
+
+        def load_second(rows):
+            units = w_down.shape[1]
+            rows, *arrays = load(
+                n, rows, [w_up[0], w_down[0]], [(width // 2, width // 2), (0, units)], 33
+            )
+            loaded.extend(arrays)
+            return rows
+
+        blocks = spread_rows(normed, n, width, load_second)
 
     with jax.named_scope("experts"):
         near, far = single(
@@ -334,7 +387,7 @@
             n,
             [jax.ShapeDtypeStruct((rows // 2, width), dtype) for dtype in (F32, BF)],
             [me_one],
-            blocks + weights,
+            blocks + loaded,
             "experts",
             6 * rows * width * w_gate.shape[2],
         )

time: 108 us -> 113 us (1.046)
  local copies, waits for them, and re-layouts: 3.41 us -> 6.76 us
  starting transfers between devices: 35.7 us -> 39 us
  waiting for transfers between devices: 46.1 us -> 43.4 us
  Pallas kernels: 19.9 us -> 21.2 us
    ppermute x24 -> x27, starting transfers between devices: 24.7 us -> 29.2 us  [swap(): return lax.ppermute(x, AXES, [(d, d ^ mask) for d in range(n)])]
    unnamed x14 -> x20, local copies, waits for them, and re-layouts: 3.11 us -> 6.37 us
    ppermute x24 -> x27, waiting for transfers between devices: 37.9 us -> 35.1 us  [swap(): return lax.ppermute(x, AXES, [(d, d ^ mask) for d in range(n)])]
    pallas_call x1, Pallas kernels: 4.57 us -> 6.15 us  [attend(): pl.pallas_call(functools.partial(attend_kernel, n), in_specs=[pl.BlockSpe...]
    all_to_all x1, starting transfers between devices: 11 us -> 9.82 us  [per_device(): latents = lax.all_to_all(latents, AXES, 0, 0, tiled=True)]
    pallas_call x1 -> x2, Pallas kernels: 10.6 us -> 10.4 us  [load(): pl.pallas_call(functools.partial(load_kernel, n, ranges), in_specs=[pl.Bl...]
  transfers between devices with their start and end apart: 25 -> 28, of which waited for: 18 -> 21; matrix products, arithmetic and copies ran while one was open for 0% -> 0% of each run, Pallas kernels for 10% -> 9%
where the time goes in v6:
time: 113 us
  waiting for transfers between devices  43.4 us (38%)
  starting transfers between devices  39 us (35%)
  Pallas kernels  21.2 us (19%)
  local copies, waits for them, and re-layouts  6.76 us (6%)
  other arithmetic  1.71 us (2%)
    ppermute x27, waiting for transfers between devices, swap(): return lax.ppermute(x, AXES, [(d, d ^ mask) for d in range(n)])  35.1 us
    ppermute x27, starting transfers between devices, swap(): return lax.ppermute(x, AXES, [(d, d ^ mask) for d in range(n)])  29.2 us
    pallas_call x2, Pallas kernels, load(): pl.pallas_call(functools.partial(load_kernel, n, ranges), in_specs=[pl.Bl...  10.4 us
    all_to_all x1, starting transfers between devices, per_device(): latents = lax.all_to_all(latents, AXES, 0, 0, tiled=True)  9.82 us
    all_to_all x1, waiting for transfers between devices, per_device(): latents = lax.all_to_all(latents, AXES, 0, 0, tiled=True)  8.22 us
    unnamed x20, local copies, waits for them, and re-layouts  6.37 us
    pallas_call x1, Pallas kernels, attend(): pl.pallas_call(functools.partial(attend_kernel, n), in_specs=[pl.BlockSpe...  6.15 us
    pallas_call x3, Pallas kernels, single(): pl.pallas_call(functools.partial(kernel, n), in_specs=[pl.BlockSpec(memor...  4.68 us
  transfers between devices with their start and end apart: 28, of which 21 were waited for; matrix products, arithmetic and copies ran while one was open for 0% of the time, Pallas kernels for 9%

profile of v6, /device:TPU:0, one launch (start us, length us, event | category | flops | bytes accessed | tf_op | source)
XLA Modules:
  0.0 113.0 jit_solution(7298293429657844543)
XLA Ops:
  0.7 6.1 %attend.1 = bf16[32,4,512]{2,1,0:T(4,128)(2,1)} custom-call(s32[1]{0:T(128)S(6)} %copy.32.len_ref, bf16[128,576]{1,0:T(8,128)(2,1)} %bitcast.89, bf16[4,576]{1,0:T(4,128)(2,1)} %bitcast.90, bf16[576,8192]{1,0:T(8,128)(2,1)} %bitcast.79), custom_call_target="tpu_custom_call" | custom-call | flops 2281701376 | bytes 9437184 | tf_op jit(solution)/shard_map/attention/attend/pallas_call | solution.py:124
  6.9 9.8 %all-to-all-start = ((bf16[32,4,512]{2,1,0:T(4,128)(2,1)}), bf16[32,4,512]{2,1,0:T(4,128)(2,1)S(1)}, u32[]{:S(2)}, u32[]{:S(2)}) async-start(bf16[32,4,512]{2,1,0:T(4,128)(2,1)} %attend.1), calls=%async_computation | async-start | bytes 262144 | tf_op jit(solution)/shard_map/heads/all_to_all | solution.py:333
  16.7 8.2 %all-to-all-done = bf16[32,4,512]{2,1,0:T(4,128)(2,1)S(1)} async-done(((bf16[32,4,512]{2,1,0:T(4,128)(2,1)}), bf16[32,4,512]{2,1,0:T(4,128)(2,1)S(1)}, u32[]{:S(2)}, u32[]{:S(2)}) %all-to-all-start) | async-done | bytes 131104 | tf_op jit(solution)/shard_map/heads/all_to_all | solution.py:333
  26.4 2.1 %collective-permute-done = bf16[64,7168]{1,0:T(8,128)(2,1)S(1)} collective-permute-done((bf16[64,7168]{1,0:T(8,128)(2,1)S(1)}, bf16[64,7168]{1,0:T(8,128)(2,1)S(1)}, u32[]{:S(2)}, u32[]{:S(2)}) %collective-permute-start) | collective-permute-done | bytes 917536 | tf_op jit(solution)/shard_map/heads/ppermute | solution.py:33
  29.9 4.7 %load.2 = (f32[32,3584]{1,0:T(8,128)S(1)}, bf16[7168,512]{1,0:T(8,128)(2,1)S(1)}, bf16[3584,512]{1,0:T(8,128)(2,1)S(1)}) custom-call(f32[32,3584]{1,0:T(8,128)S(1)} %bitcast.75, bf16[7168,512]{1,0:T(8,128)(2,1)} %bitcast.81, bf16[7168,512]{1,0:T(8,128)(2,1)} %bitcast.70), custom_call_target="tpu_custom_call" | custom-call | bytes 22020096 | tf_op jit(solution)/shard_map/heads/load/pallas_call | solution.py:206
  34.6 3.2 %copy-done = bf16[7168,512]{1,0:T(8,128)(2,1)} copy-done((bf16[7168,512]{1,0:T(8,128)(2,1)}, bf16[7168,512]{1,0:T(8,128)(2,1)S(1)}, u32[]{:S(2)}) %copy-start) | copy-done | bytes 7340056
  41.1 1.7 %collective-permute-done.4 = bf16[16,3584]{1,0:T(8,128)(2,1)S(1)} collective-permute-done((bf16[16,3584]{1,0:T(8,128)(2,1)S(1)}, bf16[16,3584]{1,0:T(8,128)(2,1)S(1)}, u32[]{:S(2)}, u32[]{:S(2)}) %collective-permute-start.4) | collective-permute-done | bytes 114720 | tf_op jit(solution)/shard_map/heads/ppermute | solution.py:33
  44.6 1.6 %collective-permute-start.7 = (bf16[4,7168]{1,0:T(4,128)(2,1)S(1)}, bf16[4,7168]{1,0:T(4,128)(2,1)S(1)}, u32[]{:S(2)}, u32[]{:S(2)}) collective-permute-start(bf16[4,7168]{1,0:T(4,128)(2,1)S(1)} %get-tuple-element.36), channel_id=1, source_target_pairs={{0,12},{1,13},{2,14},{3,15},{4,8},{5,9},{6,10},{7,11},{8,4},{9,5},... | collective-permute-start | bytes 172040 | tf_op jit(solution)/shard_map/heads/ppermute | solution.py:33
  47.0 2.0 %collective-permute-start.5 = (bf16[4,7168]{1,0:T(4,128)(2,1)S(1)}, bf16[4,7168]{1,0:T(4,128)(2,1)S(1)}, u32[]{:S(2)}, u32[]{:S(2)}) collective-permute-start(bf16[4,7168]{1,0:T(4,128)(2,1)S(1)} %get-tuple-element.38), channel_id=1, source_target_pairs={{0,4},{1,5},{2,6},{3,7},{4,0},{5,1},{6,2},{7,3},{8,12},{9,13},{10,... | collective-permute-start | bytes 172040 | tf_op jit(solution)/shard_map/heads/ppermute | solution.py:33
  52.1 2.0 %collective-permute-start.10 = (bf16[4,7296]{1,0:T(4,128)(2,1)S(1)}, bf16[4,7296]{1,0:T(4,128)(2,1)S(1)}, u32[]{:S(2)}, u32[]{:S(2)}) collective-permute-start(bf16[4,7296]{1,0:T(4,128)(2,1)S(1)} %get-tuple-element.21), channel_id=1, source_target_pairs={{0,12},{1,13},{2,14},{3,15},{4,8},{5,9},{6,10},{7,11},{8,4},{9,5},... | collective-permute-start | bytes 175112 | tf_op jit(solution)/shard_map/spread/ppermute | solution.py:33
  56.5 1.6 %collective-permute-done.10 = bf16[4,7296]{1,0:T(4,128)(2,1)S(1)} collective-permute-done((bf16[4,7296]{1,0:T(4,128)(2,1)S(1)}, bf16[4,7296]{1,0:T(4,128)(2,1)S(1)}, u32[]{:S(2)}, u32[]{:S(2)}) %collective-permute-start.10) | collective-permute-done | bytes 58400 | tf_op jit(solution)/shard_map/spread/ppermute | solution.py:33
  60.5 1.8 %collective-permute-start.11 = (bf16[16,3584]{1,0:T(8,128)(2,1)S(1)}, bf16[16,3584]{1,0:T(8,128)(2,1)S(1)}, u32[]{:S(2)}, u32[]{:S(2)}) collective-permute-start(bf16[16,3584]{1,0:T(8,128)(2,1)S(1)} %pad_maximum_fusion.7), channel_id=1, source_target_pairs={{0,2},{1,3},{2,0},{3,1},{4,6},{5,7},{6,4},{7,5},{8,10},{9,11},{10,... | collective-permute-start | bytes 344072 | tf_op jit(solution)/shard_map/spread/ppermute | solution.py:33
  62.3 3.1 %collective-permute-done.15 = bf16[16,3712]{1,0:T(8,128)(2,1)S(1)} collective-permute-done((bf16[16,3712]{1,0:T(8,128)(2,1)S(1)}, bf16[16,3712]{1,0:T(8,128)(2,1)S(1)}, u32[]{:S(2)}, u32[]{:S(2)}) %collective-permute-start.15) | collective-permute-done | bytes 118816 | tf_op jit(solution)/shard_map/spread/ppermute | solution.py:33
  65.4 2.1 %collective-permute-start.16 = (bf16[32,3712]{1,0:T(8,128)(2,1)S(1)}, bf16[32,3712]{1,0:T(8,128)(2,1)S(1)}, u32[]{:S(2)}, u32[]{:S(2)}) collective-permute-start(bf16[32,3712]{1,0:T(8,128)(2,1)S(1)} %pad_maximum_fusion.2.refs_4_), channel_id=1, source_target_pairs={{0,2},{1,3},{2,0},{3,1},{4,6},{5,7},{6,4},{7,5},{8,10},{9,11},{10,... | collective-permute-start | bytes 712712 | tf_op jit(solution)/shard_map/spread/ppermute | solution.py:33
  68.1 3.5 %collective-permute-done.16.refs_5_ = bf16[32,3712]{1,0:T(8,128)(2,1)S(1)} collective-permute-done((bf16[32,3712]{1,0:T(8,128)(2,1)S(1)}, bf16[32,3712]{1,0:T(8,128)(2,1)S(1)}, u32[]{:S(2)}, u32[]{:S(2)}) %collective-permute-start.16) | collective-permute-done | bytes 237600 | tf_op jit(solution)/shard_map/spread/ppermute | solution.py:33
  71.6 5.7 %load.3 = (bf16[32,3584]{1,0:T(8,128)(2,1)S(1)}, bf16[3584,512]{1,0:T(8,128)(2,1)S(1)}, bf16[512,7168]{1,0:T(8,128)(2,1)S(1)}) custom-call(bf16[32,3584]{1,0:T(8,128)(2,1)S(1)} %pad_maximum_fusion.3.refs_0_, bf16[7168,512]{1,0:T(8,128)(2,1)S(1)} %bitcast.73, bf16[512,7168]{1,0:T(8,128)(2,1)} %bitcast.80), custom_call_target="tpu_custom_call" | custom-call | bytes 22020096 | tf_op jit(solution)/shard_map/spread/load/pallas_call | solution.py:206
  79.4 3.1 %copy-done.1 = bf16[7168,512]{1,0:T(8,128)(2,1)S(1)} copy-done((bf16[7168,512]{1,0:T(8,128)(2,1)S(1)}, bf16[7168,512]{1,0:T(8,128)(2,1)}, u32[]{:S(2)}) %copy-start.1) | copy-done | bytes 7340056
  82.5 3.6 %experts.1 = (f32[64,7168]{1,0:T(8,128)S(1)}, bf16[64,7168]{1,0:T(8,128)(2,1)S(1)}) custom-call(s32[1]{0:T(128)} %bitcast.me_ref, bf16[32,3584]{1,0:T(8,128)(2,1)S(1)} %get-tuple-element.22.refs_0_, bf16[32,3584]{1,0:T(8,128)(2,1)S(1)} %collective-permute-done.12.refs_1_, bf16[32,3584]{1,0:T(8,128)(2,1)S(1)} %collective-permute-done.13.refs_2_, ...), custom_call_target="tpu_custom_call" | custom-call | flops 2818572288 | bytes 23887872 | tf_op jit(solution)/shard_map/experts/experts/pallas_call | solution.py:256
  86.4 2.2 %collective-permute-done.19 = bf16[64,7168]{1,0:T(8,128)(2,1)S(1)} collective-permute-done((bf16[64,7168]{1,0:T(8,128)(2,1)S(1)}, bf16[64,7168]{1,0:T(8,128)(2,1)S(1)}, u32[]{:S(2)}, u32[]{:S(2)}) %collective-permute-start.19) | collective-permute-done | bytes 917536 | tf_op jit(solution)/shard_map/collect/ppermute | solution.py:33
  89.4 2.0 %collective-permute-start.22 = (bf16[2,16,3584]{2,1,0:T(8,128)(2,1)S(1)}, bf16[2,16,3584]{2,1,0:T(8,128)(2,1)S(1)}, u32[]{:S(2)}, u32[]{:S(2)}) collective-permute-start(bf16[2,16,3584]{2,1,0:T(8,128)(2,1)S(1)} %slice_bitcast_fusion.4), channel_id=1, source_target_pairs={{0,2},{1,3},{2,0},{3,1},{4,6},{5,7},{6,4},{7,5},{8,10},{9,11},{10,... | collective-permute-start | bytes 688136 | tf_op jit(solution)/shard_map/collect/ppermute | solution.py:33
  91.4 5.3 %collective-permute-done.20 = bf16[2,16,3584]{2,1,0:T(8,128)(2,1)S(1)} collective-permute-done((bf16[2,16,3584]{2,1,0:T(8,128)(2,1)S(1)}, bf16[2,16,3584]{2,1,0:T(8,128)(2,1)S(1)}, u32[]{:S(2)}, u32[]{:S(2)}) %collective-permute-start.20) | collective-permute-done | bytes 229408 | tf_op jit(solution)/shard_map/collect/ppermute | solution.py:33
  98.9 1.8 %collective-permute-start.21 = (bf16[16,3584]{1,0:T(8,128)(2,1)S(1)}, bf16[16,3584]{1,0:T(8,128)(2,1)S(1)}, u32[]{:S(2)}, u32[]{:S(2)}) collective-permute-start(bf16[16,3584]{1,0:T(8,128)(2,1)S(1)} %fusion.11), channel_id=1, source_target_pairs={{0,2},{1,3},{2,0},{3,1},{4,6},{5,7},{6,4},{7,5},{8,10},{9,11},{10,... | collective-permute-start | bytes 344072 | tf_op jit(solution)/shard_map/collect/ppermute | solution.py:33
  105.1 1.9 %collective-permute-start.26 = (bf16[4,7168]{1,0:T(4,128)(2,1)S(1)}, bf16[4,7168]{1,0:T(4,128)(2,1)S(1)}, u32[]{:S(2)}, u32[]{:S(2)}) collective-permute-start(bf16[4,7168]{1,0:T(4,128)(2,1)S(1)} %get-tuple-element.34), channel_id=1, source_target_pairs={{0,12},{1,13},{2,14},{3,15},{4,8},{5,9},{6,10},{7,11},{8,4},{9,5},... | collective-permute-start | bytes 172040 | tf_op jit(solution)/shard_map/collect/ppermute | solution.py:33
  109.1 2.0 %collective-permute-done.26 = bf16[4,7168]{1,0:T(4,128)(2,1)S(1)} collective-permute-done((bf16[4,7168]{1,0:T(4,128)(2,1)S(1)}, bf16[4,7168]{1,0:T(4,128)(2,1)S(1)}, u32[]{:S(2)}, u32[]{:S(2)}) %collective-permute-start.26) | collective-permute-done | bytes 57376 | tf_op jit(solution)/shard_map/collect/ppermute | solution.py:33
  (92 shorter events, 31.1 us)
Async XLA Ops:
  6.9 18.1 %all-to-all-start = ((bf16[32,4,512]{2,1,0:T(4,128)(2,1)}), bf16[32,4,512]{2,1,0:T(4,128)(2,1)S(1)}, u32[]{:S(2)}, u32[]{:S(2)}) async-start(bf16[32,4,512]{2,1,0:T(4,128)(2,1)} %attend.1), calls=%async_computation | async-start | bytes 262144 | tf_op jit(solution)/shard_map/heads/all_to_all | solution.py:333
  28.7 9.2 %collective-permute-start.3 = (bf16[2,16,3584]{2,1,0:T(8,128)(2,1)S(1)}, bf16[2,16,3584]{2,1,0:T(8,128)(2,1)S(1)}, u32[]{:S(2)}, u32[]{:S(2)}) collective-permute-start(bf16[2,16,3584]{2,1,0:T(8,128)(2,1)S(1)} %slice_bitcast_fusion.8), channel_id=1, source_target_pairs={{0,2},{1,3},{2,0},{3,1},{4,6},{5,7},{6,4},{7,5},{8,10},{9,11},{10,... | collective-permute-start | bytes 688136 | tf_op jit(solution)/shard_map/heads/ppermute | solution.py:33
  29.3 10.2 %collective-permute-start.1 = (bf16[2,16,3584]{2,1,0:T(8,128)(2,1)S(1)}, bf16[2,16,3584]{2,1,0:T(8,128)(2,1)S(1)}, u32[]{:S(2)}, u32[]{:S(2)}) collective-permute-start(bf16[2,16,3584]{2,1,0:T(8,128)(2,1)S(1)} %slice_bitcast_fusion.10), channel_id=1, source_target_pairs={{0,16},{1,17},{2,18},{3,19},{4,20},{5,21},{6,22},{7,23},{8,24},{9,... | collective-permute-start | bytes 688136 | tf_op jit(solution)/shard_map/heads/ppermute | solution.py:33
  37.9 4.9 %collective-permute-start.4 = (bf16[16,3584]{1,0:T(8,128)(2,1)S(1)}, bf16[16,3584]{1,0:T(8,128)(2,1)S(1)}, u32[]{:S(2)}, u32[]{:S(2)}) collective-permute-start(bf16[16,3584]{1,0:T(8,128)(2,1)S(1)} %fusion.10), channel_id=1, source_target_pairs={{0,16},{1,17},{2,18},{3,19},{4,20},{5,21},{6,22},{7,23},{8,24},{9,... | collective-permute-start | bytes 344072 | tf_op jit(solution)/shard_map/heads/ppermute | solution.py:33
  39.6 4.9 %collective-permute-start.2 = (bf16[16,3584]{1,0:T(8,128)(2,1)S(1)}, bf16[16,3584]{1,0:T(8,128)(2,1)S(1)}, u32[]{:S(2)}, u32[]{:S(2)}) collective-permute-start(bf16[16,3584]{1,0:T(8,128)(2,1)S(1)} %fusion.9), channel_id=1, source_target_pairs={{0,2},{1,3},{2,0},{3,1},{4,6},{5,7},{6,4},{7,5},{8,10},{9,11},{10,... | collective-permute-start | bytes 344072 | tf_op jit(solution)/shard_map/heads/ppermute | solution.py:33
  44.6 6.0 %collective-permute-start.7 = (bf16[4,7168]{1,0:T(4,128)(2,1)S(1)}, bf16[4,7168]{1,0:T(4,128)(2,1)S(1)}, u32[]{:S(2)}, u32[]{:S(2)}) collective-permute-start(bf16[4,7168]{1,0:T(4,128)(2,1)S(1)} %get-tuple-element.36), channel_id=1, source_target_pairs={{0,12},{1,13},{2,14},{3,15},{4,8},{5,9},{6,10},{7,11},{8,4},{9,5},... | collective-permute-start | bytes 172040 | tf_op jit(solution)/shard_map/heads/ppermute | solution.py:33
  46.2 5.7 %collective-permute-start.6 = (bf16[4,7168]{1,0:T(4,128)(2,1)S(1)}, bf16[4,7168]{1,0:T(4,128)(2,1)S(1)}, u32[]{:S(2)}, u32[]{:S(2)}) collective-permute-start(bf16[4,7168]{1,0:T(4,128)(2,1)S(1)} %get-tuple-element.37), channel_id=1, source_target_pairs={{0,8},{1,9},{2,10},{3,11},{4,12},{5,13},{6,14},{7,15},{8,0},{9,1},... | collective-permute-start | bytes 172040 | tf_op jit(solution)/shard_map/heads/ppermute | solution.py:33
  47.0 4.8 %collective-permute-start.5 = (bf16[4,7168]{1,0:T(4,128)(2,1)S(1)}, bf16[4,7168]{1,0:T(4,128)(2,1)S(1)}, u32[]{:S(2)}, u32[]{:S(2)}) collective-permute-start(bf16[4,7168]{1,0:T(4,128)(2,1)S(1)} %get-tuple-element.38), channel_id=1, source_target_pairs={{0,4},{1,5},{2,6},{3,7},{4,0},{5,1},{6,2},{7,3},{8,12},{9,13},{10,... | collective-permute-start | bytes 172040 | tf_op jit(solution)/shard_map/heads/ppermute | solution.py:33
  52.1 6.1 %collective-permute-start.10 = (bf16[4,7296]{1,0:T(4,128)(2,1)S(1)}, bf16[4,7296]{1,0:T(4,128)(2,1)S(1)}, u32[]{:S(2)}, u32[]{:S(2)}) collective-permute-start(bf16[4,7296]{1,0:T(4,128)(2,1)S(1)} %get-tuple-element.21), channel_id=1, source_target_pairs={{0,12},{1,13},{2,14},{3,15},{4,8},{5,9},{6,10},{7,11},{8,4},{9,5},... | collective-permute-start | bytes 175112 | tf_op jit(solution)/shard_map/spread/ppermute | solution.py:33
  54.0 5.4 %collective-permute-start.9 = (bf16[4,7296]{1,0:T(4,128)(2,1)S(1)}, bf16[4,7296]{1,0:T(4,128)(2,1)S(1)}, u32[]{:S(2)}, u32[]{:S(2)}) collective-permute-start(bf16[4,7296]{1,0:T(4,128)(2,1)S(1)} %get-tuple-element.21), channel_id=1, source_target_pairs={{0,8},{1,9},{2,10},{3,11},{4,12},{5,13},{6,14},{7,15},{8,0},{9,1},... | collective-permute-start | bytes 175112 | tf_op jit(solution)/shard_map/spread/ppermute | solution.py:33
  54.9 4.8 %collective-permute-start.8 = (bf16[4,7296]{1,0:T(4,128)(2,1)S(1)}, bf16[4,7296]{1,0:T(4,128)(2,1)S(1)}, u32[]{:S(2)}, u32[]{:S(2)}) collective-permute-start(bf16[4,7296]{1,0:T(4,128)(2,1)S(1)} %get-tuple-element.21), channel_id=1, source_target_pairs={{0,4},{1,5},{2,6},{3,7},{4,0},{5,1},{6,2},{7,3},{8,12},{9,13},{10,... | collective-permute-start | bytes 175112 | tf_op jit(solution)/shard_map/spread/ppermute | solution.py:33
  59.8 5.6 %collective-permute-start.15 = (bf16[16,3712]{1,0:T(8,128)(2,1)S(1)}, bf16[16,3712]{1,0:T(8,128)(2,1)S(1)}, u32[]{:S(2)}, u32[]{:S(2)}) collective-permute-start(bf16[16,3712]{1,0:T(8,128)(2,1)S(1)} %pad_maximum_fusion.4), channel_id=1, source_target_pairs={{0,16},{1,17},{2,18},{3,19},{4,20},{5,21},{6,22},{7,23},{8,24},{9,... | collective-permute-start | bytes 356360 | tf_op jit(solution)/shard_map/spread/ppermute | solution.py:33
  60.5 7.0 %collective-permute-start.11 = (bf16[16,3584]{1,0:T(8,128)(2,1)S(1)}, bf16[16,3584]{1,0:T(8,128)(2,1)S(1)}, u32[]{:S(2)}, u32[]{:S(2)}) collective-permute-start(bf16[16,3584]{1,0:T(8,128)(2,1)S(1)} %pad_maximum_fusion.7), channel_id=1, source_target_pairs={{0,2},{1,3},{2,0},{3,1},{4,6},{5,7},{6,4},{7,5},{8,10},{9,11},{10,... | collective-permute-start | bytes 344072 | tf_op jit(solution)/shard_map/spread/ppermute | solution.py:33
  65.4 6.2 %collective-permute-start.16 = (bf16[32,3712]{1,0:T(8,128)(2,1)S(1)}, bf16[32,3712]{1,0:T(8,128)(2,1)S(1)}, u32[]{:S(2)}, u32[]{:S(2)}) collective-permute-start(bf16[32,3712]{1,0:T(8,128)(2,1)S(1)} %pad_maximum_fusion.2.refs_4_), channel_id=1, source_target_pairs={{0,2},{1,3},{2,0},{3,1},{4,6},{5,7},{6,4},{7,5},{8,10},{9,11},{10,... | collective-permute-start | bytes 712712 | tf_op jit(solution)/shard_map/spread/ppermute | solution.py:33
  67.5 10.4 %collective-permute-start.12 = (bf16[32,3584]{1,0:T(8,128)(2,1)S(1)}, bf16[32,3584]{1,0:T(8,128)(2,1)S(1)}, u32[]{:S(2)}, u32[]{:S(2)}) collective-permute-start(bf16[32,3584]{1,0:T(8,128)(2,1)S(1)} %pad_maximum_fusion.3.refs_0_), channel_id=1, source_target_pairs={{0,16},{1,17},{2,18},{3,19},{4,20},{5,21},{6,22},{7,23},{8,24},{9,... | collective-permute-start | bytes 688136 | tf_op jit(solution)/shard_map/spread/ppermute | solution.py:33
  68.1 10.9 %collective-permute-start.17 = (bf16[32,3712]{1,0:T(8,128)(2,1)S(1)}, bf16[32,3712]{1,0:T(8,128)(2,1)S(1)}, u32[]{:S(2)}, u32[]{:S(2)}) collective-permute-start(bf16[32,3712]{1,0:T(8,128)(2,1)S(1)} %pad_maximum_fusion.2.refs_4_), channel_id=1, source_target_pairs={{0,1},{1,0},{2,3},{3,2},{4,5},{5,4},{6,7},{7,6},{8,9},{9,8},{10,11... | collective-permute-start | bytes 712712 | tf_op jit(solution)/shard_map/spread/ppermute | solution.py:33
  71.6 7.8 %collective-permute-start.18 = (bf16[32,3712]{1,0:T(8,128)(2,1)S(1)}, bf16[32,3712]{1,0:T(8,128)(2,1)S(1)}, u32[]{:S(2)}, u32[]{:S(2)}) collective-permute-start(bf16[32,3712]{1,0:T(8,128)(2,1)S(1)} %collective-permute-done.16.refs_5_), channel_id=1, source_target_pairs={{0,1},{1,0},{2,3},{3,2},{4,5},{5,4},{6,7},{7,6},{8,9},{9,8},{10,11... | collective-permute-start | bytes 712712 | tf_op jit(solution)/shard_map/spread/ppermute | solution.py:33
  88.8 7.9 %collective-permute-start.20 = (bf16[2,16,3584]{2,1,0:T(8,128)(2,1)S(1)}, bf16[2,16,3584]{2,1,0:T(8,128)(2,1)S(1)}, u32[]{:S(2)}, u32[]{:S(2)}) collective-permute-start(bf16[2,16,3584]{2,1,0:T(8,128)(2,1)S(1)} %slice_bitcast_fusion.6), channel_id=1, source_target_pairs={{0,16},{1,17},{2,18},{3,19},{4,20},{5,21},{6,22},{7,23},{8,24},{9,... | collective-permute-start | bytes 688136 | tf_op jit(solution)/shard_map/collect/ppermute | solution.py:33
  89.4 7.8 %collective-permute-start.22 = (bf16[2,16,3584]{2,1,0:T(8,128)(2,1)S(1)}, bf16[2,16,3584]{2,1,0:T(8,128)(2,1)S(1)}, u32[]{:S(2)}, u32[]{:S(2)}) collective-permute-start(bf16[2,16,3584]{2,1,0:T(8,128)(2,1)S(1)} %slice_bitcast_fusion.4), channel_id=1, source_target_pairs={{0,2},{1,3},{2,0},{3,1},{4,6},{5,7},{6,4},{7,5},{8,10},{9,11},{10,... | collective-permute-start | bytes 688136 | tf_op jit(solution)/shard_map/collect/ppermute | solution.py:33
  97.4 4.9 %collective-permute-start.23 = (bf16[16,3584]{1,0:T(8,128)(2,1)S(1)}, bf16[16,3584]{1,0:T(8,128)(2,1)S(1)}, u32[]{:S(2)}, u32[]{:S(2)}) collective-permute-start(bf16[16,3584]{1,0:T(8,128)(2,1)S(1)} %fusion.12), channel_id=1, source_target_pairs={{0,16},{1,17},{2,18},{3,19},{4,20},{5,21},{6,22},{7,23},{8,24},{9,... | collective-permute-start | bytes 344072 | tf_op jit(solution)/shard_map/collect/ppermute | solution.py:33
  98.9 4.9 %collective-permute-start.21 = (bf16[16,3584]{1,0:T(8,128)(2,1)S(1)}, bf16[16,3584]{1,0:T(8,128)(2,1)S(1)}, u32[]{:S(2)}, u32[]{:S(2)}) collective-permute-start(bf16[16,3584]{1,0:T(8,128)(2,1)S(1)} %fusion.11), channel_id=1, source_target_pairs={{0,2},{1,3},{2,0},{3,1},{4,6},{5,7},{6,4},{7,5},{8,10},{9,11},{10,... | collective-permute-start | bytes 344072 | tf_op jit(solution)/shard_map/collect/ppermute | solution.py:33
  103.9 5.1 %collective-permute-start.24 = (bf16[4,7168]{1,0:T(4,128)(2,1)S(1)}, bf16[4,7168]{1,0:T(4,128)(2,1)S(1)}, u32[]{:S(2)}, u32[]{:S(2)}) collective-permute-start(bf16[4,7168]{1,0:T(4,128)(2,1)S(1)} %get-tuple-element.33), channel_id=1, source_target_pairs={{0,4},{1,5},{2,6},{3,7},{4,0},{5,1},{6,2},{7,3},{8,12},{9,13},{10,... | collective-permute-start | bytes 172040 | tf_op jit(solution)/shard_map/collect/ppermute | solution.py:33
  105.1 6.0 %collective-permute-start.26 = (bf16[4,7168]{1,0:T(4,128)(2,1)S(1)}, bf16[4,7168]{1,0:T(4,128)(2,1)S(1)}, u32[]{:S(2)}, u32[]{:S(2)}) collective-permute-start(bf16[4,7168]{1,0:T(4,128)(2,1)S(1)} %get-tuple-element.34), channel_id=1, source_target_pairs={{0,12},{1,13},{2,14},{3,15},{4,8},{5,9},{6,10},{7,11},{8,4},{9,5},... | collective-permute-start | bytes 172040 | tf_op jit(solution)/shard_map/collect/ppermute | solution.py:33
  106.9 5.3 %collective-permute-start.25 = (bf16[4,7168]{1,0:T(4,128)(2,1)S(1)}, bf16[4,7168]{1,0:T(4,128)(2,1)S(1)}, u32[]{:S(2)}, u32[]{:S(2)}) collective-permute-start(bf16[4,7168]{1,0:T(4,128)(2,1)S(1)} %get-tuple-element.35), channel_id=1, source_target_pairs={{0,8},{1,9},{2,10},{3,11},{4,12},{5,13},{6,14},{7,15},{8,0},{9,1},... | collective-permute-start | bytes 172040 | tf_op jit(solution)/shard_map/collect/ppermute | solution.py:33
  (14 other events, 217.1 us)

commit v7 on v4

--- a/solution.py
+++ b/solution.py
@@ -13,7 +13,8 @@
 VDIM = 128
 STEPS = 4
 TOPK = 8
-BLK = 2048
+BLK = 1024
+AHEAD = 4
 SPAN = 8
 AXES = ("sec", "ep")
 NT = (((1,), (1,)), ((), ()))
@@ -67,8 +68,8 @@
     new_copy = pltpu.make_async_copy(new_hbm, new_ref, small_sem.at[1])
     q_copy.start()
     new_copy.start()
-    start(0)
-    start(1)
+    for i in range(AHEAD):
+        start(i)
     r = iota2((rows, rows), 0)
     order = one_hot((r % STEPS) * heads + r // STEPS, rows)
     q_copy.wait()
@@ -84,13 +85,14 @@
     l_ref[...] = jnp.sum(p, axis=1, keepdims=True)
     acc_ref[...] = jnp.dot(p.astype(BF), new[:, :LAT], preferred_element_type=F32)
 
-    def update(i, masked):
-        start(i + 2)
+    def scores(i, masked):
         block_copy(i).wait()
-        keys = keys_ref[:, block_at(i)]
-        s = jnp.dot(q_ref[...], keys, preferred_element_type=F32)
+        s = jnp.dot(q_ref[...], keys_ref[:, block_at(i)], preferred_element_type=F32)
         if masked:
             s = jnp.where(iota2(s.shape, 1) < length - i * blk, s, -1e30)
+        return s
+
+    def absorb(i, s):
         m_old = m_ref[...]
         m = jnp.maximum(m_old, jnp.max(s, axis=1, keepdims=True))
         factor = jnp.exp2((m_old - m) * factor_base2)
@@ -98,18 +100,24 @@
         m_ref[...] = m
         l_ref[...] = l_ref[...] * factor + jnp.sum(p, axis=1, keepdims=True)
         acc_ref[...] = acc_ref[...] * factor + lax.dot_general(
-            p.astype(BF), keys[:LAT], NT, preferred_element_type=F32
-        )
-
-    full = length // blk
-
-    @pl.loop(0, full)
+            p.astype(BF), keys_ref[:LAT, block_at(i)], NT, preferred_element_type=F32
+        )
+
+    pairs = length // (2 * blk)
+
+    @pl.loop(0, pairs)
     def _(i):
-        update(i, False)
-
-    @pl.when(full * blk < length)
-    def _():
-        update(full, True)
+        for ahead in range(2):
+            start(2 * i + AHEAD + ahead)
+        first, second = scores(2 * i, False), scores(2 * i + 1, False)
+        absorb(2 * i, first)
+        absorb(2 * i + 1, second)
+
+    for tail in range(2):
+
+        @pl.when((2 * pairs + tail) * blk < length)
+        def _(tail=tail):
+            absorb(2 * pairs + tail, scores(2 * pairs + tail, True))
 
     out = (acc_ref[...] / l_ref[...]).astype(BF)
     out_ref[...] = pick(order, out).reshape(out_ref.shape).astype(BF)
@@ -202,7 +210,7 @@
         out_specs=[pl.BlockSpec(memory_space=pltpu.VMEM)] * 4,
         out_shape=[jax.ShapeDtypeStruct(a.shape, a.dtype) for a in [passed] + arrays],
         scratch_shapes=[pltpu.SemaphoreType.DMA((13,))],
-        compiler_params=pltpu.CompilerParams(vmem_limit_bytes=36 * 1024 * 1024),
+        compiler_params=pltpu.CompilerParams(vmem_limit_bytes=28 * 1024 * 1024),
         cost_estimate=pl.CostEstimate(
             flops=0, bytes_accessed=sum(4 * a.size for a in arrays), transcendentals=0
         ),
@@ -253,7 +261,7 @@
     width = near.shape[1]
     total = (near + swap(far, n, c=1).astype(F32)).reshape(4, planes * STEPS, width)
     kept = total[0]
-    for q in range(1, 4):
+    for q in (3, 2, 1):
         kept = kept + swap(total[q].astype(BF), n, q=q).astype(F32)
     kept = kept.reshape(planes, STEPS, width)
     return [kept[0]] + [swap(kept[k].astype(BF), n, k=k) for k in range(1, planes)]

time: 108 us -> 104 us (0.963)
  starting transfers between devices: 35.7 us -> 32.2 us
  local copies, waits for them, and re-layouts: 3.41 us -> 0.33 us
  waiting for transfers between devices: 46.1 us -> 47.5 us
    pallas_call x1, Pallas kernels: 4.57 us -> 8.46 us  [attend(): pl.pallas_call(functools.partial(attend_kernel, n), in_specs=[pl.BlockSpe...]
    all_to_all x1, starting transfers between devices: 11 us -> 7.51 us  [per_device(): latents = lax.all_to_all(latents, AXES, 0, 0, tiled=True)]
    unnamed x14 -> x12, local copies, waits for them, and re-layouts: 3.11 us -> 0.03 us
    pallas_call x1, Pallas kernels: 10.6 us -> 7.71 us  [load(): pl.pallas_call(functools.partial(load_kernel, n), in_specs=[pl.BlockSpec(...]
    ppermute x24, waiting for transfers between devices: 37.9 us -> 39.3 us  [swap(): return lax.ppermute(x, AXES, [(d, d ^ mask) for d in range(n)])]
  transfers between devices with their start and end apart: 25 -> 25, of which waited for: 18 -> 17; matrix products, arithmetic and copies ran while one was open for 0% -> 0% of each run, Pallas kernels for 10% -> 7%
where the time goes in v7:
time: 104 us; the launch traced here: 103 us
  waiting for transfers between devices  47.5 us (46%)
  starting transfers between devices  32.2 us (31%)
  Pallas kernels  20.9 us (20%)
  other arithmetic  1.58 us (2%)
    ppermute x24, waiting for transfers between devices, swap(): return lax.ppermute(x, AXES, [(d, d ^ mask) for d in range(n)])  39.3 us
    ppermute x24, starting transfers between devices, swap(): return lax.ppermute(x, AXES, [(d, d ^ mask) for d in range(n)])  24.7 us
    pallas_call x1, Pallas kernels, attend(): pl.pallas_call(functools.partial(attend_kernel, n), in_specs=[pl.BlockSpe...  8.46 us
    all_to_all x1, waiting for transfers between devices, per_device(): latents = lax.all_to_all(latents, AXES, 0, 0, tiled=True)  8.22 us
    pallas_call x1, Pallas kernels, load(): pl.pallas_call(functools.partial(load_kernel, n), in_specs=[pl.BlockSpec(...  7.71 us
    all_to_all x1, starting transfers between devices, per_device(): latents = lax.all_to_all(latents, AXES, 0, 0, tiled=True)  7.51 us
    pallas_call x3, Pallas kernels, single(): pl.pallas_call(functools.partial(kernel, n), in_specs=[pl.BlockSpec(memor...  4.72 us
  transfers between devices with their start and end apart: 25, of which 17 were waited for; matrix products, arithmetic and copies ran while one was open for 0% of the time, Pallas kernels for 7%

profile of v7, /device:TPU:0, one launch (start us, length us, event | category | flops | bytes accessed | tf_op | source)
XLA Modules:
  0.0 103.4 jit_solution(9224346163425456692)
XLA Ops:
  0.7 8.5 %attend.1 = bf16[32,4,512]{2,1,0:T(4,128)(2,1)} custom-call(s32[1]{0:T(128)S(6)} %copy.14.len_ref, bf16[128,576]{1,0:T(8,128)(2,1)} %bitcast.29, bf16[4,576]{1,0:T(4,128)(2,1)} %bitcast.30, bf16[576,8192]{1,0:T(8,128)(2,1)} %bitcast.25), custom_call_target="tpu_custom_call" | custom-call | flops 2281701376 | bytes 9437184 | tf_op jit(solution)/shard_map/attention/attend/pallas_call | solution.py:130
  9.1 7.5 %all-to-all-start = ((bf16[32,4,512]{2,1,0:T(4,128)(2,1)}), bf16[32,4,512]{2,1,0:T(4,128)(2,1)S(1)}, u32[]{:S(2)}, u32[]{:S(2)}) async-start(bf16[32,4,512]{2,1,0:T(4,128)(2,1)} %attend.1), calls=%async_computation | async-start | bytes 262144 | tf_op jit(solution)/shard_map/heads/all_to_all | solution.py:303
  16.7 8.2 %all-to-all-done = bf16[32,4,512]{2,1,0:T(4,128)(2,1)S(1)} async-done(((bf16[32,4,512]{2,1,0:T(4,128)(2,1)}), bf16[32,4,512]{2,1,0:T(4,128)(2,1)S(1)}, u32[]{:S(2)}, u32[]{:S(2)}) %all-to-all-start) | async-done | bytes 131104 | tf_op jit(solution)/shard_map/heads/all_to_all | solution.py:303
  26.2 2.2 %collective-permute-done = bf16[64,7168]{1,0:T(8,128)(2,1)S(1)} collective-permute-done((bf16[64,7168]{1,0:T(8,128)(2,1)S(1)}, bf16[64,7168]{1,0:T(8,128)(2,1)S(1)}, u32[]{:S(2)}, u32[]{:S(2)}) %collective-permute-start) | collective-permute-done | bytes 917536 | tf_op jit(solution)/shard_map/heads/ppermute | solution.py:32
  29.3 1.8 %collective-permute-start.3 = (bf16[16,7168]{1,0:T(8,128)(2,1)S(1)}, bf16[16,7168]{1,0:T(8,128)(2,1)S(1)}, u32[]{:S(2)}, u32[]{:S(2)}) collective-permute-start(bf16[16,7168]{1,0:T(8,128)(2,1)S(1)} %get-tuple-element.39), channel_id=1, source_target_pairs={{0,2},{1,3},{2,0},{3,1},{4,6},{5,7},{6,4},{7,5},{8,10},{9,11},{10,... | collective-permute-start | bytes 688136 | tf_op jit(solution)/shard_map/heads/ppermute | solution.py:32
  32.3 5.8 %collective-permute-done.1 = bf16[16,7168]{1,0:T(8,128)(2,1)S(1)} collective-permute-done((bf16[16,7168]{1,0:T(8,128)(2,1)S(1)}, bf16[16,7168]{1,0:T(8,128)(2,1)S(1)}, u32[]{:S(2)}, u32[]{:S(2)}) %collective-permute-start.1) | collective-permute-done | bytes 229408 | tf_op jit(solution)/shard_map/heads/ppermute | solution.py:32
  38.2 3.5 %collective-permute-done.3 = bf16[16,7168]{1,0:T(8,128)(2,1)S(1)} collective-permute-done((bf16[16,7168]{1,0:T(8,128)(2,1)S(1)}, bf16[16,7168]{1,0:T(8,128)(2,1)S(1)}, u32[]{:S(2)}, u32[]{:S(2)}) %collective-permute-start.3) | collective-permute-done | bytes 229408 | tf_op jit(solution)/shard_map/heads/ppermute | solution.py:32
  41.9 1.5 %collective-permute-start.6 = (bf16[4,7168]{1,0:T(4,128)(2,1)S(1)}, bf16[4,7168]{1,0:T(4,128)(2,1)S(1)}, u32[]{:S(2)}, u32[]{:S(2)}) collective-permute-start(bf16[4,7168]{1,0:T(4,128)(2,1)S(1)} %get-tuple-element.44), channel_id=1, source_target_pairs={{0,12},{1,13},{2,14},{3,15},{4,8},{5,9},{6,10},{7,11},{8,4},{9,5},... | collective-permute-start | bytes 172040 | tf_op jit(solution)/shard_map/heads/ppermute | solution.py:32
  44.0 2.3 %collective-permute-start.4 = (bf16[4,7168]{1,0:T(4,128)(2,1)S(1)}, bf16[4,7168]{1,0:T(4,128)(2,1)S(1)}, u32[]{:S(2)}, u32[]{:S(2)}) collective-permute-start(bf16[4,7168]{1,0:T(4,128)(2,1)S(1)} %get-tuple-element.46), channel_id=1, source_target_pairs={{0,4},{1,5},{2,6},{3,7},{4,0},{5,1},{6,2},{7,3},{8,12},{9,13},{10,... | collective-permute-start | bytes 172040 | tf_op jit(solution)/shard_map/heads/ppermute | solution.py:32
  46.4 2.1 %collective-permute-done.6.refs_3_ = bf16[4,7168]{1,0:T(4,128)(2,1)S(1)} collective-permute-done((bf16[4,7168]{1,0:T(4,128)(2,1)S(1)}, bf16[4,7168]{1,0:T(4,128)(2,1)S(1)}, u32[]{:S(2)}, u32[]{:S(2)}) %collective-permute-start.6) | collective-permute-done | bytes 57376 | tf_op jit(solution)/shard_map/heads/ppermute | solution.py:32
  52.3 2.3 %collective-permute-start.7 = (bf16[4,7296]{1,0:T(4,128)(2,1)S(1)}, bf16[4,7296]{1,0:T(4,128)(2,1)S(1)}, u32[]{:S(2)}, u32[]{:S(2)}) collective-permute-start(bf16[4,7296]{1,0:T(4,128)(2,1)S(1)} %get-tuple-element.18), channel_id=1, source_target_pairs={{0,4},{1,5},{2,6},{3,7},{4,0},{5,1},{6,2},{7,3},{8,12},{9,13},{10,... | collective-permute-start | bytes 175112 | tf_op jit(solution)/shard_map/spread/ppermute | solution.py:32
  54.6 2.3 %collective-permute-done.9 = bf16[4,7296]{1,0:T(4,128)(2,1)S(1)} collective-permute-done((bf16[4,7296]{1,0:T(4,128)(2,1)S(1)}, bf16[4,7296]{1,0:T(4,128)(2,1)S(1)}, u32[]{:S(2)}, u32[]{:S(2)}) %collective-permute-start.9) | collective-permute-done | bytes 58400 | tf_op jit(solution)/shard_map/spread/ppermute | solution.py:32
  58.3 1.6 %collective-permute-start.12 = (bf16[16,7296]{1,0:T(8,128)(2,1)S(1)}, bf16[16,7296]{1,0:T(8,128)(2,1)S(1)}, u32[]{:S(2)}, u32[]{:S(2)}) collective-permute-start(bf16[16,7296]{1,0:T(8,128)(2,1)S(1)} %pad_maximum_fusion.refs_0_), channel_id=1, source_target_pairs={{0,18},{1,19},{2,16},{3,17},{4,22},{5,23},{6,20},{7,21},{8,26},{9,... | collective-permute-start | bytes 700424 | tf_op jit(solution)/shard_map/spread/ppermute | solution.py:32
  61.9 7.7 %load_experts.1 = (bf16[16,7296]{1,0:T(8,128)(2,1)S(1)}, bf16[7168,512]{1,0:T(8,128)(2,1)S(1)}, bf16[7168,512]{1,0:T(8,128)(2,1)S(1)}, bf16[512,7168]{1,0:T(8,128)(2,1)S(1)}) custom-call(bf16[16,7296]{1,0:T(8,128)(2,1)S(1)} %pad_maximum_fusion.refs_0_, bf16[7168,512]{1,0:T(8,128)(2,1)} %bitcast.26, bf16[7168,512]{1,0:T(8,128)(2,1)} %bitcast.27, ...), custom_call_target="tpu_custom_call" | custom-call | bytes 44040192 | tf_op jit(solution)/shard_map/spread/load_experts/pallas_call | solution.py:207
  70.2 1.7 %collective-permute-done.11.refs_2_ = bf16[16,7296]{1,0:T(8,128)(2,1)S(1)} collective-permute-done((bf16[16,7296]{1,0:T(8,128)(2,1)S(1)}, bf16[16,7296]{1,0:T(8,128)(2,1)S(1)}, u32[]{:S(2)}, u32[]{:S(2)}) %collective-permute-start.11) | collective-permute-done | bytes 233504 | tf_op jit(solution)/shard_map/spread/ppermute | solution.py:32
  73.7 3.6 %experts.1 = (f32[64,7168]{1,0:T(8,128)S(1)}, bf16[64,7168]{1,0:T(8,128)(2,1)S(1)}) custom-call(s32[1]{0:T(128)} %bitcast.me_ref, bf16[16,7296]{1,0:T(8,128)(2,1)S(1)} %pad_maximum_fusion.refs_0_, bf16[16,7296]{1,0:T(8,128)(2,1)S(1)} %collective-permute-done.10.refs_1_, bf16[16,7296]{1,0:T(8,128)(2,1)S(1)} %collective-permute-done.11.refs_2_, ...), custom_call_target="tpu_custom_call" | custom-call | flops 2818572288 | bytes 23887872 | tf_op jit(solution)/shard_map/experts/experts/pallas_call | solution.py:246
  77.5 2.3 %collective-permute-done.17 = bf16[64,7168]{1,0:T(8,128)(2,1)S(1)} collective-permute-done((bf16[64,7168]{1,0:T(8,128)(2,1)S(1)}, bf16[64,7168]{1,0:T(8,128)(2,1)S(1)}, u32[]{:S(2)}, u32[]{:S(2)}) %collective-permute-start.17) | collective-permute-done | bytes 917536 | tf_op jit(solution)/shard_map/collect/ppermute | solution.py:32
  80.1 1.6 %collective-permute-start.18 = (bf16[16,7168]{1,0:T(8,128)(2,1)S(1)}, bf16[16,7168]{1,0:T(8,128)(2,1)S(1)}, u32[]{:S(2)}, u32[]{:S(2)}) collective-permute-start(bf16[16,7168]{1,0:T(8,128)(2,1)S(1)} %get-tuple-element.35), channel_id=1, source_target_pairs={{0,18},{1,19},{2,16},{3,17},{4,22},{5,23},{6,20},{7,21},{8,26},{9,... | collective-permute-start | bytes 688136 | tf_op jit(solution)/shard_map/collect/ppermute | solution.py:32
  83.7 5.9 %collective-permute-done.18 = bf16[16,7168]{1,0:T(8,128)(2,1)S(1)} collective-permute-done((bf16[16,7168]{1,0:T(8,128)(2,1)S(1)}, bf16[16,7168]{1,0:T(8,128)(2,1)S(1)}, u32[]{:S(2)}, u32[]{:S(2)}) %collective-permute-start.18) | collective-permute-done | bytes 229408 | tf_op jit(solution)/shard_map/collect/ppermute | solution.py:32
  89.6 4.1 %collective-permute-done.20 = bf16[16,7168]{1,0:T(8,128)(2,1)S(1)} collective-permute-done((bf16[16,7168]{1,0:T(8,128)(2,1)S(1)}, bf16[16,7168]{1,0:T(8,128)(2,1)S(1)}, u32[]{:S(2)}, u32[]{:S(2)}) %collective-permute-start.20) | collective-permute-done | bytes 229408 | tf_op jit(solution)/shard_map/collect/ppermute | solution.py:32
  94.0 1.6 %collective-permute-start.23 = (bf16[4,7168]{1,0:T(4,128)(2,1)S(1)}, bf16[4,7168]{1,0:T(4,128)(2,1)S(1)}, u32[]{:S(2)}, u32[]{:S(2)}) collective-permute-start(bf16[4,7168]{1,0:T(4,128)(2,1)S(1)} %get-tuple-element.42), channel_id=1, source_target_pairs={{0,12},{1,13},{2,14},{3,15},{4,8},{5,9},{6,10},{7,11},{8,4},{9,5},... | collective-permute-start | bytes 172040 | tf_op jit(solution)/shard_map/collect/ppermute | solution.py:32
  95.6 1.9 %collective-permute-start.22 = (bf16[4,7168]{1,0:T(4,128)(2,1)S(1)}, bf16[4,7168]{1,0:T(4,128)(2,1)S(1)}, u32[]{:S(2)}, u32[]{:S(2)}) collective-permute-start(bf16[4,7168]{1,0:T(4,128)(2,1)S(1)} %get-tuple-element.43), channel_id=1, source_target_pairs={{0,8},{1,9},{2,10},{3,11},{4,12},{5,13},{6,14},{7,15},{8,0},{9,1},... | collective-permute-start | bytes 172040 | tf_op jit(solution)/shard_map/collect/ppermute | solution.py:32
  98.1 2.3 %collective-permute-done.23 = bf16[4,7168]{1,0:T(4,128)(2,1)S(1)} collective-permute-done((bf16[4,7168]{1,0:T(4,128)(2,1)S(1)}, bf16[4,7168]{1,0:T(4,128)(2,1)S(1)}, u32[]{:S(2)}, u32[]{:S(2)}) %collective-permute-start.23) | collective-permute-done | bytes 57376 | tf_op jit(solution)/shard_map/collect/ppermute | solution.py:32
  100.4 2.4 %collective-permute-done.22 = bf16[4,7168]{1,0:T(4,128)(2,1)S(1)} collective-permute-done((bf16[4,7168]{1,0:T(4,128)(2,1)S(1)}, bf16[4,7168]{1,0:T(4,128)(2,1)S(1)}, u32[]{:S(2)}, u32[]{:S(2)}) %collective-permute-start.22) | collective-permute-done | bytes 57376 | tf_op jit(solution)/shard_map/collect/ppermute | solution.py:32
  (59 shorter events, 17.9 us)
Async XLA Ops:
  9.1 15.7 %all-to-all-start = ((bf16[32,4,512]{2,1,0:T(4,128)(2,1)}), bf16[32,4,512]{2,1,0:T(4,128)(2,1)S(1)}, u32[]{:S(2)}, u32[]{:S(2)}) async-start(bf16[32,4,512]{2,1,0:T(4,128)(2,1)} %attend.1), calls=%async_computation | async-start | bytes 262144 | tf_op jit(solution)/shard_map/heads/all_to_all | solution.py:303
  25.9 2.5 %collective-permute-start = (bf16[64,7168]{1,0:T(8,128)(2,1)S(1)}, bf16[64,7168]{1,0:T(8,128)(2,1)S(1)}, u32[]{:S(2)}, u32[]{:S(2)}) collective-permute-start(bf16[64,7168]{1,0:T(8,128)(2,1)S(1)} %get-tuple-element.16), channel_id=1, source_target_pairs={{0,1},{1,0},{2,3},{3,2},{4,5},{5,4},{6,7},{7,6},{8,9},{9,8},{10,11... | collective-permute-start | bytes 2752520 | tf_op jit(solution)/shard_map/heads/ppermute | solution.py:32
  28.7 9.4 %collective-permute-start.1 = (bf16[16,7168]{1,0:T(8,128)(2,1)S(1)}, bf16[16,7168]{1,0:T(8,128)(2,1)S(1)}, u32[]{:S(2)}, u32[]{:S(2)}) collective-permute-start(bf16[16,7168]{1,0:T(8,128)(2,1)S(1)} %get-tuple-element.38), channel_id=1, source_target_pairs={{0,18},{1,19},{2,16},{3,17},{4,22},{5,23},{6,20},{7,21},{8,26},{9,... | collective-permute-start | bytes 688136 | tf_op jit(solution)/shard_map/heads/ppermute | solution.py:32
  29.3 12.4 %collective-permute-start.3 = (bf16[16,7168]{1,0:T(8,128)(2,1)S(1)}, bf16[16,7168]{1,0:T(8,128)(2,1)S(1)}, u32[]{:S(2)}, u32[]{:S(2)}) collective-permute-start(bf16[16,7168]{1,0:T(8,128)(2,1)S(1)} %get-tuple-element.39), channel_id=1, source_target_pairs={{0,2},{1,3},{2,0},{3,1},{4,6},{5,7},{6,4},{7,5},{8,10},{9,11},{10,... | collective-permute-start | bytes 688136 | tf_op jit(solution)/shard_map/heads/ppermute | solution.py:32
  31.0 10.7 %collective-permute-start.2 = (bf16[16,7168]{1,0:T(8,128)(2,1)S(1)}, bf16[16,7168]{1,0:T(8,128)(2,1)S(1)}, u32[]{:S(2)}, u32[]{:S(2)}) collective-permute-start(bf16[16,7168]{1,0:T(8,128)(2,1)S(1)} %get-tuple-element.40), channel_id=1, source_target_pairs={{0,16},{1,17},{2,18},{3,19},{4,20},{5,21},{6,22},{7,23},{8,24},{9,... | collective-permute-start | bytes 688136 | tf_op jit(solution)/shard_map/heads/ppermute | solution.py:32
  41.9 6.6 %collective-permute-start.6 = (bf16[4,7168]{1,0:T(4,128)(2,1)S(1)}, bf16[4,7168]{1,0:T(4,128)(2,1)S(1)}, u32[]{:S(2)}, u32[]{:S(2)}) collective-permute-start(bf16[4,7168]{1,0:T(4,128)(2,1)S(1)} %get-tuple-element.44), channel_id=1, source_target_pairs={{0,12},{1,13},{2,14},{3,15},{4,8},{5,9},{6,10},{7,11},{8,4},{9,5},... | collective-permute-start | bytes 172040 | tf_op jit(solution)/shard_map/heads/ppermute | solution.py:32
  43.4 6.5 %collective-permute-start.5 = (bf16[4,7168]{1,0:T(4,128)(2,1)S(1)}, bf16[4,7168]{1,0:T(4,128)(2,1)S(1)}, u32[]{:S(2)}, u32[]{:S(2)}) collective-permute-start(bf16[4,7168]{1,0:T(4,128)(2,1)S(1)} %get-tuple-element.45), channel_id=1, source_target_pairs={{0,8},{1,9},{2,10},{3,11},{4,12},{5,13},{6,14},{7,15},{8,0},{9,1},... | collective-permute-start | bytes 172040 | tf_op jit(solution)/shard_map/heads/ppermute | solution.py:32
  44.0 5.8 %collective-permute-start.4 = (bf16[4,7168]{1,0:T(4,128)(2,1)S(1)}, bf16[4,7168]{1,0:T(4,128)(2,1)S(1)}, u32[]{:S(2)}, u32[]{:S(2)}) collective-permute-start(bf16[4,7168]{1,0:T(4,128)(2,1)S(1)} %get-tuple-element.46), channel_id=1, source_target_pairs={{0,4},{1,5},{2,6},{3,7},{4,0},{5,1},{6,2},{7,3},{8,12},{9,13},{10,... | collective-permute-start | bytes 172040 | tf_op jit(solution)/shard_map/heads/ppermute | solution.py:32
  50.1 6.7 %collective-permute-start.9 = (bf16[4,7296]{1,0:T(4,128)(2,1)S(1)}, bf16[4,7296]{1,0:T(4,128)(2,1)S(1)}, u32[]{:S(2)}, u32[]{:S(2)}) collective-permute-start(bf16[4,7296]{1,0:T(4,128)(2,1)S(1)} %get-tuple-element.18), channel_id=1, source_target_pairs={{0,12},{1,13},{2,14},{3,15},{4,8},{5,9},{6,10},{7,11},{8,4},{9,5},... | collective-permute-start | bytes 175112 | tf_op jit(solution)/shard_map/spread/ppermute | solution.py:32
  51.5 6.6 %collective-permute-start.8 = (bf16[4,7296]{1,0:T(4,128)(2,1)S(1)}, bf16[4,7296]{1,0:T(4,128)(2,1)S(1)}, u32[]{:S(2)}, u32[]{:S(2)}) collective-permute-start(bf16[4,7296]{1,0:T(4,128)(2,1)S(1)} %get-tuple-element.18), channel_id=1, source_target_pairs={{0,8},{1,9},{2,10},{3,11},{4,12},{5,13},{6,14},{7,15},{8,0},{9,1},... | collective-permute-start | bytes 175112 | tf_op jit(solution)/shard_map/spread/ppermute | solution.py:32
  52.3 5.9 %collective-permute-start.7 = (bf16[4,7296]{1,0:T(4,128)(2,1)S(1)}, bf16[4,7296]{1,0:T(4,128)(2,1)S(1)}, u32[]{:S(2)}, u32[]{:S(2)}) collective-permute-start(bf16[4,7296]{1,0:T(4,128)(2,1)S(1)} %get-tuple-element.18), channel_id=1, source_target_pairs={{0,4},{1,5},{2,6},{3,7},{4,0},{5,1},{6,2},{7,3},{8,12},{9,13},{10,... | collective-permute-start | bytes 175112 | tf_op jit(solution)/shard_map/spread/ppermute | solution.py:32
  58.3 11.4 %collective-permute-start.12 = (bf16[16,7296]{1,0:T(8,128)(2,1)S(1)}, bf16[16,7296]{1,0:T(8,128)(2,1)S(1)}, u32[]{:S(2)}, u32[]{:S(2)}) collective-permute-start(bf16[16,7296]{1,0:T(8,128)(2,1)S(1)} %pad_maximum_fusion.refs_0_), channel_id=1, source_target_pairs={{0,18},{1,19},{2,16},{3,17},{4,22},{5,23},{6,20},{7,21},{8,26},{9,... | collective-permute-start | bytes 700424 | tf_op jit(solution)/shard_map/spread/ppermute | solution.py:32
  60.0 11.9 %collective-permute-start.11 = (bf16[16,7296]{1,0:T(8,128)(2,1)S(1)}, bf16[16,7296]{1,0:T(8,128)(2,1)S(1)}, u32[]{:S(2)}, u32[]{:S(2)}) collective-permute-start(bf16[16,7296]{1,0:T(8,128)(2,1)S(1)} %pad_maximum_fusion.refs_0_), channel_id=1, source_target_pairs={{0,16},{1,17},{2,18},{3,19},{4,20},{5,21},{6,22},{7,23},{8,24},{9,... | collective-permute-start | bytes 700424 | tf_op jit(solution)/shard_map/spread/ppermute | solution.py:32
  61.2 10.6 %collective-permute-start.10 = (bf16[16,7296]{1,0:T(8,128)(2,1)S(1)}, bf16[16,7296]{1,0:T(8,128)(2,1)S(1)}, u32[]{:S(2)}, u32[]{:S(2)}) collective-permute-start(bf16[16,7296]{1,0:T(8,128)(2,1)S(1)} %pad_maximum_fusion.refs_0_), channel_id=1, source_target_pairs={{0,2},{1,3},{2,0},{3,1},{4,6},{5,7},{6,4},{7,5},{8,10},{9,11},{10,... | collective-permute-start | bytes 700424 | tf_op jit(solution)/shard_map/spread/ppermute | solution.py:32
  69.6 2.8 %collective-permute-start.13 = (bf16[16,7296]{1,0:T(8,128)(2,1)S(1)}, bf16[16,7296]{1,0:T(8,128)(2,1)S(1)}, u32[]{:S(2)}, u32[]{:S(2)}) collective-permute-start(bf16[16,7296]{1,0:T(8,128)(2,1)S(1)} %get-tuple-element.19), channel_id=1, source_target_pairs={{0,1},{1,0},{2,3},{3,2},{4,5},{5,4},{6,7},{7,6},{8,9},{9,8},{10,11... | collective-permute-start | bytes 700424 | tf_op jit(solution)/shard_map/spread/ppermute | solution.py:32
  69.7 2.7 %collective-permute-start.16 = (bf16[16,7296]{1,0:T(8,128)(2,1)S(1)}, bf16[16,7296]{1,0:T(8,128)(2,1)S(1)}, u32[]{:S(2)}, u32[]{:S(2)}) collective-permute-start(bf16[16,7296]{1,0:T(8,128)(2,1)S(1)} %collective-permute-done.12.refs_3_), channel_id=1, source_target_pairs={{0,1},{1,0},{2,3},{3,2},{4,5},{5,4},{6,7},{7,6},{8,9},{9,8},{10,11... | collective-permute-start | bytes 700424 | tf_op jit(solution)/shard_map/spread/ppermute | solution.py:32
  71.9 1.8 %collective-permute-start.14 = (bf16[16,7296]{1,0:T(8,128)(2,1)S(1)}, bf16[16,7296]{1,0:T(8,128)(2,1)S(1)}, u32[]{:S(2)}, u32[]{:S(2)}) collective-permute-start(bf16[16,7296]{1,0:T(8,128)(2,1)S(1)} %collective-permute-done.10.refs_1_), channel_id=1, source_target_pairs={{0,1},{1,0},{2,3},{3,2},{4,5},{5,4},{6,7},{7,6},{8,9},{9,8},{10,11... | collective-permute-start | bytes 700424 | tf_op jit(solution)/shard_map/spread/ppermute | solution.py:32
  77.3 2.5 %collective-permute-start.17 = (bf16[64,7168]{1,0:T(8,128)(2,1)S(1)}, bf16[64,7168]{1,0:T(8,128)(2,1)S(1)}, u32[]{:S(2)}, u32[]{:S(2)}) collective-permute-start(bf16[64,7168]{1,0:T(8,128)(2,1)S(1)} %get-tuple-element.24), channel_id=1, source_target_pairs={{0,1},{1,0},{2,3},{3,2},{4,5},{5,4},{6,7},{7,6},{8,9},{9,8},{10,11... | collective-permute-start | bytes 2752520 | tf_op jit(solution)/shard_map/collect/ppermute | solution.py:32
  80.1 9.5 %collective-permute-start.18 = (bf16[16,7168]{1,0:T(8,128)(2,1)S(1)}, bf16[16,7168]{1,0:T(8,128)(2,1)S(1)}, u32[]{:S(2)}, u32[]{:S(2)}) collective-permute-start(bf16[16,7168]{1,0:T(8,128)(2,1)S(1)} %get-tuple-element.35), channel_id=1, source_target_pairs={{0,18},{1,19},{2,16},{3,17},{4,22},{5,23},{6,20},{7,21},{8,26},{9,... | collective-permute-start | bytes 688136 | tf_op jit(solution)/shard_map/collect/ppermute | solution.py:32
  81.7 12.0 %collective-permute-start.20 = (bf16[16,7168]{1,0:T(8,128)(2,1)S(1)}, bf16[16,7168]{1,0:T(8,128)(2,1)S(1)}, u32[]{:S(2)}, u32[]{:S(2)}) collective-permute-start(bf16[16,7168]{1,0:T(8,128)(2,1)S(1)} %get-tuple-element.36), channel_id=1, source_target_pairs={{0,2},{1,3},{2,0},{3,1},{4,6},{5,7},{6,4},{7,5},{8,10},{9,11},{10,... | collective-permute-start | bytes 688136 | tf_op jit(solution)/shard_map/collect/ppermute | solution.py:32
  82.8 10.9 %collective-permute-start.19 = (bf16[16,7168]{1,0:T(8,128)(2,1)S(1)}, bf16[16,7168]{1,0:T(8,128)(2,1)S(1)}, u32[]{:S(2)}, u32[]{:S(2)}) collective-permute-start(bf16[16,7168]{1,0:T(8,128)(2,1)S(1)} %get-tuple-element.37), channel_id=1, source_target_pairs={{0,16},{1,17},{2,18},{3,19},{4,20},{5,21},{6,22},{7,23},{8,24},{9,... | collective-permute-start | bytes 688136 | tf_op jit(solution)/shard_map/collect/ppermute | solution.py:32
  93.9 4.2 %collective-permute-start.21 = (bf16[4,7168]{1,0:T(4,128)(2,1)S(1)}, bf16[4,7168]{1,0:T(4,128)(2,1)S(1)}, u32[]{:S(2)}, u32[]{:S(2)}) collective-permute-start(bf16[4,7168]{1,0:T(4,128)(2,1)S(1)} %get-tuple-element.41), channel_id=1, source_target_pairs={{0,4},{1,5},{2,6},{3,7},{4,0},{5,1},{6,2},{7,3},{8,12},{9,13},{10,... | collective-permute-start | bytes 172040 | tf_op jit(solution)/shard_map/collect/ppermute | solution.py:32
  94.0 6.4 %collective-permute-start.23 = (bf16[4,7168]{1,0:T(4,128)(2,1)S(1)}, bf16[4,7168]{1,0:T(4,128)(2,1)S(1)}, u32[]{:S(2)}, u32[]{:S(2)}) collective-permute-start(bf16[4,7168]{1,0:T(4,128)(2,1)S(1)} %get-tuple-element.42), channel_id=1, source_target_pairs={{0,12},{1,13},{2,14},{3,15},{4,8},{5,9},{6,10},{7,11},{8,4},{9,5},... | collective-permute-start | bytes 172040 | tf_op jit(solution)/shard_map/collect/ppermute | solution.py:32
  95.6 7.2 %collective-permute-start.22 = (bf16[4,7168]{1,0:T(4,128)(2,1)S(1)}, bf16[4,7168]{1,0:T(4,128)(2,1)S(1)}, u32[]{:S(2)}, u32[]{:S(2)}) collective-permute-start(bf16[4,7168]{1,0:T(4,128)(2,1)S(1)} %get-tuple-element.43), channel_id=1, source_target_pairs={{0,8},{1,9},{2,10},{3,11},{4,12},{5,13},{6,14},{7,15},{8,0},{9,1},... | collective-permute-start | bytes 172040 | tf_op jit(solution)/shard_map/collect/ppermute | solution.py:32
  (7 other events, 82.9 us)

commit v8 on v4

--- a/solution.py
+++ b/solution.py
@@ -14,6 +14,7 @@
 STEPS = 4
 TOPK = 8
 BLK = 2048
+LATE = 2
 SPAN = 8
 AXES = ("sec", "ep")
 NT = (((1,), (1,)), ((), ()))
@@ -145,36 +146,81 @@
     )(length, q, new, keys)
 
 
-def partner_order(n, me, rows):
+def split_rows(n, r, planes_first):
     planes = n // SPAN
-    r = iota2((rows, rows), 0)
-    c, q = r // (rows // 2), (r // (planes * STEPS)) % 4
-    k, step = (r // STEPS) % planes, r % STEPS
-    return me ^ ((q >> 1) * (n // 2) + k * 4 + (q & 1) * 2 + c), step
-
-
-def heads_kernel(n, me_ref, latents_ref, uv_ref, out_ref, near_ref, far_ref):
+    c = r // (n * STEPS // 2)
+    if planes_first:
+        return c, (r // STEPS) % 4, (r // (4 * STEPS)) % planes, r % STEPS
+    return c, (r // (planes * STEPS)) % 4, (r // STEPS) % planes, r % STEPS
+
+
+def partner_order(n, me, rows, planes_first):
+    c, q, k, step = split_rows(n, iota2((rows, rows), 0), planes_first)
+    device = me ^ ((q >> 1) * (n // 2) + k * 4 + (q & 1) * 2 + c)
+    return one_hot(device * STEPS + step, rows)
+
+
+def store_block(out, p, near_ref, far_ref):
+    rows, part = out.shape
+    here = slice(p * part, (p + 1) * part)
+    near_ref[:, here] = out[: rows // 2]
+    far_ref[:, here] = out[rows // 2 :].astype(BF)
+
+
+def halves(n, width):
+    return [jax.ShapeDtypeStruct((n * STEPS // 2, width), dtype) for dtype in (F32, BF)]
+
+
+def late_from(width):
+    return width - width // SPAN * LATE
+
+
+def core_kernel(n, near_ref, got_ref, *refs):
+    early = late_from(near_ref.shape[1])
+    total = near_ref[...] + got_ref[...].astype(F32)
+    for here, parts in ((slice(0, early), refs[:4]), (slice(early, None), refs[4:])):
+        rows = total.shape[0] // len(parts)
+        for i, ref in enumerate(parts):
+            ref[...] = total[i * rows : (i + 1) * rows, here].astype(ref.dtype)
+
+
+def second_kernel(n, *refs):
+    planes = n // SPAN
+    terms, late_terms, refs = refs[:4], refs[4 : 4 + planes], refs[4 + planes :]
+    for terms, parts in ((terms, refs[:planes]), (late_terms, refs[planes:])):
+        total = terms[0][...]
+        for ref in terms[1:]:
+            total += ref[...].astype(F32)
+        for i, ref in enumerate(parts):
+            ref[...] = total[i * STEPS : (i + 1) * STEPS].astype(ref.dtype)
+
+
+def heads_kernel(n, me_ref, latents_ref, uv_ref, out_ref, *refs):
     rows = n * STEPS
     values = jnp.dot(latents_ref[...], uv_ref[...], preferred_element_type=F32).astype(BF)
-    device, step = partner_order(n, me_ref[0], rows)
-    values = pick(one_hot(device * STEPS + step, rows), values).astype(BF)
+    moved = [pick(partner_order(n, me_ref[0], rows, f), values).astype(BF) for f in (False, True)]
     part = out_ref.shape[1] // SPAN
     for p in range(SPAN):
-        here = slice(p * part, (p + 1) * part)
-        out = jnp.dot(values, out_ref[:, here], preferred_element_type=F32)
-        near_ref[:, here] = out[: rows // 2]
-        far_ref[:, here] = out[rows // 2 :].astype(BF)
+        weights = out_ref[:, p * part : (p + 1) * part]
+        values = moved[p >= SPAN - LATE]
+        store_block(jnp.dot(values, weights, preferred_element_type=F32), p, *refs)
 
 
 def norm_kernel(n, *refs):
-    parts, (residual_ref, gain_ref, routes_ref, hidden_ref, out_ref) = refs[:-5], refs[-5:]
-    hidden = residual_ref[...].astype(F32)
-    for ref in parts:
-        hidden += ref[...].astype(F32)
-    hidden_ref[...] = hidden
-    width = hidden.shape[1]
-    mean_square = jnp.sum(hidden * hidden, axis=1, keepdims=True) / width
-    normed = hidden * lax.rsqrt(mean_square + 1e-06) * gain_ref[...].astype(F32)
+    planes = n // SPAN
+    parts, late_parts, refs = refs[:planes], refs[planes : planes + 4], refs[planes + 4 :]
+    residual_ref, gain_ref, routes_ref, hidden_ref, out_ref = refs
+    width = residual_ref.shape[1]
+    early = parts[0].shape[1]
+    square = 0.0
+    for here, terms in ((slice(0, early), parts), (slice(early, width), late_parts)):
+        hidden = residual_ref[:, here].astype(F32)
+        for ref in terms:
+            hidden += ref[...].astype(F32)
+        hidden_ref[:, here] = hidden
+        square += jnp.sum(hidden * hidden, axis=1, keepdims=True)
+    factor = lax.rsqrt(square / width + 1e-06)
+    normed = hidden_ref[...] * factor * gain_ref[...].astype(F32)
     out_ref[:, :width] = normed.astype(BF)
     out_ref[:, width:] = routes_ref[...]
 
@@ -202,7 +248,7 @@
         out_specs=[pl.BlockSpec(memory_space=pltpu.VMEM)] * 4,
         out_shape=[jax.ShapeDtypeStruct(a.shape, a.dtype) for a in [passed] + arrays],
         scratch_shapes=[pltpu.SemaphoreType.DMA((13,))],
-        compiler_params=pltpu.CompilerParams(vmem_limit_bytes=36 * 1024 * 1024),
+        compiler_params=pltpu.CompilerParams(vmem_limit_bytes=28 * 1024 * 1024),
         cost_estimate=pl.CostEstimate(
             flops=0, bytes_accessed=sum(4 * a.size for a in arrays), transcendentals=0
         ),
@@ -210,8 +256,14 @@
     )(passed, *arrays)
 
 
+def share_of(routes, expert):
+    scores = routes[:, TOPK : 2 * TOPK] + routes[:, 2 * TOPK : 3 * TOPK]
+    chosen = jnp.where(routes[:, :TOPK] == expert.astype(F32), scores, 0.0)
+    return jnp.sum(chosen, axis=1, keepdims=True) / jnp.sum(scores, axis=1, keepdims=True) * 2.5
+
+
 def expert_kernel(n, me_ref, *refs, n_ep):
-    blocks, (gate_ref, up_ref, down_ref, near_ref, far_ref) = refs[:8], refs[8:]
+    blocks, (gate_ref, up_ref, down_ref), refs = refs[:8], refs[8:11], refs[11:]
     rows = n * STEPS
     width, units = gate_ref.shape
     part = width // SPAN
@@ -224,14 +276,16 @@
         up += jnp.dot(x, up_ref[here], preferred_element_type=F32)
     act = (gate * jax.nn.sigmoid(gate) * up).astype(BF)
     routes = jnp.concatenate([ref[:, width:] for ref in blocks], axis=0).astype(F32)
-    scores = routes[:, TOPK : 2 * TOPK] + routes[:, 2 * TOPK : 3 * TOPK]
-    chosen = jnp.where(routes[:, :TOPK] == (me_ref[0] % n_ep).astype(F32), scores, 0.0)
-    coef = jnp.sum(chosen, axis=1, keepdims=True) / jnp.sum(scores, axis=1, keepdims=True) * 2.5
+    c, q, k, step = split_rows(n, iota2((rows, rows), 0), True)
+    late_order = one_hot(((c * 4 + q) * (n // SPAN) + k) * STEPS + step, rows)
+    acts = [act, pick(late_order, act).astype(BF)]
+    late_routes = pick(late_order, routes.astype(BF))
+    coefs = [share_of(r, me_ref[0] % n_ep) for r in (routes, late_routes)]
     for p in range(SPAN):
-        here = slice(p * part, (p + 1) * part)
-        out = jnp.dot(act, down_ref[:, here], preferred_element_type=F32) * coef
-        near_ref[:, here] = out[: rows // 2]
-        far_ref[:, here] = out[rows // 2 :].astype(BF)
+        late = p >= SPAN - LATE
+        down = down_ref[:, p * part : (p + 1) * part]
+        out = jnp.dot(acts[late], down, preferred_element_type=F32) * coefs[late]
+        store_block(out, p, *refs)
 
 
 def single(kernel, n, out_shape, scalars, arrays, name, flops):
@@ -248,15 +302,27 @@
     )(*scalars, *arrays)
 
 
+def kept_and_sent(count, rows, width):
+    return [jax.ShapeDtypeStruct((rows, width), BF if i else F32) for i in range(count)]
+
+
 def reduce_rows(near, far, n):
     planes = n // SPAN
     width = near.shape[1]
-    total = (near + swap(far, n, c=1).astype(F32)).reshape(4, planes * STEPS, width)
-    kept = total[0]
-    for q in range(1, 4):
-        kept = kept + swap(total[q].astype(BF), n, q=q).astype(F32)
-    kept = kept.reshape(planes, STEPS, width)
-    return [kept[0]] + [swap(kept[k].astype(BF), n, k=k) for k in range(1, planes)]
+    early = late_from(width)
+    late = width - early
+    shapes = kept_and_sent(4, planes * STEPS, early) + kept_and_sent(planes, 4 * STEPS, late)
+    parts = single(core_kernel, n, shapes, [], [near, swap(far, n, c=1)], "core_sum", near.size)
+    chips, lines = parts[:4], parts[4:]
+    chips = [chips[0]] + [swap(chips[q], n, q=q) for q in range(1, 4)]
+    lines = [lines[0]] + [swap(lines[k], n, k=k) for k in range(1, planes)]
+    shapes = kept_and_sent(planes, STEPS, early) + kept_and_sent(4, STEPS, late)
+    parts = single(second_kernel, n, shapes, [], chips + lines, "second_sum", near.size)
+    lines, chips = parts[:planes], parts[planes:]
+    return (
+        [lines[0]] + [swap(lines[k], n, k=k) for k in range(1, planes)],
+        [chips[0]] + [swap(chips[q], n, q=q) for q in range(1, 4)],
+    )
 
 
 def per_device(
@@ -293,16 +359,16 @@
 
     with jax.named_scope("heads"):
         latents = lax.all_to_all(latents, AXES, 0, 0, tiled=True)
-        near, far = single(
+        out = single(
             heads_kernel,
             n,
-            [jax.ShapeDtypeStruct((rows // 2, width), dtype) for dtype in (F32, BF)],
+            halves(n, width),
             [me_one],
             [latents.reshape(rows, LAT), w_uv[0], w_out[0]],
             "heads",
             2 * rows * VDIM * (LAT + width),
         )
-        parts = reduce_rows(near, far, n)
+        parts, late_parts = reduce_rows(*out, n)
 
     with jax.named_scope("norm"):
         high = route_scores[0].astype(BF)
@@ -317,7 +383,7 @@
                 jax.ShapeDtypeStruct((STEPS, width + 128), BF),
             ],
             [],
-            parts + [residual[0], norm_gain.reshape(1, width), routes],
+            parts + late_parts + [residual[0], norm_gain.reshape(1, width), routes],
             "norm",
             8 * STEPS * width,
         )
@@ -329,10 +395,10 @@
         blocks = blocks + [swap(x, n, c=1) for x in [along] + blocks[1:]]
 
     with jax.named_scope("experts"):
-        near, far = single(
+        out = single(
             functools.partial(expert_kernel, n_ep=n_ep),
             n,
-            [jax.ShapeDtypeStruct((rows // 2, width), dtype) for dtype in (F32, BF)],
+            halves(n, width),
             [me_one],
             blocks + weights,
             "experts",
@@ -340,10 +406,16 @@
         )
 
     with jax.named_scope("collect"):
-        result = hidden
-        for term in reduce_rows(near, far, n):
-            result = result + term.astype(F32)
-        return result.astype(BF)[None]
+        results = []
+        first = 0
+        for terms in reduce_rows(*out, n):
+            last = first + terms[0].shape[1]
+            result = hidden[:, first:last]
+            for term in terms:
+                result = result + term.astype(F32)
+            results.append(result.astype(BF))
+            first = last
+        return jnp.concatenate(results, axis=1)[None]
 
 
 def solution(mesh):

time: 108 us -> 110 us (1.019)
  starting transfers between devices: 35.7 us -> 49.1 us
  waiting for transfers between devices: 46.1 us -> 37.5 us
  local copies, waits for them, and re-layouts: 3.41 us -> 0.08 us
    ppermute x24 -> x36, starting transfers between devices: 24.7 us -> 41.8 us  [swap(): return lax.ppermute(x, AXES, [(d, d ^ mask) for d in range(n)])]
    ppermute x24 -> x36, waiting for transfers between devices: 37.9 us -> 29.3 us  [swap(): return lax.ppermute(x, AXES, [(d, d ^ mask) for d in range(n)])]
    all_to_all x1, starting transfers between devices: 11 us -> 7.36 us  [per_device(): latents = lax.all_to_all(latents, AXES, 0, 0, tiled=True)]
    unnamed x14 -> x12, local copies, waits for them, and re-layouts: 3.11 us -> 0.02 us
    pallas_call x1, Pallas kernels: 4.57 us -> 7.56 us  [attend(): pl.pallas_call(functools.partial(attend_kernel, n), in_specs=[pl.BlockSpe...]
    pallas_call x1, Pallas kernels: 10.6 us -> 7.71 us  [load(): pl.pallas_call(functools.partial(load_kernel, n), in_specs=[pl.BlockSpec(...]
    pallas_call x3 -> x7, Pallas kernels: 4.74 us -> 5.34 us  [single(): pl.pallas_call(functools.partial(kernel, n), in_specs=[pl.BlockSpec(memor...]
  transfers between devices with their start and end apart: 25 -> 37, of which waited for: 18 -> 20; matrix products, arithmetic and copies ran while one was open for 0% -> 0% of each run, Pallas kernels for 10% -> 7%
where the time goes in v8:
time: 110 us; the launch traced here: 109 us
  starting transfers between devices  49.1 us (45%)
  waiting for transfers between devices  37.5 us (34%)
  Pallas kernels  20.6 us (19%)
    ppermute x36, starting transfers between devices, swap(): return lax.ppermute(x, AXES, [(d, d ^ mask) for d in range(n)])  41.8 us
    ppermute x36, waiting for transfers between devices, swap(): return lax.ppermute(x, AXES, [(d, d ^ mask) for d in range(n)])  29.3 us
    all_to_all x1, waiting for transfers between devices, per_device(): latents = lax.all_to_all(latents, AXES, 0, 0, tiled=True)  8.22 us
    pallas_call x1, Pallas kernels, load(): pl.pallas_call(functools.partial(load_kernel, n), in_specs=[pl.BlockSpec(...  7.71 us
    pallas_call x1, Pallas kernels, attend(): pl.pallas_call(functools.partial(attend_kernel, n), in_specs=[pl.BlockSpe...  7.56 us
    all_to_all x1, starting transfers between devices, per_device(): latents = lax.all_to_all(latents, AXES, 0, 0, tiled=True)  7.36 us
    pallas_call x7, Pallas kernels, single(): pl.pallas_call(functools.partial(kernel, n), in_specs=[pl.BlockSpec(memor...  5.34 us
  transfers between devices with their start and end apart: 37, of which 20 were waited for; matrix products, arithmetic and copies ran while one was open for 0% of the time, Pallas kernels for 7%

profile of v8, /device:TPU:0, one launch (start us, length us, event | category | flops | bytes accessed | tf_op | source)
XLA Modules:
  0.0 109.3 jit_solution(7665499183809552195)
XLA Ops:
  0.8 7.6 %attend.1 = bf16[32,4,512]{2,1,0:T(4,128)(2,1)} custom-call(s32[1]{0:T(128)S(6)} %copy.14.len_ref, bf16[128,576]{1,0:T(8,128)(2,1)} %bitcast.29, bf16[4,576]{1,0:T(4,128)(2,1)} %bitcast.30, bf16[576,8192]{1,0:T(8,128)(2,1)} %bitcast.25), custom_call_target="tpu_custom_call" | custom-call | flops 2281701376 | bytes 9437184 | tf_op jit(solution)/shard_map/attention/attend/pallas_call | solution.py:123
  8.4 7.4 %all-to-all-start = ((bf16[32,4,512]{2,1,0:T(4,128)(2,1)}), bf16[32,4,512]{2,1,0:T(4,128)(2,1)S(1)}, u32[]{:S(2)}, u32[]{:S(2)}) async-start(bf16[32,4,512]{2,1,0:T(4,128)(2,1)} %attend.1), calls=%async_computation | async-start | bytes 262144 | tf_op jit(solution)/shard_map/heads/all_to_all | solution.py:361
  15.8 8.2 %all-to-all-done = bf16[32,4,512]{2,1,0:T(4,128)(2,1)S(1)} async-done(((bf16[32,4,512]{2,1,0:T(4,128)(2,1)}), bf16[32,4,512]{2,1,0:T(4,128)(2,1)S(1)}, u32[]{:S(2)}, u32[]{:S(2)}) %all-to-all-start) | async-done | bytes 131104 | tf_op jit(solution)/shard_map/heads/all_to_all | solution.py:361
  25.3 2.2 %collective-permute-done.got_ref = bf16[64,7168]{1,0:T(8,128)(2,1)S(1)} collective-permute-done((bf16[64,7168]{1,0:T(8,128)(2,1)S(1)}, bf16[64,7168]{1,0:T(8,128)(2,1)S(1)}, u32[]{:S(2)}, u32[]{:S(2)}) %collective-permute-start) | collective-permute-done | bytes 917536 | tf_op jit(solution)/shard_map/heads/ppermute | solution.py:32
  27.8 1.8 %collective-permute-start.5 = (bf16[16,1792]{1,0:T(8,128)(2,1)S(1)}, bf16[16,1792]{1,0:T(8,128)(2,1)S(1)}, u32[]{:S(2)}, u32[]{:S(2)}) collective-permute-start(bf16[16,1792]{1,0:T(8,128)(2,1)S(1)} %get-tuple-element.55), channel_id=1, source_target_pairs={{0,8},{1,9},{2,10},{3,11},{4,12},{5,13},{6,14},{7,15},{8,0},{9,1},... | collective-permute-start | bytes 172040 | tf_op jit(solution)/shard_map/heads/ppermute | solution.py:32
  29.6 2.5 %collective-permute-start.6 = (bf16[16,1792]{1,0:T(8,128)(2,1)S(1)}, bf16[16,1792]{1,0:T(8,128)(2,1)S(1)}, u32[]{:S(2)}, u32[]{:S(2)}) collective-permute-start(bf16[16,1792]{1,0:T(8,128)(2,1)S(1)} %get-tuple-element.56), channel_id=1, source_target_pairs={{0,12},{1,13},{2,14},{3,15},{4,8},{5,9},{6,10},{7,11},{8,4},{9,5},... | collective-permute-start | bytes 172040 | tf_op jit(solution)/shard_map/heads/ppermute | solution.py:32
  33.2 2.4 %collective-permute-start.3 = (bf16[16,5376]{1,0:T(8,128)(2,1)S(1)}, bf16[16,5376]{1,0:T(8,128)(2,1)S(1)}, u32[]{:S(2)}, u32[]{:S(2)}) collective-permute-start(bf16[16,5376]{1,0:T(8,128)(2,1)S(1)} %get-tuple-element.52), channel_id=1, source_target_pairs={{0,18},{1,19},{2,16},{3,17},{4,22},{5,23},{6,20},{7,21},{8,26},{9,... | collective-permute-start | bytes 516104 | tf_op jit(solution)/shard_map/heads/ppermute | solution.py:32
  35.9 2.7 %collective-permute-done.1.refs_1_ = bf16[16,5376]{1,0:T(8,128)(2,1)S(1)} collective-permute-done((bf16[16,5376]{1,0:T(8,128)(2,1)S(1)}, bf16[16,5376]{1,0:T(8,128)(2,1)S(1)}, u32[]{:S(2)}, u32[]{:S(2)}) %collective-permute-start.1) | collective-permute-done | bytes 172064 | tf_op jit(solution)/shard_map/heads/ppermute | solution.py:32
  39.8 2.9 %collective-permute-done.3.refs_3_ = bf16[16,5376]{1,0:T(8,128)(2,1)S(1)} collective-permute-done((bf16[16,5376]{1,0:T(8,128)(2,1)S(1)}, bf16[16,5376]{1,0:T(8,128)(2,1)S(1)}, u32[]{:S(2)}, u32[]{:S(2)}) %collective-permute-start.3) | collective-permute-done | bytes 172064 | tf_op jit(solution)/shard_map/heads/ppermute | solution.py:32
  44.0 2.4 %collective-permute-start.12 = (bf16[4,1792]{1,0:T(4,128)(2,1)S(1)}, bf16[4,1792]{1,0:T(4,128)(2,1)S(1)}, u32[]{:S(2)}, u32[]{:S(2)}) collective-permute-start(bf16[4,1792]{1,0:T(4,128)(2,1)S(1)} %get-tuple-element.64), channel_id=1, source_target_pairs={{0,18},{1,19},{2,16},{3,17},{4,22},{5,23},{6,20},{7,21},{8,26},{9,... | collective-permute-start | bytes 43016 | tf_op jit(solution)/shard_map/heads/ppermute | solution.py:32
  48.2 2.6 %collective-permute-start.9 = (bf16[4,5376]{1,0:T(4,128)(2,1)S(1)}, bf16[4,5376]{1,0:T(4,128)(2,1)S(1)}, u32[]{:S(2)}, u32[]{:S(2)}) collective-permute-start(bf16[4,5376]{1,0:T(4,128)(2,1)S(1)} %get-tuple-element.60), channel_id=1, source_target_pairs={{0,12},{1,13},{2,14},{3,15},{4,8},{5,9},{6,10},{7,11},{8,4},{9,5},... | collective-permute-start | bytes 129032 | tf_op jit(solution)/shard_map/heads/ppermute | solution.py:32
  51.4 2.6 %collective-permute-done.9.refs_3_ = bf16[4,5376]{1,0:T(4,128)(2,1)S(1)} collective-permute-done((bf16[4,5376]{1,0:T(4,128)(2,1)S(1)}, bf16[4,5376]{1,0:T(4,128)(2,1)S(1)}, u32[]{:S(2)}, u32[]{:S(2)}) %collective-permute-start.9) | collective-permute-done | bytes 43040 | tf_op jit(solution)/shard_map/heads/ppermute | solution.py:32
  54.2 2.7 %collective-permute-start.15 = (bf16[4,7296]{1,0:T(4,128)(2,1)S(1)}, bf16[4,7296]{1,0:T(4,128)(2,1)S(1)}, u32[]{:S(2)}, u32[]{:S(2)}) collective-permute-start(bf16[4,7296]{1,0:T(4,128)(2,1)S(1)} %get-tuple-element.66), channel_id=1, source_target_pairs={{0,12},{1,13},{2,14},{3,15},{4,8},{5,9},{6,10},{7,11},{8,4},{9,5},... | collective-permute-start | bytes 175112 | tf_op jit(solution)/shard_map/spread/ppermute | solution.py:32
  65.7 7.7 %load_experts.1 = (bf16[16,7296]{1,0:T(8,128)(2,1)S(1)}, bf16[7168,512]{1,0:T(8,128)(2,1)S(1)}, bf16[7168,512]{1,0:T(8,128)(2,1)S(1)}, bf16[512,7168]{1,0:T(8,128)(2,1)S(1)}) custom-call(bf16[16,7296]{1,0:T(8,128)(2,1)S(1)} %pad_maximum_fusion.refs_0_, bf16[7168,512]{1,0:T(8,128)(2,1)} %bitcast.26, bf16[7168,512]{1,0:T(8,128)(2,1)} %bitcast.27, ...), custom_call_target="tpu_custom_call" | custom-call | bytes 44040192 | tf_op jit(solution)/shard_map/spread/load_experts/pallas_call | solution.py:245
  75.9 3.7 %experts.1 = (f32[64,7168]{1,0:T(8,128)S(1)}, bf16[64,7168]{1,0:T(8,128)(2,1)S(1)}) custom-call(s32[1]{0:T(128)} %bitcast.me_ref, bf16[16,7296]{1,0:T(8,128)(2,1)S(1)} %pad_maximum_fusion.refs_0_, bf16[16,7296]{1,0:T(8,128)(2,1)S(1)} %collective-permute-done.16.refs_1_, bf16[16,7296]{1,0:T(8,128)(2,1)S(1)} %collective-permute-done.17.refs_2_, ...), custom_call_target="tpu_custom_call" | custom-call | flops 2818572288 | bytes 23887872 | tf_op jit(solution)/shard_map/experts/experts/pallas_call | solution.py:292
  79.9 2.3 %collective-permute-done.23.got_ref = bf16[64,7168]{1,0:T(8,128)(2,1)S(1)} collective-permute-done((bf16[64,7168]{1,0:T(8,128)(2,1)S(1)}, bf16[64,7168]{1,0:T(8,128)(2,1)S(1)}, u32[]{:S(2)}, u32[]{:S(2)}) %collective-permute-start.23) | collective-permute-done | bytes 917536 | tf_op jit(solution)/shard_map/collect/ppermute | solution.py:32
  83.4 2.4 %collective-permute-start.26 = (bf16[16,5376]{1,0:T(8,128)(2,1)S(1)}, bf16[16,5376]{1,0:T(8,128)(2,1)S(1)}, u32[]{:S(2)}, u32[]{:S(2)}) collective-permute-start(bf16[16,5376]{1,0:T(8,128)(2,1)S(1)} %get-tuple-element.76), channel_id=1, source_target_pairs={{0,18},{1,19},{2,16},{3,17},{4,22},{5,23},{6,20},{7,21},{8,26},{9,... | collective-permute-start | bytes 516104 | tf_op jit(solution)/shard_map/collect/ppermute | solution.py:32
  86.7 1.8 %collective-permute-start.28 = (bf16[16,1792]{1,0:T(8,128)(2,1)S(1)}, bf16[16,1792]{1,0:T(8,128)(2,1)S(1)}, u32[]{:S(2)}, u32[]{:S(2)}) collective-permute-start(bf16[16,1792]{1,0:T(8,128)(2,1)S(1)} %get-tuple-element.79), channel_id=1, source_target_pairs={{0,8},{1,9},{2,10},{3,11},{4,12},{5,13},{6,14},{7,15},{8,0},{9,1},... | collective-permute-start | bytes 172040 | tf_op jit(solution)/shard_map/collect/ppermute | solution.py:32
  88.6 1.9 %collective-permute-done.27.refs_5_ = bf16[16,1792]{1,0:T(8,128)(2,1)S(1)} collective-permute-done((bf16[16,1792]{1,0:T(8,128)(2,1)S(1)}, bf16[16,1792]{1,0:T(8,128)(2,1)S(1)}, u32[]{:S(2)}, u32[]{:S(2)}) %collective-permute-start.27) | collective-permute-done | bytes 57376 | tf_op jit(solution)/shard_map/collect/ppermute | solution.py:32
  90.5 2.0 %collective-permute-start.29 = (bf16[16,1792]{1,0:T(8,128)(2,1)S(1)}, bf16[16,1792]{1,0:T(8,128)(2,1)S(1)}, u32[]{:S(2)}, u32[]{:S(2)}) collective-permute-start(bf16[16,1792]{1,0:T(8,128)(2,1)S(1)} %get-tuple-element.80), channel_id=1, source_target_pairs={{0,12},{1,13},{2,14},{3,15},{4,8},{5,9},{6,10},{7,11},{8,4},{9,5},... | collective-permute-start | bytes 172040 | tf_op jit(solution)/shard_map/collect/ppermute | solution.py:32
  92.8 3.7 %collective-permute-done.29.refs_7_ = bf16[16,1792]{1,0:T(8,128)(2,1)S(1)} collective-permute-done((bf16[16,1792]{1,0:T(8,128)(2,1)S(1)}, bf16[16,1792]{1,0:T(8,128)(2,1)S(1)}, u32[]{:S(2)}, u32[]{:S(2)}) %collective-permute-start.29) | collective-permute-done | bytes 57376 | tf_op jit(solution)/shard_map/collect/ppermute | solution.py:32
  97.7 2.5 %collective-permute-start.35 = (bf16[4,1792]{1,0:T(4,128)(2,1)S(1)}, bf16[4,1792]{1,0:T(4,128)(2,1)S(1)}, u32[]{:S(2)}, u32[]{:S(2)}) collective-permute-start(bf16[4,1792]{1,0:T(4,128)(2,1)S(1)} %get-tuple-element.88), channel_id=1, source_target_pairs={{0,18},{1,19},{2,16},{3,17},{4,22},{5,23},{6,20},{7,21},{8,26},{9,... | collective-permute-start | bytes 43016 | tf_op jit(solution)/shard_map/collect/ppermute | solution.py:32
  100.2 2.6 %collective-permute-start.31 = (bf16[4,5376]{1,0:T(4,128)(2,1)S(1)}, bf16[4,5376]{1,0:T(4,128)(2,1)S(1)}, u32[]{:S(2)}, u32[]{:S(2)}) collective-permute-start(bf16[4,5376]{1,0:T(4,128)(2,1)S(1)} %get-tuple-element.83), channel_id=1, source_target_pairs={{0,8},{1,9},{2,10},{3,11},{4,12},{5,13},{6,14},{7,15},{8,0},{9,1},... | collective-permute-start | bytes 129032 | tf_op jit(solution)/shard_map/collect/ppermute | solution.py:32
  105.1 3.5 %collective-permute-done.32 = bf16[4,5376]{1,0:T(4,128)(2,1)S(1)} collective-permute-done((bf16[4,5376]{1,0:T(4,128)(2,1)S(1)}, bf16[4,5376]{1,0:T(4,128)(2,1)S(1)}, u32[]{:S(2)}, u32[]{:S(2)}) %collective-permute-start.32) | collective-permute-done | bytes 43040 | tf_op jit(solution)/shard_map/collect/ppermute | solution.py:32
  (80 shorter events, 26.2 us)
Async XLA Ops:
  8.4 15.6 %all-to-all-start = ((bf16[32,4,512]{2,1,0:T(4,128)(2,1)}), bf16[32,4,512]{2,1,0:T(4,128)(2,1)S(1)}, u32[]{:S(2)}, u32[]{:S(2)}) async-start(bf16[32,4,512]{2,1,0:T(4,128)(2,1)} %attend.1), calls=%async_computation | async-start | bytes 262144 | tf_op jit(solution)/shard_map/heads/all_to_all | solution.py:361
  27.7 5.5 %collective-permute-start.4 = (bf16[16,1792]{1,0:T(8,128)(2,1)S(1)}, bf16[16,1792]{1,0:T(8,128)(2,1)S(1)}, u32[]{:S(2)}, u32[]{:S(2)}) collective-permute-start(bf16[16,1792]{1,0:T(8,128)(2,1)S(1)} %get-tuple-element.54), channel_id=1, source_target_pairs={{0,4},{1,5},{2,6},{3,7},{4,0},{5,1},{6,2},{7,3},{8,12},{9,13},{10,... | collective-permute-start | bytes 172040 | tf_op jit(solution)/shard_map/heads/ppermute | solution.py:32
  27.8 8.1 %collective-permute-start.5 = (bf16[16,1792]{1,0:T(8,128)(2,1)S(1)}, bf16[16,1792]{1,0:T(8,128)(2,1)S(1)}, u32[]{:S(2)}, u32[]{:S(2)}) collective-permute-start(bf16[16,1792]{1,0:T(8,128)(2,1)S(1)} %get-tuple-element.55), channel_id=1, source_target_pairs={{0,8},{1,9},{2,10},{3,11},{4,12},{5,13},{6,14},{7,15},{8,0},{9,1},... | collective-permute-start | bytes 172040 | tf_op jit(solution)/shard_map/heads/ppermute | solution.py:32
  29.6 6.2 %collective-permute-start.6 = (bf16[16,1792]{1,0:T(8,128)(2,1)S(1)}, bf16[16,1792]{1,0:T(8,128)(2,1)S(1)}, u32[]{:S(2)}, u32[]{:S(2)}) collective-permute-start(bf16[16,1792]{1,0:T(8,128)(2,1)S(1)} %get-tuple-element.56), channel_id=1, source_target_pairs={{0,12},{1,13},{2,14},{3,15},{4,8},{5,9},{6,10},{7,11},{8,4},{9,5},... | collective-permute-start | bytes 172040 | tf_op jit(solution)/shard_map/heads/ppermute | solution.py:32
  32.1 6.4 %collective-permute-start.1 = (bf16[16,5376]{1,0:T(8,128)(2,1)S(1)}, bf16[16,5376]{1,0:T(8,128)(2,1)S(1)}, u32[]{:S(2)}, u32[]{:S(2)}) collective-permute-start(bf16[16,5376]{1,0:T(8,128)(2,1)S(1)} %get-tuple-element.50), channel_id=1, source_target_pairs={{0,2},{1,3},{2,0},{3,1},{4,6},{5,7},{6,4},{7,5},{8,10},{9,11},{10,... | collective-permute-start | bytes 516104 | tf_op jit(solution)/shard_map/heads/ppermute | solution.py:32
  32.7 7.1 %collective-permute-start.2 = (bf16[16,5376]{1,0:T(8,128)(2,1)S(1)}, bf16[16,5376]{1,0:T(8,128)(2,1)S(1)}, u32[]{:S(2)}, u32[]{:S(2)}) collective-permute-start(bf16[16,5376]{1,0:T(8,128)(2,1)S(1)} %get-tuple-element.51), channel_id=1, source_target_pairs={{0,16},{1,17},{2,18},{3,19},{4,20},{5,21},{6,22},{7,23},{8,24},{9,... | collective-permute-start | bytes 516104 | tf_op jit(solution)/shard_map/heads/ppermute | solution.py:32
  33.2 9.5 %collective-permute-start.3 = (bf16[16,5376]{1,0:T(8,128)(2,1)S(1)}, bf16[16,5376]{1,0:T(8,128)(2,1)S(1)}, u32[]{:S(2)}, u32[]{:S(2)}) collective-permute-start(bf16[16,5376]{1,0:T(8,128)(2,1)S(1)} %get-tuple-element.52), channel_id=1, source_target_pairs={{0,18},{1,19},{2,16},{3,17},{4,22},{5,23},{6,20},{7,21},{8,26},{9,... | collective-permute-start | bytes 516104 | tf_op jit(solution)/shard_map/heads/ppermute | solution.py:32
  42.8 5.3 %collective-permute-start.10 = (bf16[4,1792]{1,0:T(4,128)(2,1)S(1)}, bf16[4,1792]{1,0:T(4,128)(2,1)S(1)}, u32[]{:S(2)}, u32[]{:S(2)}) collective-permute-start(bf16[4,1792]{1,0:T(4,128)(2,1)S(1)} %get-tuple-element.62), channel_id=1, source_target_pairs={{0,2},{1,3},{2,0},{3,1},{4,6},{5,7},{6,4},{7,5},{8,10},{9,11},{10,... | collective-permute-start | bytes 43016 | tf_op jit(solution)/shard_map/heads/ppermute | solution.py:32
  43.3 7.6 %collective-permute-start.11 = (bf16[4,1792]{1,0:T(4,128)(2,1)S(1)}, bf16[4,1792]{1,0:T(4,128)(2,1)S(1)}, u32[]{:S(2)}, u32[]{:S(2)}) collective-permute-start(bf16[4,1792]{1,0:T(4,128)(2,1)S(1)} %get-tuple-element.63), channel_id=1, source_target_pairs={{0,16},{1,17},{2,18},{3,19},{4,20},{5,21},{6,22},{7,23},{8,24},{9,... | collective-permute-start | bytes 43016 | tf_op jit(solution)/shard_map/heads/ppermute | solution.py:32
  44.0 6.9 %collective-permute-start.12 = (bf16[4,1792]{1,0:T(4,128)(2,1)S(1)}, bf16[4,1792]{1,0:T(4,128)(2,1)S(1)}, u32[]{:S(2)}, u32[]{:S(2)}) collective-permute-start(bf16[4,1792]{1,0:T(4,128)(2,1)S(1)} %get-tuple-element.64), channel_id=1, source_target_pairs={{0,18},{1,19},{2,16},{3,17},{4,22},{5,23},{6,20},{7,21},{8,26},{9,... | collective-permute-start | bytes 43016 | tf_op jit(solution)/shard_map/heads/ppermute | solution.py:32
  48.2 5.8 %collective-permute-start.9 = (bf16[4,5376]{1,0:T(4,128)(2,1)S(1)}, bf16[4,5376]{1,0:T(4,128)(2,1)S(1)}, u32[]{:S(2)}, u32[]{:S(2)}) collective-permute-start(bf16[4,5376]{1,0:T(4,128)(2,1)S(1)} %get-tuple-element.60), channel_id=1, source_target_pairs={{0,12},{1,13},{2,14},{3,15},{4,8},{5,9},{6,10},{7,11},{8,4},{9,5},... | collective-permute-start | bytes 129032 | tf_op jit(solution)/shard_map/heads/ppermute | solution.py:32
  54.2 6.1 %collective-permute-start.15 = (bf16[4,7296]{1,0:T(4,128)(2,1)S(1)}, bf16[4,7296]{1,0:T(4,128)(2,1)S(1)}, u32[]{:S(2)}, u32[]{:S(2)}) collective-permute-start(bf16[4,7296]{1,0:T(4,128)(2,1)S(1)} %get-tuple-element.66), channel_id=1, source_target_pairs={{0,12},{1,13},{2,14},{3,15},{4,8},{5,9},{6,10},{7,11},{8,4},{9,5},... | collective-permute-start | bytes 175112 | tf_op jit(solution)/shard_map/spread/ppermute | solution.py:32
  62.1 11.4 %collective-permute-start.18 = (bf16[16,7296]{1,0:T(8,128)(2,1)S(1)}, bf16[16,7296]{1,0:T(8,128)(2,1)S(1)}, u32[]{:S(2)}, u32[]{:S(2)}) collective-permute-start(bf16[16,7296]{1,0:T(8,128)(2,1)S(1)} %pad_maximum_fusion.refs_0_), channel_id=1, source_target_pairs={{0,18},{1,19},{2,16},{3,17},{4,22},{5,23},{6,20},{7,21},{8,26},{9,... | collective-permute-start | bytes 700424 | tf_op jit(solution)/shard_map/spread/ppermute | solution.py:32
  62.7 11.3 %collective-permute-start.17 = (bf16[16,7296]{1,0:T(8,128)(2,1)S(1)}, bf16[16,7296]{1,0:T(8,128)(2,1)S(1)}, u32[]{:S(2)}, u32[]{:S(2)}) collective-permute-start(bf16[16,7296]{1,0:T(8,128)(2,1)S(1)} %pad_maximum_fusion.refs_0_), channel_id=1, source_target_pairs={{0,16},{1,17},{2,18},{3,19},{4,20},{5,21},{6,22},{7,23},{8,24},{9,... | collective-permute-start | bytes 700424 | tf_op jit(solution)/shard_map/spread/ppermute | solution.py:32
  64.0 10.0 %collective-permute-start.16 = (bf16[16,7296]{1,0:T(8,128)(2,1)S(1)}, bf16[16,7296]{1,0:T(8,128)(2,1)S(1)}, u32[]{:S(2)}, u32[]{:S(2)}) collective-permute-start(bf16[16,7296]{1,0:T(8,128)(2,1)S(1)} %pad_maximum_fusion.refs_0_), channel_id=1, source_target_pairs={{0,2},{1,3},{2,0},{3,1},{4,6},{5,7},{6,4},{7,5},{8,10},{9,11},{10,... | collective-permute-start | bytes 700424 | tf_op jit(solution)/shard_map/spread/ppermute | solution.py:32
  82.3 14.2 %collective-permute-start.24 = (bf16[16,5376]{1,0:T(8,128)(2,1)S(1)}, bf16[16,5376]{1,0:T(8,128)(2,1)S(1)}, u32[]{:S(2)}, u32[]{:S(2)}) collective-permute-start(bf16[16,5376]{1,0:T(8,128)(2,1)S(1)} %get-tuple-element.74), channel_id=1, source_target_pairs={{0,2},{1,3},{2,0},{3,1},{4,6},{5,7},{6,4},{7,5},{8,10},{9,11},{10,... | collective-permute-start | bytes 516104 | tf_op jit(solution)/shard_map/collect/ppermute | solution.py:32
  82.8 13.7 %collective-permute-start.25 = (bf16[16,5376]{1,0:T(8,128)(2,1)S(1)}, bf16[16,5376]{1,0:T(8,128)(2,1)S(1)}, u32[]{:S(2)}, u32[]{:S(2)}) collective-permute-start(bf16[16,5376]{1,0:T(8,128)(2,1)S(1)} %get-tuple-element.75), channel_id=1, source_target_pairs={{0,16},{1,17},{2,18},{3,19},{4,20},{5,21},{6,22},{7,23},{8,24},{9,... | collective-permute-start | bytes 516104 | tf_op jit(solution)/shard_map/collect/ppermute | solution.py:32
  83.4 13.1 %collective-permute-start.26 = (bf16[16,5376]{1,0:T(8,128)(2,1)S(1)}, bf16[16,5376]{1,0:T(8,128)(2,1)S(1)}, u32[]{:S(2)}, u32[]{:S(2)}) collective-permute-start(bf16[16,5376]{1,0:T(8,128)(2,1)S(1)} %get-tuple-element.76), channel_id=1, source_target_pairs={{0,18},{1,19},{2,16},{3,17},{4,22},{5,23},{6,20},{7,21},{8,26},{9,... | collective-permute-start | bytes 516104 | tf_op jit(solution)/shard_map/collect/ppermute | solution.py:32
  86.7 6.1 %collective-permute-start.28 = (bf16[16,1792]{1,0:T(8,128)(2,1)S(1)}, bf16[16,1792]{1,0:T(8,128)(2,1)S(1)}, u32[]{:S(2)}, u32[]{:S(2)}) collective-permute-start(bf16[16,1792]{1,0:T(8,128)(2,1)S(1)} %get-tuple-element.79), channel_id=1, source_target_pairs={{0,8},{1,9},{2,10},{3,11},{4,12},{5,13},{6,14},{7,15},{8,0},{9,1},... | collective-permute-start | bytes 172040 | tf_op jit(solution)/shard_map/collect/ppermute | solution.py:32
  90.5 6.0 %collective-permute-start.29 = (bf16[16,1792]{1,0:T(8,128)(2,1)S(1)}, bf16[16,1792]{1,0:T(8,128)(2,1)S(1)}, u32[]{:S(2)}, u32[]{:S(2)}) collective-permute-start(bf16[16,1792]{1,0:T(8,128)(2,1)S(1)} %get-tuple-element.80), channel_id=1, source_target_pairs={{0,12},{1,13},{2,14},{3,15},{4,8},{5,9},{6,10},{7,11},{8,4},{9,5},... | collective-permute-start | bytes 172040 | tf_op jit(solution)/shard_map/collect/ppermute | solution.py:32
  96.6 6.1 %collective-permute-start.33 = (bf16[4,1792]{1,0:T(4,128)(2,1)S(1)}, bf16[4,1792]{1,0:T(4,128)(2,1)S(1)}, u32[]{:S(2)}, u32[]{:S(2)}) collective-permute-start(bf16[4,1792]{1,0:T(4,128)(2,1)S(1)} %get-tuple-element.86), channel_id=1, source_target_pairs={{0,2},{1,3},{2,0},{3,1},{4,6},{5,7},{6,4},{7,5},{8,10},{9,11},{10,... | collective-permute-start | bytes 43016 | tf_op jit(solution)/shard_map/collect/ppermute | solution.py:32
  97.0 7.6 %collective-permute-start.34 = (bf16[4,1792]{1,0:T(4,128)(2,1)S(1)}, bf16[4,1792]{1,0:T(4,128)(2,1)S(1)}, u32[]{:S(2)}, u32[]{:S(2)}) collective-permute-start(bf16[4,1792]{1,0:T(4,128)(2,1)S(1)} %get-tuple-element.87), channel_id=1, source_target_pairs={{0,16},{1,17},{2,18},{3,19},{4,20},{5,21},{6,22},{7,23},{8,24},{9,... | collective-permute-start | bytes 43016 | tf_op jit(solution)/shard_map/collect/ppermute | solution.py:32
  97.7 6.9 %collective-permute-start.35 = (bf16[4,1792]{1,0:T(4,128)(2,1)S(1)}, bf16[4,1792]{1,0:T(4,128)(2,1)S(1)}, u32[]{:S(2)}, u32[]{:S(2)}) collective-permute-start(bf16[4,1792]{1,0:T(4,128)(2,1)S(1)} %get-tuple-element.88), channel_id=1, source_target_pairs={{0,18},{1,19},{2,16},{3,17},{4,22},{5,23},{6,20},{7,21},{8,26},{9,... | collective-permute-start | bytes 43016 | tf_op jit(solution)/shard_map/collect/ppermute | solution.py:32
  102.8 5.8 %collective-permute-start.32 = (bf16[4,5376]{1,0:T(4,128)(2,1)S(1)}, bf16[4,5376]{1,0:T(4,128)(2,1)S(1)}, u32[]{:S(2)}, u32[]{:S(2)}) collective-permute-start(bf16[4,5376]{1,0:T(4,128)(2,1)S(1)} %get-tuple-element.84), channel_id=1, source_target_pairs={{0,12},{1,13},{2,14},{3,15},{4,8},{5,9},{6,10},{7,11},{8,4},{9,5},... | collective-permute-start | bytes 129032 | tf_op jit(solution)/shard_map/collect/ppermute | solution.py:32
  (19 other events, 274.3 us)

commit v9 on v4

--- a/solution.py
+++ b/solution.py
@@ -13,6 +13,7 @@
 VDIM = 128
 STEPS = 4
 TOPK = 8
+LOADS = 4
 BLK = 2048
 SPAN = 8
 AXES = ("sec", "ep")
@@ -22,13 +23,15 @@
 VMEM_LIMIT = 16 * 1024 * 1024
 
 
-def mask_of(n, q=0, c=0, k=0):
-    return (q >> 1) * (n // 2) + k * 4 + (q & 1) * 2 + c
-
-
-def swap(x, n, **differ):
-    mask = mask_of(n, **differ)
-    return lax.ppermute(x, AXES, [(d, d ^ mask) for d in range(n)])
+def bit_orders(n):
+    top = n.bit_length() - 2
+    rest = list(range(1, top))
+    return [top] + rest, rest[:2] + [top] + rest[2:]
+
+
+def swap(x, n, step):
+    orders = bit_orders(n)
+    return lax.ppermute(x, AXES, [(d, d ^ (1 if step < 0 else 1 << orders[d & 1][step])) for d in range(n)])
 
 
 def iota2(shape, axis):
@@ -145,19 +148,24 @@
     )(length, q, new, keys)
 
 
-def partner_order(n, me, rows):
-    planes = n // SPAN
+def source_rows(n, me, rows):
     r = iota2((rows, rows), 0)
-    c, q = r // (rows // 2), (r // (planes * STEPS)) % 4
-    k, step = (r // STEPS) % planes, r % STEPS
-    return me ^ ((q >> 1) * (n // 2) + k * 4 + (q & 1) * 2 + c), step
+    other = r // (rows // 2)
+    count = n.bit_length() - 2
+    masks = []
+    for order in bit_orders(n):
+        mask = jnp.zeros_like(r)
+        for i, bit in enumerate(order):
+            mask = mask | (((r // STEPS) >> (count - 1 - i)) & 1) << bit
+        masks.append(mask)
+    mask = jnp.where((me & 1) ^ other == 0, masks[0], masks[1])
+    return (me ^ mask ^ other) * STEPS + r % STEPS
 
 
 def heads_kernel(n, me_ref, latents_ref, uv_ref, out_ref, near_ref, far_ref):
     rows = n * STEPS
     values = jnp.dot(latents_ref[...], uv_ref[...], preferred_element_type=F32).astype(BF)
-    device, step = partner_order(n, me_ref[0], rows)
-    values = pick(one_hot(device * STEPS + step, rows), values).astype(BF)
+    values = pick(one_hot(source_rows(n, me_ref[0], rows), rows), values).astype(BF)
     part = out_ref.shape[1] // SPAN
     for p in range(SPAN):
         here = slice(p * part, (p + 1) * part)
@@ -167,10 +175,8 @@
 
 
 def norm_kernel(n, *refs):
-    parts, (residual_ref, gain_ref, routes_ref, hidden_ref, out_ref) = refs[:-5], refs[-5:]
-    hidden = residual_ref[...].astype(F32)
-    for ref in parts:
-        hidden += ref[...].astype(F32)
+    kept_ref, got_ref, residual_ref, gain_ref, routes_ref, hidden_ref, out_ref = refs
+    hidden = residual_ref[...].astype(F32) + kept_ref[...] + got_ref[...].astype(F32)
     hidden_ref[...] = hidden
     width = hidden.shape[1]
     mean_square = jnp.sum(hidden * hidden, axis=1, keepdims=True) / width
@@ -179,15 +185,15 @@
     out_ref[:, width:] = routes_ref[...]
 
 
-def load_kernel(n, *refs):
-    sources, targets, sem = refs[1:4], refs[5:8], refs[8]
-    copies = [pltpu.make_async_copy(refs[0], refs[4], sem.at[12])]
-    for i in range(3):
-        step = sources[i].shape[0] // 4
-        for j in range(4):
+def load_kernel(n, count, *refs):
+    sources, targets, sem = refs[1 : 1 + count], refs[2 + count : 2 + 2 * count], refs[-1]
+    copies = [pltpu.make_async_copy(refs[0], refs[1 + count], sem.at[0])]
+    for source, target in zip(sources, targets):
+        step = source.shape[0] // LOADS
+        for j in range(LOADS):
             here = pl.ds(j * step, step)
             copies.append(
-                pltpu.make_async_copy(sources[i].at[here], targets[i].at[here], sem.at[4 * i + j])
+                pltpu.make_async_copy(source.at[here], target.at[here], sem.at[len(copies)])
             )
     for copy in copies:
         copy.start()
@@ -197,21 +203,22 @@
 
 def load(n, passed, arrays):
     return pl.pallas_call(
-        functools.partial(load_kernel, n),
-        in_specs=[pl.BlockSpec(memory_space=pltpu.VMEM)] + [pl.BlockSpec(memory_space=pl.ANY)] * 3,
-        out_specs=[pl.BlockSpec(memory_space=pltpu.VMEM)] * 4,
+        functools.partial(load_kernel, n, len(arrays)),
+        in_specs=[pl.BlockSpec(memory_space=pltpu.VMEM)]
+        + [pl.BlockSpec(memory_space=pl.ANY)] * len(arrays),
+        out_specs=[pl.BlockSpec(memory_space=pltpu.VMEM)] * (1 + len(arrays)),
         out_shape=[jax.ShapeDtypeStruct(a.shape, a.dtype) for a in [passed] + arrays],
-        scratch_shapes=[pltpu.SemaphoreType.DMA((13,))],
-        compiler_params=pltpu.CompilerParams(vmem_limit_bytes=36 * 1024 * 1024),
+        scratch_shapes=[pltpu.SemaphoreType.DMA((1 + LOADS * len(arrays),))],
+        compiler_params=pltpu.CompilerParams(vmem_limit_bytes=28 * 1024 * 1024),
         cost_estimate=pl.CostEstimate(
             flops=0, bytes_accessed=sum(4 * a.size for a in arrays), transcendentals=0
         ),
-        name="load_experts",
+        name="load",
     )(passed, *arrays)
 
 
 def expert_kernel(n, me_ref, *refs, n_ep):
-    blocks, (gate_ref, up_ref, down_ref, near_ref, far_ref) = refs[:8], refs[8:]
+    blocks, (gate_ref, up_ref, down_ref, near_ref, far_ref) = refs[:4], refs[4:]
     rows = n * STEPS
     width, units = gate_ref.shape
     part = width // SPAN
@@ -249,14 +256,21 @@
 
 
 def reduce_rows(near, far, n):
-    planes = n // SPAN
-    width = near.shape[1]
-    total = (near + swap(far, n, c=1).astype(F32)).reshape(4, planes * STEPS, width)
-    kept = total[0]
-    for q in range(1, 4):
-        kept = kept + swap(total[q].astype(BF), n, q=q).astype(F32)
-    kept = kept.reshape(planes, STEPS, width)
-    return [kept[0]] + [swap(kept[k].astype(BF), n, k=k) for k in range(1, planes)]
+    kept, got = near, swap(far, n, -1)
+    for step in range(n.bit_length() - 2):
+        total = kept + got.astype(F32)
+        half = total.shape[0] // 2
+        kept, got = total[:half], swap(total[half:].astype(BF), n, step)
+    return kept, got
+
+
+def spread_rows(rows, n, beside):
+    for step in reversed(range(1, n.bit_length() - 2)):
+        got = swap(rows, n, step)
+        rows = jnp.concatenate([rows, got], axis=0)
+    got = swap(rows, n, 0)
+    rows = beside(rows)
+    return [rows, got, swap(rows, n, -1), swap(got, n, -1)]
 
 
 def per_device(
@@ -276,7 +290,6 @@
 ):
     n_ep = lax.axis_size("ep")
     n = lax.axis_size("sec") * n_ep
-    planes = n // SPAN
     heads = queries.shape[2]
     width = residual.shape[2]
     rows = n * STEPS
@@ -302,7 +315,7 @@
             "heads",
             2 * rows * VDIM * (LAT + width),
         )
-        parts = reduce_rows(near, far, n)
+        terms = reduce_rows(near, far, n)
 
     with jax.named_scope("norm"):
         high = route_scores[0].astype(BF)
@@ -317,16 +330,20 @@
                 jax.ShapeDtypeStruct((STEPS, width + 128), BF),
             ],
             [],
-            parts + [residual[0], norm_gain.reshape(1, width), routes],
+            [*terms, residual[0], norm_gain.reshape(1, width), routes],
             "norm",
             8 * STEPS * width,
         )
 
     with jax.named_scope("spread"):
-        along = jnp.concatenate([normed] + [swap(normed, n, k=k) for k in range(1, planes)], axis=0)
-        blocks = [along] + [swap(along, n, q=q) for q in range(1, 4)]
-        along, *weights = load(n, along, [w_gate[0], w_up[0], w_down[0]])
-        blocks = blocks + [swap(x, n, c=1) for x in [along] + blocks[1:]]
+        loaded = []
+
+        def load_beside(rows):
+            rows, *weights = load(n, rows, [w_gate[0], w_up[0], w_down[0]])
+            loaded.extend(weights)
+            return rows
+
+        blocks = spread_rows(normed, n, load_beside)
 
     with jax.named_scope("experts"):
         near, far = single(
@@ -334,16 +351,14 @@
             n,
             [jax.ShapeDtypeStruct((rows // 2, width), dtype) for dtype in (F32, BF)],
             [me_one],
-            blocks + weights,
+            blocks + loaded,
             "experts",
             6 * rows * width * w_gate.shape[2],
         )
 
     with jax.named_scope("collect"):
-        result = hidden
-        for term in reduce_rows(near, far, n):
-            result = result + term.astype(F32)
-        return result.astype(BF)[None]
+        kept, got = reduce_rows(near, far, n)
+        return (hidden + kept + got.astype(F32)).astype(BF)[None]
 
 
 def solution(mesh):

time: 108 us -> 118 us (1.093)
  waiting for transfers between devices: 46.1 us -> 79.6 us
  starting transfers between devices: 35.7 us -> 14.1 us
  local copies, waits for them, and re-layouts: 3.41 us -> 0.33 us
  Pallas kernels: 19.9 us -> 21.6 us
    ppermute x24 -> x16, waiting for transfers between devices: 37.9 us -> 71.3 us  [swap(): lax.ppermute(x, AXES, [(d, d ^ (1 if step < 0 else 1 << orders[d & 1][ste...]
    ppermute x24 -> x16, starting transfers between devices: 24.7 us -> 6.84 us  [swap(): lax.ppermute(x, AXES, [(d, d ^ (1 if step < 0 else 1 << orders[d & 1][ste...]
    pallas_call x1, Pallas kernels: 4.57 us -> 9.23 us  [attend(): pl.pallas_call(functools.partial(attend_kernel, n), in_specs=[pl.BlockSpe...]
    all_to_all x1, starting transfers between devices: 11 us -> 7.31 us  [per_device(): latents = lax.all_to_all(latents, AXES, 0, 0, tiled=True)]
    unnamed x14 -> x12, local copies, waits for them, and re-layouts: 3.11 us -> 0.03 us
    pallas_call x1, Pallas kernels: 10.6 us -> 7.72 us  [load(): pl.pallas_call(functools.partial(load_kernel, n, len(arrays)), in_specs=[...]
  transfers between devices with their start and end apart: 25 -> 17, of which waited for: 18 -> 16; matrix products, arithmetic and copies ran while one was open for 0% -> 0% of each run, Pallas kernels for 10% -> 7%
where the time goes in v9:
time: 118 us
  waiting for transfers between devices  79.6 us (67%)
  Pallas kernels  21.6 us (18%)
  starting transfers between devices  14.1 us (12%)
  other arithmetic  1.66 us (1%)
    ppermute x16, waiting for transfers between devices, swap(): lax.ppermute(x, AXES, [(d, d ^ (1 if step < 0 else 1 << orders[d & 1][ste...  71.3 us
    pallas_call x1, Pallas kernels, attend(): pl.pallas_call(functools.partial(attend_kernel, n), in_specs=[pl.BlockSpe...  9.23 us
    all_to_all x1, waiting for transfers between devices, per_device(): latents = lax.all_to_all(latents, AXES, 0, 0, tiled=True)  8.22 us
    pallas_call x1, Pallas kernels, load(): pl.pallas_call(functools.partial(load_kernel, n, len(arrays)), in_specs=[...  7.72 us
    all_to_all x1, starting transfers between devices, per_device(): latents = lax.all_to_all(latents, AXES, 0, 0, tiled=True)  7.31 us
    ppermute x16, starting transfers between devices, swap(): lax.ppermute(x, AXES, [(d, d ^ (1 if step < 0 else 1 << orders[d & 1][ste...  6.84 us
    pallas_call x3, Pallas kernels, single(): pl.pallas_call(functools.partial(kernel, n), in_specs=[pl.BlockSpec(memor...  4.67 us
  transfers between devices with their start and end apart: 17, of which 16 were waited for; matrix products, arithmetic and copies ran while one was open for 0% of the time, Pallas kernels for 7%

profile of v9, /device:TPU:0, one launch (start us, length us, event | category | flops | bytes accessed | tf_op | source)
XLA Modules:
  0.0 118.2 jit_solution(13567225639540048511)
XLA Ops:
  0.7 9.2 %attend.1 = bf16[32,4,512]{2,1,0:T(4,128)(2,1)} custom-call(s32[1]{0:T(128)S(6)} %copy.14.len_ref, bf16[128,576]{1,0:T(8,128)(2,1)} %bitcast.29, bf16[4,576]{1,0:T(4,128)(2,1)} %bitcast.30, bf16[576,8192]{1,0:T(8,128)(2,1)} %bitcast.25), custom_call_target="tpu_custom_call" | custom-call | flops 2281701376 | bytes 9437184 | tf_op jit(solution)/shard_map/attention/attend/pallas_call | solution.py:125
  9.9 7.3 %all-to-all-start = ((bf16[32,4,512]{2,1,0:T(4,128)(2,1)}), bf16[32,4,512]{2,1,0:T(4,128)(2,1)S(1)}, u32[]{:S(2)}, u32[]{:S(2)}) async-start(bf16[32,4,512]{2,1,0:T(4,128)(2,1)} %attend.1), calls=%async_computation | async-start | bytes 262144 | tf_op jit(solution)/shard_map/heads/all_to_all | solution.py:308
  17.2 8.2 %all-to-all-done = bf16[32,4,512]{2,1,0:T(4,128)(2,1)S(1)} async-done(((bf16[32,4,512]{2,1,0:T(4,128)(2,1)}), bf16[32,4,512]{2,1,0:T(4,128)(2,1)S(1)}, u32[]{:S(2)}, u32[]{:S(2)}) %all-to-all-start) | async-done | bytes 131104 | tf_op jit(solution)/shard_map/heads/all_to_all | solution.py:308
  25.5 0.9 heads.1
  26.7 2.2 %collective-permute-done = bf16[64,7168]{1,0:T(8,128)(2,1)S(1)} collective-permute-done((bf16[64,7168]{1,0:T(8,128)(2,1)S(1)}, bf16[64,7168]{1,0:T(8,128)(2,1)S(1)}, u32[]{:S(2)}, u32[]{:S(2)}) %collective-permute-start) | collective-permute-done | bytes 917536 | tf_op jit(solution)/shard_map/heads/ppermute | solution.py:34
  29.2 0.8 collective-permute-start.1
  30.1 7.7 %collective-permute-done.1 = bf16[32,7168]{1,0:T(8,128)(2,1)S(1)} collective-permute-done((bf16[32,7168]{1,0:T(8,128)(2,1)S(1)}, bf16[32,7168]{1,0:T(8,128)(2,1)S(1)}, u32[]{:S(2)}, u32[]{:S(2)}) %collective-permute-start.1) | collective-permute-done | bytes 458784 | tf_op jit(solution)/shard_map/heads/ppermute | solution.py:34
  38.5 5.5 %collective-permute-done.2 = bf16[16,7168]{1,0:T(8,128)(2,1)S(1)} collective-permute-done((bf16[16,7168]{1,0:T(8,128)(2,1)S(1)}, bf16[16,7168]{1,0:T(8,128)(2,1)S(1)}, u32[]{:S(2)}, u32[]{:S(2)}) %collective-permute-start.2) | collective-permute-done | bytes 229408 | tf_op jit(solution)/shard_map/heads/ppermute | solution.py:34
  44.2 4.7 %collective-permute-done.3 = bf16[8,7168]{1,0:T(8,128)(2,1)S(1)} collective-permute-done((bf16[8,7168]{1,0:T(8,128)(2,1)S(1)}, bf16[8,7168]{1,0:T(8,128)(2,1)S(1)}, u32[]{:S(2)}, u32[]{:S(2)}) %collective-permute-start.3) | collective-permute-done | bytes 114720 | tf_op jit(solution)/shard_map/heads/ppermute | solution.py:34
  49.0 0.8 collective-permute-start.4
  49.8 5.4 %collective-permute-done.4.refs_1_ = bf16[4,7168]{1,0:T(4,128)(2,1)S(1)} collective-permute-done((bf16[4,7168]{1,0:T(4,128)(2,1)S(1)}, bf16[4,7168]{1,0:T(4,128)(2,1)S(1)}, u32[]{:S(2)}, u32[]{:S(2)}) %collective-permute-start.4) | collective-permute-done | bytes 57376 | tf_op jit(solution)/shard_map/heads/ppermute | solution.py:34
  55.5 5.1 %collective-permute-done.5 = bf16[4,7296]{1,0:T(4,128)(2,1)S(1)} collective-permute-done((bf16[4,7296]{1,0:T(4,128)(2,1)S(1)}, bf16[4,7296]{1,0:T(4,128)(2,1)S(1)}, u32[]{:S(2)}, u32[]{:S(2)}) %collective-permute-start.5) | collective-permute-done | bytes 58400 | tf_op jit(solution)/shard_map/spread/ppermute | solution.py:34
  60.8 4.9 %collective-permute-done.6 = bf16[8,7296]{1,0:T(8,128)(2,1)S(1)} collective-permute-done((bf16[8,7296]{1,0:T(8,128)(2,1)S(1)}, bf16[8,7296]{1,0:T(8,128)(2,1)S(1)}, u32[]{:S(2)}, u32[]{:S(2)}) %collective-permute-start.6) | collective-permute-done | bytes 116768 | tf_op jit(solution)/shard_map/spread/ppermute | solution.py:34
  66.3 8.2 %collective-permute-done.7 = bf16[16,7296]{1,0:T(8,128)(2,1)S(1)} collective-permute-done((bf16[16,7296]{1,0:T(8,128)(2,1)S(1)}, bf16[16,7296]{1,0:T(8,128)(2,1)S(1)}, u32[]{:S(2)}, u32[]{:S(2)}) %collective-permute-start.7) | collective-permute-done | bytes 233504 | tf_op jit(solution)/shard_map/spread/ppermute | solution.py:34
  74.6 1.1 collective-permute-start.8
  75.7 7.7 %load.1 = (bf16[32,7296]{1,0:T(8,128)(2,1)S(1)}, bf16[7168,512]{1,0:T(8,128)(2,1)S(1)}, bf16[7168,512]{1,0:T(8,128)(2,1)S(1)}, bf16[512,7168]{1,0:T(8,128)(2,1)S(1)}) custom-call(bf16[32,7296]{1,0:T(8,128)(2,1)S(1)} %pad_maximum_fusion.refs_0_, bf16[7168,512]{1,0:T(8,128)(2,1)} %bitcast.26, bf16[7168,512]{1,0:T(8,128)(2,1)} %bitcast.27, ...), custom_call_target="tpu_custom_call" | custom-call | bytes 44040192 | tf_op jit(solution)/shard_map/spread/load/pallas_call | solution.py:205
  84.0 1.3 %collective-permute-done.9.refs_2_ = bf16[32,7296]{1,0:T(8,128)(2,1)S(1)} collective-permute-done((bf16[32,7296]{1,0:T(8,128)(2,1)S(1)}, bf16[32,7296]{1,0:T(8,128)(2,1)S(1)}, u32[]{:S(2)}, u32[]{:S(2)}) %collective-permute-start.9) | collective-permute-done | bytes 466976 | tf_op jit(solution)/shard_map/spread/ppermute | solution.py:34
  86.0 3.6 %experts.1 = (f32[64,7168]{1,0:T(8,128)S(1)}, bf16[64,7168]{1,0:T(8,128)(2,1)S(1)}) custom-call(s32[1]{0:T(128)} %bitcast.me_ref, bf16[32,7296]{1,0:T(8,128)(2,1)S(1)} %get-tuple-element.19.refs_0_, bf16[32,7296]{1,0:T(8,128)(2,1)S(1)} %collective-permute-done.8.refs_1_, bf16[32,7296]{1,0:T(8,128)(2,1)S(1)} %collective-permute-done.9.refs_2_, ...), custom_call_target="tpu_custom_call" | custom-call | flops 2818572288 | bytes 23887872 | tf_op jit(solution)/shard_map/experts/experts/pallas_call | solution.py:245
  89.8 2.3 %collective-permute-done.11 = bf16[64,7168]{1,0:T(8,128)(2,1)S(1)} collective-permute-done((bf16[64,7168]{1,0:T(8,128)(2,1)S(1)}, bf16[64,7168]{1,0:T(8,128)(2,1)S(1)}, u32[]{:S(2)}, u32[]{:S(2)}) %collective-permute-start.11) | collective-permute-done | bytes 917536 | tf_op jit(solution)/shard_map/collect/ppermute | solution.py:34
  92.3 1.0 collective-permute-start.12
  93.4 7.5 %collective-permute-done.12 = bf16[32,7168]{1,0:T(8,128)(2,1)S(1)} collective-permute-done((bf16[32,7168]{1,0:T(8,128)(2,1)S(1)}, bf16[32,7168]{1,0:T(8,128)(2,1)S(1)}, u32[]{:S(2)}, u32[]{:S(2)}) %collective-permute-start.12) | collective-permute-done | bytes 458784 | tf_op jit(solution)/shard_map/collect/ppermute | solution.py:34
  101.1 6.0 %collective-permute-done.13 = bf16[16,7168]{1,0:T(8,128)(2,1)S(1)} collective-permute-done((bf16[16,7168]{1,0:T(8,128)(2,1)S(1)}, bf16[16,7168]{1,0:T(8,128)(2,1)S(1)}, u32[]{:S(2)}, u32[]{:S(2)}) %collective-permute-start.13) | collective-permute-done | bytes 229408 | tf_op jit(solution)/shard_map/collect/ppermute | solution.py:34
  107.5 4.5 %collective-permute-done.14 = bf16[8,7168]{1,0:T(8,128)(2,1)S(1)} collective-permute-done((bf16[8,7168]{1,0:T(8,128)(2,1)S(1)}, bf16[8,7168]{1,0:T(8,128)(2,1)S(1)}, u32[]{:S(2)}, u32[]{:S(2)}) %collective-permute-start.14) | collective-permute-done | bytes 114720 | tf_op jit(solution)/shard_map/collect/ppermute | solution.py:34
  112.3 5.3 %collective-permute-done.15 = bf16[4,7168]{1,0:T(4,128)(2,1)S(1)} collective-permute-done((bf16[4,7168]{1,0:T(4,128)(2,1)S(1)}, bf16[4,7168]{1,0:T(4,128)(2,1)S(1)}, u32[]{:S(2)}, u32[]{:S(2)}) %collective-permute-start.15) | collective-permute-done | bytes 57376 | tf_op jit(solution)/shard_map/collect/ppermute | solution.py:34
  (53 shorter events, 5.9 us)
Async XLA Ops:
  0.7 24.8 %copy-start = (bf16[1,128,7168]{2,1,0:T(8,128)(2,1)S(1)}, bf16[1,128,7168]{2,1,0:T(8,128)(2,1)}, u32[]{:S(2)}) copy-start(bf16[1,128,7168]{2,1,0:T(8,128)(2,1)} %param.22) | copy-start | bytes 5505028
  0.7 24.8 %copy-start.1 = (bf16[1,512,128]{2,1,0:T(8,128)(2,1)S(1)}, bf16[1,512,128]{2,1,0:T(8,128)(2,1)}, u32[]{:S(2)}) copy-start(bf16[1,512,128]{2,1,0:T(8,128)(2,1)} %param.21) | copy-start | bytes 393220
  9.9 15.5 %all-to-all-start = ((bf16[32,4,512]{2,1,0:T(4,128)(2,1)}), bf16[32,4,512]{2,1,0:T(4,128)(2,1)S(1)}, u32[]{:S(2)}, u32[]{:S(2)}) async-start(bf16[32,4,512]{2,1,0:T(4,128)(2,1)} %attend.1), calls=%async_computation | async-start | bytes 262144 | tf_op jit(solution)/shard_map/heads/all_to_all | solution.py:308
  26.4 2.5 %collective-permute-start = (bf16[64,7168]{1,0:T(8,128)(2,1)S(1)}, bf16[64,7168]{1,0:T(8,128)(2,1)S(1)}, u32[]{:S(2)}, u32[]{:S(2)}) collective-permute-start(bf16[64,7168]{1,0:T(8,128)(2,1)S(1)} %get-tuple-element.16), channel_id=1, source_target_pairs={{0,1},{1,0},{2,3},{3,2},{4,5},{5,4},{6,7},{7,6},{8,9},{9,8},{10,11... | collective-permute-start | bytes 2752520 | tf_op jit(solution)/shard_map/heads/ppermute | solution.py:34
  29.1 9.4 %copy-start.3 = (bf16[7168]{0:T(1024)(128)(2,1)S(1)}, bf16[7168]{0:T(1024)(128)(2,1)}, u32[]{:S(2)}) copy-start(bf16[7168]{0:T(1024)(128)(2,1)} %param.20) | copy-start | bytes 43012
  29.1 9.4 %copy-start.5 = (f32[1,4,8]{2,1,0:T(4,128)S(1)}, f32[1,4,8]{2,1,0:T(4,128)}, u32[]{:S(2)}) copy-start(f32[1,4,8]{2,1,0:T(4,128)} %param.18) | copy-start | bytes 388
  29.2 15.0 %copy-start.4 = (s32[1,4,8]{2,1,0:T(4,128)S(1)}, s32[1,4,8]{2,1,0:T(4,128)}, u32[]{:S(2)}) copy-start(s32[1,4,8]{2,1,0:T(4,128)} %param.17) | copy-start | bytes 388
  29.2 8.5 %collective-permute-start.1 = (bf16[32,7168]{1,0:T(8,128)(2,1)S(1)}, bf16[32,7168]{1,0:T(8,128)(2,1)S(1)}, u32[]{:S(2)}, u32[]{:S(2)}) collective-permute-start(bf16[32,7168]{1,0:T(8,128)(2,1)S(1)} %slice.110), channel_id=1, source_target_pairs={{0,16},{1,3},{2,18},{3,1},{4,20},{5,7},{6,22},{7,5},{8,24},{9,11},... | collective-permute-start | bytes 1376264 | tf_op jit(solution)/shard_map/heads/ppermute | solution.py:34
  37.9 17.4 %copy-start.2 = (bf16[1,4,7168]{2,1,0:T(4,128)(2,1)S(1)}, bf16[1,4,7168]{2,1,0:T(4,128)(2,1)}, u32[]{:S(2)}) copy-start(bf16[1,4,7168]{2,1,0:T(4,128)(2,1)} %param.19) | copy-start | bytes 172036
  37.9 6.1 %collective-permute-start.2 = (bf16[16,7168]{1,0:T(8,128)(2,1)S(1)}, bf16[16,7168]{1,0:T(8,128)(2,1)S(1)}, u32[]{:S(2)}, u32[]{:S(2)}) collective-permute-start(bf16[16,7168]{1,0:T(8,128)(2,1)S(1)} %slice.112), channel_id=1, source_target_pairs={{0,2},{1,5},{2,0},{3,7},{4,6},{5,1},{6,4},{7,3},{8,10},{9,13},{10,... | collective-permute-start | bytes 688136 | tf_op jit(solution)/shard_map/heads/ppermute | solution.py:34
  44.1 4.9 %collective-permute-start.3 = (bf16[8,7168]{1,0:T(8,128)(2,1)S(1)}, bf16[8,7168]{1,0:T(8,128)(2,1)S(1)}, u32[]{:S(2)}, u32[]{:S(2)}) collective-permute-start(bf16[8,7168]{1,0:T(8,128)(2,1)S(1)} %slice.114), channel_id=1, source_target_pairs={{0,4},{1,17},{2,6},{3,19},{4,0},{5,21},{6,2},{7,23},{8,12},{9,25},... | collective-permute-start | bytes 344072 | tf_op jit(solution)/shard_map/heads/ppermute | solution.py:34
  49.0 6.3 %collective-permute-start.4 = (bf16[4,7168]{1,0:T(4,128)(2,1)S(1)}, bf16[4,7168]{1,0:T(4,128)(2,1)S(1)}, u32[]{:S(2)}, u32[]{:S(2)}) collective-permute-start(bf16[4,7168]{1,0:T(4,128)(2,1)S(1)} %slice.116), channel_id=1, source_target_pairs={{0,8},{1,9},{2,10},{3,11},{4,12},{5,13},{6,14},{7,15},{8,0},{9,1},... | collective-permute-start | bytes 172040 | tf_op jit(solution)/shard_map/heads/ppermute | solution.py:34
  55.5 5.2 %collective-permute-start.5 = (bf16[4,7296]{1,0:T(4,128)(2,1)S(1)}, bf16[4,7296]{1,0:T(4,128)(2,1)S(1)}, u32[]{:S(2)}, u32[]{:S(2)}) collective-permute-start(bf16[4,7296]{1,0:T(4,128)(2,1)S(1)} %get-tuple-element.18), channel_id=1, source_target_pairs={{0,8},{1,9},{2,10},{3,11},{4,12},{5,13},{6,14},{7,15},{8,0},{9,1},... | collective-permute-start | bytes 175112 | tf_op jit(solution)/shard_map/spread/ppermute | solution.py:34
  60.7 5.0 %collective-permute-start.6 = (bf16[8,7296]{1,0:T(8,128)(2,1)S(1)}, bf16[8,7296]{1,0:T(8,128)(2,1)S(1)}, u32[]{:S(2)}, u32[]{:S(2)}) collective-permute-start(bf16[8,7296]{1,0:T(8,128)(2,1)S(1)} %pad_maximum_fusion.2), channel_id=1, source_target_pairs={{0,4},{1,17},{2,6},{3,19},{4,0},{5,21},{6,2},{7,23},{8,12},{9,25},... | collective-permute-start | bytes 350216 | tf_op jit(solution)/shard_map/spread/ppermute | solution.py:34
  65.8 8.7 %collective-permute-start.7 = (bf16[16,7296]{1,0:T(8,128)(2,1)S(1)}, bf16[16,7296]{1,0:T(8,128)(2,1)S(1)}, u32[]{:S(2)}, u32[]{:S(2)}) collective-permute-start(bf16[16,7296]{1,0:T(8,128)(2,1)S(1)} %pad_maximum_fusion.1), channel_id=1, source_target_pairs={{0,2},{1,5},{2,0},{3,7},{4,6},{5,1},{6,4},{7,3},{8,10},{9,13},{10,... | collective-permute-start | bytes 700424 | tf_op jit(solution)/shard_map/spread/ppermute | solution.py:34
  74.6 8.9 %collective-permute-start.8 = (bf16[32,7296]{1,0:T(8,128)(2,1)S(1)}, bf16[32,7296]{1,0:T(8,128)(2,1)S(1)}, u32[]{:S(2)}, u32[]{:S(2)}) collective-permute-start(bf16[32,7296]{1,0:T(8,128)(2,1)S(1)} %pad_maximum_fusion.refs_0_), channel_id=1, source_target_pairs={{0,16},{1,3},{2,18},{3,1},{4,20},{5,7},{6,22},{7,5},{8,24},{9,11},... | collective-permute-start | bytes 1400840 | tf_op jit(solution)/shard_map/spread/ppermute | solution.py:34
  83.4 1.9 %collective-permute-start.9 = (bf16[32,7296]{1,0:T(8,128)(2,1)S(1)}, bf16[32,7296]{1,0:T(8,128)(2,1)S(1)}, u32[]{:S(2)}, u32[]{:S(2)}) collective-permute-start(bf16[32,7296]{1,0:T(8,128)(2,1)S(1)} %get-tuple-element.19.refs_0_), channel_id=1, source_target_pairs={{0,1},{1,0},{2,3},{3,2},{4,5},{5,4},{6,7},{7,6},{8,9},{9,8},{10,11... | collective-permute-start | bytes 1400840 | tf_op jit(solution)/shard_map/spread/ppermute | solution.py:34
  83.5 2.5 %collective-permute-start.10 = (bf16[32,7296]{1,0:T(8,128)(2,1)S(1)}, bf16[32,7296]{1,0:T(8,128)(2,1)S(1)}, u32[]{:S(2)}, u32[]{:S(2)}) collective-permute-start(bf16[32,7296]{1,0:T(8,128)(2,1)S(1)} %collective-permute-done.8.refs_1_), channel_id=1, source_target_pairs={{0,1},{1,0},{2,3},{3,2},{4,5},{5,4},{6,7},{7,6},{8,9},{9,8},{10,11... | collective-permute-start | bytes 1400840 | tf_op jit(solution)/shard_map/spread/ppermute | solution.py:34
  89.6 2.5 %collective-permute-start.11 = (bf16[64,7168]{1,0:T(8,128)(2,1)S(1)}, bf16[64,7168]{1,0:T(8,128)(2,1)S(1)}, u32[]{:S(2)}, u32[]{:S(2)}) collective-permute-start(bf16[64,7168]{1,0:T(8,128)(2,1)S(1)} %get-tuple-element.24), channel_id=1, source_target_pairs={{0,1},{1,0},{2,3},{3,2},{4,5},{5,4},{6,7},{7,6},{8,9},{9,8},{10,11... | collective-permute-start | bytes 2752520 | tf_op jit(solution)/shard_map/collect/ppermute | solution.py:34
  92.3 8.5 %collective-permute-start.12 = (bf16[32,7168]{1,0:T(8,128)(2,1)S(1)}, bf16[32,7168]{1,0:T(8,128)(2,1)S(1)}, u32[]{:S(2)}, u32[]{:S(2)}) collective-permute-start(bf16[32,7168]{1,0:T(8,128)(2,1)S(1)} %slice.109), channel_id=1, source_target_pairs={{0,16},{1,3},{2,18},{3,1},{4,20},{5,7},{6,22},{7,5},{8,24},{9,11},... | collective-permute-start | bytes 1376264 | tf_op jit(solution)/shard_map/collect/ppermute | solution.py:34
  101.0 6.1 %collective-permute-start.13 = (bf16[16,7168]{1,0:T(8,128)(2,1)S(1)}, bf16[16,7168]{1,0:T(8,128)(2,1)S(1)}, u32[]{:S(2)}, u32[]{:S(2)}) collective-permute-start(bf16[16,7168]{1,0:T(8,128)(2,1)S(1)} %slice.111), channel_id=1, source_target_pairs={{0,2},{1,5},{2,0},{3,7},{4,6},{5,1},{6,4},{7,3},{8,10},{9,13},{10,... | collective-permute-start | bytes 688136 | tf_op jit(solution)/shard_map/collect/ppermute | solution.py:34
  107.2 4.9 %collective-permute-start.14 = (bf16[8,7168]{1,0:T(8,128)(2,1)S(1)}, bf16[8,7168]{1,0:T(8,128)(2,1)S(1)}, u32[]{:S(2)}, u32[]{:S(2)}) collective-permute-start(bf16[8,7168]{1,0:T(8,128)(2,1)S(1)} %slice.113), channel_id=1, source_target_pairs={{0,4},{1,17},{2,6},{3,19},{4,0},{5,21},{6,2},{7,23},{8,12},{9,25},... | collective-permute-start | bytes 344072 | tf_op jit(solution)/shard_map/collect/ppermute | solution.py:34
  112.1 5.5 %collective-permute-start.15 = (bf16[4,7168]{1,0:T(4,128)(2,1)S(1)}, bf16[4,7168]{1,0:T(4,128)(2,1)S(1)}, u32[]{:S(2)}, u32[]{:S(2)}) collective-permute-start(bf16[4,7168]{1,0:T(4,128)(2,1)S(1)} %slice.115), channel_id=1, source_target_pairs={{0,8},{1,9},{2,10},{3,11},{4,12},{5,13},{6,14},{7,15},{8,0},{9,1},... | collective-permute-start | bytes 172040 | tf_op jit(solution)/shard_map/collect/ppermute | solution.py:34

commit v10 on v4

--- a/solution.py
+++ b/solution.py
@@ -22,13 +22,18 @@
 VMEM_LIMIT = 16 * 1024 * 1024
 
 
-def mask_of(n, q=0, c=0, k=0):
-    return (q >> 1) * (n // 2) + k * 4 + (q & 1) * 2 + c
-
-
-def swap(x, n, **differ):
-    mask = mask_of(n, **differ)
-    return lax.ppermute(x, AXES, [(d, d ^ mask) for d in range(n)])
+def partners(n):
+    chips = [(q >> 1) * (n // 2) + (q & 1) * 2 for q in range(4)]
+    planes = [k * 4 for k in range(n // SPAN)]
+    return [(chips, planes), (planes, chips) if len(planes) == 4 else (chips, planes)]
+
+
+def swap(x, n, stage, i):
+    return lax.ppermute(x, AXES, [(d, d ^ partners(n)[d & 1][stage][i]) for d in range(n)])
+
+
+def swap_core(x, n):
+    return lax.ppermute(x, AXES, [(d, d ^ 1) for d in range(n)])
 
 
 def iota2(shape, axis):
@@ -145,19 +150,25 @@
     )(length, q, new, keys)
 
 
-def partner_order(n, me, rows):
-    planes = n // SPAN
+def source_rows(n, me, rows):
     r = iota2((rows, rows), 0)
-    c, q = r // (rows // 2), (r // (planes * STEPS)) % 4
-    k, step = (r // STEPS) % planes, r % STEPS
-    return me ^ ((q >> 1) * (n // 2) + k * 4 + (q & 1) * 2 + c), step
+    other = r // (rows // 2)
+    masks = []
+    for firsts, seconds in partners(n):
+        i, j = (r // (len(seconds) * STEPS)) % len(firsts), (r // STEPS) % len(seconds)
+        mask = jnp.zeros_like(r)
+        for index, options in ((i, firsts), (j, seconds)):
+            for value, option in enumerate(options):
+                mask = mask | jnp.where(index == value, option, 0)
+        masks.append(mask)
+    mask = jnp.where((me & 1) ^ other == 0, masks[0], masks[1])
+    return (me ^ mask ^ other) * STEPS + r % STEPS
 
 
 def heads_kernel(n, me_ref, latents_ref, uv_ref, out_ref, near_ref, far_ref):
     rows = n * STEPS
     values = jnp.dot(latents_ref[...], uv_ref[...], preferred_element_type=F32).astype(BF)
-    device, step = partner_order(n, me_ref[0], rows)
-    values = pick(one_hot(device * STEPS + step, rows), values).astype(BF)
+    values = pick(one_hot(source_rows(n, me_ref[0], rows), rows), values).astype(BF)
     part = out_ref.shape[1] // SPAN
     for p in range(SPAN):
         here = slice(p * part, (p + 1) * part)
@@ -202,7 +213,7 @@
         out_specs=[pl.BlockSpec(memory_space=pltpu.VMEM)] * 4,
         out_shape=[jax.ShapeDtypeStruct(a.shape, a.dtype) for a in [passed] + arrays],
         scratch_shapes=[pltpu.SemaphoreType.DMA((13,))],
-        compiler_params=pltpu.CompilerParams(vmem_limit_bytes=36 * 1024 * 1024),
+        compiler_params=pltpu.CompilerParams(vmem_limit_bytes=28 * 1024 * 1024),
         cost_estimate=pl.CostEstimate(
             flops=0, bytes_accessed=sum(4 * a.size for a in arrays), transcendentals=0
         ),
@@ -249,14 +260,15 @@
 
 
 def reduce_rows(near, far, n):
-    planes = n // SPAN
+    firsts, seconds = (len(masks) for masks in partners(n)[0])
     width = near.shape[1]
-    total = (near + swap(far, n, c=1).astype(F32)).reshape(4, planes * STEPS, width)
+    total = near + swap_core(far, n).astype(F32)
+    total = total.reshape(firsts, seconds * STEPS, width)
     kept = total[0]
-    for q in range(1, 4):
-        kept = kept + swap(total[q].astype(BF), n, q=q).astype(F32)
-    kept = kept.reshape(planes, STEPS, width)
-    return [kept[0]] + [swap(kept[k].astype(BF), n, k=k) for k in range(1, planes)]
+    for i in reversed(range(1, firsts)):
+        kept = kept + swap(total[i].astype(BF), n, 0, i).astype(F32)
+    kept = kept.reshape(seconds, STEPS, width)
+    return [kept[0]] + [swap(kept[j].astype(BF), n, 1, j) for j in range(1, seconds)]
 
 
 def per_device(
@@ -276,7 +288,6 @@
 ):
     n_ep = lax.axis_size("ep")
     n = lax.axis_size("sec") * n_ep
-    planes = n // SPAN
     heads = queries.shape[2]
     width = residual.shape[2]
     rows = n * STEPS
@@ -323,10 +334,11 @@
         )
 
     with jax.named_scope("spread"):
-        along = jnp.concatenate([normed] + [swap(normed, n, k=k) for k in range(1, planes)], axis=0)
-        blocks = [along] + [swap(along, n, q=q) for q in range(1, 4)]
+        along = [normed] + [swap(normed, n, 1, j) for j in range(1, n // SPAN)]
+        along = jnp.concatenate(along, axis=0)
+        blocks = [along] + [swap(along, n, 0, i) for i in range(1, 4)]
         along, *weights = load(n, along, [w_gate[0], w_up[0], w_down[0]])
-        blocks = blocks + [swap(x, n, c=1) for x in [along] + blocks[1:]]
+        blocks = blocks + [swap_core(x, n) for x in [along] + blocks[1:]]
 
     with jax.named_scope("experts"):
         near, far = single(

time: 108 us -> 92.1 us (0.85)
  waiting for transfers between devices: 46.1 us -> 36.2 us
  starting transfers between devices: 35.7 us -> 31.5 us
  local copies, waits for them, and re-layouts: 3.41 us -> 0.33 us
  Pallas kernels: 19.9 us -> 21.6 us
    ppermute x24, waiting for transfers between devices: 37.9 us -> 27.9 us  [the longest x18 22 us: swap(): lax.ppermute(x, AXES, [(d, d ^ partners(n)[d & 1][stage][i]) for d in ran...]
    pallas_call x1, Pallas kernels: 4.57 us -> 9.22 us  [attend(): pl.pallas_call(functools.partial(attend_kernel, n), in_specs=[pl.BlockSpe...]
    all_to_all x1, starting transfers between devices: 11 us -> 6.74 us  [per_device(): latents = lax.all_to_all(latents, AXES, 0, 0, tiled=True)]
    unnamed x14 -> x12, local copies, waits for them, and re-layouts: 3.11 us -> 0.03 us
    pallas_call x1, Pallas kernels: 10.6 us -> 7.71 us  [load(): pl.pallas_call(functools.partial(load_kernel, n), in_specs=[pl.BlockSpec(...]
  transfers between devices with their start and end apart: 25 -> 25, of which waited for: 18 -> 19; matrix products, arithmetic and copies ran while one was open for 0% -> 0% of each run, Pallas kernels for 10% -> 8%
where the time goes in v10:
time: 92.1 us
  waiting for transfers between devices  36.2 us (39%)
  starting transfers between devices  31.5 us (34%)
  Pallas kernels  21.6 us (23%)
  other arithmetic  1.58 us (2%)
    ppermute x18, starting transfers between devices, swap(): lax.ppermute(x, AXES, [(d, d ^ partners(n)[d & 1][stage][i]) for d in ran...  23.1 us
    ppermute x18, waiting for transfers between devices, swap(): lax.ppermute(x, AXES, [(d, d ^ partners(n)[d & 1][stage][i]) for d in ran...  22 us
    pallas_call x1, Pallas kernels, attend(): pl.pallas_call(functools.partial(attend_kernel, n), in_specs=[pl.BlockSpe...  9.22 us
    all_to_all x1, waiting for transfers between devices, per_device(): latents = lax.all_to_all(latents, AXES, 0, 0, tiled=True)  8.22 us
    pallas_call x1, Pallas kernels, load(): pl.pallas_call(functools.partial(load_kernel, n), in_specs=[pl.BlockSpec(...  7.71 us
    all_to_all x1, starting transfers between devices, per_device(): latents = lax.all_to_all(latents, AXES, 0, 0, tiled=True)  6.74 us
    ppermute x6, waiting for transfers between devices, swap_core(): return lax.ppermute(x, AXES, [(d, d ^ 1) for d in range(n)])  5.97 us
    pallas_call x3, Pallas kernels, single(): pl.pallas_call(functools.partial(kernel, n), in_specs=[pl.BlockSpec(memor...  4.7 us
  transfers between devices with their start and end apart: 25, of which 19 were waited for; matrix products, arithmetic and copies ran while one was open for 0% of the time, Pallas kernels for 8%

profile of v10, /device:TPU:0, one launch (start us, length us, event | category | flops | bytes accessed | tf_op | source)
XLA Modules:
  0.0 92.1 jit_solution(11375050866808434006)
XLA Ops:
  0.7 9.2 %attend.1 = bf16[32,4,512]{2,1,0:T(4,128)(2,1)} custom-call(s32[1]{0:T(128)S(6)} %copy.14.len_ref, bf16[128,576]{1,0:T(8,128)(2,1)} %bitcast.29, bf16[4,576]{1,0:T(4,128)(2,1)} %bitcast.30, bf16[576,8192]{1,0:T(8,128)(2,1)} %bitcast.25), custom_call_target="tpu_custom_call" | custom-call | flops 2281701376 | bytes 9437184 | tf_op jit(solution)/shard_map/attention/attend/pallas_call | solution.py:127
  9.9 6.7 %all-to-all-start = ((bf16[32,4,512]{2,1,0:T(4,128)(2,1)}), bf16[32,4,512]{2,1,0:T(4,128)(2,1)S(1)}, u32[]{:S(2)}, u32[]{:S(2)}) async-start(bf16[32,4,512]{2,1,0:T(4,128)(2,1)} %attend.1), calls=%async_computation | async-start | bytes 262144 | tf_op jit(solution)/shard_map/heads/all_to_all | solution.py:306
  16.7 8.2 %all-to-all-done = bf16[32,4,512]{2,1,0:T(4,128)(2,1)S(1)} async-done(((bf16[32,4,512]{2,1,0:T(4,128)(2,1)}), bf16[32,4,512]{2,1,0:T(4,128)(2,1)S(1)}, u32[]{:S(2)}, u32[]{:S(2)}) %all-to-all-start) | async-done | bytes 131104 | tf_op jit(solution)/shard_map/heads/all_to_all | solution.py:306
  26.2 2.2 %collective-permute-done = bf16[64,7168]{1,0:T(8,128)(2,1)S(1)} collective-permute-done((bf16[64,7168]{1,0:T(8,128)(2,1)S(1)}, bf16[64,7168]{1,0:T(8,128)(2,1)S(1)}, u32[]{:S(2)}, u32[]{:S(2)}) %collective-permute-start) | collective-permute-done | bytes 917536 | tf_op jit(solution)/shard_map/heads/ppermute | solution.py:36
  29.3 1.7 %collective-permute-start.3 = (bf16[16,7168]{1,0:T(8,128)(2,1)S(1)}, bf16[16,7168]{1,0:T(8,128)(2,1)S(1)}, u32[]{:S(2)}, u32[]{:S(2)}) collective-permute-start(bf16[16,7168]{1,0:T(8,128)(2,1)S(1)} %get-tuple-element.39), channel_id=1, source_target_pairs={{0,2},{1,5},{2,0},{3,7},{4,6},{5,1},{6,4},{7,3},{8,10},{9,13},{10,... | collective-permute-start | bytes 688136 | tf_op jit(solution)/shard_map/heads/ppermute | solution.py:32
  32.3 3.5 %collective-permute-done.1 = bf16[16,7168]{1,0:T(8,128)(2,1)S(1)} collective-permute-done((bf16[16,7168]{1,0:T(8,128)(2,1)S(1)}, bf16[16,7168]{1,0:T(8,128)(2,1)S(1)}, u32[]{:S(2)}, u32[]{:S(2)}) %collective-permute-start.1) | collective-permute-done | bytes 229408 | tf_op jit(solution)/shard_map/heads/ppermute | solution.py:32
  35.8 2.0 %collective-permute-done.3 = bf16[16,7168]{1,0:T(8,128)(2,1)S(1)} collective-permute-done((bf16[16,7168]{1,0:T(8,128)(2,1)S(1)}, bf16[16,7168]{1,0:T(8,128)(2,1)S(1)}, u32[]{:S(2)}, u32[]{:S(2)}) %collective-permute-start.3) | collective-permute-done | bytes 229408 | tf_op jit(solution)/shard_map/heads/ppermute | solution.py:32
  37.9 1.7 %collective-permute-start.6 = (bf16[4,7168]{1,0:T(4,128)(2,1)S(1)}, bf16[4,7168]{1,0:T(4,128)(2,1)S(1)}, u32[]{:S(2)}, u32[]{:S(2)}) collective-permute-start(bf16[4,7168]{1,0:T(4,128)(2,1)S(1)} %get-tuple-element.44), channel_id=1, source_target_pairs={{0,12},{1,19},{2,14},{3,17},{4,8},{5,23},{6,10},{7,21},{8,4},{9,27... | collective-permute-start | bytes 172040 | tf_op jit(solution)/shard_map/heads/ppermute | solution.py:32
  39.9 2.4 %collective-permute-start.4 = (bf16[4,7168]{1,0:T(4,128)(2,1)S(1)}, bf16[4,7168]{1,0:T(4,128)(2,1)S(1)}, u32[]{:S(2)}, u32[]{:S(2)}) collective-permute-start(bf16[4,7168]{1,0:T(4,128)(2,1)S(1)} %get-tuple-element.46), channel_id=1, source_target_pairs={{0,4},{1,3},{2,6},{3,1},{4,0},{5,7},{6,2},{7,5},{8,12},{9,11},{10,... | collective-permute-start | bytes 172040 | tf_op jit(solution)/shard_map/heads/ppermute | solution.py:32
  42.5 1.5 %collective-permute-done.6.refs_3_ = bf16[4,7168]{1,0:T(4,128)(2,1)S(1)} collective-permute-done((bf16[4,7168]{1,0:T(4,128)(2,1)S(1)}, bf16[4,7168]{1,0:T(4,128)(2,1)S(1)}, u32[]{:S(2)}, u32[]{:S(2)}) %collective-permute-start.6) | collective-permute-done | bytes 57376 | tf_op jit(solution)/shard_map/heads/ppermute | solution.py:32
  45.4 1.8 %collective-permute-start.9 = (bf16[4,7296]{1,0:T(4,128)(2,1)S(1)}, bf16[4,7296]{1,0:T(4,128)(2,1)S(1)}, u32[]{:S(2)}, u32[]{:S(2)}) collective-permute-start(bf16[4,7296]{1,0:T(4,128)(2,1)S(1)} %get-tuple-element.18), channel_id=1, source_target_pairs={{0,12},{1,19},{2,14},{3,17},{4,8},{5,23},{6,10},{7,21},{8,4},{9,27... | collective-permute-start | bytes 175112 | tf_op jit(solution)/shard_map/spread/ppermute | solution.py:32
  48.3 1.6 %collective-permute-start.7 = (bf16[4,7296]{1,0:T(4,128)(2,1)S(1)}, bf16[4,7296]{1,0:T(4,128)(2,1)S(1)}, u32[]{:S(2)}, u32[]{:S(2)}) collective-permute-start(bf16[4,7296]{1,0:T(4,128)(2,1)S(1)} %get-tuple-element.18), channel_id=1, source_target_pairs={{0,4},{1,3},{2,6},{3,1},{4,0},{5,7},{6,2},{7,5},{8,12},{9,11},{10,... | collective-permute-start | bytes 175112 | tf_op jit(solution)/shard_map/spread/ppermute | solution.py:32
  49.9 1.6 %collective-permute-done.9 = bf16[4,7296]{1,0:T(4,128)(2,1)S(1)} collective-permute-done((bf16[4,7296]{1,0:T(4,128)(2,1)S(1)}, bf16[4,7296]{1,0:T(4,128)(2,1)S(1)}, u32[]{:S(2)}, u32[]{:S(2)}) %collective-permute-start.9) | collective-permute-done | bytes 58400 | tf_op jit(solution)/shard_map/spread/ppermute | solution.py:32
  51.5 1.4 %collective-permute-done.8 = bf16[4,7296]{1,0:T(4,128)(2,1)S(1)} collective-permute-done((bf16[4,7296]{1,0:T(4,128)(2,1)S(1)}, bf16[4,7296]{1,0:T(4,128)(2,1)S(1)}, u32[]{:S(2)}, u32[]{:S(2)}) %collective-permute-start.8) | collective-permute-done | bytes 58400 | tf_op jit(solution)/shard_map/spread/ppermute | solution.py:32
  53.2 1.3 %collective-permute-start.12 = (bf16[16,7296]{1,0:T(8,128)(2,1)S(1)}, bf16[16,7296]{1,0:T(8,128)(2,1)S(1)}, u32[]{:S(2)}, u32[]{:S(2)}) collective-permute-start(bf16[16,7296]{1,0:T(8,128)(2,1)S(1)} %pad_maximum_fusion.refs_0_), channel_id=1, source_target_pairs={{0,18},{1,13},{2,16},{3,15},{4,22},{5,9},{6,20},{7,11},{8,26},{9,5... | collective-permute-start | bytes 700424 | tf_op jit(solution)/shard_map/spread/ppermute | solution.py:32
  56.8 7.7 %load_experts.1 = (bf16[16,7296]{1,0:T(8,128)(2,1)S(1)}, bf16[7168,512]{1,0:T(8,128)(2,1)S(1)}, bf16[7168,512]{1,0:T(8,128)(2,1)S(1)}, bf16[512,7168]{1,0:T(8,128)(2,1)S(1)}) custom-call(bf16[16,7296]{1,0:T(8,128)(2,1)S(1)} %pad_maximum_fusion.refs_0_, bf16[7168,512]{1,0:T(8,128)(2,1)} %bitcast.26, bf16[7168,512]{1,0:T(8,128)(2,1)} %bitcast.27, ...), custom_call_target="tpu_custom_call" | custom-call | bytes 44040192 | tf_op jit(solution)/shard_map/spread/load_experts/pallas_call | solution.py:210
  67.1 3.6 %experts.1 = (f32[64,7168]{1,0:T(8,128)S(1)}, bf16[64,7168]{1,0:T(8,128)(2,1)S(1)}) custom-call(s32[1]{0:T(128)} %bitcast.me_ref, bf16[16,7296]{1,0:T(8,128)(2,1)S(1)} %pad_maximum_fusion.refs_0_, bf16[16,7296]{1,0:T(8,128)(2,1)S(1)} %collective-permute-done.10.refs_1_, bf16[16,7296]{1,0:T(8,128)(2,1)S(1)} %collective-permute-done.11.refs_2_, ...), custom_call_target="tpu_custom_call" | custom-call | flops 2818572288 | bytes 23887872 | tf_op jit(solution)/shard_map/experts/experts/pallas_call | solution.py:249
  70.9 2.3 %collective-permute-done.17 = bf16[64,7168]{1,0:T(8,128)(2,1)S(1)} collective-permute-done((bf16[64,7168]{1,0:T(8,128)(2,1)S(1)}, bf16[64,7168]{1,0:T(8,128)(2,1)S(1)}, u32[]{:S(2)}, u32[]{:S(2)}) %collective-permute-start.17) | collective-permute-done | bytes 917536 | tf_op jit(solution)/shard_map/collect/ppermute | solution.py:36
  73.5 1.3 %collective-permute-start.18 = (bf16[16,7168]{1,0:T(8,128)(2,1)S(1)}, bf16[16,7168]{1,0:T(8,128)(2,1)S(1)}, u32[]{:S(2)}, u32[]{:S(2)}) collective-permute-start(bf16[16,7168]{1,0:T(8,128)(2,1)S(1)} %get-tuple-element.35), channel_id=1, source_target_pairs={{0,18},{1,13},{2,16},{3,15},{4,22},{5,9},{6,20},{7,11},{8,26},{9,5... | collective-permute-start | bytes 688136 | tf_op jit(solution)/shard_map/collect/ppermute | solution.py:32
  74.8 1.4 %collective-permute-start.20 = (bf16[16,7168]{1,0:T(8,128)(2,1)S(1)}, bf16[16,7168]{1,0:T(8,128)(2,1)S(1)}, u32[]{:S(2)}, u32[]{:S(2)}) collective-permute-start(bf16[16,7168]{1,0:T(8,128)(2,1)S(1)} %get-tuple-element.36), channel_id=1, source_target_pairs={{0,2},{1,5},{2,0},{3,7},{4,6},{5,1},{6,4},{7,3},{8,10},{9,13},{10,... | collective-permute-start | bytes 688136 | tf_op jit(solution)/shard_map/collect/ppermute | solution.py:32
  77.0 3.5 %collective-permute-done.18 = bf16[16,7168]{1,0:T(8,128)(2,1)S(1)} collective-permute-done((bf16[16,7168]{1,0:T(8,128)(2,1)S(1)}, bf16[16,7168]{1,0:T(8,128)(2,1)S(1)}, u32[]{:S(2)}, u32[]{:S(2)}) %collective-permute-start.18) | collective-permute-done | bytes 229408 | tf_op jit(solution)/shard_map/collect/ppermute | solution.py:32
  80.6 2.4 %collective-permute-done.20 = bf16[16,7168]{1,0:T(8,128)(2,1)S(1)} collective-permute-done((bf16[16,7168]{1,0:T(8,128)(2,1)S(1)}, bf16[16,7168]{1,0:T(8,128)(2,1)S(1)}, u32[]{:S(2)}, u32[]{:S(2)}) %collective-permute-start.20) | collective-permute-done | bytes 229408 | tf_op jit(solution)/shard_map/collect/ppermute | solution.py:32
  84.2 1.7 %collective-permute-start.23 = (bf16[4,7168]{1,0:T(4,128)(2,1)S(1)}, bf16[4,7168]{1,0:T(4,128)(2,1)S(1)}, u32[]{:S(2)}, u32[]{:S(2)}) collective-permute-start(bf16[4,7168]{1,0:T(4,128)(2,1)S(1)} %get-tuple-element.42), channel_id=1, source_target_pairs={{0,12},{1,19},{2,14},{3,17},{4,8},{5,23},{6,10},{7,21},{8,4},{9,27... | collective-permute-start | bytes 172040 | tf_op jit(solution)/shard_map/collect/ppermute | solution.py:32
  87.4 2.8 %collective-permute-done.23 = bf16[4,7168]{1,0:T(4,128)(2,1)S(1)} collective-permute-done((bf16[4,7168]{1,0:T(4,128)(2,1)S(1)}, bf16[4,7168]{1,0:T(4,128)(2,1)S(1)}, u32[]{:S(2)}, u32[]{:S(2)}) %collective-permute-start.23) | collective-permute-done | bytes 57376 | tf_op jit(solution)/shard_map/collect/ppermute | solution.py:32
  (59 shorter events, 17.8 us)
Async XLA Ops:
  9.9 15.0 %all-to-all-start = ((bf16[32,4,512]{2,1,0:T(4,128)(2,1)}), bf16[32,4,512]{2,1,0:T(4,128)(2,1)S(1)}, u32[]{:S(2)}, u32[]{:S(2)}) async-start(bf16[32,4,512]{2,1,0:T(4,128)(2,1)} %attend.1), calls=%async_computation | async-start | bytes 262144 | tf_op jit(solution)/shard_map/heads/all_to_all | solution.py:306
  25.8 2.5 %collective-permute-start = (bf16[64,7168]{1,0:T(8,128)(2,1)S(1)}, bf16[64,7168]{1,0:T(8,128)(2,1)S(1)}, u32[]{:S(2)}, u32[]{:S(2)}) collective-permute-start(bf16[64,7168]{1,0:T(8,128)(2,1)S(1)} %get-tuple-element.16), channel_id=1, source_target_pairs={{0,1},{1,0},{2,3},{3,2},{4,5},{5,4},{6,7},{7,6},{8,9},{9,8},{10,11... | collective-permute-start | bytes 2752520 | tf_op jit(solution)/shard_map/heads/ppermute | solution.py:36
  28.7 7.1 %collective-permute-start.1 = (bf16[16,7168]{1,0:T(8,128)(2,1)S(1)}, bf16[16,7168]{1,0:T(8,128)(2,1)S(1)}, u32[]{:S(2)}, u32[]{:S(2)}) collective-permute-start(bf16[16,7168]{1,0:T(8,128)(2,1)S(1)} %get-tuple-element.38), channel_id=1, source_target_pairs={{0,18},{1,13},{2,16},{3,15},{4,22},{5,9},{6,20},{7,11},{8,26},{9,5... | collective-permute-start | bytes 688136 | tf_op jit(solution)/shard_map/heads/ppermute | solution.py:32
  29.3 8.5 %collective-permute-start.3 = (bf16[16,7168]{1,0:T(8,128)(2,1)S(1)}, bf16[16,7168]{1,0:T(8,128)(2,1)S(1)}, u32[]{:S(2)}, u32[]{:S(2)}) collective-permute-start(bf16[16,7168]{1,0:T(8,128)(2,1)S(1)} %get-tuple-element.39), channel_id=1, source_target_pairs={{0,2},{1,5},{2,0},{3,7},{4,6},{5,1},{6,4},{7,3},{8,10},{9,13},{10,... | collective-permute-start | bytes 688136 | tf_op jit(solution)/shard_map/heads/ppermute | solution.py:32
  31.0 6.7 %collective-permute-start.2 = (bf16[16,7168]{1,0:T(8,128)(2,1)S(1)}, bf16[16,7168]{1,0:T(8,128)(2,1)S(1)}, u32[]{:S(2)}, u32[]{:S(2)}) collective-permute-start(bf16[16,7168]{1,0:T(8,128)(2,1)S(1)} %get-tuple-element.40), channel_id=1, source_target_pairs={{0,16},{1,9},{2,18},{3,11},{4,20},{5,13},{6,22},{7,15},{8,24},{9,1... | collective-permute-start | bytes 688136 | tf_op jit(solution)/shard_map/heads/ppermute | solution.py:32
  37.9 6.0 %collective-permute-start.6 = (bf16[4,7168]{1,0:T(4,128)(2,1)S(1)}, bf16[4,7168]{1,0:T(4,128)(2,1)S(1)}, u32[]{:S(2)}, u32[]{:S(2)}) collective-permute-start(bf16[4,7168]{1,0:T(4,128)(2,1)S(1)} %get-tuple-element.44), channel_id=1, source_target_pairs={{0,12},{1,19},{2,14},{3,17},{4,8},{5,23},{6,10},{7,21},{8,4},{9,27... | collective-permute-start | bytes 172040 | tf_op jit(solution)/shard_map/heads/ppermute | solution.py:32
  39.6 5.6 %collective-permute-start.5 = (bf16[4,7168]{1,0:T(4,128)(2,1)S(1)}, bf16[4,7168]{1,0:T(4,128)(2,1)S(1)}, u32[]{:S(2)}, u32[]{:S(2)}) collective-permute-start(bf16[4,7168]{1,0:T(4,128)(2,1)S(1)} %get-tuple-element.45), channel_id=1, source_target_pairs={{0,8},{1,17},{2,10},{3,19},{4,12},{5,21},{6,14},{7,23},{8,0},{9,25... | collective-permute-start | bytes 172040 | tf_op jit(solution)/shard_map/heads/ppermute | solution.py:32
  39.9 5.3 %collective-permute-start.4 = (bf16[4,7168]{1,0:T(4,128)(2,1)S(1)}, bf16[4,7168]{1,0:T(4,128)(2,1)S(1)}, u32[]{:S(2)}, u32[]{:S(2)}) collective-permute-start(bf16[4,7168]{1,0:T(4,128)(2,1)S(1)} %get-tuple-element.46), channel_id=1, source_target_pairs={{0,4},{1,3},{2,6},{3,1},{4,0},{5,7},{6,2},{7,5},{8,12},{9,11},{10,... | collective-permute-start | bytes 172040 | tf_op jit(solution)/shard_map/heads/ppermute | solution.py:32
  45.4 6.1 %collective-permute-start.9 = (bf16[4,7296]{1,0:T(4,128)(2,1)S(1)}, bf16[4,7296]{1,0:T(4,128)(2,1)S(1)}, u32[]{:S(2)}, u32[]{:S(2)}) collective-permute-start(bf16[4,7296]{1,0:T(4,128)(2,1)S(1)} %get-tuple-element.18), channel_id=1, source_target_pairs={{0,12},{1,19},{2,14},{3,17},{4,8},{5,23},{6,10},{7,21},{8,4},{9,27... | collective-permute-start | bytes 175112 | tf_op jit(solution)/shard_map/spread/ppermute | solution.py:32
  47.2 5.6 %collective-permute-start.8 = (bf16[4,7296]{1,0:T(4,128)(2,1)S(1)}, bf16[4,7296]{1,0:T(4,128)(2,1)S(1)}, u32[]{:S(2)}, u32[]{:S(2)}) collective-permute-start(bf16[4,7296]{1,0:T(4,128)(2,1)S(1)} %get-tuple-element.18), channel_id=1, source_target_pairs={{0,8},{1,17},{2,10},{3,19},{4,12},{5,21},{6,14},{7,23},{8,0},{9,25... | collective-permute-start | bytes 175112 | tf_op jit(solution)/shard_map/spread/ppermute | solution.py:32
  48.3 4.8 %collective-permute-start.7 = (bf16[4,7296]{1,0:T(4,128)(2,1)S(1)}, bf16[4,7296]{1,0:T(4,128)(2,1)S(1)}, u32[]{:S(2)}, u32[]{:S(2)}) collective-permute-start(bf16[4,7296]{1,0:T(4,128)(2,1)S(1)} %get-tuple-element.18), channel_id=1, source_target_pairs={{0,4},{1,3},{2,6},{3,1},{4,0},{5,7},{6,2},{7,5},{8,12},{9,11},{10,... | collective-permute-start | bytes 175112 | tf_op jit(solution)/shard_map/spread/ppermute | solution.py:32
  53.2 11.4 %collective-permute-start.12 = (bf16[16,7296]{1,0:T(8,128)(2,1)S(1)}, bf16[16,7296]{1,0:T(8,128)(2,1)S(1)}, u32[]{:S(2)}, u32[]{:S(2)}) collective-permute-start(bf16[16,7296]{1,0:T(8,128)(2,1)S(1)} %pad_maximum_fusion.refs_0_), channel_id=1, source_target_pairs={{0,18},{1,13},{2,16},{3,15},{4,22},{5,9},{6,20},{7,11},{8,26},{9,5... | collective-permute-start | bytes 700424 | tf_op jit(solution)/shard_map/spread/ppermute | solution.py:32
  54.5 10.6 %collective-permute-start.11 = (bf16[16,7296]{1,0:T(8,128)(2,1)S(1)}, bf16[16,7296]{1,0:T(8,128)(2,1)S(1)}, u32[]{:S(2)}, u32[]{:S(2)}) collective-permute-start(bf16[16,7296]{1,0:T(8,128)(2,1)S(1)} %pad_maximum_fusion.refs_0_), channel_id=1, source_target_pairs={{0,16},{1,9},{2,18},{3,11},{4,20},{5,13},{6,22},{7,15},{8,24},{9,1... | collective-permute-start | bytes 700424 | tf_op jit(solution)/shard_map/spread/ppermute | solution.py:32
  55.8 9.4 %collective-permute-start.10 = (bf16[16,7296]{1,0:T(8,128)(2,1)S(1)}, bf16[16,7296]{1,0:T(8,128)(2,1)S(1)}, u32[]{:S(2)}, u32[]{:S(2)}) collective-permute-start(bf16[16,7296]{1,0:T(8,128)(2,1)S(1)} %pad_maximum_fusion.refs_0_), channel_id=1, source_target_pairs={{0,2},{1,5},{2,0},{3,7},{4,6},{5,1},{6,4},{7,3},{8,10},{9,13},{10,... | collective-permute-start | bytes 700424 | tf_op jit(solution)/shard_map/spread/ppermute | solution.py:32
  64.6 1.8 %collective-permute-start.16 = (bf16[16,7296]{1,0:T(8,128)(2,1)S(1)}, bf16[16,7296]{1,0:T(8,128)(2,1)S(1)}, u32[]{:S(2)}, u32[]{:S(2)}) collective-permute-start(bf16[16,7296]{1,0:T(8,128)(2,1)S(1)} %collective-permute-done.12.refs_3_), channel_id=1, source_target_pairs={{0,1},{1,0},{2,3},{3,2},{4,5},{5,4},{6,7},{7,6},{8,9},{9,8},{10,11... | collective-permute-start | bytes 700424 | tf_op jit(solution)/shard_map/spread/ppermute | solution.py:36
  65.1 1.6 %collective-permute-start.15 = (bf16[16,7296]{1,0:T(8,128)(2,1)S(1)}, bf16[16,7296]{1,0:T(8,128)(2,1)S(1)}, u32[]{:S(2)}, u32[]{:S(2)}) collective-permute-start(bf16[16,7296]{1,0:T(8,128)(2,1)S(1)} %collective-permute-done.11.refs_2_), channel_id=1, source_target_pairs={{0,1},{1,0},{2,3},{3,2},{4,5},{5,4},{6,7},{7,6},{8,9},{9,8},{10,11... | collective-permute-start | bytes 700424 | tf_op jit(solution)/shard_map/spread/ppermute | solution.py:36
  65.2 1.9 %collective-permute-start.14 = (bf16[16,7296]{1,0:T(8,128)(2,1)S(1)}, bf16[16,7296]{1,0:T(8,128)(2,1)S(1)}, u32[]{:S(2)}, u32[]{:S(2)}) collective-permute-start(bf16[16,7296]{1,0:T(8,128)(2,1)S(1)} %collective-permute-done.10.refs_1_), channel_id=1, source_target_pairs={{0,1},{1,0},{2,3},{3,2},{4,5},{5,4},{6,7},{7,6},{8,9},{9,8},{10,11... | collective-permute-start | bytes 700424 | tf_op jit(solution)/shard_map/spread/ppermute | solution.py:36
  70.7 2.5 %collective-permute-start.17 = (bf16[64,7168]{1,0:T(8,128)(2,1)S(1)}, bf16[64,7168]{1,0:T(8,128)(2,1)S(1)}, u32[]{:S(2)}, u32[]{:S(2)}) collective-permute-start(bf16[64,7168]{1,0:T(8,128)(2,1)S(1)} %get-tuple-element.24), channel_id=1, source_target_pairs={{0,1},{1,0},{2,3},{3,2},{4,5},{5,4},{6,7},{7,6},{8,9},{9,8},{10,11... | collective-permute-start | bytes 2752520 | tf_op jit(solution)/shard_map/collect/ppermute | solution.py:36
  73.5 7.1 %collective-permute-start.18 = (bf16[16,7168]{1,0:T(8,128)(2,1)S(1)}, bf16[16,7168]{1,0:T(8,128)(2,1)S(1)}, u32[]{:S(2)}, u32[]{:S(2)}) collective-permute-start(bf16[16,7168]{1,0:T(8,128)(2,1)S(1)} %get-tuple-element.35), channel_id=1, source_target_pairs={{0,18},{1,13},{2,16},{3,15},{4,22},{5,9},{6,20},{7,11},{8,26},{9,5... | collective-permute-start | bytes 688136 | tf_op jit(solution)/shard_map/collect/ppermute | solution.py:32
  74.8 8.2 %collective-permute-start.20 = (bf16[16,7168]{1,0:T(8,128)(2,1)S(1)}, bf16[16,7168]{1,0:T(8,128)(2,1)S(1)}, u32[]{:S(2)}, u32[]{:S(2)}) collective-permute-start(bf16[16,7168]{1,0:T(8,128)(2,1)S(1)} %get-tuple-element.36), channel_id=1, source_target_pairs={{0,2},{1,5},{2,0},{3,7},{4,6},{5,1},{6,4},{7,3},{8,10},{9,13},{10,... | collective-permute-start | bytes 688136 | tf_op jit(solution)/shard_map/collect/ppermute | solution.py:32
  76.2 6.8 %collective-permute-start.19 = (bf16[16,7168]{1,0:T(8,128)(2,1)S(1)}, bf16[16,7168]{1,0:T(8,128)(2,1)S(1)}, u32[]{:S(2)}, u32[]{:S(2)}) collective-permute-start(bf16[16,7168]{1,0:T(8,128)(2,1)S(1)} %get-tuple-element.37), channel_id=1, source_target_pairs={{0,16},{1,9},{2,18},{3,11},{4,20},{5,13},{6,22},{7,15},{8,24},{9,1... | collective-permute-start | bytes 688136 | tf_op jit(solution)/shard_map/collect/ppermute | solution.py:32
  83.1 4.2 %collective-permute-start.21 = (bf16[4,7168]{1,0:T(4,128)(2,1)S(1)}, bf16[4,7168]{1,0:T(4,128)(2,1)S(1)}, u32[]{:S(2)}, u32[]{:S(2)}) collective-permute-start(bf16[4,7168]{1,0:T(4,128)(2,1)S(1)} %get-tuple-element.41), channel_id=1, source_target_pairs={{0,4},{1,3},{2,6},{3,1},{4,0},{5,7},{6,2},{7,5},{8,12},{9,11},{10,... | collective-permute-start | bytes 172040 | tf_op jit(solution)/shard_map/collect/ppermute | solution.py:32
  84.2 6.0 %collective-permute-start.23 = (bf16[4,7168]{1,0:T(4,128)(2,1)S(1)}, bf16[4,7168]{1,0:T(4,128)(2,1)S(1)}, u32[]{:S(2)}, u32[]{:S(2)}) collective-permute-start(bf16[4,7168]{1,0:T(4,128)(2,1)S(1)} %get-tuple-element.42), channel_id=1, source_target_pairs={{0,12},{1,19},{2,14},{3,17},{4,8},{5,23},{6,10},{7,21},{8,4},{9,27... | collective-permute-start | bytes 172040 | tf_op jit(solution)/shard_map/collect/ppermute | solution.py:32
  85.9 5.5 %collective-permute-start.22 = (bf16[4,7168]{1,0:T(4,128)(2,1)S(1)}, bf16[4,7168]{1,0:T(4,128)(2,1)S(1)}, u32[]{:S(2)}, u32[]{:S(2)}) collective-permute-start(bf16[4,7168]{1,0:T(4,128)(2,1)S(1)} %get-tuple-element.43), channel_id=1, source_target_pairs={{0,8},{1,17},{2,10},{3,19},{4,12},{5,21},{6,14},{7,23},{8,0},{9,25... | collective-permute-start | bytes 172040 | tf_op jit(solution)/shard_map/collect/ppermute | solution.py:32
  (7 other events, 78.3 us)

commit v11 on v10

--- a/solution.py
+++ b/solution.py
@@ -20,6 +20,7 @@
 BF = jnp.bfloat16
 F32 = jnp.float32
 VMEM_LIMIT = 16 * 1024 * 1024
+LOAD_LIMIT, EXPERT_LIMIT = 34, 30
 
 
 def partners(n):
@@ -191,14 +192,14 @@
 
 
 def load_kernel(n, *refs):
-    sources, targets, sem = refs[1:4], refs[5:8], refs[8]
-    copies = [pltpu.make_async_copy(refs[0], refs[4], sem.at[12])]
-    for i in range(3):
-        step = sources[i].shape[0] // 4
-        for j in range(4):
+    sources, targets, sem = refs[1:3], refs[4:6], refs[6]
+    copies = [pltpu.make_async_copy(refs[0], refs[3], sem.at[16])]
+    for i in range(2):
+        step = sources[i].shape[0] // 8
+        for j in range(8):
             here = pl.ds(j * step, step)
             copies.append(
-                pltpu.make_async_copy(sources[i].at[here], targets[i].at[here], sem.at[4 * i + j])
+                pltpu.make_async_copy(sources[i].at[here], targets[i].at[here], sem.at[8 * i + j])
             )
     for copy in copies:
         copy.start()
@@ -209,11 +210,11 @@
 def load(n, passed, arrays):
     return pl.pallas_call(
         functools.partial(load_kernel, n),
-        in_specs=[pl.BlockSpec(memory_space=pltpu.VMEM)] + [pl.BlockSpec(memory_space=pl.ANY)] * 3,
-        out_specs=[pl.BlockSpec(memory_space=pltpu.VMEM)] * 4,
+        in_specs=[pl.BlockSpec(memory_space=pltpu.VMEM)] + [pl.BlockSpec(memory_space=pl.ANY)] * 2,
+        out_specs=[pl.BlockSpec(memory_space=pltpu.VMEM)] * 3,
         out_shape=[jax.ShapeDtypeStruct(a.shape, a.dtype) for a in [passed] + arrays],
-        scratch_shapes=[pltpu.SemaphoreType.DMA((13,))],
-        compiler_params=pltpu.CompilerParams(vmem_limit_bytes=28 * 1024 * 1024),
+        scratch_shapes=[pltpu.SemaphoreType.DMA((17,))],
+        compiler_params=pltpu.CompilerParams(vmem_limit_bytes=LOAD_LIMIT * 1024 * 1024),
         cost_estimate=pl.CostEstimate(
             flops=0, bytes_accessed=sum(4 * a.size for a in arrays), transcendentals=0
         ),
@@ -221,8 +222,15 @@
     )(passed, *arrays)
 
 
-def expert_kernel(n, me_ref, *refs, n_ep):
-    blocks, (gate_ref, up_ref, down_ref, near_ref, far_ref) = refs[:8], refs[8:]
+def expert_kernel(n, n_ep, me_ref, *refs):
+    blocks, (gate_ref, up_ref, down_hbm, near_ref, far_ref, down_ref, sem) = refs[:8], refs[8:]
+    step = down_ref.shape[0] // 8
+    copies = []
+    for j in range(8):
+        here = pl.ds(j * step, step)
+        copies.append(pltpu.make_async_copy(down_hbm.at[here], down_ref.at[here], sem.at[j]))
+    for copy in copies:
+        copy.start()
     rows = n * STEPS
     width, units = gate_ref.shape
     part = width // SPAN
@@ -238,11 +246,33 @@
     scores = routes[:, TOPK : 2 * TOPK] + routes[:, 2 * TOPK : 3 * TOPK]
     chosen = jnp.where(routes[:, :TOPK] == (me_ref[0] % n_ep).astype(F32), scores, 0.0)
     coef = jnp.sum(chosen, axis=1, keepdims=True) / jnp.sum(scores, axis=1, keepdims=True) * 2.5
+    for copy in copies:
+        copy.wait()
     for p in range(SPAN):
         here = slice(p * part, (p + 1) * part)
         out = jnp.dot(act, down_ref[:, here], preferred_element_type=F32) * coef
         near_ref[:, here] = out[: rows // 2]
         far_ref[:, here] = out[rows // 2 :].astype(BF)
+
+
+def run_experts(n, n_ep, me, blocks, gate, up, down):
+    rows = n * STEPS
+    units, width = down.shape
+    return pl.pallas_call(
+        functools.partial(expert_kernel, n, n_ep),
+        in_specs=[pl.BlockSpec(memory_space=pltpu.SMEM)]
+        + [pl.BlockSpec(memory_space=pltpu.VMEM)] * (len(blocks) + 2)
+        + [pl.BlockSpec(memory_space=pl.ANY)],
+        out_shape=[jax.ShapeDtypeStruct((rows // 2, width), dtype) for dtype in (F32, BF)],
+        scratch_shapes=[pltpu.VMEM(down.shape, BF), pltpu.SemaphoreType.DMA((8,))],
+        compiler_params=pltpu.CompilerParams(vmem_limit_bytes=EXPERT_LIMIT * 1024 * 1024),
+        cost_estimate=pl.CostEstimate(
+            flops=6 * rows * width * units,
+            bytes_accessed=6 * width * units,
+            transcendentals=rows * units,
+        ),
+        name="experts",
+    )(me, *blocks, gate, up, down)
 
 
 def single(kernel, n, out_shape, scalars, arrays, name, flops):
@@ -259,14 +289,15 @@
     )(*scalars, *arrays)
 
 
-def reduce_rows(near, far, n):
+def reduce_rows(near, far, n, beside=lambda rows: rows):
     firsts, seconds = (len(masks) for masks in partners(n)[0])
     width = near.shape[1]
     total = near + swap_core(far, n).astype(F32)
     total = total.reshape(firsts, seconds * STEPS, width)
-    kept = total[0]
-    for i in reversed(range(1, firsts)):
-        kept = kept + swap(total[i].astype(BF), n, 0, i).astype(F32)
+    got = [swap(total[i].astype(BF), n, 0, i) for i in range(1, firsts)]
+    kept = beside(total[0])
+    for term in reversed(got):
+        kept = kept + term.astype(F32)
     kept = kept.reshape(seconds, STEPS, width)
     return [kept[0]] + [swap(kept[j].astype(BF), n, 1, j) for j in range(1, seconds)]
 
@@ -313,7 +344,14 @@
             "heads",
             2 * rows * VDIM * (LAT + width),
         )
-        parts = reduce_rows(near, far, n)
+        loaded = []
+
+        def load_beside(rows):
+            rows, *weights = load(n, rows, [w_gate[0], w_up[0]])
+            loaded.extend(weights)
+            return rows
+
+        parts = reduce_rows(near, far, n, load_beside)
 
     with jax.named_scope("norm"):
         high = route_scores[0].astype(BF)
@@ -337,19 +375,10 @@
         along = [normed] + [swap(normed, n, 1, j) for j in range(1, n // SPAN)]
         along = jnp.concatenate(along, axis=0)
         blocks = [along] + [swap(along, n, 0, i) for i in range(1, 4)]
-        along, *weights = load(n, along, [w_gate[0], w_up[0], w_down[0]])
-        blocks = blocks + [swap_core(x, n) for x in [along] + blocks[1:]]
+        blocks = blocks + [swap_core(x, n) for x in blocks]
 
     with jax.named_scope("experts"):
-        near, far = single(
-            functools.partial(expert_kernel, n_ep=n_ep),
-            n,
-            [jax.ShapeDtypeStruct((rows // 2, width), dtype) for dtype in (F32, BF)],
-            [me_one],
-            blocks + weights,
-            "experts",
-            6 * rows * width * w_gate.shape[2],
-        )
+        near, far = run_experts(n, n_ep, me_one, blocks, *loaded, w_down[0])
 
     with jax.named_scope("collect"):
         result = hidden

time: 92.1 us -> 93.6 us (1.016)
  starting transfers between devices: 31.5 us -> 37.4 us
  Pallas kernels: 21.6 us -> 18 us
  waiting for transfers between devices: 36.2 us -> 35.1 us
    pallas_call x0 -> x1, Pallas kernels: none -> 6.68 us  [run_experts(): pl.pallas_call(functools.partial(expert_kernel, n, n_ep), in_specs=[pl.Bl...]
    all_to_all x1, starting transfers between devices: 6.74 us -> 11.9 us  [per_device(): latents = lax.all_to_all(latents, AXES, 0, 0, tiled=True)]
    pallas_call x1, Pallas kernels: 9.22 us -> 4.58 us  [attend(): pl.pallas_call(functools.partial(attend_kernel, n), in_specs=[pl.BlockSpe...]
    pallas_call x3 -> x2, Pallas kernels: 4.7 us -> 1.13 us  [single(): pl.pallas_call(functools.partial(kernel, n), in_specs=[pl.BlockSpec(memor...]
    pallas_call x1, Pallas kernels: 7.71 us -> 5.61 us  [load(): pl.pallas_call(functools.partial(load_kernel, n), in_specs=[pl.BlockSpec(...]
  transfers between devices with their start and end apart: 25 -> 25, of which waited for: 19 -> 17; matrix products, arithmetic and copies ran while one was open for 0% -> 0% of each run, Pallas kernels for 8% -> 6%
where the time goes in v11:
time: 93.6 us; the launch traced here: 93.4 us
  starting transfers between devices  37.4 us (40%)
  waiting for transfers between devices  35.1 us (38%)
  Pallas kernels  18 us (19%)
  other arithmetic  1.59 us (2%)
    ppermute x18, starting transfers between devices, swap(): lax.ppermute(x, AXES, [(d, d ^ partners(n)[d & 1][stage][i]) for d in ran...  23.1 us
    ppermute x18, waiting for transfers between devices, swap(): lax.ppermute(x, AXES, [(d, d ^ partners(n)[d & 1][stage][i]) for d in ran...  21 us
    all_to_all x1, starting transfers between devices, per_device(): latents = lax.all_to_all(latents, AXES, 0, 0, tiled=True)  11.9 us
    all_to_all x1, waiting for transfers between devices, per_device(): latents = lax.all_to_all(latents, AXES, 0, 0, tiled=True)  8.22 us
    pallas_call x1, Pallas kernels, run_experts(): pl.pallas_call(functools.partial(expert_kernel, n, n_ep), in_specs=[pl.Bl...  6.68 us
    ppermute x6, waiting for transfers between devices, swap_core(): return lax.ppermute(x, AXES, [(d, d ^ 1) for d in range(n)])  5.86 us
    pallas_call x1, Pallas kernels, load(): pl.pallas_call(functools.partial(load_kernel, n), in_specs=[pl.BlockSpec(...  5.61 us
    pallas_call x1, Pallas kernels, attend(): pl.pallas_call(functools.partial(attend_kernel, n), in_specs=[pl.BlockSpe...  4.58 us
  transfers between devices with their start and end apart: 25, of which 17 were waited for; matrix products, arithmetic and copies ran while one was open for 0% of the time, Pallas kernels for 6%

profile of v11, /device:TPU:0, one launch (start us, length us, event | category | flops | bytes accessed | tf_op | source)
XLA Modules:
  0.0 93.4 jit_solution(509125990907938016)
XLA Ops:
  0.7 4.6 %attend.1 = bf16[32,4,512]{2,1,0:T(4,128)(2,1)} custom-call(s32[1]{0:T(128)S(6)} %copy.14.len_ref, bf16[128,576]{1,0:T(8,128)(2,1)} %bitcast.29, bf16[4,576]{1,0:T(4,128)(2,1)} %bitcast.30, bf16[576,8192]{1,0:T(8,128)(2,1)} %bitcast.25), custom_call_target="tpu_custom_call" | custom-call | flops 2281701376 | bytes 9437184 | tf_op jit(solution)/shard_map/attention/attend/pallas_call | solution.py:128
  5.3 11.9 %all-to-all-start = ((bf16[32,4,512]{2,1,0:T(4,128)(2,1)}), bf16[32,4,512]{2,1,0:T(4,128)(2,1)S(1)}, u32[]{:S(2)}, u32[]{:S(2)}) async-start(bf16[32,4,512]{2,1,0:T(4,128)(2,1)} %attend.1), calls=%async_computation | async-start | bytes 262144 | tf_op jit(solution)/shard_map/heads/all_to_all | solution.py:337
  17.2 8.2 %all-to-all-done = bf16[32,4,512]{2,1,0:T(4,128)(2,1)S(1)} async-done(((bf16[32,4,512]{2,1,0:T(4,128)(2,1)}), bf16[32,4,512]{2,1,0:T(4,128)(2,1)S(1)}, u32[]{:S(2)}, u32[]{:S(2)}) %all-to-all-start) | async-done | bytes 131104 | tf_op jit(solution)/shard_map/heads/all_to_all | solution.py:337
  26.7 2.2 %collective-permute-done = bf16[64,7168]{1,0:T(8,128)(2,1)S(1)} collective-permute-done((bf16[64,7168]{1,0:T(8,128)(2,1)S(1)}, bf16[64,7168]{1,0:T(8,128)(2,1)S(1)}, u32[]{:S(2)}, u32[]{:S(2)}) %collective-permute-start) | collective-permute-done | bytes 917536 | tf_op jit(solution)/shard_map/heads/ppermute | solution.py:37
  29.8 1.7 %collective-permute-start.3 = (bf16[16,7168]{1,0:T(8,128)(2,1)S(1)}, bf16[16,7168]{1,0:T(8,128)(2,1)S(1)}, u32[]{:S(2)}, u32[]{:S(2)}) collective-permute-start(bf16[16,7168]{1,0:T(8,128)(2,1)S(1)} %get-tuple-element.37), channel_id=1, source_target_pairs={{0,2},{1,5},{2,0},{3,7},{4,6},{5,1},{6,4},{7,3},{8,10},{9,13},{10,... | collective-permute-start | bytes 688136 | tf_op jit(solution)/shard_map/heads/ppermute | solution.py:33
  32.9 5.6 %load_experts.1 = (f32[16,7168]{1,0:T(8,128)S(1)}, bf16[7168,512]{1,0:T(8,128)(2,1)S(1)}, bf16[7168,512]{1,0:T(8,128)(2,1)S(1)}) custom-call(f32[16,7168]{1,0:T(8,128)S(1)} %slice.92.refs_0_, bf16[7168,512]{1,0:T(8,128)(2,1)} %bitcast.26, bf16[7168,512]{1,0:T(8,128)(2,1)} %bitcast.27), custom_call_target="tpu_custom_call" | custom-call | bytes 29360128 | tf_op jit(solution)/shard_map/heads/load_experts/pallas_call | solution.py:211
  38.8 1.4 %collective-permute-start.6 = (bf16[4,7168]{1,0:T(4,128)(2,1)S(1)}, bf16[4,7168]{1,0:T(4,128)(2,1)S(1)}, u32[]{:S(2)}, u32[]{:S(2)}) collective-permute-start(bf16[4,7168]{1,0:T(4,128)(2,1)S(1)} %get-tuple-element.42), channel_id=1, source_target_pairs={{0,12},{1,19},{2,14},{3,17},{4,8},{5,23},{6,10},{7,21},{8,4},{9,27... | collective-permute-start | bytes 172040 | tf_op jit(solution)/shard_map/heads/ppermute | solution.py:33
  40.5 2.7 %collective-permute-start.4 = (bf16[4,7168]{1,0:T(4,128)(2,1)S(1)}, bf16[4,7168]{1,0:T(4,128)(2,1)S(1)}, u32[]{:S(2)}, u32[]{:S(2)}) collective-permute-start(bf16[4,7168]{1,0:T(4,128)(2,1)S(1)} %get-tuple-element.44), channel_id=1, source_target_pairs={{0,4},{1,3},{2,6},{3,1},{4,0},{5,7},{6,2},{7,5},{8,12},{9,11},{10,... | collective-permute-start | bytes 172040 | tf_op jit(solution)/shard_map/heads/ppermute | solution.py:33
  43.3 1.5 %collective-permute-done.6.refs_3_ = bf16[4,7168]{1,0:T(4,128)(2,1)S(1)} collective-permute-done((bf16[4,7168]{1,0:T(4,128)(2,1)S(1)}, bf16[4,7168]{1,0:T(4,128)(2,1)S(1)}, u32[]{:S(2)}, u32[]{:S(2)}) %collective-permute-start.6) | collective-permute-done | bytes 57376 | tf_op jit(solution)/shard_map/heads/ppermute | solution.py:33
  46.2 1.8 %collective-permute-start.9 = (bf16[4,7296]{1,0:T(4,128)(2,1)S(1)}, bf16[4,7296]{1,0:T(4,128)(2,1)S(1)}, u32[]{:S(2)}, u32[]{:S(2)}) collective-permute-start(bf16[4,7296]{1,0:T(4,128)(2,1)S(1)} %get-tuple-element.18), channel_id=1, source_target_pairs={{0,12},{1,19},{2,14},{3,17},{4,8},{5,23},{6,10},{7,21},{8,4},{9,27... | collective-permute-start | bytes 175112 | tf_op jit(solution)/shard_map/spread/ppermute | solution.py:33
  49.1 1.6 %collective-permute-start.7 = (bf16[4,7296]{1,0:T(4,128)(2,1)S(1)}, bf16[4,7296]{1,0:T(4,128)(2,1)S(1)}, u32[]{:S(2)}, u32[]{:S(2)}) collective-permute-start(bf16[4,7296]{1,0:T(4,128)(2,1)S(1)} %get-tuple-element.18), channel_id=1, source_target_pairs={{0,4},{1,3},{2,6},{3,1},{4,0},{5,7},{6,2},{7,5},{8,12},{9,11},{10,... | collective-permute-start | bytes 175112 | tf_op jit(solution)/shard_map/spread/ppermute | solution.py:33
  50.7 1.6 %collective-permute-done.9 = bf16[4,7296]{1,0:T(4,128)(2,1)S(1)} collective-permute-done((bf16[4,7296]{1,0:T(4,128)(2,1)S(1)}, bf16[4,7296]{1,0:T(4,128)(2,1)S(1)}, u32[]{:S(2)}, u32[]{:S(2)}) %collective-permute-start.9) | collective-permute-done | bytes 58400 | tf_op jit(solution)/shard_map/spread/ppermute | solution.py:33
  52.3 1.4 %collective-permute-done.8 = bf16[4,7296]{1,0:T(4,128)(2,1)S(1)} collective-permute-done((bf16[4,7296]{1,0:T(4,128)(2,1)S(1)}, bf16[4,7296]{1,0:T(4,128)(2,1)S(1)}, u32[]{:S(2)}, u32[]{:S(2)}) %collective-permute-start.8) | collective-permute-done | bytes 58400 | tf_op jit(solution)/shard_map/spread/ppermute | solution.py:33
  57.6 3.6 %collective-permute-done.12.refs_3_ = bf16[16,7296]{1,0:T(8,128)(2,1)S(1)} collective-permute-done((bf16[16,7296]{1,0:T(8,128)(2,1)S(1)}, bf16[16,7296]{1,0:T(8,128)(2,1)S(1)}, u32[]{:S(2)}, u32[]{:S(2)}) %collective-permute-start.12) | collective-permute-done | bytes 233504 | tf_op jit(solution)/shard_map/spread/ppermute | solution.py:33
  61.2 1.7 %collective-permute-done.11.refs_2_ = bf16[16,7296]{1,0:T(8,128)(2,1)S(1)} collective-permute-done((bf16[16,7296]{1,0:T(8,128)(2,1)S(1)}, bf16[16,7296]{1,0:T(8,128)(2,1)S(1)}, u32[]{:S(2)}, u32[]{:S(2)}) %collective-permute-start.11) | collective-permute-done | bytes 233504 | tf_op jit(solution)/shard_map/spread/ppermute | solution.py:33
  62.9 1.7 %collective-permute-start.15 = (bf16[16,7296]{1,0:T(8,128)(2,1)S(1)}, bf16[16,7296]{1,0:T(8,128)(2,1)S(1)}, u32[]{:S(2)}, u32[]{:S(2)}) collective-permute-start(bf16[16,7296]{1,0:T(8,128)(2,1)S(1)} %collective-permute-done.11.refs_2_), channel_id=1, source_target_pairs={{0,1},{1,0},{2,3},{3,2},{4,5},{5,4},{6,7},{7,6},{8,9},{9,8},{10,11... | collective-permute-start | bytes 700424 | tf_op jit(solution)/shard_map/spread/ppermute | solution.py:37
  66.0 6.7 %experts.1 = (f32[64,7168]{1,0:T(8,128)S(1)}, bf16[64,7168]{1,0:T(8,128)(2,1)S(1)}) custom-call(s32[1]{0:T(128)} %bitcast.me_ref, bf16[16,7296]{1,0:T(8,128)(2,1)S(1)} %pad_maximum_fusion.refs_0_, bf16[16,7296]{1,0:T(8,128)(2,1)S(1)} %collective-permute-done.10.refs_1_, bf16[16,7296]{1,0:T(8,128)(2,1)S(1)} %collective-permute-done.11.refs_2_, ...), custom_call_target="tpu_custom_call" | custom-call | flops 2818572288 | bytes 22020096 | tf_op jit(solution)/shard_map/experts/experts/pallas_call | solution.py:261
  73.1 2.2 %collective-permute-done.17 = bf16[64,7168]{1,0:T(8,128)(2,1)S(1)} collective-permute-done((bf16[64,7168]{1,0:T(8,128)(2,1)S(1)}, bf16[64,7168]{1,0:T(8,128)(2,1)S(1)}, u32[]{:S(2)}, u32[]{:S(2)}) %collective-permute-start.17) | collective-permute-done | bytes 917536 | tf_op jit(solution)/shard_map/collect/ppermute | solution.py:37
  76.5 1.4 %collective-permute-start.20 = (bf16[16,7168]{1,0:T(8,128)(2,1)S(1)}, bf16[16,7168]{1,0:T(8,128)(2,1)S(1)}, u32[]{:S(2)}, u32[]{:S(2)}) collective-permute-start(bf16[16,7168]{1,0:T(8,128)(2,1)S(1)} %get-tuple-element.34), channel_id=1, source_target_pairs={{0,2},{1,5},{2,0},{3,7},{4,6},{5,1},{6,4},{7,3},{8,10},{9,13},{10,... | collective-permute-start | bytes 688136 | tf_op jit(solution)/shard_map/collect/ppermute | solution.py:33
  79.1 3.5 %collective-permute-done.18 = bf16[16,7168]{1,0:T(8,128)(2,1)S(1)} collective-permute-done((bf16[16,7168]{1,0:T(8,128)(2,1)S(1)}, bf16[16,7168]{1,0:T(8,128)(2,1)S(1)}, u32[]{:S(2)}, u32[]{:S(2)}) %collective-permute-start.18) | collective-permute-done | bytes 229408 | tf_op jit(solution)/shard_map/collect/ppermute | solution.py:33
  82.6 2.3 %collective-permute-done.20 = bf16[16,7168]{1,0:T(8,128)(2,1)S(1)} collective-permute-done((bf16[16,7168]{1,0:T(8,128)(2,1)S(1)}, bf16[16,7168]{1,0:T(8,128)(2,1)S(1)}, u32[]{:S(2)}, u32[]{:S(2)}) %collective-permute-start.20) | collective-permute-done | bytes 229408 | tf_op jit(solution)/shard_map/collect/ppermute | solution.py:33
  85.3 1.7 %collective-permute-start.23 = (bf16[4,7168]{1,0:T(4,128)(2,1)S(1)}, bf16[4,7168]{1,0:T(4,128)(2,1)S(1)}, u32[]{:S(2)}, u32[]{:S(2)}) collective-permute-start(bf16[4,7168]{1,0:T(4,128)(2,1)S(1)} %get-tuple-element.40), channel_id=1, source_target_pairs={{0,12},{1,19},{2,14},{3,17},{4,8},{5,23},{6,10},{7,21},{8,4},{9,27... | collective-permute-start | bytes 172040 | tf_op jit(solution)/shard_map/collect/ppermute | solution.py:33
  87.0 1.7 %collective-permute-start.22 = (bf16[4,7168]{1,0:T(4,128)(2,1)S(1)}, bf16[4,7168]{1,0:T(4,128)(2,1)S(1)}, u32[]{:S(2)}, u32[]{:S(2)}) collective-permute-start(bf16[4,7168]{1,0:T(4,128)(2,1)S(1)} %get-tuple-element.41), channel_id=1, source_target_pairs={{0,8},{1,17},{2,10},{3,19},{4,12},{5,21},{6,14},{7,23},{8,0},{9,25... | collective-permute-start | bytes 172040 | tf_op jit(solution)/shard_map/collect/ppermute | solution.py:33
  89.4 2.0 %collective-permute-done.23 = bf16[4,7168]{1,0:T(4,128)(2,1)S(1)} collective-permute-done((bf16[4,7168]{1,0:T(4,128)(2,1)S(1)}, bf16[4,7168]{1,0:T(4,128)(2,1)S(1)}, u32[]{:S(2)}, u32[]{:S(2)}) %collective-permute-start.23) | collective-permute-done | bytes 57376 | tf_op jit(solution)/shard_map/collect/ppermute | solution.py:33
  (60 shorter events, 18.0 us)
Async XLA Ops:
  5.3 20.2 %all-to-all-start = ((bf16[32,4,512]{2,1,0:T(4,128)(2,1)}), bf16[32,4,512]{2,1,0:T(4,128)(2,1)S(1)}, u32[]{:S(2)}, u32[]{:S(2)}) async-start(bf16[32,4,512]{2,1,0:T(4,128)(2,1)} %attend.1), calls=%async_computation | async-start | bytes 262144 | tf_op jit(solution)/shard_map/heads/all_to_all | solution.py:337
  26.4 2.5 %collective-permute-start = (bf16[64,7168]{1,0:T(8,128)(2,1)S(1)}, bf16[64,7168]{1,0:T(8,128)(2,1)S(1)}, u32[]{:S(2)}, u32[]{:S(2)}) collective-permute-start(bf16[64,7168]{1,0:T(8,128)(2,1)S(1)} %get-tuple-element.15), channel_id=1, source_target_pairs={{0,1},{1,0},{2,3},{3,2},{4,5},{5,4},{6,7},{7,6},{8,9},{9,8},{10,11... | collective-permute-start | bytes 2752520 | tf_op jit(solution)/shard_map/heads/ppermute | solution.py:37
  29.2 9.3 %collective-permute-start.1 = (bf16[16,7168]{1,0:T(8,128)(2,1)S(1)}, bf16[16,7168]{1,0:T(8,128)(2,1)S(1)}, u32[]{:S(2)}, u32[]{:S(2)}) collective-permute-start(bf16[16,7168]{1,0:T(8,128)(2,1)S(1)} %get-tuple-element.36), channel_id=1, source_target_pairs={{0,18},{1,13},{2,16},{3,15},{4,22},{5,9},{6,20},{7,11},{8,26},{9,5... | collective-permute-start | bytes 688136 | tf_op jit(solution)/shard_map/heads/ppermute | solution.py:33
  29.8 8.7 %collective-permute-start.3 = (bf16[16,7168]{1,0:T(8,128)(2,1)S(1)}, bf16[16,7168]{1,0:T(8,128)(2,1)S(1)}, u32[]{:S(2)}, u32[]{:S(2)}) collective-permute-start(bf16[16,7168]{1,0:T(8,128)(2,1)S(1)} %get-tuple-element.37), channel_id=1, source_target_pairs={{0,2},{1,5},{2,0},{3,7},{4,6},{5,1},{6,4},{7,3},{8,10},{9,13},{10,... | collective-permute-start | bytes 688136 | tf_op jit(solution)/shard_map/heads/ppermute | solution.py:33
  31.5 7.0 %collective-permute-start.2 = (bf16[16,7168]{1,0:T(8,128)(2,1)S(1)}, bf16[16,7168]{1,0:T(8,128)(2,1)S(1)}, u32[]{:S(2)}, u32[]{:S(2)}) collective-permute-start(bf16[16,7168]{1,0:T(8,128)(2,1)S(1)} %get-tuple-element.38), channel_id=1, source_target_pairs={{0,16},{1,9},{2,18},{3,11},{4,20},{5,13},{6,22},{7,15},{8,24},{9,1... | collective-permute-start | bytes 688136 | tf_op jit(solution)/shard_map/heads/ppermute | solution.py:33
  38.8 6.1 %collective-permute-start.6 = (bf16[4,7168]{1,0:T(4,128)(2,1)S(1)}, bf16[4,7168]{1,0:T(4,128)(2,1)S(1)}, u32[]{:S(2)}, u32[]{:S(2)}) collective-permute-start(bf16[4,7168]{1,0:T(4,128)(2,1)S(1)} %get-tuple-element.42), channel_id=1, source_target_pairs={{0,12},{1,19},{2,14},{3,17},{4,8},{5,23},{6,10},{7,21},{8,4},{9,27... | collective-permute-start | bytes 172040 | tf_op jit(solution)/shard_map/heads/ppermute | solution.py:33
  40.1 5.9 %collective-permute-start.5 = (bf16[4,7168]{1,0:T(4,128)(2,1)S(1)}, bf16[4,7168]{1,0:T(4,128)(2,1)S(1)}, u32[]{:S(2)}, u32[]{:S(2)}) collective-permute-start(bf16[4,7168]{1,0:T(4,128)(2,1)S(1)} %get-tuple-element.43), channel_id=1, source_target_pairs={{0,8},{1,17},{2,10},{3,19},{4,12},{5,21},{6,14},{7,23},{8,0},{9,25... | collective-permute-start | bytes 172040 | tf_op jit(solution)/shard_map/heads/ppermute | solution.py:33
  40.5 5.5 %collective-permute-start.4 = (bf16[4,7168]{1,0:T(4,128)(2,1)S(1)}, bf16[4,7168]{1,0:T(4,128)(2,1)S(1)}, u32[]{:S(2)}, u32[]{:S(2)}) collective-permute-start(bf16[4,7168]{1,0:T(4,128)(2,1)S(1)} %get-tuple-element.44), channel_id=1, source_target_pairs={{0,4},{1,3},{2,6},{3,1},{4,0},{5,7},{6,2},{7,5},{8,12},{9,11},{10,... | collective-permute-start | bytes 172040 | tf_op jit(solution)/shard_map/heads/ppermute | solution.py:33
  46.2 6.1 %collective-permute-start.9 = (bf16[4,7296]{1,0:T(4,128)(2,1)S(1)}, bf16[4,7296]{1,0:T(4,128)(2,1)S(1)}, u32[]{:S(2)}, u32[]{:S(2)}) collective-permute-start(bf16[4,7296]{1,0:T(4,128)(2,1)S(1)} %get-tuple-element.18), channel_id=1, source_target_pairs={{0,12},{1,19},{2,14},{3,17},{4,8},{5,23},{6,10},{7,21},{8,4},{9,27... | collective-permute-start | bytes 175112 | tf_op jit(solution)/shard_map/spread/ppermute | solution.py:33
  48.0 5.6 %collective-permute-start.8 = (bf16[4,7296]{1,0:T(4,128)(2,1)S(1)}, bf16[4,7296]{1,0:T(4,128)(2,1)S(1)}, u32[]{:S(2)}, u32[]{:S(2)}) collective-permute-start(bf16[4,7296]{1,0:T(4,128)(2,1)S(1)} %get-tuple-element.18), channel_id=1, source_target_pairs={{0,8},{1,17},{2,10},{3,19},{4,12},{5,21},{6,14},{7,23},{8,0},{9,25... | collective-permute-start | bytes 175112 | tf_op jit(solution)/shard_map/spread/ppermute | solution.py:33
  49.1 4.8 %collective-permute-start.7 = (bf16[4,7296]{1,0:T(4,128)(2,1)S(1)}, bf16[4,7296]{1,0:T(4,128)(2,1)S(1)}, u32[]{:S(2)}, u32[]{:S(2)}) collective-permute-start(bf16[4,7296]{1,0:T(4,128)(2,1)S(1)} %get-tuple-element.18), channel_id=1, source_target_pairs={{0,4},{1,3},{2,6},{3,1},{4,0},{5,7},{6,2},{7,5},{8,12},{9,11},{10,... | collective-permute-start | bytes 175112 | tf_op jit(solution)/shard_map/spread/ppermute | solution.py:33
  54.1 7.1 %collective-permute-start.12 = (bf16[16,7296]{1,0:T(8,128)(2,1)S(1)}, bf16[16,7296]{1,0:T(8,128)(2,1)S(1)}, u32[]{:S(2)}, u32[]{:S(2)}) collective-permute-start(bf16[16,7296]{1,0:T(8,128)(2,1)S(1)} %pad_maximum_fusion.refs_0_), channel_id=1, source_target_pairs={{0,18},{1,13},{2,16},{3,15},{4,22},{5,9},{6,20},{7,11},{8,26},{9,5... | collective-permute-start | bytes 700424 | tf_op jit(solution)/shard_map/spread/ppermute | solution.py:33
  55.1 7.8 %collective-permute-start.11 = (bf16[16,7296]{1,0:T(8,128)(2,1)S(1)}, bf16[16,7296]{1,0:T(8,128)(2,1)S(1)}, u32[]{:S(2)}, u32[]{:S(2)}) collective-permute-start(bf16[16,7296]{1,0:T(8,128)(2,1)S(1)} %pad_maximum_fusion.refs_0_), channel_id=1, source_target_pairs={{0,16},{1,9},{2,18},{3,11},{4,20},{5,13},{6,22},{7,15},{8,24},{9,1... | collective-permute-start | bytes 700424 | tf_op jit(solution)/shard_map/spread/ppermute | solution.py:33
  56.3 8.2 %collective-permute-start.10 = (bf16[16,7296]{1,0:T(8,128)(2,1)S(1)}, bf16[16,7296]{1,0:T(8,128)(2,1)S(1)}, u32[]{:S(2)}, u32[]{:S(2)}) collective-permute-start(bf16[16,7296]{1,0:T(8,128)(2,1)S(1)} %pad_maximum_fusion.refs_0_), channel_id=1, source_target_pairs={{0,2},{1,5},{2,0},{3,7},{4,6},{5,1},{6,4},{7,3},{8,10},{9,13},{10,... | collective-permute-start | bytes 700424 | tf_op jit(solution)/shard_map/spread/ppermute | solution.py:33
  57.6 6.9 %collective-permute-start.13 = (bf16[16,7296]{1,0:T(8,128)(2,1)S(1)}, bf16[16,7296]{1,0:T(8,128)(2,1)S(1)}, u32[]{:S(2)}, u32[]{:S(2)}) collective-permute-start(bf16[16,7296]{1,0:T(8,128)(2,1)S(1)} %pad_maximum_fusion.refs_0_), channel_id=1, source_target_pairs={{0,1},{1,0},{2,3},{3,2},{4,5},{5,4},{6,7},{7,6},{8,9},{9,8},{10,11... | collective-permute-start | bytes 700424 | tf_op jit(solution)/shard_map/spread/ppermute | solution.py:37
  61.2 3.3 %collective-permute-start.16 = (bf16[16,7296]{1,0:T(8,128)(2,1)S(1)}, bf16[16,7296]{1,0:T(8,128)(2,1)S(1)}, u32[]{:S(2)}, u32[]{:S(2)}) collective-permute-start(bf16[16,7296]{1,0:T(8,128)(2,1)S(1)} %collective-permute-done.12.refs_3_), channel_id=1, source_target_pairs={{0,1},{1,0},{2,3},{3,2},{4,5},{5,4},{6,7},{7,6},{8,9},{9,8},{10,11... | collective-permute-start | bytes 700424 | tf_op jit(solution)/shard_map/spread/ppermute | solution.py:37
  62.9 2.8 %collective-permute-start.15 = (bf16[16,7296]{1,0:T(8,128)(2,1)S(1)}, bf16[16,7296]{1,0:T(8,128)(2,1)S(1)}, u32[]{:S(2)}, u32[]{:S(2)}) collective-permute-start(bf16[16,7296]{1,0:T(8,128)(2,1)S(1)} %collective-permute-done.11.refs_2_), channel_id=1, source_target_pairs={{0,1},{1,0},{2,3},{3,2},{4,5},{5,4},{6,7},{7,6},{8,9},{9,8},{10,11... | collective-permute-start | bytes 700424 | tf_op jit(solution)/shard_map/spread/ppermute | solution.py:37
  72.7 2.5 %collective-permute-start.17 = (bf16[64,7168]{1,0:T(8,128)(2,1)S(1)}, bf16[64,7168]{1,0:T(8,128)(2,1)S(1)}, u32[]{:S(2)}, u32[]{:S(2)}) collective-permute-start(bf16[64,7168]{1,0:T(8,128)(2,1)S(1)} %get-tuple-element.22), channel_id=1, source_target_pairs={{0,1},{1,0},{2,3},{3,2},{4,5},{5,4},{6,7},{7,6},{8,9},{9,8},{10,11... | collective-permute-start | bytes 2752520 | tf_op jit(solution)/shard_map/collect/ppermute | solution.py:37
  75.5 7.1 %collective-permute-start.18 = (bf16[16,7168]{1,0:T(8,128)(2,1)S(1)}, bf16[16,7168]{1,0:T(8,128)(2,1)S(1)}, u32[]{:S(2)}, u32[]{:S(2)}) collective-permute-start(bf16[16,7168]{1,0:T(8,128)(2,1)S(1)} %get-tuple-element.33), channel_id=1, source_target_pairs={{0,18},{1,13},{2,16},{3,15},{4,22},{5,9},{6,20},{7,11},{8,26},{9,5... | collective-permute-start | bytes 688136 | tf_op jit(solution)/shard_map/collect/ppermute | solution.py:33
  76.5 8.5 %collective-permute-start.20 = (bf16[16,7168]{1,0:T(8,128)(2,1)S(1)}, bf16[16,7168]{1,0:T(8,128)(2,1)S(1)}, u32[]{:S(2)}, u32[]{:S(2)}) collective-permute-start(bf16[16,7168]{1,0:T(8,128)(2,1)S(1)} %get-tuple-element.34), channel_id=1, source_target_pairs={{0,2},{1,5},{2,0},{3,7},{4,6},{5,1},{6,4},{7,3},{8,10},{9,13},{10,... | collective-permute-start | bytes 688136 | tf_op jit(solution)/shard_map/collect/ppermute | solution.py:33
  77.8 7.1 %collective-permute-start.19 = (bf16[16,7168]{1,0:T(8,128)(2,1)S(1)}, bf16[16,7168]{1,0:T(8,128)(2,1)S(1)}, u32[]{:S(2)}, u32[]{:S(2)}) collective-permute-start(bf16[16,7168]{1,0:T(8,128)(2,1)S(1)} %get-tuple-element.35), channel_id=1, source_target_pairs={{0,16},{1,9},{2,18},{3,11},{4,20},{5,13},{6,22},{7,15},{8,24},{9,1... | collective-permute-start | bytes 688136 | tf_op jit(solution)/shard_map/collect/ppermute | solution.py:33
  85.1 4.2 %collective-permute-start.21 = (bf16[4,7168]{1,0:T(4,128)(2,1)S(1)}, bf16[4,7168]{1,0:T(4,128)(2,1)S(1)}, u32[]{:S(2)}, u32[]{:S(2)}) collective-permute-start(bf16[4,7168]{1,0:T(4,128)(2,1)S(1)} %get-tuple-element.39), channel_id=1, source_target_pairs={{0,4},{1,3},{2,6},{3,1},{4,0},{5,7},{6,2},{7,5},{8,12},{9,11},{10,... | collective-permute-start | bytes 172040 | tf_op jit(solution)/shard_map/collect/ppermute | solution.py:33
  85.3 6.1 %collective-permute-start.23 = (bf16[4,7168]{1,0:T(4,128)(2,1)S(1)}, bf16[4,7168]{1,0:T(4,128)(2,1)S(1)}, u32[]{:S(2)}, u32[]{:S(2)}) collective-permute-start(bf16[4,7168]{1,0:T(4,128)(2,1)S(1)} %get-tuple-element.40), channel_id=1, source_target_pairs={{0,12},{1,19},{2,14},{3,17},{4,8},{5,23},{6,10},{7,21},{8,4},{9,27... | collective-permute-start | bytes 172040 | tf_op jit(solution)/shard_map/collect/ppermute | solution.py:33
  87.0 5.7 %collective-permute-start.22 = (bf16[4,7168]{1,0:T(4,128)(2,1)S(1)}, bf16[4,7168]{1,0:T(4,128)(2,1)S(1)}, u32[]{:S(2)}, u32[]{:S(2)}) collective-permute-start(bf16[4,7168]{1,0:T(4,128)(2,1)S(1)} %get-tuple-element.41), channel_id=1, source_target_pairs={{0,8},{1,17},{2,10},{3,19},{4,12},{5,21},{6,14},{7,23},{8,0},{9,25... | collective-permute-start | bytes 172040 | tf_op jit(solution)/shard_map/collect/ppermute | solution.py:33
  (7 other events, 70.2 us)

commit v12 on v10

--- a/solution.py
+++ b/solution.py
@@ -20,6 +20,7 @@
 BF = jnp.bfloat16
 F32 = jnp.float32
 VMEM_LIMIT = 16 * 1024 * 1024
+LOAD_LIMIT = 28
 
 
 def partners(n):
@@ -48,7 +49,7 @@
     return jnp.dot(matrix, rows, preferred_element_type=F32)
 
 
-def attend_kernel(n, len_ref, q_hbm, new_hbm, keys_hbm, out_ref, q_ref, new_ref, keys_ref, m_ref, l_ref, acc_ref, small_sem, sem):
+def attend_kernel(n, len_ref, me_ref, q_hbm, new_hbm, keys_hbm, keep_ref, give_ref, q_ref, new_ref, keys_ref, m_ref, l_ref, acc_ref, small_sem, sem):
     rows = q_ref.shape[0]
     heads = rows // STEPS
     factor_base2 = (VDIM + ROPE) ** (-0.5) * math.log2(math.e)
@@ -75,7 +76,8 @@
     start(0)
     start(1)
     r = iota2((rows, rows), 0)
-    order = one_hot((r % STEPS) * heads + r // STEPS, rows)
+    head = (r // STEPS) % (n // 2) * 2 + (r // (rows // 2) ^ (me_ref[0] & 1))
+    order = one_hot((r % STEPS) * heads + head, rows)
     q_copy.wait()
     new_copy.wait()
 
@@ -117,18 +119,20 @@
         update(full, True)
 
     out = (acc_ref[...] / l_ref[...]).astype(BF)
-    out_ref[...] = pick(order, out).reshape(out_ref.shape).astype(BF)
-
-
-def attend(n, length, q, new, keys):
+    out = pick(order, out)
+    keep_ref[...] = out[: rows // 2].reshape(keep_ref.shape).astype(BF)
+    give_ref[...] = out[rows // 2 :].reshape(give_ref.shape).astype(BF)
+
+
+def attend(n, length, me, q, new, keys):
     rows, width = q.shape
     cached = keys.shape[1]
     blocks = cached // min(BLK, cached)
     return pl.pallas_call(
         functools.partial(attend_kernel, n),
-        in_specs=[pl.BlockSpec(memory_space=pltpu.SMEM)]
+        in_specs=[pl.BlockSpec(memory_space=pltpu.SMEM)] * 2
         + [pl.BlockSpec(memory_space=pl.ANY)] * 3,
-        out_specs=pl.BlockSpec(memory_space=pltpu.VMEM),
+        out_specs=[pl.BlockSpec(memory_space=pltpu.VMEM)] * 2,
         scratch_shapes=[
             pltpu.VMEM(q.shape, BF),
             pltpu.VMEM(new.shape, BF),
@@ -139,7 +143,7 @@
             pltpu.SemaphoreType.DMA((2,)),
             pltpu.SemaphoreType.DMA((blocks,)),
         ],
-        out_shape=jax.ShapeDtypeStruct((rows // STEPS, STEPS, LAT), BF),
+        out_shape=[jax.ShapeDtypeStruct((rows // STEPS // 2, STEPS, LAT), BF)] * 2,
         compiler_params=pltpu.CompilerParams(vmem_limit_bytes=56 * 1024 * 1024),
         cost_estimate=pl.CostEstimate(
             flops=2 * rows * cached * (width + LAT),
@@ -147,7 +151,7 @@
             transcendentals=rows * cached,
         ),
         name="attend",
-    )(length, q, new, keys)
+    )(length, me, q, new, keys)
 
 
 def source_rows(n, me, rows):
@@ -162,7 +166,8 @@
                 mask = mask | jnp.where(index == value, option, 0)
         masks.append(mask)
     mask = jnp.where((me & 1) ^ other == 0, masks[0], masks[1])
-    return (me ^ mask ^ other) * STEPS + r % STEPS
+    device = me ^ mask ^ other
+    return (device >> 1) * 2 * STEPS + ((device ^ me) & 1) * STEPS + r % STEPS
 
 
 def heads_kernel(n, me_ref, latents_ref, uv_ref, out_ref, near_ref, far_ref):
@@ -192,13 +197,13 @@
 
 def load_kernel(n, *refs):
     sources, targets, sem = refs[1:4], refs[5:8], refs[8]
-    copies = [pltpu.make_async_copy(refs[0], refs[4], sem.at[12])]
+    copies = [pltpu.make_async_copy(refs[0], refs[4], sem.at[24])]
     for i in range(3):
-        step = sources[i].shape[0] // 4
-        for j in range(4):
+        step = sources[i].shape[0] // 8
+        for j in range(8):
             here = pl.ds(j * step, step)
             copies.append(
-                pltpu.make_async_copy(sources[i].at[here], targets[i].at[here], sem.at[4 * i + j])
+                pltpu.make_async_copy(sources[i].at[here], targets[i].at[here], sem.at[8 * i + j])
             )
     for copy in copies:
         copy.start()
@@ -212,8 +217,8 @@
         in_specs=[pl.BlockSpec(memory_space=pltpu.VMEM)] + [pl.BlockSpec(memory_space=pl.ANY)] * 3,
         out_specs=[pl.BlockSpec(memory_space=pltpu.VMEM)] * 4,
         out_shape=[jax.ShapeDtypeStruct(a.shape, a.dtype) for a in [passed] + arrays],
-        scratch_shapes=[pltpu.SemaphoreType.DMA((13,))],
-        compiler_params=pltpu.CompilerParams(vmem_limit_bytes=28 * 1024 * 1024),
+        scratch_shapes=[pltpu.SemaphoreType.DMA((25,))],
+        compiler_params=pltpu.CompilerParams(vmem_limit_bytes=LOAD_LIMIT * 1024 * 1024),
         cost_estimate=pl.CostEstimate(
             flops=0, bytes_accessed=sum(4 * a.size for a in arrays), transcendentals=0
         ),
@@ -259,14 +264,15 @@
     )(*scalars, *arrays)
 
 
-def reduce_rows(near, far, n):
+def reduce_rows(near, far, n, beside=lambda rows: rows):
     firsts, seconds = (len(masks) for masks in partners(n)[0])
     width = near.shape[1]
     total = near + swap_core(far, n).astype(F32)
     total = total.reshape(firsts, seconds * STEPS, width)
-    kept = total[0]
-    for i in reversed(range(1, firsts)):
-        kept = kept + swap(total[i].astype(BF), n, 0, i).astype(F32)
+    got = [swap(total[i].astype(BF), n, 0, i) for i in range(1, firsts)]
+    kept = beside(total[0])
+    for term in reversed(got):
+        kept = kept + term.astype(F32)
     kept = kept.reshape(seconds, STEPS, width)
     return [kept[0]] + [swap(kept[j].astype(BF), n, 1, j) for j in range(1, seconds)]
 
@@ -294,16 +300,19 @@
     me_one = lax.axis_index(AXES).astype(jnp.int32).reshape(1)
 
     with jax.named_scope("attention"):
-        latents = attend(
+        latents, others = attend(
             n,
             cache_len,
+            me_one,
             queries[0].reshape(STEPS * heads, queries.shape[3]),
             new_latent[0],
             jnp.swapaxes(cache_latent[0], 0, 1),
         )
 
     with jax.named_scope("heads"):
-        latents = lax.all_to_all(latents, AXES, 0, 0, tiled=True)
+        latents = jnp.concatenate([latents, swap_core(others, n)], axis=1)
+        cores = [[2 * chip + core for chip in range(n // 2)] for core in range(2)]
+        latents = lax.all_to_all(latents, AXES, 0, 0, axis_index_groups=cores, tiled=True)
         near, far = single(
             heads_kernel,
             n,
@@ -313,7 +322,14 @@
             "heads",
             2 * rows * VDIM * (LAT + width),
         )
-        parts = reduce_rows(near, far, n)
+        loaded = []
+
+        def load_beside(rows):
+            rows, *weights = load(n, rows, [w_gate[0], w_up[0], w_down[0]])
+            loaded.extend(weights)
+            return rows
+
+        parts = reduce_rows(near, far, n, load_beside)
 
     with jax.named_scope("norm"):
         high = route_scores[0].astype(BF)
@@ -337,8 +353,7 @@
         along = [normed] + [swap(normed, n, 1, j) for j in range(1, n // SPAN)]
         along = jnp.concatenate(along, axis=0)
         blocks = [along] + [swap(along, n, 0, i) for i in range(1, 4)]
-        along, *weights = load(n, along, [w_gate[0], w_up[0], w_down[0]])
-        blocks = blocks + [swap_core(x, n) for x in [along] + blocks[1:]]
+        blocks = blocks + [swap_core(x, n) for x in blocks]
 
     with jax.named_scope("experts"):
         near, far = single(
@@ -346,7 +361,7 @@
             n,
             [jax.ShapeDtypeStruct((rows // 2, width), dtype) for dtype in (F32, BF)],
             [me_one],
-            blocks + weights,
+            blocks + loaded,
             "experts",
             6 * rows * width * w_gate.shape[2],
         )

time: 92.1 us -> 95.3 us (1.035)
  blocking collectives: 0 us -> 16.5 us
  starting transfers between devices: 31.5 us -> 23.6 us
  waiting for transfers between devices: 36.2 us -> 30.7 us
  Pallas kernels: 21.6 us -> 20.1 us
  other arithmetic: 1.58 us -> 2.56 us
    all_to_all x0 -> x1, blocking collectives: none -> 16.5 us  [per_device(): lax.all_to_all(latents, AXES, 0, 0, axis_index_groups=cores, tiled=True)]
    all_to_all x1 -> x0, waiting for transfers between devices: 8.22 us -> none  [per_device(): latents = lax.all_to_all(latents, AXES, 0, 0, tiled=True)]
    all_to_all x1 -> x0, starting transfers between devices: 6.74 us -> none  [per_device(): latents = lax.all_to_all(latents, AXES, 0, 0, tiled=True)]
    ppermute x6 -> x7, waiting for transfers between devices: 5.97 us -> 7.64 us  [swap_core(): return lax.ppermute(x, AXES, [(d, d ^ 1) for d in range(n)])]
    pallas_call x1, Pallas kernels: 9.22 us -> 7.65 us  [attend(): pl.pallas_call(functools.partial(attend_kernel, n), in_specs=[pl.BlockSpe...]
    ppermute x6 -> x7, starting transfers between devices: 1.64 us -> 0.45 us  [swap_core(): return lax.ppermute(x, AXES, [(d, d ^ 1) for d in range(n)])]
    ppermute x18, waiting for transfers between devices: 22 us -> 23.1 us  [swap(): lax.ppermute(x, AXES, [(d, d ^ partners(n)[d & 1][stage][i]) for d in ran...]
  transfers between devices with their start and end apart: 25 -> 25, of which waited for: 19 -> 17; matrix products, arithmetic and copies ran while one was open for 0% -> 0% of each run, Pallas kernels for 8% -> 8%
where the time goes in v12:
time: 95.3 us; the launch traced here: 94.7 us
  waiting for transfers between devices  30.7 us (32%)
  starting transfers between devices  23.6 us (25%)
  Pallas kernels  20.1 us (21%)
  blocking collectives  16.5 us (17%)
  other arithmetic  2.56 us (3%)
    ppermute x18, starting transfers between devices, swap(): lax.ppermute(x, AXES, [(d, d ^ partners(n)[d & 1][stage][i]) for d in ran...  23.1 us
    ppermute x18, waiting for transfers between devices, swap(): lax.ppermute(x, AXES, [(d, d ^ partners(n)[d & 1][stage][i]) for d in ran...  23.1 us
    all_to_all x1, blocking collectives, per_device(): lax.all_to_all(latents, AXES, 0, 0, axis_index_groups=cores, tiled=True)  16.5 us
    pallas_call x1, Pallas kernels, load(): pl.pallas_call(functools.partial(load_kernel, n), in_specs=[pl.BlockSpec(...  7.77 us
    pallas_call x1, Pallas kernels, attend(): pl.pallas_call(functools.partial(attend_kernel, n), in_specs=[pl.BlockSpe...  7.65 us
    ppermute x7, waiting for transfers between devices, swap_core(): return lax.ppermute(x, AXES, [(d, d ^ 1) for d in range(n)])  7.64 us
    pallas_call x3, Pallas kernels, single(): pl.pallas_call(functools.partial(kernel, n), in_specs=[pl.BlockSpec(memor...  4.7 us
  transfers between devices with their start and end apart: 25, of which 17 were waited for; matrix products, arithmetic and copies ran while one was open for 0% of the time, Pallas kernels for 8%

profile of v12, /device:TPU:0, one launch (start us, length us, event | category | flops | bytes accessed | tf_op | source)
XLA Modules:
  0.0 94.7 jit_solution(14588995632623962698)
XLA Ops:
  0.7 7.7 %attend.1 = (bf16[16,4,512]{2,1,0:T(4,128)(2,1)}, bf16[16,4,512]{2,1,0:T(4,128)(2,1)}) custom-call(s32[1]{0:T(128)S(6)} %copy.14.len_ref, s32[1]{0:T(128)} %bitcast.me_ref, bf16[128,576]{1,0:T(8,128)(2,1)} %bitcast.31, bf16[4,576]{1,0:T(4,128)(2,1)} %bitcast.32, bf16[576,8192]{1,0:T(8,128)(2,1)} %bitcast.27), custom_call_target="tpu_custom_call" | custom-call | flops 2281701376 | bytes 9437184 | tf_op jit(solution)/shard_map/attention/attend/pallas_call | solution.py:131
  8.4 1.5 %collective-permute-done = bf16[16,4,512]{2,1,0:T(4,128)(2,1)S(1)} collective-permute-done((bf16[16,4,512]{2,1,0:T(4,128)(2,1)}, bf16[16,4,512]{2,1,0:T(4,128)(2,1)S(1)}, u32[]{:S(2)}, u32[]{:S(2)}) %collective-permute-start) | collective-permute-done | bytes 65568 | tf_op jit(solution)/shard_map/heads/ppermute | solution.py:37
  10.8 16.5 %all_to_all.5 = bf16[16,8,512]{2,1,0:T(8,128)(2,1)S(1)} all-to-all(bf16[16,8,512]{2,1,0:T(8,128)(2,1)S(1)} %pad_maximum_fusion.1), channel_id=1, replica_groups={{0,2,4,6,8,10,12,14,16,18,20,22,24,26,28,30},{1,3,5,7,9,11,13,15,17,19,..., dimensions={0} | all-to-all | bytes 262144 | tf_op jit(solution)/shard_map/heads/all_to_all | solution.py:315
  28.3 2.5 %collective-permute-done.1 = bf16[64,7168]{1,0:T(8,128)(2,1)S(1)} collective-permute-done((bf16[64,7168]{1,0:T(8,128)(2,1)S(1)}, bf16[64,7168]{1,0:T(8,128)(2,1)S(1)}, u32[]{:S(2)}, u32[]{:S(2)}) %collective-permute-start.1) | collective-permute-done | bytes 917536 | tf_op jit(solution)/shard_map/heads/ppermute | solution.py:37
  32.2 1.3 %collective-permute-start.4 = (bf16[16,7168]{1,0:T(8,128)(2,1)S(1)}, bf16[16,7168]{1,0:T(8,128)(2,1)S(1)}, u32[]{:S(2)}, u32[]{:S(2)}) collective-permute-start(bf16[16,7168]{1,0:T(8,128)(2,1)S(1)} %get-tuple-element.43), channel_id=1, source_target_pairs={{0,2},{1,5},{2,0},{3,7},{4,6},{5,1},{6,4},{7,3},{8,10},{9,13},{10,... | collective-permute-start | bytes 688136 | tf_op jit(solution)/shard_map/heads/ppermute | solution.py:33
  34.7 7.8 %load_experts.1 = (f32[16,7168]{1,0:T(8,128)S(1)}, bf16[7168,512]{1,0:T(8,128)(2,1)S(1)}, bf16[7168,512]{1,0:T(8,128)(2,1)S(1)}, bf16[512,7168]{1,0:T(8,128)(2,1)S(1)}) custom-call(f32[16,7168]{1,0:T(8,128)S(1)} %slice.92.refs_0_, bf16[7168,512]{1,0:T(8,128)(2,1)} %bitcast.28, bf16[7168,512]{1,0:T(8,128)(2,1)} %bitcast.29, bf16[512,7168]{1,0:T(8,128)(2,1)} %bitcast.30), custom_call_target="tpu_custom_call" | custom-call | bytes 44040192 | tf_op jit(solution)/shard_map/heads/load_experts/pallas_call | solution.py:215
  42.7 1.7 %collective-permute-start.7 = (bf16[4,7168]{1,0:T(4,128)(2,1)S(1)}, bf16[4,7168]{1,0:T(4,128)(2,1)S(1)}, u32[]{:S(2)}, u32[]{:S(2)}) collective-permute-start(bf16[4,7168]{1,0:T(4,128)(2,1)S(1)} %get-tuple-element.48), channel_id=1, source_target_pairs={{0,12},{1,19},{2,14},{3,17},{4,8},{5,23},{6,10},{7,21},{8,4},{9,27... | collective-permute-start | bytes 172040 | tf_op jit(solution)/shard_map/heads/ppermute | solution.py:33
  44.9 2.2 %collective-permute-start.5 = (bf16[4,7168]{1,0:T(4,128)(2,1)S(1)}, bf16[4,7168]{1,0:T(4,128)(2,1)S(1)}, u32[]{:S(2)}, u32[]{:S(2)}) collective-permute-start(bf16[4,7168]{1,0:T(4,128)(2,1)S(1)} %get-tuple-element.50), channel_id=1, source_target_pairs={{0,4},{1,3},{2,6},{3,1},{4,0},{5,7},{6,2},{7,5},{8,12},{9,11},{10,... | collective-permute-start | bytes 172040 | tf_op jit(solution)/shard_map/heads/ppermute | solution.py:33
  47.3 1.5 %collective-permute-done.7.refs_3_ = bf16[4,7168]{1,0:T(4,128)(2,1)S(1)} collective-permute-done((bf16[4,7168]{1,0:T(4,128)(2,1)S(1)}, bf16[4,7168]{1,0:T(4,128)(2,1)S(1)}, u32[]{:S(2)}, u32[]{:S(2)}) %collective-permute-start.7) | collective-permute-done | bytes 57376 | tf_op jit(solution)/shard_map/heads/ppermute | solution.py:33
  50.2 1.8 %collective-permute-start.10 = (bf16[4,7296]{1,0:T(4,128)(2,1)S(1)}, bf16[4,7296]{1,0:T(4,128)(2,1)S(1)}, u32[]{:S(2)}, u32[]{:S(2)}) collective-permute-start(bf16[4,7296]{1,0:T(4,128)(2,1)S(1)} %get-tuple-element.23), channel_id=1, source_target_pairs={{0,12},{1,19},{2,14},{3,17},{4,8},{5,23},{6,10},{7,21},{8,4},{9,27... | collective-permute-start | bytes 175112 | tf_op jit(solution)/shard_map/spread/ppermute | solution.py:33
  53.1 1.6 %collective-permute-start.8 = (bf16[4,7296]{1,0:T(4,128)(2,1)S(1)}, bf16[4,7296]{1,0:T(4,128)(2,1)S(1)}, u32[]{:S(2)}, u32[]{:S(2)}) collective-permute-start(bf16[4,7296]{1,0:T(4,128)(2,1)S(1)} %get-tuple-element.23), channel_id=1, source_target_pairs={{0,4},{1,3},{2,6},{3,1},{4,0},{5,7},{6,2},{7,5},{8,12},{9,11},{10,... | collective-permute-start | bytes 175112 | tf_op jit(solution)/shard_map/spread/ppermute | solution.py:33
  54.7 1.6 %collective-permute-done.10 = bf16[4,7296]{1,0:T(4,128)(2,1)S(1)} collective-permute-done((bf16[4,7296]{1,0:T(4,128)(2,1)S(1)}, bf16[4,7296]{1,0:T(4,128)(2,1)S(1)}, u32[]{:S(2)}, u32[]{:S(2)}) %collective-permute-start.10) | collective-permute-done | bytes 58400 | tf_op jit(solution)/shard_map/spread/ppermute | solution.py:33
  56.3 1.9 %collective-permute-done.9 = bf16[4,7296]{1,0:T(4,128)(2,1)S(1)} collective-permute-done((bf16[4,7296]{1,0:T(4,128)(2,1)S(1)}, bf16[4,7296]{1,0:T(4,128)(2,1)S(1)}, u32[]{:S(2)}, u32[]{:S(2)}) %collective-permute-start.9) | collective-permute-done | bytes 58400 | tf_op jit(solution)/shard_map/spread/ppermute | solution.py:33
  59.5 1.4 %collective-permute-start.12 = (bf16[16,7296]{1,0:T(8,128)(2,1)S(1)}, bf16[16,7296]{1,0:T(8,128)(2,1)S(1)}, u32[]{:S(2)}, u32[]{:S(2)}) collective-permute-start(bf16[16,7296]{1,0:T(8,128)(2,1)S(1)} %pad_maximum_fusion.refs_0_), channel_id=1, source_target_pairs={{0,16},{1,9},{2,18},{3,11},{4,20},{5,13},{6,22},{7,15},{8,24},{9,1... | collective-permute-start | bytes 700424 | tf_op jit(solution)/shard_map/spread/ppermute | solution.py:33
  61.9 3.6 %collective-permute-done.13.refs_3_ = bf16[16,7296]{1,0:T(8,128)(2,1)S(1)} collective-permute-done((bf16[16,7296]{1,0:T(8,128)(2,1)S(1)}, bf16[16,7296]{1,0:T(8,128)(2,1)S(1)}, u32[]{:S(2)}, u32[]{:S(2)}) %collective-permute-start.13) | collective-permute-done | bytes 233504 | tf_op jit(solution)/shard_map/spread/ppermute | solution.py:33
  65.5 2.0 %collective-permute-done.12.refs_2_ = bf16[16,7296]{1,0:T(8,128)(2,1)S(1)} collective-permute-done((bf16[16,7296]{1,0:T(8,128)(2,1)S(1)}, bf16[16,7296]{1,0:T(8,128)(2,1)S(1)}, u32[]{:S(2)}, u32[]{:S(2)}) %collective-permute-start.12) | collective-permute-done | bytes 233504 | tf_op jit(solution)/shard_map/spread/ppermute | solution.py:33
  69.4 3.6 %experts.1 = (f32[64,7168]{1,0:T(8,128)S(1)}, bf16[64,7168]{1,0:T(8,128)(2,1)S(1)}) custom-call(s32[1]{0:T(128)} %bitcast.me_ref, bf16[16,7296]{1,0:T(8,128)(2,1)S(1)} %pad_maximum_fusion.refs_0_, bf16[16,7296]{1,0:T(8,128)(2,1)S(1)} %collective-permute-done.11.refs_1_, bf16[16,7296]{1,0:T(8,128)(2,1)S(1)} %collective-permute-done.12.refs_2_, ...), custom_call_target="tpu_custom_call" | custom-call | flops 2818572288 | bytes 23887872 | tf_op jit(solution)/shard_map/experts/experts/pallas_call | solution.py:254
  73.2 2.3 %collective-permute-done.18 = bf16[64,7168]{1,0:T(8,128)(2,1)S(1)} collective-permute-done((bf16[64,7168]{1,0:T(8,128)(2,1)S(1)}, bf16[64,7168]{1,0:T(8,128)(2,1)S(1)}, u32[]{:S(2)}, u32[]{:S(2)}) %collective-permute-start.18) | collective-permute-done | bytes 917536 | tf_op jit(solution)/shard_map/collect/ppermute | solution.py:37
  75.8 1.3 %collective-permute-start.19 = (bf16[16,7168]{1,0:T(8,128)(2,1)S(1)}, bf16[16,7168]{1,0:T(8,128)(2,1)S(1)}, u32[]{:S(2)}, u32[]{:S(2)}) collective-permute-start(bf16[16,7168]{1,0:T(8,128)(2,1)S(1)} %get-tuple-element.39), channel_id=1, source_target_pairs={{0,18},{1,13},{2,16},{3,15},{4,22},{5,9},{6,20},{7,11},{8,26},{9,5... | collective-permute-start | bytes 688136 | tf_op jit(solution)/shard_map/collect/ppermute | solution.py:33
  79.4 3.5 %collective-permute-done.19 = bf16[16,7168]{1,0:T(8,128)(2,1)S(1)} collective-permute-done((bf16[16,7168]{1,0:T(8,128)(2,1)S(1)}, bf16[16,7168]{1,0:T(8,128)(2,1)S(1)}, u32[]{:S(2)}, u32[]{:S(2)}) %collective-permute-start.19) | collective-permute-done | bytes 229408 | tf_op jit(solution)/shard_map/collect/ppermute | solution.py:33
  82.9 2.4 %collective-permute-done.21 = bf16[16,7168]{1,0:T(8,128)(2,1)S(1)} collective-permute-done((bf16[16,7168]{1,0:T(8,128)(2,1)S(1)}, bf16[16,7168]{1,0:T(8,128)(2,1)S(1)}, u32[]{:S(2)}, u32[]{:S(2)}) %collective-permute-start.21) | collective-permute-done | bytes 229408 | tf_op jit(solution)/shard_map/collect/ppermute | solution.py:33
  85.5 1.3 %collective-permute-start.22 = (bf16[4,7168]{1,0:T(4,128)(2,1)S(1)}, bf16[4,7168]{1,0:T(4,128)(2,1)S(1)}, u32[]{:S(2)}, u32[]{:S(2)}) collective-permute-start(bf16[4,7168]{1,0:T(4,128)(2,1)S(1)} %get-tuple-element.45), channel_id=1, source_target_pairs={{0,4},{1,3},{2,6},{3,1},{4,0},{5,7},{6,2},{7,5},{8,12},{9,11},{10,... | collective-permute-start | bytes 172040 | tf_op jit(solution)/shard_map/collect/ppermute | solution.py:33
  86.8 1.4 %collective-permute-start.24 = (bf16[4,7168]{1,0:T(4,128)(2,1)S(1)}, bf16[4,7168]{1,0:T(4,128)(2,1)S(1)}, u32[]{:S(2)}, u32[]{:S(2)}) collective-permute-start(bf16[4,7168]{1,0:T(4,128)(2,1)S(1)} %get-tuple-element.46), channel_id=1, source_target_pairs={{0,12},{1,19},{2,14},{3,17},{4,8},{5,23},{6,10},{7,21},{8,4},{9,27... | collective-permute-start | bytes 172040 | tf_op jit(solution)/shard_map/collect/ppermute | solution.py:33
  89.8 2.9 %collective-permute-done.24 = bf16[4,7168]{1,0:T(4,128)(2,1)S(1)} collective-permute-done((bf16[4,7168]{1,0:T(4,128)(2,1)S(1)}, bf16[4,7168]{1,0:T(4,128)(2,1)S(1)}, u32[]{:S(2)}, u32[]{:S(2)}) %collective-permute-start.24) | collective-permute-done | bytes 57376 | tf_op jit(solution)/shard_map/collect/ppermute | solution.py:33
  (61 shorter events, 18.6 us)
Async XLA Ops:
  8.3 1.5 %collective-permute-start = (bf16[16,4,512]{2,1,0:T(4,128)(2,1)}, bf16[16,4,512]{2,1,0:T(4,128)(2,1)S(1)}, u32[]{:S(2)}, u32[]{:S(2)}) collective-permute-start(bf16[16,4,512]{2,1,0:T(4,128)(2,1)} %get-tuple-element.18), channel_id=1, source_target_pairs={{0,1},{1,0},{2,3},{3,2},{4,5},{5,4},{6,7},{7,6},{8,9},{9,8},{10,11... | collective-permute-start | bytes 196616 | tf_op jit(solution)/shard_map/heads/ppermute | solution.py:37
  28.2 2.5 %collective-permute-start.1 = (bf16[64,7168]{1,0:T(8,128)(2,1)S(1)}, bf16[64,7168]{1,0:T(8,128)(2,1)S(1)}, u32[]{:S(2)}, u32[]{:S(2)}) collective-permute-start(bf16[64,7168]{1,0:T(8,128)(2,1)S(1)} %get-tuple-element.20), channel_id=1, source_target_pairs={{0,1},{1,0},{2,3},{3,2},{4,5},{5,4},{6,7},{7,6},{8,9},{9,8},{10,11... | collective-permute-start | bytes 2752520 | tf_op jit(solution)/shard_map/heads/ppermute | solution.py:37
  31.0 11.4 %collective-permute-start.2 = (bf16[16,7168]{1,0:T(8,128)(2,1)S(1)}, bf16[16,7168]{1,0:T(8,128)(2,1)S(1)}, u32[]{:S(2)}, u32[]{:S(2)}) collective-permute-start(bf16[16,7168]{1,0:T(8,128)(2,1)S(1)} %get-tuple-element.42), channel_id=1, source_target_pairs={{0,18},{1,13},{2,16},{3,15},{4,22},{5,9},{6,20},{7,11},{8,26},{9,5... | collective-permute-start | bytes 688136 | tf_op jit(solution)/shard_map/heads/ppermute | solution.py:33
  32.2 10.3 %collective-permute-start.4 = (bf16[16,7168]{1,0:T(8,128)(2,1)S(1)}, bf16[16,7168]{1,0:T(8,128)(2,1)S(1)}, u32[]{:S(2)}, u32[]{:S(2)}) collective-permute-start(bf16[16,7168]{1,0:T(8,128)(2,1)S(1)} %get-tuple-element.43), channel_id=1, source_target_pairs={{0,2},{1,5},{2,0},{3,7},{4,6},{5,1},{6,4},{7,3},{8,10},{9,13},{10,... | collective-permute-start | bytes 688136 | tf_op jit(solution)/shard_map/heads/ppermute | solution.py:33
  33.5 9.0 %collective-permute-start.3 = (bf16[16,7168]{1,0:T(8,128)(2,1)S(1)}, bf16[16,7168]{1,0:T(8,128)(2,1)S(1)}, u32[]{:S(2)}, u32[]{:S(2)}) collective-permute-start(bf16[16,7168]{1,0:T(8,128)(2,1)S(1)} %get-tuple-element.44), channel_id=1, source_target_pairs={{0,16},{1,9},{2,18},{3,11},{4,20},{5,13},{6,22},{7,15},{8,24},{9,1... | collective-permute-start | bytes 688136 | tf_op jit(solution)/shard_map/heads/ppermute | solution.py:33
  42.7 6.0 %collective-permute-start.7 = (bf16[4,7168]{1,0:T(4,128)(2,1)S(1)}, bf16[4,7168]{1,0:T(4,128)(2,1)S(1)}, u32[]{:S(2)}, u32[]{:S(2)}) collective-permute-start(bf16[4,7168]{1,0:T(4,128)(2,1)S(1)} %get-tuple-element.48), channel_id=1, source_target_pairs={{0,12},{1,19},{2,14},{3,17},{4,8},{5,23},{6,10},{7,21},{8,4},{9,27... | collective-permute-start | bytes 172040 | tf_op jit(solution)/shard_map/heads/ppermute | solution.py:33
  44.5 5.5 %collective-permute-start.6 = (bf16[4,7168]{1,0:T(4,128)(2,1)S(1)}, bf16[4,7168]{1,0:T(4,128)(2,1)S(1)}, u32[]{:S(2)}, u32[]{:S(2)}) collective-permute-start(bf16[4,7168]{1,0:T(4,128)(2,1)S(1)} %get-tuple-element.49), channel_id=1, source_target_pairs={{0,8},{1,17},{2,10},{3,19},{4,12},{5,21},{6,14},{7,23},{8,0},{9,25... | collective-permute-start | bytes 172040 | tf_op jit(solution)/shard_map/heads/ppermute | solution.py:33
  44.9 5.1 %collective-permute-start.5 = (bf16[4,7168]{1,0:T(4,128)(2,1)S(1)}, bf16[4,7168]{1,0:T(4,128)(2,1)S(1)}, u32[]{:S(2)}, u32[]{:S(2)}) collective-permute-start(bf16[4,7168]{1,0:T(4,128)(2,1)S(1)} %get-tuple-element.50), channel_id=1, source_target_pairs={{0,4},{1,3},{2,6},{3,1},{4,0},{5,7},{6,2},{7,5},{8,12},{9,11},{10,... | collective-permute-start | bytes 172040 | tf_op jit(solution)/shard_map/heads/ppermute | solution.py:33
  50.2 6.1 %collective-permute-start.10 = (bf16[4,7296]{1,0:T(4,128)(2,1)S(1)}, bf16[4,7296]{1,0:T(4,128)(2,1)S(1)}, u32[]{:S(2)}, u32[]{:S(2)}) collective-permute-start(bf16[4,7296]{1,0:T(4,128)(2,1)S(1)} %get-tuple-element.23), channel_id=1, source_target_pairs={{0,12},{1,19},{2,14},{3,17},{4,8},{5,23},{6,10},{7,21},{8,4},{9,27... | collective-permute-start | bytes 175112 | tf_op jit(solution)/shard_map/spread/ppermute | solution.py:33
  52.0 6.2 %collective-permute-start.9 = (bf16[4,7296]{1,0:T(4,128)(2,1)S(1)}, bf16[4,7296]{1,0:T(4,128)(2,1)S(1)}, u32[]{:S(2)}, u32[]{:S(2)}) collective-permute-start(bf16[4,7296]{1,0:T(4,128)(2,1)S(1)} %get-tuple-element.23), channel_id=1, source_target_pairs={{0,8},{1,17},{2,10},{3,19},{4,12},{5,21},{6,14},{7,23},{8,0},{9,25... | collective-permute-start | bytes 175112 | tf_op jit(solution)/shard_map/spread/ppermute | solution.py:33
  53.1 5.1 %collective-permute-start.8 = (bf16[4,7296]{1,0:T(4,128)(2,1)S(1)}, bf16[4,7296]{1,0:T(4,128)(2,1)S(1)}, u32[]{:S(2)}, u32[]{:S(2)}) collective-permute-start(bf16[4,7296]{1,0:T(4,128)(2,1)S(1)} %get-tuple-element.23), channel_id=1, source_target_pairs={{0,4},{1,3},{2,6},{3,1},{4,0},{5,7},{6,2},{7,5},{8,12},{9,11},{10,... | collective-permute-start | bytes 175112 | tf_op jit(solution)/shard_map/spread/ppermute | solution.py:33
  58.3 7.1 %collective-permute-start.13 = (bf16[16,7296]{1,0:T(8,128)(2,1)S(1)}, bf16[16,7296]{1,0:T(8,128)(2,1)S(1)}, u32[]{:S(2)}, u32[]{:S(2)}) collective-permute-start(bf16[16,7296]{1,0:T(8,128)(2,1)S(1)} %pad_maximum_fusion.refs_0_), channel_id=1, source_target_pairs={{0,18},{1,13},{2,16},{3,15},{4,22},{5,9},{6,20},{7,11},{8,26},{9,5... | collective-permute-start | bytes 700424 | tf_op jit(solution)/shard_map/spread/ppermute | solution.py:33
  59.5 8.0 %collective-permute-start.12 = (bf16[16,7296]{1,0:T(8,128)(2,1)S(1)}, bf16[16,7296]{1,0:T(8,128)(2,1)S(1)}, u32[]{:S(2)}, u32[]{:S(2)}) collective-permute-start(bf16[16,7296]{1,0:T(8,128)(2,1)S(1)} %pad_maximum_fusion.refs_0_), channel_id=1, source_target_pairs={{0,16},{1,9},{2,18},{3,11},{4,20},{5,13},{6,22},{7,15},{8,24},{9,1... | collective-permute-start | bytes 700424 | tf_op jit(solution)/shard_map/spread/ppermute | solution.py:33
  60.9 7.0 %collective-permute-start.11 = (bf16[16,7296]{1,0:T(8,128)(2,1)S(1)}, bf16[16,7296]{1,0:T(8,128)(2,1)S(1)}, u32[]{:S(2)}, u32[]{:S(2)}) collective-permute-start(bf16[16,7296]{1,0:T(8,128)(2,1)S(1)} %pad_maximum_fusion.refs_0_), channel_id=1, source_target_pairs={{0,2},{1,5},{2,0},{3,7},{4,6},{5,1},{6,4},{7,3},{8,10},{9,13},{10,... | collective-permute-start | bytes 700424 | tf_op jit(solution)/shard_map/spread/ppermute | solution.py:33
  61.9 6.1 %collective-permute-start.14 = (bf16[16,7296]{1,0:T(8,128)(2,1)S(1)}, bf16[16,7296]{1,0:T(8,128)(2,1)S(1)}, u32[]{:S(2)}, u32[]{:S(2)}) collective-permute-start(bf16[16,7296]{1,0:T(8,128)(2,1)S(1)} %pad_maximum_fusion.refs_0_), channel_id=1, source_target_pairs={{0,1},{1,0},{2,3},{3,2},{4,5},{5,4},{6,7},{7,6},{8,9},{9,8},{10,11... | collective-permute-start | bytes 700424 | tf_op jit(solution)/shard_map/spread/ppermute | solution.py:37
  65.5 2.5 %collective-permute-start.17 = (bf16[16,7296]{1,0:T(8,128)(2,1)S(1)}, bf16[16,7296]{1,0:T(8,128)(2,1)S(1)}, u32[]{:S(2)}, u32[]{:S(2)}) collective-permute-start(bf16[16,7296]{1,0:T(8,128)(2,1)S(1)} %collective-permute-done.13.refs_3_), channel_id=1, source_target_pairs={{0,1},{1,0},{2,3},{3,2},{4,5},{5,4},{6,7},{7,6},{8,9},{9,8},{10,11... | collective-permute-start | bytes 700424 | tf_op jit(solution)/shard_map/spread/ppermute | solution.py:37
  67.4 1.5 %collective-permute-start.16 = (bf16[16,7296]{1,0:T(8,128)(2,1)S(1)}, bf16[16,7296]{1,0:T(8,128)(2,1)S(1)}, u32[]{:S(2)}, u32[]{:S(2)}) collective-permute-start(bf16[16,7296]{1,0:T(8,128)(2,1)S(1)} %collective-permute-done.12.refs_2_), channel_id=1, source_target_pairs={{0,1},{1,0},{2,3},{3,2},{4,5},{5,4},{6,7},{7,6},{8,9},{9,8},{10,11... | collective-permute-start | bytes 700424 | tf_op jit(solution)/shard_map/spread/ppermute | solution.py:37
  73.0 2.5 %collective-permute-start.18 = (bf16[64,7168]{1,0:T(8,128)(2,1)S(1)}, bf16[64,7168]{1,0:T(8,128)(2,1)S(1)}, u32[]{:S(2)}, u32[]{:S(2)}) collective-permute-start(bf16[64,7168]{1,0:T(8,128)(2,1)S(1)} %get-tuple-element.28), channel_id=1, source_target_pairs={{0,1},{1,0},{2,3},{3,2},{4,5},{5,4},{6,7},{7,6},{8,9},{9,8},{10,11... | collective-permute-start | bytes 2752520 | tf_op jit(solution)/shard_map/collect/ppermute | solution.py:37
  75.8 7.1 %collective-permute-start.19 = (bf16[16,7168]{1,0:T(8,128)(2,1)S(1)}, bf16[16,7168]{1,0:T(8,128)(2,1)S(1)}, u32[]{:S(2)}, u32[]{:S(2)}) collective-permute-start(bf16[16,7168]{1,0:T(8,128)(2,1)S(1)} %get-tuple-element.39), channel_id=1, source_target_pairs={{0,18},{1,13},{2,16},{3,15},{4,22},{5,9},{6,20},{7,11},{8,26},{9,5... | collective-permute-start | bytes 688136 | tf_op jit(solution)/shard_map/collect/ppermute | solution.py:33
  77.1 8.1 %collective-permute-start.21 = (bf16[16,7168]{1,0:T(8,128)(2,1)S(1)}, bf16[16,7168]{1,0:T(8,128)(2,1)S(1)}, u32[]{:S(2)}, u32[]{:S(2)}) collective-permute-start(bf16[16,7168]{1,0:T(8,128)(2,1)S(1)} %get-tuple-element.40), channel_id=1, source_target_pairs={{0,2},{1,5},{2,0},{3,7},{4,6},{5,1},{6,4},{7,3},{8,10},{9,13},{10,... | collective-permute-start | bytes 688136 | tf_op jit(solution)/shard_map/collect/ppermute | solution.py:33
  78.3 7.0 %collective-permute-start.20 = (bf16[16,7168]{1,0:T(8,128)(2,1)S(1)}, bf16[16,7168]{1,0:T(8,128)(2,1)S(1)}, u32[]{:S(2)}, u32[]{:S(2)}) collective-permute-start(bf16[16,7168]{1,0:T(8,128)(2,1)S(1)} %get-tuple-element.41), channel_id=1, source_target_pairs={{0,16},{1,9},{2,18},{3,11},{4,20},{5,13},{6,22},{7,15},{8,24},{9,1... | collective-permute-start | bytes 688136 | tf_op jit(solution)/shard_map/collect/ppermute | solution.py:33
  85.5 4.4 %collective-permute-start.22 = (bf16[4,7168]{1,0:T(4,128)(2,1)S(1)}, bf16[4,7168]{1,0:T(4,128)(2,1)S(1)}, u32[]{:S(2)}, u32[]{:S(2)}) collective-permute-start(bf16[4,7168]{1,0:T(4,128)(2,1)S(1)} %get-tuple-element.45), channel_id=1, source_target_pairs={{0,4},{1,3},{2,6},{3,1},{4,0},{5,7},{6,2},{7,5},{8,12},{9,11},{10,... | collective-permute-start | bytes 172040 | tf_op jit(solution)/shard_map/collect/ppermute | solution.py:33
  86.8 6.0 %collective-permute-start.24 = (bf16[4,7168]{1,0:T(4,128)(2,1)S(1)}, bf16[4,7168]{1,0:T(4,128)(2,1)S(1)}, u32[]{:S(2)}, u32[]{:S(2)}) collective-permute-start(bf16[4,7168]{1,0:T(4,128)(2,1)S(1)} %get-tuple-element.46), channel_id=1, source_target_pairs={{0,12},{1,19},{2,14},{3,17},{4,8},{5,23},{6,10},{7,21},{8,4},{9,27... | collective-permute-start | bytes 172040 | tf_op jit(solution)/shard_map/collect/ppermute | solution.py:33
  88.1 5.8 %collective-permute-start.23 = (bf16[4,7168]{1,0:T(4,128)(2,1)S(1)}, bf16[4,7168]{1,0:T(4,128)(2,1)S(1)}, u32[]{:S(2)}, u32[]{:S(2)}) collective-permute-start(bf16[4,7168]{1,0:T(4,128)(2,1)S(1)} %get-tuple-element.47), channel_id=1, source_target_pairs={{0,8},{1,17},{2,10},{3,19},{4,12},{5,21},{6,14},{7,23},{8,0},{9,25... | collective-permute-start | bytes 172040 | tf_op jit(solution)/shard_map/collect/ppermute | solution.py:33
  (7 other events, 73.9 us)

commit v13 on v10

--- a/solution.py
+++ b/solution.py
@@ -20,6 +20,7 @@
 BF = jnp.bfloat16
 F32 = jnp.float32
 VMEM_LIMIT = 16 * 1024 * 1024
+LOAD_LIMIT = 28
 
 
 def partners(n):
@@ -177,28 +178,44 @@
         far_ref[:, here] = out[rows // 2 :].astype(BF)
 
 
-def norm_kernel(n, *refs):
-    parts, (residual_ref, gain_ref, routes_ref, hidden_ref, out_ref) = refs[:-5], refs[-5:]
-    hidden = residual_ref[...].astype(F32)
-    for ref in parts:
-        hidden += ref[...].astype(F32)
-    hidden_ref[...] = hidden
-    width = hidden.shape[1]
+def carry_kernel(n, *refs):
+    terms, (residual_ref, routes_ref, mine_ref, sent_ref) = refs[:-4], refs[-4:]
+    width = residual_ref.shape[1]
+    total = terms[0][...]
+    for ref in terms[1:]:
+        total += ref[...].astype(F32)
+    mine_ref[:, :width] = total
+    mine_ref[:STEPS, :width] = total[:STEPS] + residual_ref[...].astype(F32)
+    mine_ref[:, width:] = jnp.zeros((total.shape[0], mine_ref.shape[1] - width), F32)
+    mine_ref[:STEPS, width:] = routes_ref[...].astype(F32)
+    sent_ref[...] = mine_ref[...].astype(BF)
+
+
+def norm_kernel(n, mine_ref, *refs):
+    got, (gain_ref, hidden_ref, out_ref) = refs[:-3], refs[-3:]
+    width = gain_ref.shape[1]
+    total = mine_ref[...]
+    for j, ref in enumerate(got, 1):
+        rows = ref[...].astype(F32)
+        parts = [(j ^ b) * STEPS for b in range(len(got) + 1)]
+        total += jnp.concatenate([rows[first : first + STEPS] for first in parts], axis=0)
+    hidden = total[:, :width]
+    hidden_ref[...] = hidden[:STEPS]
     mean_square = jnp.sum(hidden * hidden, axis=1, keepdims=True) / width
     normed = hidden * lax.rsqrt(mean_square + 1e-06) * gain_ref[...].astype(F32)
     out_ref[:, :width] = normed.astype(BF)
-    out_ref[:, width:] = routes_ref[...]
+    out_ref[:, width:] = total[:, width:].astype(BF)
 
 
 def load_kernel(n, *refs):
     sources, targets, sem = refs[1:4], refs[5:8], refs[8]
-    copies = [pltpu.make_async_copy(refs[0], refs[4], sem.at[12])]
+    copies = [pltpu.make_async_copy(refs[0], refs[4], sem.at[24])]
     for i in range(3):
-        step = sources[i].shape[0] // 4
-        for j in range(4):
+        step = sources[i].shape[0] // 8
+        for j in range(8):
             here = pl.ds(j * step, step)
             copies.append(
-                pltpu.make_async_copy(sources[i].at[here], targets[i].at[here], sem.at[4 * i + j])
+                pltpu.make_async_copy(sources[i].at[here], targets[i].at[here], sem.at[8 * i + j])
             )
     for copy in copies:
         copy.start()
@@ -212,8 +229,8 @@
         in_specs=[pl.BlockSpec(memory_space=pltpu.VMEM)] + [pl.BlockSpec(memory_space=pl.ANY)] * 3,
         out_specs=[pl.BlockSpec(memory_space=pltpu.VMEM)] * 4,
         out_shape=[jax.ShapeDtypeStruct(a.shape, a.dtype) for a in [passed] + arrays],
-        scratch_shapes=[pltpu.SemaphoreType.DMA((13,))],
-        compiler_params=pltpu.CompilerParams(vmem_limit_bytes=28 * 1024 * 1024),
+        scratch_shapes=[pltpu.SemaphoreType.DMA((25,))],
+        compiler_params=pltpu.CompilerParams(vmem_limit_bytes=LOAD_LIMIT * 1024 * 1024),
         cost_estimate=pl.CostEstimate(
             flops=0, bytes_accessed=sum(4 * a.size for a in arrays), transcendentals=0
         ),
@@ -259,16 +276,11 @@
     )(*scalars, *arrays)
 
 
-def reduce_rows(near, far, n):
-    firsts, seconds = (len(masks) for masks in partners(n)[0])
-    width = near.shape[1]
+def first_stage(near, far, n):
+    firsts = len(partners(n)[0][0])
     total = near + swap_core(far, n).astype(F32)
-    total = total.reshape(firsts, seconds * STEPS, width)
-    kept = total[0]
-    for i in reversed(range(1, firsts)):
-        kept = kept + swap(total[i].astype(BF), n, 0, i).astype(F32)
-    kept = kept.reshape(seconds, STEPS, width)
-    return [kept[0]] + [swap(kept[j].astype(BF), n, 1, j) for j in range(1, seconds)]
+    total = total.reshape(firsts, total.shape[0] // firsts, total.shape[1])
+    return [total[0]] + [swap(total[i].astype(BF), n, 0, i) for i in range(1, firsts)]
 
 
 def per_device(
@@ -313,32 +325,38 @@
             "heads",
             2 * rows * VDIM * (LAT + width),
         )
-        parts = reduce_rows(near, far, n)
+        terms = first_stage(near, far, n)
 
     with jax.named_scope("norm"):
         high = route_scores[0].astype(BF)
         low = (route_scores[0] - high.astype(F32)).astype(BF)
         routes = jnp.concatenate([route_ids[0].astype(BF), high, low], axis=1)
         routes = jnp.pad(routes, ((0, 0), (0, 128 - 3 * TOPK)))
-        hidden, normed = single(
+        shape = (terms[0].shape[0], width + 128)
+        mine, sent = single(
+            carry_kernel,
+            n,
+            [jax.ShapeDtypeStruct(shape, dtype) for dtype in (F32, BF)],
+            [],
+            terms + [residual[0], routes],
+            "carry",
+            terms[0].size,
+        )
+        got = [swap(sent, n, 1, j) for j in range(1, n // SPAN)]
+        mine, *loaded = load(n, mine, [w_gate[0], w_up[0], w_down[0]])
+        hidden, along = single(
             norm_kernel,
             n,
-            [
-                jax.ShapeDtypeStruct((STEPS, width), F32),
-                jax.ShapeDtypeStruct((STEPS, width + 128), BF),
-            ],
+            [jax.ShapeDtypeStruct((STEPS, width), F32), jax.ShapeDtypeStruct(shape, BF)],
             [],
-            parts + [residual[0], norm_gain.reshape(1, width), routes],
+            [mine] + got + [norm_gain.reshape(1, width)],
             "norm",
-            8 * STEPS * width,
+            8 * mine.size,
         )
 
     with jax.named_scope("spread"):
-        along = [normed] + [swap(normed, n, 1, j) for j in range(1, n // SPAN)]
-        along = jnp.concatenate(along, axis=0)
         blocks = [along] + [swap(along, n, 0, i) for i in range(1, 4)]
-        along, *weights = load(n, along, [w_gate[0], w_up[0], w_down[0]])
-        blocks = blocks + [swap_core(x, n) for x in [along] + blocks[1:]]
+        blocks = blocks + [swap_core(x, n) for x in blocks]
 
     with jax.named_scope("experts"):
         near, far = single(
@@ -346,15 +364,19 @@
             n,
             [jax.ShapeDtypeStruct((rows // 2, width), dtype) for dtype in (F32, BF)],
             [me_one],
-            blocks + weights,
+            blocks + loaded,
             "experts",
             6 * rows * width * w_gate.shape[2],
         )
 
     with jax.named_scope("collect"):
-        result = hidden
-        for term in reduce_rows(near, far, n):
-            result = result + term.astype(F32)
+        kept = 0.0
+        for term in first_stage(near, far, n):
+            kept = kept + term.astype(F32)
+        kept = kept.reshape(n // SPAN, STEPS, width)
+        result = hidden + kept[0]
+        for j in range(1, n // SPAN):
+            result = result + swap(kept[j].astype(BF), n, 1, j).astype(F32)
         return result.astype(BF)[None]
 
 

time: 92.1 us -> 90.7 us (0.985)
  starting transfers between devices: 31.5 us -> 28.1 us
  waiting for transfers between devices: 36.2 us -> 37.4 us
    ppermute x18 -> x15, starting transfers between devices: 23.1 us -> 18.7 us  [swap(): lax.ppermute(x, AXES, [(d, d ^ partners(n)[d & 1][stage][i]) for d in ran...]
    ppermute x6, starting transfers between devices: 1.64 us -> 3.1 us  [swap_core(): return lax.ppermute(x, AXES, [(d, d ^ 1) for d in range(n)])]
    ppermute x18 -> x15, waiting for transfers between devices: 22 us -> 23.4 us  [swap(): lax.ppermute(x, AXES, [(d, d ^ partners(n)[d & 1][stage][i]) for d in ran...]
    pallas_call x3 -> x4, Pallas kernels: 4.7 us -> 5 us  [single(): pl.pallas_call(functools.partial(kernel, n), in_specs=[pl.BlockSpec(memor...]
  transfers between devices with their start and end apart: 25 -> 22, of which waited for: 19 -> 16; matrix products, arithmetic and copies ran while one was open for 0% -> 0% of each run, Pallas kernels for 8% -> 9%
where the time goes in v13:
time: 90.7 us; the launch traced here: 90 us
  waiting for transfers between devices  37.4 us (41%)
  starting transfers between devices  28.1 us (31%)
  Pallas kernels  22 us (24%)
  other arithmetic  1.33 us (1%)
    ppermute x15, waiting for transfers between devices, swap(): lax.ppermute(x, AXES, [(d, d ^ partners(n)[d & 1][stage][i]) for d in ran...  23.4 us
    ppermute x15, starting transfers between devices, swap(): lax.ppermute(x, AXES, [(d, d ^ partners(n)[d & 1][stage][i]) for d in ran...  18.7 us
    pallas_call x1, Pallas kernels, attend(): pl.pallas_call(functools.partial(attend_kernel, n), in_specs=[pl.BlockSpe...  9.22 us
    all_to_all x1, waiting for transfers between devices, per_device(): latents = lax.all_to_all(latents, AXES, 0, 0, tiled=True)  8.22 us
    pallas_call x1, Pallas kernels, load(): pl.pallas_call(functools.partial(load_kernel, n), in_specs=[pl.BlockSpec(...  7.78 us
    all_to_all x1, starting transfers between devices, per_device(): latents = lax.all_to_all(latents, AXES, 0, 0, tiled=True)  6.34 us
    ppermute x6, waiting for transfers between devices, swap_core(): return lax.ppermute(x, AXES, [(d, d ^ 1) for d in range(n)])  5.85 us
    pallas_call x4, Pallas kernels, single(): pl.pallas_call(functools.partial(kernel, n), in_specs=[pl.BlockSpec(memor...  5 us
  transfers between devices with their start and end apart: 22, of which 16 were waited for; matrix products, arithmetic and copies ran while one was open for 0% of the time, Pallas kernels for 9%

profile of v13, /device:TPU:0, one launch (start us, length us, event | category | flops | bytes accessed | tf_op | source)
XLA Modules:
  0.0 90.0 jit_solution(14119554344680789712)
XLA Ops:
  0.7 9.2 %attend.1 = bf16[32,4,512]{2,1,0:T(4,128)(2,1)} custom-call(s32[1]{0:T(128)S(6)} %copy.14.len_ref, bf16[128,576]{1,0:T(8,128)(2,1)} %bitcast.29, bf16[4,576]{1,0:T(4,128)(2,1)} %bitcast.30, bf16[576,8192]{1,0:T(8,128)(2,1)} %bitcast.25), custom_call_target="tpu_custom_call" | custom-call | flops 2281701376 | bytes 9437184 | tf_op jit(solution)/shard_map/attention/attend/pallas_call | solution.py:128
  9.9 6.3 %all-to-all-start = ((bf16[32,4,512]{2,1,0:T(4,128)(2,1)}), bf16[32,4,512]{2,1,0:T(4,128)(2,1)S(1)}, u32[]{:S(2)}, u32[]{:S(2)}) async-start(bf16[32,4,512]{2,1,0:T(4,128)(2,1)} %attend.1), calls=%async_computation | async-start | bytes 262144 | tf_op jit(solution)/shard_map/heads/all_to_all | solution.py:318
  16.3 8.2 %all-to-all-done = bf16[32,4,512]{2,1,0:T(4,128)(2,1)S(1)} async-done(((bf16[32,4,512]{2,1,0:T(4,128)(2,1)}), bf16[32,4,512]{2,1,0:T(4,128)(2,1)S(1)}, u32[]{:S(2)}, u32[]{:S(2)}) %all-to-all-start) | async-done | bytes 131104 | tf_op jit(solution)/shard_map/heads/all_to_all | solution.py:318
  25.8 2.2 %collective-permute-done = bf16[64,7168]{1,0:T(8,128)(2,1)S(1)} collective-permute-done((bf16[64,7168]{1,0:T(8,128)(2,1)S(1)}, bf16[64,7168]{1,0:T(8,128)(2,1)S(1)}, u32[]{:S(2)}, u32[]{:S(2)}) %collective-permute-start) | collective-permute-done | bytes 917536 | tf_op jit(solution)/shard_map/heads/ppermute | solution.py:37
  28.9 1.5 %collective-permute-start.2 = (bf16[16,7168]{1,0:T(8,128)(2,1)S(1)}, bf16[16,7168]{1,0:T(8,128)(2,1)S(1)}, u32[]{:S(2)}, u32[]{:S(2)}) collective-permute-start(bf16[16,7168]{1,0:T(8,128)(2,1)S(1)} %get-tuple-element.41), channel_id=1, source_target_pairs={{0,16},{1,9},{2,18},{3,11},{4,20},{5,13},{6,22},{7,15},{8,24},{9,1... | collective-permute-start | bytes 688136 | tf_op jit(solution)/shard_map/heads/ppermute | solution.py:33
  30.4 1.5 %collective-permute-start.1 = (bf16[16,7168]{1,0:T(8,128)(2,1)S(1)}, bf16[16,7168]{1,0:T(8,128)(2,1)S(1)}, u32[]{:S(2)}, u32[]{:S(2)}) collective-permute-start(bf16[16,7168]{1,0:T(8,128)(2,1)S(1)} %get-tuple-element.42), channel_id=1, source_target_pairs={{0,2},{1,5},{2,0},{3,7},{4,6},{5,1},{6,4},{7,3},{8,10},{9,13},{10,... | collective-permute-start | bytes 688136 | tf_op jit(solution)/shard_map/heads/ppermute | solution.py:33
  32.0 3.4 %collective-permute-done.3.refs_3_ = bf16[16,7168]{1,0:T(8,128)(2,1)S(1)} collective-permute-done((bf16[16,7168]{1,0:T(8,128)(2,1)S(1)}, bf16[16,7168]{1,0:T(8,128)(2,1)S(1)}, u32[]{:S(2)}, u32[]{:S(2)}) %collective-permute-start.3) | collective-permute-done | bytes 229408 | tf_op jit(solution)/shard_map/heads/ppermute | solution.py:33
  35.4 1.4 %collective-permute-done.2.refs_2_ = bf16[16,7168]{1,0:T(8,128)(2,1)S(1)} collective-permute-done((bf16[16,7168]{1,0:T(8,128)(2,1)S(1)}, bf16[16,7168]{1,0:T(8,128)(2,1)S(1)}, u32[]{:S(2)}, u32[]{:S(2)}) %collective-permute-start.2) | collective-permute-done | bytes 229408 | tf_op jit(solution)/shard_map/heads/ppermute | solution.py:33
  38.0 1.4 %collective-permute-start.6 = (bf16[16,7296]{1,0:T(8,128)(2,1)S(1)}, bf16[16,7296]{1,0:T(8,128)(2,1)S(1)}, u32[]{:S(2)}, u32[]{:S(2)}) collective-permute-start(bf16[16,7296]{1,0:T(8,128)(2,1)S(1)} %get-tuple-element.21), channel_id=1, source_target_pairs={{0,12},{1,19},{2,14},{3,17},{4,8},{5,23},{6,10},{7,21},{8,4},{9,27... | collective-permute-start | bytes 700424 | tf_op jit(solution)/shard_map/norm/ppermute | solution.py:33
  39.6 2.8 %collective-permute-start.4 = (bf16[16,7296]{1,0:T(8,128)(2,1)S(1)}, bf16[16,7296]{1,0:T(8,128)(2,1)S(1)}, u32[]{:S(2)}, u32[]{:S(2)}) collective-permute-start(bf16[16,7296]{1,0:T(8,128)(2,1)S(1)} %get-tuple-element.21), channel_id=1, source_target_pairs={{0,4},{1,3},{2,6},{3,1},{4,0},{5,7},{6,2},{7,5},{8,12},{9,11},{10,... | collective-permute-start | bytes 700424 | tf_op jit(solution)/shard_map/norm/ppermute | solution.py:33
  42.5 7.8 %load_experts.1 = (f32[16,7296]{1,0:T(8,128)S(1)}, bf16[7168,512]{1,0:T(8,128)(2,1)S(1)}, bf16[7168,512]{1,0:T(8,128)(2,1)S(1)}, bf16[512,7168]{1,0:T(8,128)(2,1)S(1)}) custom-call(f32[16,7296]{1,0:T(8,128)S(1)} %get-tuple-element.19.refs_0_, bf16[7168,512]{1,0:T(8,128)(2,1)} %bitcast.26, bf16[7168,512]{1,0:T(8,128)(2,1)} %bitcast.27, bf16[512,7168]{1,0:T(8,128)(2,1)} %bitcast.28), custom_call_target="tpu_custom_call" | custom-call | bytes 44040192 | tf_op jit(solution)/shard_map/norm/load_experts/pallas_call | solution.py:227
  51.4 1.4 %collective-permute-start.9 = (bf16[16,7296]{1,0:T(8,128)(2,1)S(1)}, bf16[16,7296]{1,0:T(8,128)(2,1)S(1)}, u32[]{:S(2)}, u32[]{:S(2)}) collective-permute-start(bf16[16,7296]{1,0:T(8,128)(2,1)S(1)} %get-tuple-element.23.refs_0_), channel_id=1, source_target_pairs={{0,18},{1,13},{2,16},{3,15},{4,22},{5,9},{6,20},{7,11},{8,26},{9,5... | collective-permute-start | bytes 700424 | tf_op jit(solution)/shard_map/spread/ppermute | solution.py:33
  52.9 1.5 %collective-permute-start.8 = (bf16[16,7296]{1,0:T(8,128)(2,1)S(1)}, bf16[16,7296]{1,0:T(8,128)(2,1)S(1)}, u32[]{:S(2)}, u32[]{:S(2)}) collective-permute-start(bf16[16,7296]{1,0:T(8,128)(2,1)S(1)} %get-tuple-element.23.refs_0_), channel_id=1, source_target_pairs={{0,16},{1,9},{2,18},{3,11},{4,20},{5,13},{6,22},{7,15},{8,24},{9,1... | collective-permute-start | bytes 700424 | tf_op jit(solution)/shard_map/spread/ppermute | solution.py:33
  55.0 3.5 %collective-permute-done.9.refs_3_ = bf16[16,7296]{1,0:T(8,128)(2,1)S(1)} collective-permute-done((bf16[16,7296]{1,0:T(8,128)(2,1)S(1)}, bf16[16,7296]{1,0:T(8,128)(2,1)S(1)}, u32[]{:S(2)}, u32[]{:S(2)}) %collective-permute-start.9) | collective-permute-done | bytes 233504 | tf_op jit(solution)/shard_map/spread/ppermute | solution.py:33
  58.5 2.4 %collective-permute-done.8.refs_2_ = bf16[16,7296]{1,0:T(8,128)(2,1)S(1)} collective-permute-done((bf16[16,7296]{1,0:T(8,128)(2,1)S(1)}, bf16[16,7296]{1,0:T(8,128)(2,1)S(1)}, u32[]{:S(2)}, u32[]{:S(2)}) %collective-permute-start.8) | collective-permute-done | bytes 233504 | tf_op jit(solution)/shard_map/spread/ppermute | solution.py:33
  60.9 2.4 %collective-permute-start.12 = (bf16[16,7296]{1,0:T(8,128)(2,1)S(1)}, bf16[16,7296]{1,0:T(8,128)(2,1)S(1)}, u32[]{:S(2)}, u32[]{:S(2)}) collective-permute-start(bf16[16,7296]{1,0:T(8,128)(2,1)S(1)} %collective-permute-done.8.refs_2_), channel_id=1, source_target_pairs={{0,1},{1,0},{2,3},{3,2},{4,5},{5,4},{6,7},{7,6},{8,9},{9,8},{10,11... | collective-permute-start | bytes 700424 | tf_op jit(solution)/shard_map/spread/ppermute | solution.py:37
  64.7 3.6 %experts.1 = (f32[64,7168]{1,0:T(8,128)S(1)}, bf16[64,7168]{1,0:T(8,128)(2,1)S(1)}) custom-call(s32[1]{0:T(128)} %bitcast.me_ref, bf16[16,7296]{1,0:T(8,128)(2,1)S(1)} %get-tuple-element.23.refs_0_, bf16[16,7296]{1,0:T(8,128)(2,1)S(1)} %collective-permute-done.7.refs_1_, bf16[16,7296]{1,0:T(8,128)(2,1)S(1)} %collective-permute-done.8.refs_2_, ...), custom_call_target="tpu_custom_call" | custom-call | flops 2818572288 | bytes 23887872 | tf_op jit(solution)/shard_map/experts/experts/pallas_call | solution.py:266
  68.7 2.1 %collective-permute-done.14 = bf16[64,7168]{1,0:T(8,128)(2,1)S(1)} collective-permute-done((bf16[64,7168]{1,0:T(8,128)(2,1)S(1)}, bf16[64,7168]{1,0:T(8,128)(2,1)S(1)}, u32[]{:S(2)}, u32[]{:S(2)}) %collective-permute-start.14) | collective-permute-done | bytes 917536 | tf_op jit(solution)/shard_map/collect/ppermute | solution.py:37
  71.2 1.4 %collective-permute-start.15 = (bf16[16,7168]{1,0:T(8,128)(2,1)S(1)}, bf16[16,7168]{1,0:T(8,128)(2,1)S(1)}, u32[]{:S(2)}, u32[]{:S(2)}) collective-permute-start(bf16[16,7168]{1,0:T(8,128)(2,1)S(1)} %get-tuple-element.37), channel_id=1, source_target_pairs={{0,2},{1,5},{2,0},{3,7},{4,6},{5,1},{6,4},{7,3},{8,10},{9,13},{10,... | collective-permute-start | bytes 688136 | tf_op jit(solution)/shard_map/collect/ppermute | solution.py:33
  74.7 5.0 %collective-permute-done.15 = bf16[16,7168]{1,0:T(8,128)(2,1)S(1)} collective-permute-done((bf16[16,7168]{1,0:T(8,128)(2,1)S(1)}, bf16[16,7168]{1,0:T(8,128)(2,1)S(1)}, u32[]{:S(2)}, u32[]{:S(2)}) %collective-permute-start.15) | collective-permute-done | bytes 229408 | tf_op jit(solution)/shard_map/collect/ppermute | solution.py:33
  79.7 1.5 %collective-permute-done.16 = bf16[16,7168]{1,0:T(8,128)(2,1)S(1)} collective-permute-done((bf16[16,7168]{1,0:T(8,128)(2,1)S(1)}, bf16[16,7168]{1,0:T(8,128)(2,1)S(1)}, u32[]{:S(2)}, u32[]{:S(2)}) %collective-permute-start.16) | collective-permute-done | bytes 229408 | tf_op jit(solution)/shard_map/collect/ppermute | solution.py:33
  81.5 2.1 %collective-permute-start.20 = (bf16[4,7168]{1,0:T(4,128)(2,1)S(1)}, bf16[4,7168]{1,0:T(4,128)(2,1)S(1)}, u32[]{:S(2)}, u32[]{:S(2)}) collective-permute-start(bf16[4,7168]{1,0:T(4,128)(2,1)S(1)} %get-tuple-element.44), channel_id=1, source_target_pairs={{0,12},{1,19},{2,14},{3,17},{4,8},{5,23},{6,10},{7,21},{8,4},{9,27... | collective-permute-start | bytes 172040 | tf_op jit(solution)/shard_map/collect/ppermute | solution.py:33
  85.8 1.9 %collective-permute-done.20 = bf16[4,7168]{1,0:T(4,128)(2,1)S(1)} collective-permute-done((bf16[4,7168]{1,0:T(4,128)(2,1)S(1)}, bf16[4,7168]{1,0:T(4,128)(2,1)S(1)}, u32[]{:S(2)}, u32[]{:S(2)}) %collective-permute-start.20) | collective-permute-done | bytes 57376 | tf_op jit(solution)/shard_map/collect/ppermute | solution.py:33
  87.6 1.7 %collective-permute-done.19 = bf16[4,7168]{1,0:T(4,128)(2,1)S(1)} collective-permute-done((bf16[4,7168]{1,0:T(4,128)(2,1)S(1)}, bf16[4,7168]{1,0:T(4,128)(2,1)S(1)}, u32[]{:S(2)}, u32[]{:S(2)}) %collective-permute-start.19) | collective-permute-done | bytes 57376 | tf_op jit(solution)/shard_map/collect/ppermute | solution.py:33
  (51 shorter events, 12.9 us)
Async XLA Ops:
  0.7 23.9 %copy-start = (bf16[1,128,7168]{2,1,0:T(8,128)(2,1)S(1)}, bf16[1,128,7168]{2,1,0:T(8,128)(2,1)}, u32[]{:S(2)}) copy-start(bf16[1,128,7168]{2,1,0:T(8,128)(2,1)} %param.22) | copy-start | bytes 5505028
  0.7 23.9 %copy-start.1 = (bf16[1,512,128]{2,1,0:T(8,128)(2,1)S(1)}, bf16[1,512,128]{2,1,0:T(8,128)(2,1)}, u32[]{:S(2)}) copy-start(bf16[1,512,128]{2,1,0:T(8,128)(2,1)} %param.21) | copy-start | bytes 393220
  9.9 14.6 %all-to-all-start = ((bf16[32,4,512]{2,1,0:T(4,128)(2,1)}), bf16[32,4,512]{2,1,0:T(4,128)(2,1)S(1)}, u32[]{:S(2)}, u32[]{:S(2)}) async-start(bf16[32,4,512]{2,1,0:T(4,128)(2,1)} %attend.1), calls=%async_computation | async-start | bytes 262144 | tf_op jit(solution)/shard_map/heads/all_to_all | solution.py:318
  25.5 2.5 %collective-permute-start = (bf16[64,7168]{1,0:T(8,128)(2,1)S(1)}, bf16[64,7168]{1,0:T(8,128)(2,1)S(1)}, u32[]{:S(2)}, u32[]{:S(2)}) collective-permute-start(bf16[64,7168]{1,0:T(8,128)(2,1)S(1)} %get-tuple-element.18), channel_id=1, source_target_pairs={{0,1},{1,0},{2,3},{3,2},{4,5},{5,4},{6,7},{7,6},{8,9},{9,8},{10,11... | collective-permute-start | bytes 2752520 | tf_op jit(solution)/shard_map/heads/ppermute | solution.py:37
  28.3 7.1 %collective-permute-start.3 = (bf16[16,7168]{1,0:T(8,128)(2,1)S(1)}, bf16[16,7168]{1,0:T(8,128)(2,1)S(1)}, u32[]{:S(2)}, u32[]{:S(2)}) collective-permute-start(bf16[16,7168]{1,0:T(8,128)(2,1)S(1)} %get-tuple-element.40), channel_id=1, source_target_pairs={{0,18},{1,13},{2,16},{3,15},{4,22},{5,9},{6,20},{7,11},{8,26},{9,5... | collective-permute-start | bytes 688136 | tf_op jit(solution)/shard_map/heads/ppermute | solution.py:33
  28.9 7.9 %collective-permute-start.2 = (bf16[16,7168]{1,0:T(8,128)(2,1)S(1)}, bf16[16,7168]{1,0:T(8,128)(2,1)S(1)}, u32[]{:S(2)}, u32[]{:S(2)}) collective-permute-start(bf16[16,7168]{1,0:T(8,128)(2,1)S(1)} %get-tuple-element.41), channel_id=1, source_target_pairs={{0,16},{1,9},{2,18},{3,11},{4,20},{5,13},{6,22},{7,15},{8,24},{9,1... | collective-permute-start | bytes 688136 | tf_op jit(solution)/shard_map/heads/ppermute | solution.py:33
  30.4 7.4 %collective-permute-start.1 = (bf16[16,7168]{1,0:T(8,128)(2,1)S(1)}, bf16[16,7168]{1,0:T(8,128)(2,1)S(1)}, u32[]{:S(2)}, u32[]{:S(2)}) collective-permute-start(bf16[16,7168]{1,0:T(8,128)(2,1)S(1)} %get-tuple-element.42), channel_id=1, source_target_pairs={{0,2},{1,5},{2,0},{3,7},{4,6},{5,1},{6,4},{7,3},{8,10},{9,13},{10,... | collective-permute-start | bytes 688136 | tf_op jit(solution)/shard_map/heads/ppermute | solution.py:33
  38.0 12.3 %collective-permute-start.6 = (bf16[16,7296]{1,0:T(8,128)(2,1)S(1)}, bf16[16,7296]{1,0:T(8,128)(2,1)S(1)}, u32[]{:S(2)}, u32[]{:S(2)}) collective-permute-start(bf16[16,7296]{1,0:T(8,128)(2,1)S(1)} %get-tuple-element.21), channel_id=1, source_target_pairs={{0,12},{1,19},{2,14},{3,17},{4,8},{5,23},{6,10},{7,21},{8,4},{9,27... | collective-permute-start | bytes 700424 | tf_op jit(solution)/shard_map/norm/ppermute | solution.py:33
  39.4 11.8 %collective-permute-start.5 = (bf16[16,7296]{1,0:T(8,128)(2,1)S(1)}, bf16[16,7296]{1,0:T(8,128)(2,1)S(1)}, u32[]{:S(2)}, u32[]{:S(2)}) collective-permute-start(bf16[16,7296]{1,0:T(8,128)(2,1)S(1)} %get-tuple-element.21), channel_id=1, source_target_pairs={{0,8},{1,17},{2,10},{3,19},{4,12},{5,21},{6,14},{7,23},{8,0},{9,25... | collective-permute-start | bytes 700424 | tf_op jit(solution)/shard_map/norm/ppermute | solution.py:33
  39.6 11.5 %collective-permute-start.4 = (bf16[16,7296]{1,0:T(8,128)(2,1)S(1)}, bf16[16,7296]{1,0:T(8,128)(2,1)S(1)}, u32[]{:S(2)}, u32[]{:S(2)}) collective-permute-start(bf16[16,7296]{1,0:T(8,128)(2,1)S(1)} %get-tuple-element.21), channel_id=1, source_target_pairs={{0,4},{1,3},{2,6},{3,1},{4,0},{5,7},{6,2},{7,5},{8,12},{9,11},{10,... | collective-permute-start | bytes 700424 | tf_op jit(solution)/shard_map/norm/ppermute | solution.py:33
  51.4 7.1 %collective-permute-start.9 = (bf16[16,7296]{1,0:T(8,128)(2,1)S(1)}, bf16[16,7296]{1,0:T(8,128)(2,1)S(1)}, u32[]{:S(2)}, u32[]{:S(2)}) collective-permute-start(bf16[16,7296]{1,0:T(8,128)(2,1)S(1)} %get-tuple-element.23.refs_0_), channel_id=1, source_target_pairs={{0,18},{1,13},{2,16},{3,15},{4,22},{5,9},{6,20},{7,11},{8,26},{9,5... | collective-permute-start | bytes 700424 | tf_op jit(solution)/shard_map/spread/ppermute | solution.py:33
  52.9 8.0 %collective-permute-start.8 = (bf16[16,7296]{1,0:T(8,128)(2,1)S(1)}, bf16[16,7296]{1,0:T(8,128)(2,1)S(1)}, u32[]{:S(2)}, u32[]{:S(2)}) collective-permute-start(bf16[16,7296]{1,0:T(8,128)(2,1)S(1)} %get-tuple-element.23.refs_0_), channel_id=1, source_target_pairs={{0,16},{1,9},{2,18},{3,11},{4,20},{5,13},{6,22},{7,15},{8,24},{9,1... | collective-permute-start | bytes 700424 | tf_op jit(solution)/shard_map/spread/ppermute | solution.py:33
  54.3 8.9 %collective-permute-start.7 = (bf16[16,7296]{1,0:T(8,128)(2,1)S(1)}, bf16[16,7296]{1,0:T(8,128)(2,1)S(1)}, u32[]{:S(2)}, u32[]{:S(2)}) collective-permute-start(bf16[16,7296]{1,0:T(8,128)(2,1)S(1)} %get-tuple-element.23.refs_0_), channel_id=1, source_target_pairs={{0,2},{1,5},{2,0},{3,7},{4,6},{5,1},{6,4},{7,3},{8,10},{9,13},{10,... | collective-permute-start | bytes 700424 | tf_op jit(solution)/shard_map/spread/ppermute | solution.py:33
  55.0 8.3 %collective-permute-start.10 = (bf16[16,7296]{1,0:T(8,128)(2,1)S(1)}, bf16[16,7296]{1,0:T(8,128)(2,1)S(1)}, u32[]{:S(2)}, u32[]{:S(2)}) collective-permute-start(bf16[16,7296]{1,0:T(8,128)(2,1)S(1)} %get-tuple-element.23.refs_0_), channel_id=1, source_target_pairs={{0,1},{1,0},{2,3},{3,2},{4,5},{5,4},{6,7},{7,6},{8,9},{9,8},{10,11... | collective-permute-start | bytes 700424 | tf_op jit(solution)/shard_map/spread/ppermute | solution.py:37
  58.5 4.7 %collective-permute-start.13 = (bf16[16,7296]{1,0:T(8,128)(2,1)S(1)}, bf16[16,7296]{1,0:T(8,128)(2,1)S(1)}, u32[]{:S(2)}, u32[]{:S(2)}) collective-permute-start(bf16[16,7296]{1,0:T(8,128)(2,1)S(1)} %collective-permute-done.9.refs_3_), channel_id=1, source_target_pairs={{0,1},{1,0},{2,3},{3,2},{4,5},{5,4},{6,7},{7,6},{8,9},{9,8},{10,11... | collective-permute-start | bytes 700424 | tf_op jit(solution)/shard_map/spread/ppermute | solution.py:37
  60.9 3.5 %collective-permute-start.12 = (bf16[16,7296]{1,0:T(8,128)(2,1)S(1)}, bf16[16,7296]{1,0:T(8,128)(2,1)S(1)}, u32[]{:S(2)}, u32[]{:S(2)}) collective-permute-start(bf16[16,7296]{1,0:T(8,128)(2,1)S(1)} %collective-permute-done.8.refs_2_), channel_id=1, source_target_pairs={{0,1},{1,0},{2,3},{3,2},{4,5},{5,4},{6,7},{7,6},{8,9},{9,8},{10,11... | collective-permute-start | bytes 700424 | tf_op jit(solution)/shard_map/spread/ppermute | solution.py:37
  63.2 1.5 %collective-permute-start.11 = (bf16[16,7296]{1,0:T(8,128)(2,1)S(1)}, bf16[16,7296]{1,0:T(8,128)(2,1)S(1)}, u32[]{:S(2)}, u32[]{:S(2)}) collective-permute-start(bf16[16,7296]{1,0:T(8,128)(2,1)S(1)} %collective-permute-done.7.refs_1_), channel_id=1, source_target_pairs={{0,1},{1,0},{2,3},{3,2},{4,5},{5,4},{6,7},{7,6},{8,9},{9,8},{10,11... | collective-permute-start | bytes 700424 | tf_op jit(solution)/shard_map/spread/ppermute | solution.py:37
  68.3 2.5 %collective-permute-start.14 = (bf16[64,7168]{1,0:T(8,128)(2,1)S(1)}, bf16[64,7168]{1,0:T(8,128)(2,1)S(1)}, u32[]{:S(2)}, u32[]{:S(2)}) collective-permute-start(bf16[64,7168]{1,0:T(8,128)(2,1)S(1)} %get-tuple-element.28), channel_id=1, source_target_pairs={{0,1},{1,0},{2,3},{3,2},{4,5},{5,4},{6,7},{7,6},{8,9},{9,8},{10,11... | collective-permute-start | bytes 2752520 | tf_op jit(solution)/shard_map/collect/ppermute | solution.py:37
  71.2 8.5 %collective-permute-start.15 = (bf16[16,7168]{1,0:T(8,128)(2,1)S(1)}, bf16[16,7168]{1,0:T(8,128)(2,1)S(1)}, u32[]{:S(2)}, u32[]{:S(2)}) collective-permute-start(bf16[16,7168]{1,0:T(8,128)(2,1)S(1)} %get-tuple-element.37), channel_id=1, source_target_pairs={{0,2},{1,5},{2,0},{3,7},{4,6},{5,1},{6,4},{7,3},{8,10},{9,13},{10,... | collective-permute-start | bytes 688136 | tf_op jit(solution)/shard_map/collect/ppermute | solution.py:33
  72.5 7.2 %collective-permute-start.17 = (bf16[16,7168]{1,0:T(8,128)(2,1)S(1)}, bf16[16,7168]{1,0:T(8,128)(2,1)S(1)}, u32[]{:S(2)}, u32[]{:S(2)}) collective-permute-start(bf16[16,7168]{1,0:T(8,128)(2,1)S(1)} %get-tuple-element.38), channel_id=1, source_target_pairs={{0,18},{1,13},{2,16},{3,15},{4,22},{5,9},{6,20},{7,11},{8,26},{9,5... | collective-permute-start | bytes 688136 | tf_op jit(solution)/shard_map/collect/ppermute | solution.py:33
  73.5 7.7 %collective-permute-start.16 = (bf16[16,7168]{1,0:T(8,128)(2,1)S(1)}, bf16[16,7168]{1,0:T(8,128)(2,1)S(1)}, u32[]{:S(2)}, u32[]{:S(2)}) collective-permute-start(bf16[16,7168]{1,0:T(8,128)(2,1)S(1)} %get-tuple-element.39), channel_id=1, source_target_pairs={{0,16},{1,9},{2,18},{3,11},{4,20},{5,13},{6,22},{7,15},{8,24},{9,1... | collective-permute-start | bytes 688136 | tf_op jit(solution)/shard_map/collect/ppermute | solution.py:33
  81.4 4.4 %collective-permute-start.18 = (bf16[4,7168]{1,0:T(4,128)(2,1)S(1)}, bf16[4,7168]{1,0:T(4,128)(2,1)S(1)}, u32[]{:S(2)}, u32[]{:S(2)}) collective-permute-start(bf16[4,7168]{1,0:T(4,128)(2,1)S(1)} %get-tuple-element.43), channel_id=1, source_target_pairs={{0,4},{1,3},{2,6},{3,1},{4,0},{5,7},{6,2},{7,5},{8,12},{9,11},{10,... | collective-permute-start | bytes 172040 | tf_op jit(solution)/shard_map/collect/ppermute | solution.py:33
  81.5 6.1 %collective-permute-start.20 = (bf16[4,7168]{1,0:T(4,128)(2,1)S(1)}, bf16[4,7168]{1,0:T(4,128)(2,1)S(1)}, u32[]{:S(2)}, u32[]{:S(2)}) collective-permute-start(bf16[4,7168]{1,0:T(4,128)(2,1)S(1)} %get-tuple-element.44), channel_id=1, source_target_pairs={{0,12},{1,19},{2,14},{3,17},{4,8},{5,23},{6,10},{7,21},{8,4},{9,27... | collective-permute-start | bytes 172040 | tf_op jit(solution)/shard_map/collect/ppermute | solution.py:33
  83.6 5.7 %collective-permute-start.19 = (bf16[4,7168]{1,0:T(4,128)(2,1)S(1)}, bf16[4,7168]{1,0:T(4,128)(2,1)S(1)}, u32[]{:S(2)}, u32[]{:S(2)}) collective-permute-start(bf16[4,7168]{1,0:T(4,128)(2,1)S(1)} %get-tuple-element.45), channel_id=1, source_target_pairs={{0,8},{1,17},{2,10},{3,19},{4,12},{5,21},{6,14},{7,23},{8,0},{9,25... | collective-permute-start | bytes 172040 | tf_op jit(solution)/shard_map/collect/ppermute | solution.py:33
  (4 other events, 43.5 us)

commit v14 on v13

--- a/solution.py
+++ b/solution.py
@@ -20,7 +20,9 @@
 BF = jnp.bfloat16
 F32 = jnp.float32
 VMEM_LIMIT = 16 * 1024 * 1024
-LOAD_LIMIT = 28
+LOADS = 8
+EARLY = 4
+LOAD_LIMITS = (48, 35)
 
 
 def partners(n):
@@ -207,15 +209,16 @@
     out_ref[:, width:] = total[:, width:].astype(BF)
 
 
-def load_kernel(n, *refs):
-    sources, targets, sem = refs[1:4], refs[5:8], refs[8]
-    copies = [pltpu.make_async_copy(refs[0], refs[4], sem.at[24])]
-    for i in range(3):
-        step = sources[i].shape[0] // 8
-        for j in range(8):
-            here = pl.ds(j * step, step)
+def load_kernel(n, ranges, *refs):
+    count = len(ranges)
+    sources, targets, sem = refs[1 : 1 + count], refs[2 + count : 2 + 2 * count], refs[-1]
+    copies = [pltpu.make_async_copy(refs[0], refs[1 + count], sem.at[0])]
+    for source, target, (first, rows) in zip(sources, targets, ranges):
+        step = rows // LOADS
+        for j in range(LOADS):
+            there, here = pl.ds(first + j * step, step), pl.ds(j * step, step)
             copies.append(
-                pltpu.make_async_copy(sources[i].at[here], targets[i].at[here], sem.at[8 * i + j])
+                pltpu.make_async_copy(source.at[there], target.at[here], sem.at[len(copies)])
             )
     for copy in copies:
         copy.start()
@@ -223,32 +226,37 @@
         copy.wait()
 
 
-def load(n, passed, arrays):
+def load(n, passed, arrays, ranges, limit):
+    shapes = [(rows, a.shape[1]) for a, (_, rows) in zip(arrays, ranges)]
     return pl.pallas_call(
-        functools.partial(load_kernel, n),
-        in_specs=[pl.BlockSpec(memory_space=pltpu.VMEM)] + [pl.BlockSpec(memory_space=pl.ANY)] * 3,
-        out_specs=[pl.BlockSpec(memory_space=pltpu.VMEM)] * 4,
-        out_shape=[jax.ShapeDtypeStruct(a.shape, a.dtype) for a in [passed] + arrays],
-        scratch_shapes=[pltpu.SemaphoreType.DMA((25,))],
-        compiler_params=pltpu.CompilerParams(vmem_limit_bytes=LOAD_LIMIT * 1024 * 1024),
+        functools.partial(load_kernel, n, ranges),
+        in_specs=[pl.BlockSpec(memory_space=pltpu.VMEM)]
+        + [pl.BlockSpec(memory_space=pl.ANY)] * len(arrays),
+        out_specs=[pl.BlockSpec(memory_space=pltpu.VMEM)] * (1 + len(arrays)),
+        out_shape=[jax.ShapeDtypeStruct(passed.shape, passed.dtype)]
+        + [jax.ShapeDtypeStruct(shape, BF) for shape in shapes],
+        scratch_shapes=[pltpu.SemaphoreType.DMA((1 + LOADS * len(arrays),))],
+        compiler_params=pltpu.CompilerParams(vmem_limit_bytes=limit * 1024 * 1024),
         cost_estimate=pl.CostEstimate(
-            flops=0, bytes_accessed=sum(4 * a.size for a in arrays), transcendentals=0
+            flops=0, bytes_accessed=sum(4 * r * c for r, c in shapes), transcendentals=0
         ),
-        name="load_experts",
+        name="load",
     )(passed, *arrays)
 
 
 def expert_kernel(n, me_ref, *refs, n_ep):
-    blocks, (gate_ref, up_ref, down_ref, near_ref, far_ref) = refs[:8], refs[8:]
+    blocks, (early_ref, gate_ref, up_ref, down_ref, near_ref, far_ref) = refs[:8], refs[8:]
     rows = n * STEPS
-    width, units = gate_ref.shape
+    width, units = up_ref.shape
     part = width // SPAN
     gate = jnp.zeros((rows, units), F32)
     up = jnp.zeros((rows, units), F32)
     for p in range(SPAN):
         here = slice(p * part, (p + 1) * part)
         x = jnp.concatenate([ref[:, here] for ref in blocks], axis=0)
-        gate += jnp.dot(x, gate_ref[here], preferred_element_type=F32)
+        late = p - EARLY
+        gate_part = early_ref[here] if late < 0 else gate_ref[late * part : (late + 1) * part]
+        gate += jnp.dot(x, gate_part, preferred_element_type=F32)
         up += jnp.dot(x, up_ref[here], preferred_element_type=F32)
     act = (gate * jax.nn.sigmoid(gate) * up).astype(BF)
     routes = jnp.concatenate([ref[:, width:] for ref in blocks], axis=0).astype(F32)
@@ -276,11 +284,12 @@
     )(*scalars, *arrays)
 
 
-def first_stage(near, far, n):
-    firsts = len(partners(n)[0][0])
+def first_stage(near, far, n, order, beside=lambda rows: rows):
+    firsts = len(order) + 1
     total = near + swap_core(far, n).astype(F32)
     total = total.reshape(firsts, total.shape[0] // firsts, total.shape[1])
-    return [total[0]] + [swap(total[i].astype(BF), n, 0, i) for i in range(1, firsts)]
+    got = [swap(total[i].astype(BF), n, 0, i) for i in order]
+    return [beside(total[0])] + got
 
 
 def per_device(
@@ -325,7 +334,15 @@
             "heads",
             2 * rows * VDIM * (LAT + width),
         )
-        terms = first_stage(near, far, n)
+        early = width // SPAN * EARLY
+        loaded = []
+
+        def load_early(rows):
+            rows, *weights = load(n, rows, [w_gate[0]], [(0, early)], LOAD_LIMITS[0])
+            loaded.extend(weights)
+            return rows
+
+        terms = first_stage(near, far, n, (1, 2, 3), load_early)
 
     with jax.named_scope("norm"):
         high = route_scores[0].astype(BF)
@@ -343,7 +360,9 @@
             terms[0].size,
         )
         got = [swap(sent, n, 1, j) for j in range(1, n // SPAN)]
-        mine, *loaded = load(n, mine, [w_gate[0], w_up[0], w_down[0]])
+        rest = [(early, width - early), (0, width), (0, w_down.shape[1])]
+        mine, *weights = load(n, mine, [w_gate[0], w_up[0], w_down[0]], rest, LOAD_LIMITS[1])
+        loaded.extend(weights)
         hidden, along = single(
             norm_kernel,
             n,
@@ -371,11 +390,11 @@
 
     with jax.named_scope("collect"):
         kept = 0.0
-        for term in first_stage(near, far, n):
+        for term in first_stage(near, far, n, (3, 2, 1)):
             kept = kept + term.astype(F32)
         kept = kept.reshape(n // SPAN, STEPS, width)
         result = hidden + kept[0]
-        for j in range(1, n // SPAN):
+        for j in reversed(range(1, n // SPAN)):
             result = result + swap(kept[j].astype(BF), n, 1, j).astype(F32)
         return result.astype(BF)[None]
 

time: 90.7 us -> 88.6 us (0.977)
  waiting for transfers between devices: 37.4 us -> 34 us
  Pallas kernels: 22 us -> 23.3 us
    ppermute x15, waiting for transfers between devices: 23.4 us -> 19.9 us  [swap(): lax.ppermute(x, AXES, [(d, d ^ partners(n)[d & 1][stage][i]) for d in ran...]
    pallas_call x1 -> x2, Pallas kernels: 7.78 us -> 9.08 us  [load(): pl.pallas_call(functools.partial(load_kernel, n, ranges), in_specs=[pl.Bl...]
    ppermute x6, starting transfers between devices: 3.1 us -> 2.07 us  [swap_core(): return lax.ppermute(x, AXES, [(d, d ^ 1) for d in range(n)])]
    all_to_all x1, starting transfers between devices: 6.34 us -> 7.3 us  [per_device(): latents = lax.all_to_all(latents, AXES, 0, 0, tiled=True)]
  transfers between devices with their start and end apart: 22 -> 22, of which waited for: 16 -> 15; matrix products, arithmetic and copies ran while one was open for 0% -> 0% of each run, Pallas kernels for 9% -> 10%
where the time goes in v14:
time: 88.6 us; the launch traced here: 88.7 us
  waiting for transfers between devices  34 us (38%)
  starting transfers between devices  28.9 us (33%)
  Pallas kernels  23.3 us (26%)
  other arithmetic  1.33 us (2%)
    ppermute x15, waiting for transfers between devices, swap(): lax.ppermute(x, AXES, [(d, d ^ partners(n)[d & 1][stage][i]) for d in ran...  19.9 us
    ppermute x15, starting transfers between devices, swap(): lax.ppermute(x, AXES, [(d, d ^ partners(n)[d & 1][stage][i]) for d in ran...  19.6 us
    pallas_call x1, Pallas kernels, attend(): pl.pallas_call(functools.partial(attend_kernel, n), in_specs=[pl.BlockSpe...  9.21 us
    pallas_call x2, Pallas kernels, load(): pl.pallas_call(functools.partial(load_kernel, n, ranges), in_specs=[pl.Bl...  9.08 us
    all_to_all x1, waiting for transfers between devices, per_device(): latents = lax.all_to_all(latents, AXES, 0, 0, tiled=True)  8.22 us
    all_to_all x1, starting transfers between devices, per_device(): latents = lax.all_to_all(latents, AXES, 0, 0, tiled=True)  7.3 us
    ppermute x6, waiting for transfers between devices, swap_core(): return lax.ppermute(x, AXES, [(d, d ^ 1) for d in range(n)])  5.83 us
    pallas_call x4, Pallas kernels, single(): pl.pallas_call(functools.partial(kernel, n), in_specs=[pl.BlockSpec(memor...  4.98 us
  transfers between devices with their start and end apart: 22, of which 15 were waited for; matrix products, arithmetic and copies ran while one was open for 0% of the time, Pallas kernels for 10%

profile of v14, /device:TPU:0, one launch (start us, length us, event | category | flops | bytes accessed | tf_op | source)
XLA Modules:
  0.0 88.7 jit_solution(2526204996901432982)
XLA Ops:
  0.7 9.2 %attend.1 = bf16[32,4,512]{2,1,0:T(4,128)(2,1)} custom-call(s32[1]{0:T(128)S(6)} %copy.14.len_ref, bf16[128,576]{1,0:T(8,128)(2,1)} %bitcast.30, bf16[4,576]{1,0:T(4,128)(2,1)} %bitcast.31, bf16[576,8192]{1,0:T(8,128)(2,1)} %bitcast.27), custom_call_target="tpu_custom_call" | custom-call | flops 2281701376 | bytes 9437184 | tf_op jit(solution)/shard_map/attention/attend/pallas_call | solution.py:130
  9.9 7.3 %all-to-all-start = ((bf16[32,4,512]{2,1,0:T(4,128)(2,1)}), bf16[32,4,512]{2,1,0:T(4,128)(2,1)S(1)}, u32[]{:S(2)}, u32[]{:S(2)}) async-start(bf16[32,4,512]{2,1,0:T(4,128)(2,1)} %attend.1), calls=%async_computation | async-start | bytes 262144 | tf_op jit(solution)/shard_map/heads/all_to_all | solution.py:327
  17.2 8.2 %all-to-all-done = bf16[32,4,512]{2,1,0:T(4,128)(2,1)S(1)} async-done(((bf16[32,4,512]{2,1,0:T(4,128)(2,1)}), bf16[32,4,512]{2,1,0:T(4,128)(2,1)S(1)}, u32[]{:S(2)}, u32[]{:S(2)}) %all-to-all-start) | async-done | bytes 131104 | tf_op jit(solution)/shard_map/heads/all_to_all | solution.py:327
  26.7 2.2 %collective-permute-done = bf16[64,7168]{1,0:T(8,128)(2,1)S(1)} collective-permute-done((bf16[64,7168]{1,0:T(8,128)(2,1)S(1)}, bf16[64,7168]{1,0:T(8,128)(2,1)S(1)}, u32[]{:S(2)}, u32[]{:S(2)}) %collective-permute-start) | collective-permute-done | bytes 917536 | tf_op jit(solution)/shard_map/heads/ppermute | solution.py:39
  29.8 1.5 %collective-permute-start.2 = (bf16[16,7168]{1,0:T(8,128)(2,1)S(1)}, bf16[16,7168]{1,0:T(8,128)(2,1)S(1)}, u32[]{:S(2)}, u32[]{:S(2)}) collective-permute-start(bf16[16,7168]{1,0:T(8,128)(2,1)S(1)} %get-tuple-element.45), channel_id=1, source_target_pairs={{0,16},{1,9},{2,18},{3,11},{4,20},{5,13},{6,22},{7,15},{8,24},{9,1... | collective-permute-start | bytes 688136 | tf_op jit(solution)/shard_map/heads/ppermute | solution.py:35
  31.3 1.5 %collective-permute-start.1 = (bf16[16,7168]{1,0:T(8,128)(2,1)S(1)}, bf16[16,7168]{1,0:T(8,128)(2,1)S(1)}, u32[]{:S(2)}, u32[]{:S(2)}) collective-permute-start(bf16[16,7168]{1,0:T(8,128)(2,1)S(1)} %get-tuple-element.46), channel_id=1, source_target_pairs={{0,2},{1,5},{2,0},{3,7},{4,6},{5,1},{6,4},{7,3},{8,10},{9,13},{10,... | collective-permute-start | bytes 688136 | tf_op jit(solution)/shard_map/heads/ppermute | solution.py:35
  32.9 2.3 %load.2 = (f32[16,7168]{1,0:T(8,128)S(1)}, bf16[3584,512]{1,0:T(8,128)(2,1)S(1)}) custom-call(f32[16,7168]{1,0:T(8,128)S(1)} %slice.69.refs_0_, bf16[7168,512]{1,0:T(8,128)(2,1)} %bitcast.25), custom_call_target="tpu_custom_call" | custom-call | bytes 7340032 | tf_op jit(solution)/shard_map/heads/load/pallas_call | solution.py:231
  36.3 1.4 %collective-permute-done.2.refs_2_ = bf16[16,7168]{1,0:T(8,128)(2,1)S(1)} collective-permute-done((bf16[16,7168]{1,0:T(8,128)(2,1)S(1)}, bf16[16,7168]{1,0:T(8,128)(2,1)S(1)}, u32[]{:S(2)}, u32[]{:S(2)}) %collective-permute-start.2) | collective-permute-done | bytes 229408 | tf_op jit(solution)/shard_map/heads/ppermute | solution.py:35
  38.9 1.4 %collective-permute-start.6 = (bf16[16,7296]{1,0:T(8,128)(2,1)S(1)}, bf16[16,7296]{1,0:T(8,128)(2,1)S(1)}, u32[]{:S(2)}, u32[]{:S(2)}) collective-permute-start(bf16[16,7296]{1,0:T(8,128)(2,1)S(1)} %get-tuple-element.24), channel_id=1, source_target_pairs={{0,12},{1,19},{2,14},{3,17},{4,8},{5,23},{6,10},{7,21},{8,4},{9,27... | collective-permute-start | bytes 700424 | tf_op jit(solution)/shard_map/norm/ppermute | solution.py:35
  40.5 2.8 %collective-permute-start.4 = (bf16[16,7296]{1,0:T(8,128)(2,1)S(1)}, bf16[16,7296]{1,0:T(8,128)(2,1)S(1)}, u32[]{:S(2)}, u32[]{:S(2)}) collective-permute-start(bf16[16,7296]{1,0:T(8,128)(2,1)S(1)} %get-tuple-element.24), channel_id=1, source_target_pairs={{0,4},{1,3},{2,6},{3,1},{4,0},{5,7},{6,2},{7,5},{8,12},{9,11},{10,... | collective-permute-start | bytes 700424 | tf_op jit(solution)/shard_map/norm/ppermute | solution.py:35
  43.4 6.7 %load.3 = (f32[16,7296]{1,0:T(8,128)S(1)}, bf16[3584,512]{1,0:T(8,128)(2,1)S(1)}, bf16[7168,512]{1,0:T(8,128)(2,1)S(1)}, bf16[512,7168]{1,0:T(8,128)(2,1)S(1)}) custom-call(f32[16,7296]{1,0:T(8,128)S(1)} %get-tuple-element.22.refs_0_, bf16[7168,512]{1,0:T(8,128)(2,1)} %bitcast.26, bf16[7168,512]{1,0:T(8,128)(2,1)} %bitcast.28, bf16[512,7168]{1,0:T(8,128)(2,1)} %bitcast.29), custom_call_target="tpu_custom_call" | custom-call | bytes 36700160 | tf_op jit(solution)/shard_map/norm/load/pallas_call | solution.py:231
  50.1 1.9 %collective-permute-done.5.refs_1_ = bf16[16,7296]{1,0:T(8,128)(2,1)S(1)} collective-permute-done((bf16[16,7296]{1,0:T(8,128)(2,1)S(1)}, bf16[16,7296]{1,0:T(8,128)(2,1)S(1)}, u32[]{:S(2)}, u32[]{:S(2)}) %collective-permute-start.5) | collective-permute-done | bytes 233504 | tf_op jit(solution)/shard_map/norm/ppermute | solution.py:35
  52.3 1.4 %collective-permute-start.9 = (bf16[16,7296]{1,0:T(8,128)(2,1)S(1)}, bf16[16,7296]{1,0:T(8,128)(2,1)S(1)}, u32[]{:S(2)}, u32[]{:S(2)}) collective-permute-start(bf16[16,7296]{1,0:T(8,128)(2,1)S(1)} %get-tuple-element.26.refs_0_), channel_id=1, source_target_pairs={{0,18},{1,13},{2,16},{3,15},{4,22},{5,9},{6,20},{7,11},{8,26},{9,5... | collective-permute-start | bytes 700424 | tf_op jit(solution)/shard_map/spread/ppermute | solution.py:35
  53.8 1.5 %collective-permute-start.8 = (bf16[16,7296]{1,0:T(8,128)(2,1)S(1)}, bf16[16,7296]{1,0:T(8,128)(2,1)S(1)}, u32[]{:S(2)}, u32[]{:S(2)}) collective-permute-start(bf16[16,7296]{1,0:T(8,128)(2,1)S(1)} %get-tuple-element.26.refs_0_), channel_id=1, source_target_pairs={{0,16},{1,9},{2,18},{3,11},{4,20},{5,13},{6,22},{7,15},{8,24},{9,1... | collective-permute-start | bytes 700424 | tf_op jit(solution)/shard_map/spread/ppermute | solution.py:35
  55.9 3.5 %collective-permute-done.9.refs_3_ = bf16[16,7296]{1,0:T(8,128)(2,1)S(1)} collective-permute-done((bf16[16,7296]{1,0:T(8,128)(2,1)S(1)}, bf16[16,7296]{1,0:T(8,128)(2,1)S(1)}, u32[]{:S(2)}, u32[]{:S(2)}) %collective-permute-start.9) | collective-permute-done | bytes 233504 | tf_op jit(solution)/shard_map/spread/ppermute | solution.py:35
  59.4 2.4 %collective-permute-done.8.refs_2_ = bf16[16,7296]{1,0:T(8,128)(2,1)S(1)} collective-permute-done((bf16[16,7296]{1,0:T(8,128)(2,1)S(1)}, bf16[16,7296]{1,0:T(8,128)(2,1)S(1)}, u32[]{:S(2)}, u32[]{:S(2)}) %collective-permute-start.8) | collective-permute-done | bytes 233504 | tf_op jit(solution)/shard_map/spread/ppermute | solution.py:35
  64.6 3.6 %experts.1 = (f32[64,7168]{1,0:T(8,128)S(1)}, bf16[64,7168]{1,0:T(8,128)(2,1)S(1)}) custom-call(s32[1]{0:T(128)} %bitcast.me_ref, bf16[16,7296]{1,0:T(8,128)(2,1)S(1)} %get-tuple-element.26.refs_0_, bf16[16,7296]{1,0:T(8,128)(2,1)S(1)} %collective-permute-done.7.refs_1_, bf16[16,7296]{1,0:T(8,128)(2,1)S(1)} %collective-permute-done.8.refs_2_, ...), custom_call_target="tpu_custom_call" | custom-call | flops 2818572288 | bytes 23887872 | tf_op jit(solution)/shard_map/experts/experts/pallas_call | solution.py:274
  68.6 2.1 %collective-permute-done.14 = bf16[64,7168]{1,0:T(8,128)(2,1)S(1)} collective-permute-done((bf16[64,7168]{1,0:T(8,128)(2,1)S(1)}, bf16[64,7168]{1,0:T(8,128)(2,1)S(1)}, u32[]{:S(2)}, u32[]{:S(2)}) %collective-permute-start.14) | collective-permute-done | bytes 917536 | tf_op jit(solution)/shard_map/collect/ppermute | solution.py:39
  71.1 1.4 %collective-permute-start.15 = (bf16[16,7168]{1,0:T(8,128)(2,1)S(1)}, bf16[16,7168]{1,0:T(8,128)(2,1)S(1)}, u32[]{:S(2)}, u32[]{:S(2)}) collective-permute-start(bf16[16,7168]{1,0:T(8,128)(2,1)S(1)} %get-tuple-element.41), channel_id=1, source_target_pairs={{0,18},{1,13},{2,16},{3,15},{4,22},{5,9},{6,20},{7,11},{8,26},{9,5... | collective-permute-start | bytes 688136 | tf_op jit(solution)/shard_map/collect/ppermute | solution.py:35
  74.6 3.5 %collective-permute-done.15 = bf16[16,7168]{1,0:T(8,128)(2,1)S(1)} collective-permute-done((bf16[16,7168]{1,0:T(8,128)(2,1)S(1)}, bf16[16,7168]{1,0:T(8,128)(2,1)S(1)}, u32[]{:S(2)}, u32[]{:S(2)}) %collective-permute-start.15) | collective-permute-done | bytes 229408 | tf_op jit(solution)/shard_map/collect/ppermute | solution.py:35
  78.1 2.4 %collective-permute-done.17 = bf16[16,7168]{1,0:T(8,128)(2,1)S(1)} collective-permute-done((bf16[16,7168]{1,0:T(8,128)(2,1)S(1)}, bf16[16,7168]{1,0:T(8,128)(2,1)S(1)}, u32[]{:S(2)}, u32[]{:S(2)}) %collective-permute-start.17) | collective-permute-done | bytes 229408 | tf_op jit(solution)/shard_map/collect/ppermute | solution.py:35
  80.7 1.9 %collective-permute-start.18 = (bf16[4,7168]{1,0:T(4,128)(2,1)S(1)}, bf16[4,7168]{1,0:T(4,128)(2,1)S(1)}, u32[]{:S(2)}, u32[]{:S(2)}) collective-permute-start(bf16[4,7168]{1,0:T(4,128)(2,1)S(1)} %get-tuple-element.47), channel_id=1, source_target_pairs={{0,12},{1,19},{2,14},{3,17},{4,8},{5,23},{6,10},{7,21},{8,4},{9,27... | collective-permute-start | bytes 172040 | tf_op jit(solution)/shard_map/collect/ppermute | solution.py:35
  82.6 2.6 %collective-permute-start.19 = (bf16[4,7168]{1,0:T(4,128)(2,1)S(1)}, bf16[4,7168]{1,0:T(4,128)(2,1)S(1)}, u32[]{:S(2)}, u32[]{:S(2)}) collective-permute-start(bf16[4,7168]{1,0:T(4,128)(2,1)S(1)} %get-tuple-element.49), channel_id=1, source_target_pairs={{0,8},{1,17},{2,10},{3,19},{4,12},{5,21},{6,14},{7,23},{8,0},{9,25... | collective-permute-start | bytes 172040 | tf_op jit(solution)/shard_map/collect/ppermute | solution.py:35
  85.1 1.7 %collective-permute-done.18 = bf16[4,7168]{1,0:T(4,128)(2,1)S(1)} collective-permute-done((bf16[4,7168]{1,0:T(4,128)(2,1)S(1)}, bf16[4,7168]{1,0:T(4,128)(2,1)S(1)}, u32[]{:S(2)}, u32[]{:S(2)}) %collective-permute-start.18) | collective-permute-done | bytes 57376 | tf_op jit(solution)/shard_map/collect/ppermute | solution.py:35
  (52 shorter events, 13.3 us)
Async XLA Ops:
  0.7 24.8 %copy-start = (bf16[1,128,7168]{2,1,0:T(8,128)(2,1)S(1)}, bf16[1,128,7168]{2,1,0:T(8,128)(2,1)}, u32[]{:S(2)}) copy-start(bf16[1,128,7168]{2,1,0:T(8,128)(2,1)} %param.22) | copy-start | bytes 5505028
  0.7 24.8 %copy-start.1 = (bf16[1,512,128]{2,1,0:T(8,128)(2,1)S(1)}, bf16[1,512,128]{2,1,0:T(8,128)(2,1)}, u32[]{:S(2)}) copy-start(bf16[1,512,128]{2,1,0:T(8,128)(2,1)} %param.21) | copy-start | bytes 393220
  9.9 15.5 %all-to-all-start = ((bf16[32,4,512]{2,1,0:T(4,128)(2,1)}), bf16[32,4,512]{2,1,0:T(4,128)(2,1)S(1)}, u32[]{:S(2)}, u32[]{:S(2)}) async-start(bf16[32,4,512]{2,1,0:T(4,128)(2,1)} %attend.1), calls=%async_computation | async-start | bytes 262144 | tf_op jit(solution)/shard_map/heads/all_to_all | solution.py:327
  26.4 2.5 %collective-permute-start = (bf16[64,7168]{1,0:T(8,128)(2,1)S(1)}, bf16[64,7168]{1,0:T(8,128)(2,1)S(1)}, u32[]{:S(2)}, u32[]{:S(2)}) collective-permute-start(bf16[64,7168]{1,0:T(8,128)(2,1)S(1)} %get-tuple-element.20), channel_id=1, source_target_pairs={{0,1},{1,0},{2,3},{3,2},{4,5},{5,4},{6,7},{7,6},{8,9},{9,8},{10,11... | collective-permute-start | bytes 2752520 | tf_op jit(solution)/shard_map/heads/ppermute | solution.py:39
  29.2 7.1 %collective-permute-start.3 = (bf16[16,7168]{1,0:T(8,128)(2,1)S(1)}, bf16[16,7168]{1,0:T(8,128)(2,1)S(1)}, u32[]{:S(2)}, u32[]{:S(2)}) collective-permute-start(bf16[16,7168]{1,0:T(8,128)(2,1)S(1)} %get-tuple-element.44), channel_id=1, source_target_pairs={{0,18},{1,13},{2,16},{3,15},{4,22},{5,9},{6,20},{7,11},{8,26},{9,5... | collective-permute-start | bytes 688136 | tf_op jit(solution)/shard_map/heads/ppermute | solution.py:35
  29.8 7.9 %collective-permute-start.2 = (bf16[16,7168]{1,0:T(8,128)(2,1)S(1)}, bf16[16,7168]{1,0:T(8,128)(2,1)S(1)}, u32[]{:S(2)}, u32[]{:S(2)}) collective-permute-start(bf16[16,7168]{1,0:T(8,128)(2,1)S(1)} %get-tuple-element.45), channel_id=1, source_target_pairs={{0,16},{1,9},{2,18},{3,11},{4,20},{5,13},{6,22},{7,15},{8,24},{9,1... | collective-permute-start | bytes 688136 | tf_op jit(solution)/shard_map/heads/ppermute | solution.py:35
  31.3 7.4 %collective-permute-start.1 = (bf16[16,7168]{1,0:T(8,128)(2,1)S(1)}, bf16[16,7168]{1,0:T(8,128)(2,1)S(1)}, u32[]{:S(2)}, u32[]{:S(2)}) collective-permute-start(bf16[16,7168]{1,0:T(8,128)(2,1)S(1)} %get-tuple-element.46), channel_id=1, source_target_pairs={{0,2},{1,5},{2,0},{3,7},{4,6},{5,1},{6,4},{7,3},{8,10},{9,13},{10,... | collective-permute-start | bytes 688136 | tf_op jit(solution)/shard_map/heads/ppermute | solution.py:35
  38.9 11.2 %collective-permute-start.6 = (bf16[16,7296]{1,0:T(8,128)(2,1)S(1)}, bf16[16,7296]{1,0:T(8,128)(2,1)S(1)}, u32[]{:S(2)}, u32[]{:S(2)}) collective-permute-start(bf16[16,7296]{1,0:T(8,128)(2,1)S(1)} %get-tuple-element.24), channel_id=1, source_target_pairs={{0,12},{1,19},{2,14},{3,17},{4,8},{5,23},{6,10},{7,21},{8,4},{9,27... | collective-permute-start | bytes 700424 | tf_op jit(solution)/shard_map/norm/ppermute | solution.py:35
  40.3 11.8 %collective-permute-start.5 = (bf16[16,7296]{1,0:T(8,128)(2,1)S(1)}, bf16[16,7296]{1,0:T(8,128)(2,1)S(1)}, u32[]{:S(2)}, u32[]{:S(2)}) collective-permute-start(bf16[16,7296]{1,0:T(8,128)(2,1)S(1)} %get-tuple-element.24), channel_id=1, source_target_pairs={{0,8},{1,17},{2,10},{3,19},{4,12},{5,21},{6,14},{7,23},{8,0},{9,25... | collective-permute-start | bytes 700424 | tf_op jit(solution)/shard_map/norm/ppermute | solution.py:35
  40.5 11.5 %collective-permute-start.4 = (bf16[16,7296]{1,0:T(8,128)(2,1)S(1)}, bf16[16,7296]{1,0:T(8,128)(2,1)S(1)}, u32[]{:S(2)}, u32[]{:S(2)}) collective-permute-start(bf16[16,7296]{1,0:T(8,128)(2,1)S(1)} %get-tuple-element.24), channel_id=1, source_target_pairs={{0,4},{1,3},{2,6},{3,1},{4,0},{5,7},{6,2},{7,5},{8,12},{9,11},{10,... | collective-permute-start | bytes 700424 | tf_op jit(solution)/shard_map/norm/ppermute | solution.py:35
  52.3 7.1 %collective-permute-start.9 = (bf16[16,7296]{1,0:T(8,128)(2,1)S(1)}, bf16[16,7296]{1,0:T(8,128)(2,1)S(1)}, u32[]{:S(2)}, u32[]{:S(2)}) collective-permute-start(bf16[16,7296]{1,0:T(8,128)(2,1)S(1)} %get-tuple-element.26.refs_0_), channel_id=1, source_target_pairs={{0,18},{1,13},{2,16},{3,15},{4,22},{5,9},{6,20},{7,11},{8,26},{9,5... | collective-permute-start | bytes 700424 | tf_op jit(solution)/shard_map/spread/ppermute | solution.py:35
  53.8 8.0 %collective-permute-start.8 = (bf16[16,7296]{1,0:T(8,128)(2,1)S(1)}, bf16[16,7296]{1,0:T(8,128)(2,1)S(1)}, u32[]{:S(2)}, u32[]{:S(2)}) collective-permute-start(bf16[16,7296]{1,0:T(8,128)(2,1)S(1)} %get-tuple-element.26.refs_0_), channel_id=1, source_target_pairs={{0,16},{1,9},{2,18},{3,11},{4,20},{5,13},{6,22},{7,15},{8,24},{9,1... | collective-permute-start | bytes 700424 | tf_op jit(solution)/shard_map/spread/ppermute | solution.py:35
  55.3 7.9 %collective-permute-start.7 = (bf16[16,7296]{1,0:T(8,128)(2,1)S(1)}, bf16[16,7296]{1,0:T(8,128)(2,1)S(1)}, u32[]{:S(2)}, u32[]{:S(2)}) collective-permute-start(bf16[16,7296]{1,0:T(8,128)(2,1)S(1)} %get-tuple-element.26.refs_0_), channel_id=1, source_target_pairs={{0,2},{1,5},{2,0},{3,7},{4,6},{5,1},{6,4},{7,3},{8,10},{9,13},{10,... | collective-permute-start | bytes 700424 | tf_op jit(solution)/shard_map/spread/ppermute | solution.py:35
  55.9 7.3 %collective-permute-start.10 = (bf16[16,7296]{1,0:T(8,128)(2,1)S(1)}, bf16[16,7296]{1,0:T(8,128)(2,1)S(1)}, u32[]{:S(2)}, u32[]{:S(2)}) collective-permute-start(bf16[16,7296]{1,0:T(8,128)(2,1)S(1)} %get-tuple-element.26.refs_0_), channel_id=1, source_target_pairs={{0,1},{1,0},{2,3},{3,2},{4,5},{5,4},{6,7},{7,6},{8,9},{9,8},{10,11... | collective-permute-start | bytes 700424 | tf_op jit(solution)/shard_map/spread/ppermute | solution.py:39
  59.4 3.7 %collective-permute-start.13 = (bf16[16,7296]{1,0:T(8,128)(2,1)S(1)}, bf16[16,7296]{1,0:T(8,128)(2,1)S(1)}, u32[]{:S(2)}, u32[]{:S(2)}) collective-permute-start(bf16[16,7296]{1,0:T(8,128)(2,1)S(1)} %collective-permute-done.9.refs_3_), channel_id=1, source_target_pairs={{0,1},{1,0},{2,3},{3,2},{4,5},{5,4},{6,7},{7,6},{8,9},{9,8},{10,11... | collective-permute-start | bytes 700424 | tf_op jit(solution)/shard_map/spread/ppermute | solution.py:39
  61.8 2.5 %collective-permute-start.12 = (bf16[16,7296]{1,0:T(8,128)(2,1)S(1)}, bf16[16,7296]{1,0:T(8,128)(2,1)S(1)}, u32[]{:S(2)}, u32[]{:S(2)}) collective-permute-start(bf16[16,7296]{1,0:T(8,128)(2,1)S(1)} %collective-permute-done.8.refs_2_), channel_id=1, source_target_pairs={{0,1},{1,0},{2,3},{3,2},{4,5},{5,4},{6,7},{7,6},{8,9},{9,8},{10,11... | collective-permute-start | bytes 700424 | tf_op jit(solution)/shard_map/spread/ppermute | solution.py:39
  63.1 1.5 %collective-permute-start.11 = (bf16[16,7296]{1,0:T(8,128)(2,1)S(1)}, bf16[16,7296]{1,0:T(8,128)(2,1)S(1)}, u32[]{:S(2)}, u32[]{:S(2)}) collective-permute-start(bf16[16,7296]{1,0:T(8,128)(2,1)S(1)} %collective-permute-done.7.refs_1_), channel_id=1, source_target_pairs={{0,1},{1,0},{2,3},{3,2},{4,5},{5,4},{6,7},{7,6},{8,9},{9,8},{10,11... | collective-permute-start | bytes 700424 | tf_op jit(solution)/shard_map/spread/ppermute | solution.py:39
  68.2 2.5 %collective-permute-start.14 = (bf16[64,7168]{1,0:T(8,128)(2,1)S(1)}, bf16[64,7168]{1,0:T(8,128)(2,1)S(1)}, u32[]{:S(2)}, u32[]{:S(2)}) collective-permute-start(bf16[64,7168]{1,0:T(8,128)(2,1)S(1)} %get-tuple-element.32), channel_id=1, source_target_pairs={{0,1},{1,0},{2,3},{3,2},{4,5},{5,4},{6,7},{7,6},{8,9},{9,8},{10,11... | collective-permute-start | bytes 2752520 | tf_op jit(solution)/shard_map/collect/ppermute | solution.py:39
  71.1 7.1 %collective-permute-start.15 = (bf16[16,7168]{1,0:T(8,128)(2,1)S(1)}, bf16[16,7168]{1,0:T(8,128)(2,1)S(1)}, u32[]{:S(2)}, u32[]{:S(2)}) collective-permute-start(bf16[16,7168]{1,0:T(8,128)(2,1)S(1)} %get-tuple-element.41), channel_id=1, source_target_pairs={{0,18},{1,13},{2,16},{3,15},{4,22},{5,9},{6,20},{7,11},{8,26},{9,5... | collective-permute-start | bytes 688136 | tf_op jit(solution)/shard_map/collect/ppermute | solution.py:35
  72.4 8.1 %collective-permute-start.17 = (bf16[16,7168]{1,0:T(8,128)(2,1)S(1)}, bf16[16,7168]{1,0:T(8,128)(2,1)S(1)}, u32[]{:S(2)}, u32[]{:S(2)}) collective-permute-start(bf16[16,7168]{1,0:T(8,128)(2,1)S(1)} %get-tuple-element.42), channel_id=1, source_target_pairs={{0,2},{1,5},{2,0},{3,7},{4,6},{5,1},{6,4},{7,3},{8,10},{9,13},{10,... | collective-permute-start | bytes 688136 | tf_op jit(solution)/shard_map/collect/ppermute | solution.py:35
  73.4 7.1 %collective-permute-start.16 = (bf16[16,7168]{1,0:T(8,128)(2,1)S(1)}, bf16[16,7168]{1,0:T(8,128)(2,1)S(1)}, u32[]{:S(2)}, u32[]{:S(2)}) collective-permute-start(bf16[16,7168]{1,0:T(8,128)(2,1)S(1)} %get-tuple-element.43), channel_id=1, source_target_pairs={{0,16},{1,9},{2,18},{3,11},{4,20},{5,13},{6,22},{7,15},{8,24},{9,1... | collective-permute-start | bytes 688136 | tf_op jit(solution)/shard_map/collect/ppermute | solution.py:35
  80.7 6.1 %collective-permute-start.18 = (bf16[4,7168]{1,0:T(4,128)(2,1)S(1)}, bf16[4,7168]{1,0:T(4,128)(2,1)S(1)}, u32[]{:S(2)}, u32[]{:S(2)}) collective-permute-start(bf16[4,7168]{1,0:T(4,128)(2,1)S(1)} %get-tuple-element.47), channel_id=1, source_target_pairs={{0,12},{1,19},{2,14},{3,17},{4,8},{5,23},{6,10},{7,21},{8,4},{9,27... | collective-permute-start | bytes 172040 | tf_op jit(solution)/shard_map/collect/ppermute | solution.py:35
  82.6 5.4 %collective-permute-start.20 = (bf16[4,7168]{1,0:T(4,128)(2,1)S(1)}, bf16[4,7168]{1,0:T(4,128)(2,1)S(1)}, u32[]{:S(2)}, u32[]{:S(2)}) collective-permute-start(bf16[4,7168]{1,0:T(4,128)(2,1)S(1)} %get-tuple-element.48), channel_id=1, source_target_pairs={{0,4},{1,3},{2,6},{3,1},{4,0},{5,7},{6,2},{7,5},{8,12},{9,11},{10,... | collective-permute-start | bytes 172040 | tf_op jit(solution)/shard_map/collect/ppermute | solution.py:35
  82.6 5.4 %collective-permute-start.19 = (bf16[4,7168]{1,0:T(4,128)(2,1)S(1)}, bf16[4,7168]{1,0:T(4,128)(2,1)S(1)}, u32[]{:S(2)}, u32[]{:S(2)}) collective-permute-start(bf16[4,7168]{1,0:T(4,128)(2,1)S(1)} %get-tuple-element.49), channel_id=1, source_target_pairs={{0,8},{1,17},{2,10},{3,19},{4,12},{5,21},{6,14},{7,23},{8,0},{9,25... | collective-permute-start | bytes 172040 | tf_op jit(solution)/shard_map/collect/ppermute | solution.py:35
  (4 other events, 36.9 us)

commit v15 on v14

--- a/solution.py
+++ b/solution.py
@@ -76,7 +76,6 @@
     q_copy.start()
     new_copy.start()
     start(0)
-    start(1)
     r = iota2((rows, rows), 0)
     order = one_hot((r % STEPS) * heads + r // STEPS, rows)
     q_copy.wait()
@@ -90,7 +89,15 @@
     p = jnp.exp2((s - m) * factor_base2)
     m_ref[...] = m
     l_ref[...] = jnp.sum(p, axis=1, keepdims=True)
-    acc_ref[...] = jnp.dot(p.astype(BF), new[:, :LAT], preferred_element_type=F32)
+    acc = jnp.dot(p.astype(BF), new[:, :LAT], preferred_element_type=F32)
+    acc_ref[...] = jnp.transpose(acc)
+
+    def as_row(column):
+        same = iota2((rows, rows), 0) == iota2((rows, rows), 1)
+        return jnp.sum(jnp.where(same, column, 0.0), axis=0, keepdims=True)
+
+
+    start(1)
 
     def update(i, masked):
         start(i + 2)
@@ -105,8 +112,8 @@
         p = jnp.exp2((s - m) * factor_base2)
         m_ref[...] = m
         l_ref[...] = l_ref[...] * factor + jnp.sum(p, axis=1, keepdims=True)
-        acc_ref[...] = acc_ref[...] * factor + lax.dot_general(
-            p.astype(BF), keys[:LAT], NT, preferred_element_type=F32
+        acc_ref[...] = acc_ref[...] * as_row(factor) + lax.dot_general(
+            keys[:LAT], p.astype(BF), NT, preferred_element_type=F32
         )
 
     full = length // blk
@@ -119,8 +126,9 @@
     def _():
         update(full, True)
 
-    out = (acc_ref[...] / l_ref[...]).astype(BF)
-    out_ref[...] = pick(order, out).reshape(out_ref.shape).astype(BF)
+    out = (acc_ref[...] * as_row(1.0 / l_ref[...])).astype(BF)
+    moved = lax.dot_general(order, out, NT, preferred_element_type=F32)
+    out_ref[...] = moved.reshape(out_ref.shape).astype(BF)
 
 
 def attend(n, length, q, new, keys):
@@ -138,7 +146,7 @@
             pltpu.VMEM(keys.shape, BF),
             pltpu.VMEM((rows, 1), F32),
             pltpu.VMEM((rows, 1), F32),
-            pltpu.VMEM((rows, LAT), F32),
+            pltpu.VMEM((LAT, rows), F32),
             pltpu.SemaphoreType.DMA((2,)),
             pltpu.SemaphoreType.DMA((blocks,)),
         ],

time: 88.6 us -> 88.3 us (level)
  Pallas kernels: 23.3 us -> 20 us
  starting transfers between devices: 28.9 us -> 31.9 us
    pallas_call x1, Pallas kernels: 9.21 us -> 5.9 us  [attend(): pl.pallas_call(functools.partial(attend_kernel, n), in_specs=[pl.BlockSpe...]
    all_to_all x1, starting transfers between devices: 7.3 us -> 10.3 us  [per_device(): latents = lax.all_to_all(latents, AXES, 0, 0, tiled=True)]
where the time goes in v15:
time: 88.3 us
  waiting for transfers between devices  34 us (39%)
  starting transfers between devices  31.9 us (36%)
  Pallas kernels  20 us (23%)
  other arithmetic  1.33 us (2%)
    ppermute x15, waiting for transfers between devices, swap(): lax.ppermute(x, AXES, [(d, d ^ partners(n)[d & 1][stage][i]) for d in ran...  19.9 us
    ppermute x15, starting transfers between devices, swap(): lax.ppermute(x, AXES, [(d, d ^ partners(n)[d & 1][stage][i]) for d in ran...  19.6 us
    all_to_all x1, starting transfers between devices, per_device(): latents = lax.all_to_all(latents, AXES, 0, 0, tiled=True)  10.3 us
    pallas_call x2, Pallas kernels, load(): pl.pallas_call(functools.partial(load_kernel, n, ranges), in_specs=[pl.Bl...  9.08 us
    all_to_all x1, waiting for transfers between devices, per_device(): latents = lax.all_to_all(latents, AXES, 0, 0, tiled=True)  8.22 us
    pallas_call x1, Pallas kernels, attend(): pl.pallas_call(functools.partial(attend_kernel, n), in_specs=[pl.BlockSpe...  5.9 us
    ppermute x6, waiting for transfers between devices, swap_core(): return lax.ppermute(x, AXES, [(d, d ^ 1) for d in range(n)])  5.83 us
    pallas_call x4, Pallas kernels, single(): pl.pallas_call(functools.partial(kernel, n), in_specs=[pl.BlockSpec(memor...  4.98 us
  transfers between devices with their start and end apart: 22, of which 15 were waited for; matrix products, arithmetic and copies ran while one was open for 0% of the time, Pallas kernels for 10%

profile of v15, /device:TPU:0, one launch (start us, length us, event | category | flops | bytes accessed | tf_op | source)
XLA Modules:
  0.0 88.3 jit_solution(11285334826818535199)
XLA Ops:
  0.7 5.9 %attend.1 = bf16[32,4,512]{2,1,0:T(4,128)(2,1)} custom-call(s32[1]{0:T(128)S(6)} %copy.14.len_ref, bf16[128,576]{1,0:T(8,128)(2,1)} %bitcast.30, bf16[4,576]{1,0:T(4,128)(2,1)} %bitcast.31, bf16[576,8192]{1,0:T(8,128)(2,1)} %bitcast.27), custom_call_target="tpu_custom_call" | custom-call | flops 2281701376 | bytes 9437184 | tf_op jit(solution)/shard_map/attention/attend/pallas_call | solution.py:138
  6.6 10.3 %all-to-all-start = ((bf16[32,4,512]{2,1,0:T(4,128)(2,1)}), bf16[32,4,512]{2,1,0:T(4,128)(2,1)S(1)}, u32[]{:S(2)}, u32[]{:S(2)}) async-start(bf16[32,4,512]{2,1,0:T(4,128)(2,1)} %attend.1), calls=%async_computation | async-start | bytes 262144 | tf_op jit(solution)/shard_map/heads/all_to_all | solution.py:335
  16.9 8.2 %all-to-all-done = bf16[32,4,512]{2,1,0:T(4,128)(2,1)S(1)} async-done(((bf16[32,4,512]{2,1,0:T(4,128)(2,1)}), bf16[32,4,512]{2,1,0:T(4,128)(2,1)S(1)}, u32[]{:S(2)}, u32[]{:S(2)}) %all-to-all-start) | async-done | bytes 131104 | tf_op jit(solution)/shard_map/heads/all_to_all | solution.py:335
  26.4 2.2 %collective-permute-done = bf16[64,7168]{1,0:T(8,128)(2,1)S(1)} collective-permute-done((bf16[64,7168]{1,0:T(8,128)(2,1)S(1)}, bf16[64,7168]{1,0:T(8,128)(2,1)S(1)}, u32[]{:S(2)}, u32[]{:S(2)}) %collective-permute-start) | collective-permute-done | bytes 917536 | tf_op jit(solution)/shard_map/heads/ppermute | solution.py:39
  29.5 1.5 %collective-permute-start.2 = (bf16[16,7168]{1,0:T(8,128)(2,1)S(1)}, bf16[16,7168]{1,0:T(8,128)(2,1)S(1)}, u32[]{:S(2)}, u32[]{:S(2)}) collective-permute-start(bf16[16,7168]{1,0:T(8,128)(2,1)S(1)} %get-tuple-element.45), channel_id=1, source_target_pairs={{0,16},{1,9},{2,18},{3,11},{4,20},{5,13},{6,22},{7,15},{8,24},{9,1... | collective-permute-start | bytes 688136 | tf_op jit(solution)/shard_map/heads/ppermute | solution.py:35
  31.0 1.5 %collective-permute-start.1 = (bf16[16,7168]{1,0:T(8,128)(2,1)S(1)}, bf16[16,7168]{1,0:T(8,128)(2,1)S(1)}, u32[]{:S(2)}, u32[]{:S(2)}) collective-permute-start(bf16[16,7168]{1,0:T(8,128)(2,1)S(1)} %get-tuple-element.46), channel_id=1, source_target_pairs={{0,2},{1,5},{2,0},{3,7},{4,6},{5,1},{6,4},{7,3},{8,10},{9,13},{10,... | collective-permute-start | bytes 688136 | tf_op jit(solution)/shard_map/heads/ppermute | solution.py:35
  32.6 2.3 %load.2 = (f32[16,7168]{1,0:T(8,128)S(1)}, bf16[3584,512]{1,0:T(8,128)(2,1)S(1)}) custom-call(f32[16,7168]{1,0:T(8,128)S(1)} %slice.69.refs_0_, bf16[7168,512]{1,0:T(8,128)(2,1)} %bitcast.25), custom_call_target="tpu_custom_call" | custom-call | bytes 7340032 | tf_op jit(solution)/shard_map/heads/load/pallas_call | solution.py:239
  36.0 1.4 %collective-permute-done.2.refs_2_ = bf16[16,7168]{1,0:T(8,128)(2,1)S(1)} collective-permute-done((bf16[16,7168]{1,0:T(8,128)(2,1)S(1)}, bf16[16,7168]{1,0:T(8,128)(2,1)S(1)}, u32[]{:S(2)}, u32[]{:S(2)}) %collective-permute-start.2) | collective-permute-done | bytes 229408 | tf_op jit(solution)/shard_map/heads/ppermute | solution.py:35
  38.6 1.4 %collective-permute-start.6 = (bf16[16,7296]{1,0:T(8,128)(2,1)S(1)}, bf16[16,7296]{1,0:T(8,128)(2,1)S(1)}, u32[]{:S(2)}, u32[]{:S(2)}) collective-permute-start(bf16[16,7296]{1,0:T(8,128)(2,1)S(1)} %get-tuple-element.24), channel_id=1, source_target_pairs={{0,12},{1,19},{2,14},{3,17},{4,8},{5,23},{6,10},{7,21},{8,4},{9,27... | collective-permute-start | bytes 700424 | tf_op jit(solution)/shard_map/norm/ppermute | solution.py:35
  40.2 2.8 %collective-permute-start.4 = (bf16[16,7296]{1,0:T(8,128)(2,1)S(1)}, bf16[16,7296]{1,0:T(8,128)(2,1)S(1)}, u32[]{:S(2)}, u32[]{:S(2)}) collective-permute-start(bf16[16,7296]{1,0:T(8,128)(2,1)S(1)} %get-tuple-element.24), channel_id=1, source_target_pairs={{0,4},{1,3},{2,6},{3,1},{4,0},{5,7},{6,2},{7,5},{8,12},{9,11},{10,... | collective-permute-start | bytes 700424 | tf_op jit(solution)/shard_map/norm/ppermute | solution.py:35
  43.1 6.7 %load.3 = (f32[16,7296]{1,0:T(8,128)S(1)}, bf16[3584,512]{1,0:T(8,128)(2,1)S(1)}, bf16[7168,512]{1,0:T(8,128)(2,1)S(1)}, bf16[512,7168]{1,0:T(8,128)(2,1)S(1)}) custom-call(f32[16,7296]{1,0:T(8,128)S(1)} %get-tuple-element.22.refs_0_, bf16[7168,512]{1,0:T(8,128)(2,1)} %bitcast.26, bf16[7168,512]{1,0:T(8,128)(2,1)} %bitcast.28, bf16[512,7168]{1,0:T(8,128)(2,1)} %bitcast.29), custom_call_target="tpu_custom_call" | custom-call | bytes 36700160 | tf_op jit(solution)/shard_map/norm/load/pallas_call | solution.py:239
  49.8 1.9 %collective-permute-done.5.refs_1_ = bf16[16,7296]{1,0:T(8,128)(2,1)S(1)} collective-permute-done((bf16[16,7296]{1,0:T(8,128)(2,1)S(1)}, bf16[16,7296]{1,0:T(8,128)(2,1)S(1)}, u32[]{:S(2)}, u32[]{:S(2)}) %collective-permute-start.5) | collective-permute-done | bytes 233504 | tf_op jit(solution)/shard_map/norm/ppermute | solution.py:35
  52.0 1.4 %collective-permute-start.9 = (bf16[16,7296]{1,0:T(8,128)(2,1)S(1)}, bf16[16,7296]{1,0:T(8,128)(2,1)S(1)}, u32[]{:S(2)}, u32[]{:S(2)}) collective-permute-start(bf16[16,7296]{1,0:T(8,128)(2,1)S(1)} %get-tuple-element.26.refs_0_), channel_id=1, source_target_pairs={{0,18},{1,13},{2,16},{3,15},{4,22},{5,9},{6,20},{7,11},{8,26},{9,5... | collective-permute-start | bytes 700424 | tf_op jit(solution)/shard_map/spread/ppermute | solution.py:35
  53.5 1.5 %collective-permute-start.8 = (bf16[16,7296]{1,0:T(8,128)(2,1)S(1)}, bf16[16,7296]{1,0:T(8,128)(2,1)S(1)}, u32[]{:S(2)}, u32[]{:S(2)}) collective-permute-start(bf16[16,7296]{1,0:T(8,128)(2,1)S(1)} %get-tuple-element.26.refs_0_), channel_id=1, source_target_pairs={{0,16},{1,9},{2,18},{3,11},{4,20},{5,13},{6,22},{7,15},{8,24},{9,1... | collective-permute-start | bytes 700424 | tf_op jit(solution)/shard_map/spread/ppermute | solution.py:35
  55.6 3.5 %collective-permute-done.9.refs_3_ = bf16[16,7296]{1,0:T(8,128)(2,1)S(1)} collective-permute-done((bf16[16,7296]{1,0:T(8,128)(2,1)S(1)}, bf16[16,7296]{1,0:T(8,128)(2,1)S(1)}, u32[]{:S(2)}, u32[]{:S(2)}) %collective-permute-start.9) | collective-permute-done | bytes 233504 | tf_op jit(solution)/shard_map/spread/ppermute | solution.py:35
  59.1 2.4 %collective-permute-done.8.refs_2_ = bf16[16,7296]{1,0:T(8,128)(2,1)S(1)} collective-permute-done((bf16[16,7296]{1,0:T(8,128)(2,1)S(1)}, bf16[16,7296]{1,0:T(8,128)(2,1)S(1)}, u32[]{:S(2)}, u32[]{:S(2)}) %collective-permute-start.8) | collective-permute-done | bytes 233504 | tf_op jit(solution)/shard_map/spread/ppermute | solution.py:35
  64.3 3.6 %experts.1 = (f32[64,7168]{1,0:T(8,128)S(1)}, bf16[64,7168]{1,0:T(8,128)(2,1)S(1)}) custom-call(s32[1]{0:T(128)} %bitcast.me_ref, bf16[16,7296]{1,0:T(8,128)(2,1)S(1)} %get-tuple-element.26.refs_0_, bf16[16,7296]{1,0:T(8,128)(2,1)S(1)} %collective-permute-done.7.refs_1_, bf16[16,7296]{1,0:T(8,128)(2,1)S(1)} %collective-permute-done.8.refs_2_, ...), custom_call_target="tpu_custom_call" | custom-call | flops 2818572288 | bytes 23887872 | tf_op jit(solution)/shard_map/experts/experts/pallas_call | solution.py:282
  68.3 2.1 %collective-permute-done.14 = bf16[64,7168]{1,0:T(8,128)(2,1)S(1)} collective-permute-done((bf16[64,7168]{1,0:T(8,128)(2,1)S(1)}, bf16[64,7168]{1,0:T(8,128)(2,1)S(1)}, u32[]{:S(2)}, u32[]{:S(2)}) %collective-permute-start.14) | collective-permute-done | bytes 917536 | tf_op jit(solution)/shard_map/collect/ppermute | solution.py:39
  70.7 1.4 %collective-permute-start.15 = (bf16[16,7168]{1,0:T(8,128)(2,1)S(1)}, bf16[16,7168]{1,0:T(8,128)(2,1)S(1)}, u32[]{:S(2)}, u32[]{:S(2)}) collective-permute-start(bf16[16,7168]{1,0:T(8,128)(2,1)S(1)} %get-tuple-element.41), channel_id=1, source_target_pairs={{0,18},{1,13},{2,16},{3,15},{4,22},{5,9},{6,20},{7,11},{8,26},{9,5... | collective-permute-start | bytes 688136 | tf_op jit(solution)/shard_map/collect/ppermute | solution.py:35
  74.3 3.5 %collective-permute-done.15 = bf16[16,7168]{1,0:T(8,128)(2,1)S(1)} collective-permute-done((bf16[16,7168]{1,0:T(8,128)(2,1)S(1)}, bf16[16,7168]{1,0:T(8,128)(2,1)S(1)}, u32[]{:S(2)}, u32[]{:S(2)}) %collective-permute-start.15) | collective-permute-done | bytes 229408 | tf_op jit(solution)/shard_map/collect/ppermute | solution.py:35
  77.8 2.4 %collective-permute-done.17 = bf16[16,7168]{1,0:T(8,128)(2,1)S(1)} collective-permute-done((bf16[16,7168]{1,0:T(8,128)(2,1)S(1)}, bf16[16,7168]{1,0:T(8,128)(2,1)S(1)}, u32[]{:S(2)}, u32[]{:S(2)}) %collective-permute-start.17) | collective-permute-done | bytes 229408 | tf_op jit(solution)/shard_map/collect/ppermute | solution.py:35
  80.4 1.9 %collective-permute-start.18 = (bf16[4,7168]{1,0:T(4,128)(2,1)S(1)}, bf16[4,7168]{1,0:T(4,128)(2,1)S(1)}, u32[]{:S(2)}, u32[]{:S(2)}) collective-permute-start(bf16[4,7168]{1,0:T(4,128)(2,1)S(1)} %get-tuple-element.47), channel_id=1, source_target_pairs={{0,12},{1,19},{2,14},{3,17},{4,8},{5,23},{6,10},{7,21},{8,4},{9,27... | collective-permute-start | bytes 172040 | tf_op jit(solution)/shard_map/collect/ppermute | solution.py:35
  82.2 2.6 %collective-permute-start.19 = (bf16[4,7168]{1,0:T(4,128)(2,1)S(1)}, bf16[4,7168]{1,0:T(4,128)(2,1)S(1)}, u32[]{:S(2)}, u32[]{:S(2)}) collective-permute-start(bf16[4,7168]{1,0:T(4,128)(2,1)S(1)} %get-tuple-element.49), channel_id=1, source_target_pairs={{0,8},{1,17},{2,10},{3,19},{4,12},{5,21},{6,14},{7,23},{8,0},{9,25... | collective-permute-start | bytes 172040 | tf_op jit(solution)/shard_map/collect/ppermute | solution.py:35
  84.8 1.6 %collective-permute-done.18 = bf16[4,7168]{1,0:T(4,128)(2,1)S(1)} collective-permute-done((bf16[4,7168]{1,0:T(4,128)(2,1)S(1)}, bf16[4,7168]{1,0:T(4,128)(2,1)S(1)}, u32[]{:S(2)}, u32[]{:S(2)}) %collective-permute-start.18) | collective-permute-done | bytes 57376 | tf_op jit(solution)/shard_map/collect/ppermute | solution.py:35
  (52 shorter events, 13.3 us)
Async XLA Ops:
  0.7 24.5 %copy-start = (bf16[1,128,7168]{2,1,0:T(8,128)(2,1)S(1)}, bf16[1,128,7168]{2,1,0:T(8,128)(2,1)}, u32[]{:S(2)}) copy-start(bf16[1,128,7168]{2,1,0:T(8,128)(2,1)} %param.22) | copy-start | bytes 5505028
  0.7 24.5 %copy-start.1 = (bf16[1,512,128]{2,1,0:T(8,128)(2,1)S(1)}, bf16[1,512,128]{2,1,0:T(8,128)(2,1)}, u32[]{:S(2)}) copy-start(bf16[1,512,128]{2,1,0:T(8,128)(2,1)} %param.21) | copy-start | bytes 393220
  6.6 18.5 %all-to-all-start = ((bf16[32,4,512]{2,1,0:T(4,128)(2,1)}), bf16[32,4,512]{2,1,0:T(4,128)(2,1)S(1)}, u32[]{:S(2)}, u32[]{:S(2)}) async-start(bf16[32,4,512]{2,1,0:T(4,128)(2,1)} %attend.1), calls=%async_computation | async-start | bytes 262144 | tf_op jit(solution)/shard_map/heads/all_to_all | solution.py:335
  26.1 2.5 %collective-permute-start = (bf16[64,7168]{1,0:T(8,128)(2,1)S(1)}, bf16[64,7168]{1,0:T(8,128)(2,1)S(1)}, u32[]{:S(2)}, u32[]{:S(2)}) collective-permute-start(bf16[64,7168]{1,0:T(8,128)(2,1)S(1)} %get-tuple-element.20), channel_id=1, source_target_pairs={{0,1},{1,0},{2,3},{3,2},{4,5},{5,4},{6,7},{7,6},{8,9},{9,8},{10,11... | collective-permute-start | bytes 2752520 | tf_op jit(solution)/shard_map/heads/ppermute | solution.py:39
  28.9 7.1 %collective-permute-start.3 = (bf16[16,7168]{1,0:T(8,128)(2,1)S(1)}, bf16[16,7168]{1,0:T(8,128)(2,1)S(1)}, u32[]{:S(2)}, u32[]{:S(2)}) collective-permute-start(bf16[16,7168]{1,0:T(8,128)(2,1)S(1)} %get-tuple-element.44), channel_id=1, source_target_pairs={{0,18},{1,13},{2,16},{3,15},{4,22},{5,9},{6,20},{7,11},{8,26},{9,5... | collective-permute-start | bytes 688136 | tf_op jit(solution)/shard_map/heads/ppermute | solution.py:35
  29.5 7.9 %collective-permute-start.2 = (bf16[16,7168]{1,0:T(8,128)(2,1)S(1)}, bf16[16,7168]{1,0:T(8,128)(2,1)S(1)}, u32[]{:S(2)}, u32[]{:S(2)}) collective-permute-start(bf16[16,7168]{1,0:T(8,128)(2,1)S(1)} %get-tuple-element.45), channel_id=1, source_target_pairs={{0,16},{1,9},{2,18},{3,11},{4,20},{5,13},{6,22},{7,15},{8,24},{9,1... | collective-permute-start | bytes 688136 | tf_op jit(solution)/shard_map/heads/ppermute | solution.py:35
  31.0 7.4 %collective-permute-start.1 = (bf16[16,7168]{1,0:T(8,128)(2,1)S(1)}, bf16[16,7168]{1,0:T(8,128)(2,1)S(1)}, u32[]{:S(2)}, u32[]{:S(2)}) collective-permute-start(bf16[16,7168]{1,0:T(8,128)(2,1)S(1)} %get-tuple-element.46), channel_id=1, source_target_pairs={{0,2},{1,5},{2,0},{3,7},{4,6},{5,1},{6,4},{7,3},{8,10},{9,13},{10,... | collective-permute-start | bytes 688136 | tf_op jit(solution)/shard_map/heads/ppermute | solution.py:35
  38.6 11.2 %collective-permute-start.6 = (bf16[16,7296]{1,0:T(8,128)(2,1)S(1)}, bf16[16,7296]{1,0:T(8,128)(2,1)S(1)}, u32[]{:S(2)}, u32[]{:S(2)}) collective-permute-start(bf16[16,7296]{1,0:T(8,128)(2,1)S(1)} %get-tuple-element.24), channel_id=1, source_target_pairs={{0,12},{1,19},{2,14},{3,17},{4,8},{5,23},{6,10},{7,21},{8,4},{9,27... | collective-permute-start | bytes 700424 | tf_op jit(solution)/shard_map/norm/ppermute | solution.py:35
  40.0 11.8 %collective-permute-start.5 = (bf16[16,7296]{1,0:T(8,128)(2,1)S(1)}, bf16[16,7296]{1,0:T(8,128)(2,1)S(1)}, u32[]{:S(2)}, u32[]{:S(2)}) collective-permute-start(bf16[16,7296]{1,0:T(8,128)(2,1)S(1)} %get-tuple-element.24), channel_id=1, source_target_pairs={{0,8},{1,17},{2,10},{3,19},{4,12},{5,21},{6,14},{7,23},{8,0},{9,25... | collective-permute-start | bytes 700424 | tf_op jit(solution)/shard_map/norm/ppermute | solution.py:35
  40.2 11.5 %collective-permute-start.4 = (bf16[16,7296]{1,0:T(8,128)(2,1)S(1)}, bf16[16,7296]{1,0:T(8,128)(2,1)S(1)}, u32[]{:S(2)}, u32[]{:S(2)}) collective-permute-start(bf16[16,7296]{1,0:T(8,128)(2,1)S(1)} %get-tuple-element.24), channel_id=1, source_target_pairs={{0,4},{1,3},{2,6},{3,1},{4,0},{5,7},{6,2},{7,5},{8,12},{9,11},{10,... | collective-permute-start | bytes 700424 | tf_op jit(solution)/shard_map/norm/ppermute | solution.py:35
  52.0 7.1 %collective-permute-start.9 = (bf16[16,7296]{1,0:T(8,128)(2,1)S(1)}, bf16[16,7296]{1,0:T(8,128)(2,1)S(1)}, u32[]{:S(2)}, u32[]{:S(2)}) collective-permute-start(bf16[16,7296]{1,0:T(8,128)(2,1)S(1)} %get-tuple-element.26.refs_0_), channel_id=1, source_target_pairs={{0,18},{1,13},{2,16},{3,15},{4,22},{5,9},{6,20},{7,11},{8,26},{9,5... | collective-permute-start | bytes 700424 | tf_op jit(solution)/shard_map/spread/ppermute | solution.py:35
  53.5 8.0 %collective-permute-start.8 = (bf16[16,7296]{1,0:T(8,128)(2,1)S(1)}, bf16[16,7296]{1,0:T(8,128)(2,1)S(1)}, u32[]{:S(2)}, u32[]{:S(2)}) collective-permute-start(bf16[16,7296]{1,0:T(8,128)(2,1)S(1)} %get-tuple-element.26.refs_0_), channel_id=1, source_target_pairs={{0,16},{1,9},{2,18},{3,11},{4,20},{5,13},{6,22},{7,15},{8,24},{9,1... | collective-permute-start | bytes 700424 | tf_op jit(solution)/shard_map/spread/ppermute | solution.py:35
  55.0 7.9 %collective-permute-start.7 = (bf16[16,7296]{1,0:T(8,128)(2,1)S(1)}, bf16[16,7296]{1,0:T(8,128)(2,1)S(1)}, u32[]{:S(2)}, u32[]{:S(2)}) collective-permute-start(bf16[16,7296]{1,0:T(8,128)(2,1)S(1)} %get-tuple-element.26.refs_0_), channel_id=1, source_target_pairs={{0,2},{1,5},{2,0},{3,7},{4,6},{5,1},{6,4},{7,3},{8,10},{9,13},{10,... | collective-permute-start | bytes 700424 | tf_op jit(solution)/shard_map/spread/ppermute | solution.py:35
  55.6 7.2 %collective-permute-start.10 = (bf16[16,7296]{1,0:T(8,128)(2,1)S(1)}, bf16[16,7296]{1,0:T(8,128)(2,1)S(1)}, u32[]{:S(2)}, u32[]{:S(2)}) collective-permute-start(bf16[16,7296]{1,0:T(8,128)(2,1)S(1)} %get-tuple-element.26.refs_0_), channel_id=1, source_target_pairs={{0,1},{1,0},{2,3},{3,2},{4,5},{5,4},{6,7},{7,6},{8,9},{9,8},{10,11... | collective-permute-start | bytes 700424 | tf_op jit(solution)/shard_map/spread/ppermute | solution.py:39
  59.1 3.7 %collective-permute-start.13 = (bf16[16,7296]{1,0:T(8,128)(2,1)S(1)}, bf16[16,7296]{1,0:T(8,128)(2,1)S(1)}, u32[]{:S(2)}, u32[]{:S(2)}) collective-permute-start(bf16[16,7296]{1,0:T(8,128)(2,1)S(1)} %collective-permute-done.9.refs_3_), channel_id=1, source_target_pairs={{0,1},{1,0},{2,3},{3,2},{4,5},{5,4},{6,7},{7,6},{8,9},{9,8},{10,11... | collective-permute-start | bytes 700424 | tf_op jit(solution)/shard_map/spread/ppermute | solution.py:39
  61.5 2.4 %collective-permute-start.12 = (bf16[16,7296]{1,0:T(8,128)(2,1)S(1)}, bf16[16,7296]{1,0:T(8,128)(2,1)S(1)}, u32[]{:S(2)}, u32[]{:S(2)}) collective-permute-start(bf16[16,7296]{1,0:T(8,128)(2,1)S(1)} %collective-permute-done.8.refs_2_), channel_id=1, source_target_pairs={{0,1},{1,0},{2,3},{3,2},{4,5},{5,4},{6,7},{7,6},{8,9},{9,8},{10,11... | collective-permute-start | bytes 700424 | tf_op jit(solution)/shard_map/spread/ppermute | solution.py:39
  62.8 1.5 %collective-permute-start.11 = (bf16[16,7296]{1,0:T(8,128)(2,1)S(1)}, bf16[16,7296]{1,0:T(8,128)(2,1)S(1)}, u32[]{:S(2)}, u32[]{:S(2)}) collective-permute-start(bf16[16,7296]{1,0:T(8,128)(2,1)S(1)} %collective-permute-done.7.refs_1_), channel_id=1, source_target_pairs={{0,1},{1,0},{2,3},{3,2},{4,5},{5,4},{6,7},{7,6},{8,9},{9,8},{10,11... | collective-permute-start | bytes 700424 | tf_op jit(solution)/shard_map/spread/ppermute | solution.py:39
  67.9 2.5 %collective-permute-start.14 = (bf16[64,7168]{1,0:T(8,128)(2,1)S(1)}, bf16[64,7168]{1,0:T(8,128)(2,1)S(1)}, u32[]{:S(2)}, u32[]{:S(2)}) collective-permute-start(bf16[64,7168]{1,0:T(8,128)(2,1)S(1)} %get-tuple-element.32), channel_id=1, source_target_pairs={{0,1},{1,0},{2,3},{3,2},{4,5},{5,4},{6,7},{7,6},{8,9},{9,8},{10,11... | collective-permute-start | bytes 2752520 | tf_op jit(solution)/shard_map/collect/ppermute | solution.py:39
  70.7 7.1 %collective-permute-start.15 = (bf16[16,7168]{1,0:T(8,128)(2,1)S(1)}, bf16[16,7168]{1,0:T(8,128)(2,1)S(1)}, u32[]{:S(2)}, u32[]{:S(2)}) collective-permute-start(bf16[16,7168]{1,0:T(8,128)(2,1)S(1)} %get-tuple-element.41), channel_id=1, source_target_pairs={{0,18},{1,13},{2,16},{3,15},{4,22},{5,9},{6,20},{7,11},{8,26},{9,5... | collective-permute-start | bytes 688136 | tf_op jit(solution)/shard_map/collect/ppermute | solution.py:35
  72.1 8.1 %collective-permute-start.17 = (bf16[16,7168]{1,0:T(8,128)(2,1)S(1)}, bf16[16,7168]{1,0:T(8,128)(2,1)S(1)}, u32[]{:S(2)}, u32[]{:S(2)}) collective-permute-start(bf16[16,7168]{1,0:T(8,128)(2,1)S(1)} %get-tuple-element.42), channel_id=1, source_target_pairs={{0,2},{1,5},{2,0},{3,7},{4,6},{5,1},{6,4},{7,3},{8,10},{9,13},{10,... | collective-permute-start | bytes 688136 | tf_op jit(solution)/shard_map/collect/ppermute | solution.py:35
  73.1 7.0 %collective-permute-start.16 = (bf16[16,7168]{1,0:T(8,128)(2,1)S(1)}, bf16[16,7168]{1,0:T(8,128)(2,1)S(1)}, u32[]{:S(2)}, u32[]{:S(2)}) collective-permute-start(bf16[16,7168]{1,0:T(8,128)(2,1)S(1)} %get-tuple-element.43), channel_id=1, source_target_pairs={{0,16},{1,9},{2,18},{3,11},{4,20},{5,13},{6,22},{7,15},{8,24},{9,1... | collective-permute-start | bytes 688136 | tf_op jit(solution)/shard_map/collect/ppermute | solution.py:35
  80.4 6.1 %collective-permute-start.18 = (bf16[4,7168]{1,0:T(4,128)(2,1)S(1)}, bf16[4,7168]{1,0:T(4,128)(2,1)S(1)}, u32[]{:S(2)}, u32[]{:S(2)}) collective-permute-start(bf16[4,7168]{1,0:T(4,128)(2,1)S(1)} %get-tuple-element.47), channel_id=1, source_target_pairs={{0,12},{1,19},{2,14},{3,17},{4,8},{5,23},{6,10},{7,21},{8,4},{9,27... | collective-permute-start | bytes 172040 | tf_op jit(solution)/shard_map/collect/ppermute | solution.py:35
  82.2 5.4 %collective-permute-start.20 = (bf16[4,7168]{1,0:T(4,128)(2,1)S(1)}, bf16[4,7168]{1,0:T(4,128)(2,1)S(1)}, u32[]{:S(2)}, u32[]{:S(2)}) collective-permute-start(bf16[4,7168]{1,0:T(4,128)(2,1)S(1)} %get-tuple-element.48), channel_id=1, source_target_pairs={{0,4},{1,3},{2,6},{3,1},{4,0},{5,7},{6,2},{7,5},{8,12},{9,11},{10,... | collective-permute-start | bytes 172040 | tf_op jit(solution)/shard_map/collect/ppermute | solution.py:35
  82.2 5.4 %collective-permute-start.19 = (bf16[4,7168]{1,0:T(4,128)(2,1)S(1)}, bf16[4,7168]{1,0:T(4,128)(2,1)S(1)}, u32[]{:S(2)}, u32[]{:S(2)}) collective-permute-start(bf16[4,7168]{1,0:T(4,128)(2,1)S(1)} %get-tuple-element.49), channel_id=1, source_target_pairs={{0,8},{1,17},{2,10},{3,19},{4,12},{5,21},{6,14},{7,23},{8,0},{9,25... | collective-permute-start | bytes 172040 | tf_op jit(solution)/shard_map/collect/ppermute | solution.py:35
  (4 other events, 39.9 us)

commit v16 on v15

--- a/solution.py
+++ b/solution.py
@@ -14,6 +14,7 @@
 STEPS = 4
 TOPK = 8
 BLK = 2048
+KEY_COPIES = 6
 SPAN = 8
 AXES = ("sec", "ep")
 NT = (((1,), (1,)), ((), ()))
@@ -61,15 +62,22 @@
     def block_at(i):
         return pl.ds(pl.multiple_of(i * blk, blk), blk)
 
-    def block_copy(i):
-        return pltpu.make_async_copy(
-            keys_hbm.at[:, block_at(i)], keys_ref.at[:, block_at(i)], sem.at[i]
-        )
+    step = keys_ref.shape[0] // KEY_COPIES
+
+    def block_copies(i):
+        copies = []
+        for part in range(KEY_COPIES):
+            here = (pl.ds(part * step, step), block_at(i))
+            copies.append(
+                pltpu.make_async_copy(keys_hbm.at[here], keys_ref.at[here], sem.at[i, part])
+            )
+        return copies
 
     def start(i):
         @pl.when(i * blk < length)
         def _():
-            block_copy(i).start()
+            for copy in block_copies(i):
+                copy.start()
 
     q_copy = pltpu.make_async_copy(q_hbm, q_ref, small_sem.at[0])
     new_copy = pltpu.make_async_copy(new_hbm, new_ref, small_sem.at[1])
@@ -83,8 +91,8 @@
 
     new = new_ref[...]
     s = lax.dot_general(q_ref[...], new, NT, preferred_element_type=F32)
-    step = iota2(s.shape, 0) // heads
-    s = jnp.where(iota2(s.shape, 1) <= step, s, -1e30)
+    query_step = iota2(s.shape, 0) // heads
+    s = jnp.where(iota2(s.shape, 1) <= query_step, s, -1e30)
     m = jnp.max(s, axis=1, keepdims=True)
     p = jnp.exp2((s - m) * factor_base2)
     m_ref[...] = m
@@ -101,7 +109,8 @@
 
     def update(i, masked):
         start(i + 2)
-        block_copy(i).wait()
+        for copy in block_copies(i):
+            copy.wait()
         keys = keys_ref[:, block_at(i)]
         s = jnp.dot(q_ref[...], keys, preferred_element_type=F32)
         if masked:
@@ -148,7 +157,7 @@
             pltpu.VMEM((rows, 1), F32),
             pltpu.VMEM((LAT, rows), F32),
             pltpu.SemaphoreType.DMA((2,)),
-            pltpu.SemaphoreType.DMA((blocks,)),
+            pltpu.SemaphoreType.DMA((blocks, KEY_COPIES)),
         ],
         out_shape=jax.ShapeDtypeStruct((rows // STEPS, STEPS, LAT), BF),
         compiler_params=pltpu.CompilerParams(vmem_limit_bytes=56 * 1024 * 1024),

time: 88.3 us -> 88.4 us (level)
  no operation moved by 1% of the time
where the time goes in v16:
time: 88.4 us; the launch traced here: 88.2 us
  waiting for transfers between devices  34 us (38%)
  starting transfers between devices  31.4 us (36%)
  Pallas kernels  20.3 us (23%)
  other arithmetic  1.33 us (2%)
    ppermute x15, waiting for transfers between devices, swap(): lax.ppermute(x, AXES, [(d, d ^ partners(n)[d & 1][stage][i]) for d in ran...  19.9 us
    ppermute x15, starting transfers between devices, swap(): lax.ppermute(x, AXES, [(d, d ^ partners(n)[d & 1][stage][i]) for d in ran...  19.6 us
    all_to_all x1, starting transfers between devices, per_device(): latents = lax.all_to_all(latents, AXES, 0, 0, tiled=True)  9.79 us
    pallas_call x2, Pallas kernels, load(): pl.pallas_call(functools.partial(load_kernel, n, ranges), in_specs=[pl.Bl...  9.08 us
    all_to_all x1, waiting for transfers between devices, per_device(): latents = lax.all_to_all(latents, AXES, 0, 0, tiled=True)  8.22 us
    pallas_call x1, Pallas kernels, attend(): pl.pallas_call(functools.partial(attend_kernel, n), in_specs=[pl.BlockSpe...  6.28 us
    ppermute x6, waiting for transfers between devices, swap_core(): return lax.ppermute(x, AXES, [(d, d ^ 1) for d in range(n)])  5.83 us
    pallas_call x4, Pallas kernels, single(): pl.pallas_call(functools.partial(kernel, n), in_specs=[pl.BlockSpec(memor...  4.98 us
  transfers between devices with their start and end apart: 22, of which 15 were waited for; matrix products, arithmetic and copies ran while one was open for 0% of the time, Pallas kernels for 10%

profile of v16, /device:TPU:0, one launch (start us, length us, event | category | flops | bytes accessed | tf_op | source)
XLA Modules:
  0.0 88.2 jit_solution(9941416799712697550)
XLA Ops:
  0.7 6.3 %attend.1 = bf16[32,4,512]{2,1,0:T(4,128)(2,1)} custom-call(s32[1]{0:T(128)S(6)} %copy.14.len_ref, bf16[128,576]{1,0:T(8,128)(2,1)} %bitcast.30, bf16[4,576]{1,0:T(4,128)(2,1)} %bitcast.31, bf16[576,8192]{1,0:T(8,128)(2,1)} %bitcast.27), custom_call_target="tpu_custom_call" | custom-call | flops 2281701376 | bytes 9437184 | tf_op jit(solution)/shard_map/attention/attend/pallas_call | solution.py:147
  7.0 9.8 %all-to-all-start = ((bf16[32,4,512]{2,1,0:T(4,128)(2,1)}), bf16[32,4,512]{2,1,0:T(4,128)(2,1)S(1)}, u32[]{:S(2)}, u32[]{:S(2)}) async-start(bf16[32,4,512]{2,1,0:T(4,128)(2,1)} %attend.1), calls=%async_computation | async-start | bytes 262144 | tf_op jit(solution)/shard_map/heads/all_to_all | solution.py:344
  16.8 8.2 %all-to-all-done = bf16[32,4,512]{2,1,0:T(4,128)(2,1)S(1)} async-done(((bf16[32,4,512]{2,1,0:T(4,128)(2,1)}), bf16[32,4,512]{2,1,0:T(4,128)(2,1)S(1)}, u32[]{:S(2)}, u32[]{:S(2)}) %all-to-all-start) | async-done | bytes 131104 | tf_op jit(solution)/shard_map/heads/all_to_all | solution.py:344
  26.3 2.2 %collective-permute-done = bf16[64,7168]{1,0:T(8,128)(2,1)S(1)} collective-permute-done((bf16[64,7168]{1,0:T(8,128)(2,1)S(1)}, bf16[64,7168]{1,0:T(8,128)(2,1)S(1)}, u32[]{:S(2)}, u32[]{:S(2)}) %collective-permute-start) | collective-permute-done | bytes 917536 | tf_op jit(solution)/shard_map/heads/ppermute | solution.py:40
  29.4 1.5 %collective-permute-start.2 = (bf16[16,7168]{1,0:T(8,128)(2,1)S(1)}, bf16[16,7168]{1,0:T(8,128)(2,1)S(1)}, u32[]{:S(2)}, u32[]{:S(2)}) collective-permute-start(bf16[16,7168]{1,0:T(8,128)(2,1)S(1)} %get-tuple-element.45), channel_id=1, source_target_pairs={{0,16},{1,9},{2,18},{3,11},{4,20},{5,13},{6,22},{7,15},{8,24},{9,1... | collective-permute-start | bytes 688136 | tf_op jit(solution)/shard_map/heads/ppermute | solution.py:36
  30.8 1.5 %collective-permute-start.1 = (bf16[16,7168]{1,0:T(8,128)(2,1)S(1)}, bf16[16,7168]{1,0:T(8,128)(2,1)S(1)}, u32[]{:S(2)}, u32[]{:S(2)}) collective-permute-start(bf16[16,7168]{1,0:T(8,128)(2,1)S(1)} %get-tuple-element.46), channel_id=1, source_target_pairs={{0,2},{1,5},{2,0},{3,7},{4,6},{5,1},{6,4},{7,3},{8,10},{9,13},{10,... | collective-permute-start | bytes 688136 | tf_op jit(solution)/shard_map/heads/ppermute | solution.py:36
  32.5 2.3 %load.2 = (f32[16,7168]{1,0:T(8,128)S(1)}, bf16[3584,512]{1,0:T(8,128)(2,1)S(1)}) custom-call(f32[16,7168]{1,0:T(8,128)S(1)} %slice.69.refs_0_, bf16[7168,512]{1,0:T(8,128)(2,1)} %bitcast.25), custom_call_target="tpu_custom_call" | custom-call | bytes 7340032 | tf_op jit(solution)/shard_map/heads/load/pallas_call | solution.py:248
  35.9 1.4 %collective-permute-done.2.refs_2_ = bf16[16,7168]{1,0:T(8,128)(2,1)S(1)} collective-permute-done((bf16[16,7168]{1,0:T(8,128)(2,1)S(1)}, bf16[16,7168]{1,0:T(8,128)(2,1)S(1)}, u32[]{:S(2)}, u32[]{:S(2)}) %collective-permute-start.2) | collective-permute-done | bytes 229408 | tf_op jit(solution)/shard_map/heads/ppermute | solution.py:36
  38.5 1.4 %collective-permute-start.6 = (bf16[16,7296]{1,0:T(8,128)(2,1)S(1)}, bf16[16,7296]{1,0:T(8,128)(2,1)S(1)}, u32[]{:S(2)}, u32[]{:S(2)}) collective-permute-start(bf16[16,7296]{1,0:T(8,128)(2,1)S(1)} %get-tuple-element.24), channel_id=1, source_target_pairs={{0,12},{1,19},{2,14},{3,17},{4,8},{5,23},{6,10},{7,21},{8,4},{9,27... | collective-permute-start | bytes 700424 | tf_op jit(solution)/shard_map/norm/ppermute | solution.py:36
  40.1 2.8 %collective-permute-start.4 = (bf16[16,7296]{1,0:T(8,128)(2,1)S(1)}, bf16[16,7296]{1,0:T(8,128)(2,1)S(1)}, u32[]{:S(2)}, u32[]{:S(2)}) collective-permute-start(bf16[16,7296]{1,0:T(8,128)(2,1)S(1)} %get-tuple-element.24), channel_id=1, source_target_pairs={{0,4},{1,3},{2,6},{3,1},{4,0},{5,7},{6,2},{7,5},{8,12},{9,11},{10,... | collective-permute-start | bytes 700424 | tf_op jit(solution)/shard_map/norm/ppermute | solution.py:36
  42.9 6.7 %load.3 = (f32[16,7296]{1,0:T(8,128)S(1)}, bf16[3584,512]{1,0:T(8,128)(2,1)S(1)}, bf16[7168,512]{1,0:T(8,128)(2,1)S(1)}, bf16[512,7168]{1,0:T(8,128)(2,1)S(1)}) custom-call(f32[16,7296]{1,0:T(8,128)S(1)} %get-tuple-element.22.refs_0_, bf16[7168,512]{1,0:T(8,128)(2,1)} %bitcast.26, bf16[7168,512]{1,0:T(8,128)(2,1)} %bitcast.28, bf16[512,7168]{1,0:T(8,128)(2,1)} %bitcast.29), custom_call_target="tpu_custom_call" | custom-call | bytes 36700160 | tf_op jit(solution)/shard_map/norm/load/pallas_call | solution.py:248
  49.7 1.9 %collective-permute-done.5.refs_1_ = bf16[16,7296]{1,0:T(8,128)(2,1)S(1)} collective-permute-done((bf16[16,7296]{1,0:T(8,128)(2,1)S(1)}, bf16[16,7296]{1,0:T(8,128)(2,1)S(1)}, u32[]{:S(2)}, u32[]{:S(2)}) %collective-permute-start.5) | collective-permute-done | bytes 233504 | tf_op jit(solution)/shard_map/norm/ppermute | solution.py:36
  51.9 1.4 %collective-permute-start.9 = (bf16[16,7296]{1,0:T(8,128)(2,1)S(1)}, bf16[16,7296]{1,0:T(8,128)(2,1)S(1)}, u32[]{:S(2)}, u32[]{:S(2)}) collective-permute-start(bf16[16,7296]{1,0:T(8,128)(2,1)S(1)} %get-tuple-element.26.refs_0_), channel_id=1, source_target_pairs={{0,18},{1,13},{2,16},{3,15},{4,22},{5,9},{6,20},{7,11},{8,26},{9,5... | collective-permute-start | bytes 700424 | tf_op jit(solution)/shard_map/spread/ppermute | solution.py:36
  53.3 1.5 %collective-permute-start.8 = (bf16[16,7296]{1,0:T(8,128)(2,1)S(1)}, bf16[16,7296]{1,0:T(8,128)(2,1)S(1)}, u32[]{:S(2)}, u32[]{:S(2)}) collective-permute-start(bf16[16,7296]{1,0:T(8,128)(2,1)S(1)} %get-tuple-element.26.refs_0_), channel_id=1, source_target_pairs={{0,16},{1,9},{2,18},{3,11},{4,20},{5,13},{6,22},{7,15},{8,24},{9,1... | collective-permute-start | bytes 700424 | tf_op jit(solution)/shard_map/spread/ppermute | solution.py:36
  55.5 3.5 %collective-permute-done.9.refs_3_ = bf16[16,7296]{1,0:T(8,128)(2,1)S(1)} collective-permute-done((bf16[16,7296]{1,0:T(8,128)(2,1)S(1)}, bf16[16,7296]{1,0:T(8,128)(2,1)S(1)}, u32[]{:S(2)}, u32[]{:S(2)}) %collective-permute-start.9) | collective-permute-done | bytes 233504 | tf_op jit(solution)/shard_map/spread/ppermute | solution.py:36
  59.0 2.4 %collective-permute-done.8.refs_2_ = bf16[16,7296]{1,0:T(8,128)(2,1)S(1)} collective-permute-done((bf16[16,7296]{1,0:T(8,128)(2,1)S(1)}, bf16[16,7296]{1,0:T(8,128)(2,1)S(1)}, u32[]{:S(2)}, u32[]{:S(2)}) %collective-permute-start.8) | collective-permute-done | bytes 233504 | tf_op jit(solution)/shard_map/spread/ppermute | solution.py:36
  64.2 3.6 %experts.1 = (f32[64,7168]{1,0:T(8,128)S(1)}, bf16[64,7168]{1,0:T(8,128)(2,1)S(1)}) custom-call(s32[1]{0:T(128)} %bitcast.me_ref, bf16[16,7296]{1,0:T(8,128)(2,1)S(1)} %get-tuple-element.26.refs_0_, bf16[16,7296]{1,0:T(8,128)(2,1)S(1)} %collective-permute-done.7.refs_1_, bf16[16,7296]{1,0:T(8,128)(2,1)S(1)} %collective-permute-done.8.refs_2_, ...), custom_call_target="tpu_custom_call" | custom-call | flops 2818572288 | bytes 23887872 | tf_op jit(solution)/shard_map/experts/experts/pallas_call | solution.py:291
  68.2 2.1 %collective-permute-done.14 = bf16[64,7168]{1,0:T(8,128)(2,1)S(1)} collective-permute-done((bf16[64,7168]{1,0:T(8,128)(2,1)S(1)}, bf16[64,7168]{1,0:T(8,128)(2,1)S(1)}, u32[]{:S(2)}, u32[]{:S(2)}) %collective-permute-start.14) | collective-permute-done | bytes 917536 | tf_op jit(solution)/shard_map/collect/ppermute | solution.py:40
  70.6 1.4 %collective-permute-start.15 = (bf16[16,7168]{1,0:T(8,128)(2,1)S(1)}, bf16[16,7168]{1,0:T(8,128)(2,1)S(1)}, u32[]{:S(2)}, u32[]{:S(2)}) collective-permute-start(bf16[16,7168]{1,0:T(8,128)(2,1)S(1)} %get-tuple-element.41), channel_id=1, source_target_pairs={{0,18},{1,13},{2,16},{3,15},{4,22},{5,9},{6,20},{7,11},{8,26},{9,5... | collective-permute-start | bytes 688136 | tf_op jit(solution)/shard_map/collect/ppermute | solution.py:36
  74.1 3.5 %collective-permute-done.15 = bf16[16,7168]{1,0:T(8,128)(2,1)S(1)} collective-permute-done((bf16[16,7168]{1,0:T(8,128)(2,1)S(1)}, bf16[16,7168]{1,0:T(8,128)(2,1)S(1)}, u32[]{:S(2)}, u32[]{:S(2)}) %collective-permute-start.15) | collective-permute-done | bytes 229408 | tf_op jit(solution)/shard_map/collect/ppermute | solution.py:36
  77.7 2.4 %collective-permute-done.17 = bf16[16,7168]{1,0:T(8,128)(2,1)S(1)} collective-permute-done((bf16[16,7168]{1,0:T(8,128)(2,1)S(1)}, bf16[16,7168]{1,0:T(8,128)(2,1)S(1)}, u32[]{:S(2)}, u32[]{:S(2)}) %collective-permute-start.17) | collective-permute-done | bytes 229408 | tf_op jit(solution)/shard_map/collect/ppermute | solution.py:36
  80.2 1.9 %collective-permute-start.18 = (bf16[4,7168]{1,0:T(4,128)(2,1)S(1)}, bf16[4,7168]{1,0:T(4,128)(2,1)S(1)}, u32[]{:S(2)}, u32[]{:S(2)}) collective-permute-start(bf16[4,7168]{1,0:T(4,128)(2,1)S(1)} %get-tuple-element.47), channel_id=1, source_target_pairs={{0,12},{1,19},{2,14},{3,17},{4,8},{5,23},{6,10},{7,21},{8,4},{9,27... | collective-permute-start | bytes 172040 | tf_op jit(solution)/shard_map/collect/ppermute | solution.py:36
  82.1 2.6 %collective-permute-start.19 = (bf16[4,7168]{1,0:T(4,128)(2,1)S(1)}, bf16[4,7168]{1,0:T(4,128)(2,1)S(1)}, u32[]{:S(2)}, u32[]{:S(2)}) collective-permute-start(bf16[4,7168]{1,0:T(4,128)(2,1)S(1)} %get-tuple-element.49), channel_id=1, source_target_pairs={{0,8},{1,17},{2,10},{3,19},{4,12},{5,21},{6,14},{7,23},{8,0},{9,25... | collective-permute-start | bytes 172040 | tf_op jit(solution)/shard_map/collect/ppermute | solution.py:36
  84.7 1.6 %collective-permute-done.18 = bf16[4,7168]{1,0:T(4,128)(2,1)S(1)} collective-permute-done((bf16[4,7168]{1,0:T(4,128)(2,1)S(1)}, bf16[4,7168]{1,0:T(4,128)(2,1)S(1)}, u32[]{:S(2)}, u32[]{:S(2)}) %collective-permute-start.18) | collective-permute-done | bytes 57376 | tf_op jit(solution)/shard_map/collect/ppermute | solution.py:36
  (52 shorter events, 13.3 us)
Async XLA Ops:
  0.7 24.4 %copy-start = (bf16[1,128,7168]{2,1,0:T(8,128)(2,1)S(1)}, bf16[1,128,7168]{2,1,0:T(8,128)(2,1)}, u32[]{:S(2)}) copy-start(bf16[1,128,7168]{2,1,0:T(8,128)(2,1)} %param.22) | copy-start | bytes 5505028
  0.7 24.4 %copy-start.1 = (bf16[1,512,128]{2,1,0:T(8,128)(2,1)S(1)}, bf16[1,512,128]{2,1,0:T(8,128)(2,1)}, u32[]{:S(2)}) copy-start(bf16[1,512,128]{2,1,0:T(8,128)(2,1)} %param.21) | copy-start | bytes 393220
  7.0 18.0 %all-to-all-start = ((bf16[32,4,512]{2,1,0:T(4,128)(2,1)}), bf16[32,4,512]{2,1,0:T(4,128)(2,1)S(1)}, u32[]{:S(2)}, u32[]{:S(2)}) async-start(bf16[32,4,512]{2,1,0:T(4,128)(2,1)} %attend.1), calls=%async_computation | async-start | bytes 262144 | tf_op jit(solution)/shard_map/heads/all_to_all | solution.py:344
  26.0 2.5 %collective-permute-start = (bf16[64,7168]{1,0:T(8,128)(2,1)S(1)}, bf16[64,7168]{1,0:T(8,128)(2,1)S(1)}, u32[]{:S(2)}, u32[]{:S(2)}) collective-permute-start(bf16[64,7168]{1,0:T(8,128)(2,1)S(1)} %get-tuple-element.20), channel_id=1, source_target_pairs={{0,1},{1,0},{2,3},{3,2},{4,5},{5,4},{6,7},{7,6},{8,9},{9,8},{10,11... | collective-permute-start | bytes 2752520 | tf_op jit(solution)/shard_map/heads/ppermute | solution.py:40
  28.8 7.1 %collective-permute-start.3 = (bf16[16,7168]{1,0:T(8,128)(2,1)S(1)}, bf16[16,7168]{1,0:T(8,128)(2,1)S(1)}, u32[]{:S(2)}, u32[]{:S(2)}) collective-permute-start(bf16[16,7168]{1,0:T(8,128)(2,1)S(1)} %get-tuple-element.44), channel_id=1, source_target_pairs={{0,18},{1,13},{2,16},{3,15},{4,22},{5,9},{6,20},{7,11},{8,26},{9,5... | collective-permute-start | bytes 688136 | tf_op jit(solution)/shard_map/heads/ppermute | solution.py:36
  29.4 7.9 %collective-permute-start.2 = (bf16[16,7168]{1,0:T(8,128)(2,1)S(1)}, bf16[16,7168]{1,0:T(8,128)(2,1)S(1)}, u32[]{:S(2)}, u32[]{:S(2)}) collective-permute-start(bf16[16,7168]{1,0:T(8,128)(2,1)S(1)} %get-tuple-element.45), channel_id=1, source_target_pairs={{0,16},{1,9},{2,18},{3,11},{4,20},{5,13},{6,22},{7,15},{8,24},{9,1... | collective-permute-start | bytes 688136 | tf_op jit(solution)/shard_map/heads/ppermute | solution.py:36
  30.8 7.4 %collective-permute-start.1 = (bf16[16,7168]{1,0:T(8,128)(2,1)S(1)}, bf16[16,7168]{1,0:T(8,128)(2,1)S(1)}, u32[]{:S(2)}, u32[]{:S(2)}) collective-permute-start(bf16[16,7168]{1,0:T(8,128)(2,1)S(1)} %get-tuple-element.46), channel_id=1, source_target_pairs={{0,2},{1,5},{2,0},{3,7},{4,6},{5,1},{6,4},{7,3},{8,10},{9,13},{10,... | collective-permute-start | bytes 688136 | tf_op jit(solution)/shard_map/heads/ppermute | solution.py:36
  38.5 11.2 %collective-permute-start.6 = (bf16[16,7296]{1,0:T(8,128)(2,1)S(1)}, bf16[16,7296]{1,0:T(8,128)(2,1)S(1)}, u32[]{:S(2)}, u32[]{:S(2)}) collective-permute-start(bf16[16,7296]{1,0:T(8,128)(2,1)S(1)} %get-tuple-element.24), channel_id=1, source_target_pairs={{0,12},{1,19},{2,14},{3,17},{4,8},{5,23},{6,10},{7,21},{8,4},{9,27... | collective-permute-start | bytes 700424 | tf_op jit(solution)/shard_map/norm/ppermute | solution.py:36
  39.9 11.8 %collective-permute-start.5 = (bf16[16,7296]{1,0:T(8,128)(2,1)S(1)}, bf16[16,7296]{1,0:T(8,128)(2,1)S(1)}, u32[]{:S(2)}, u32[]{:S(2)}) collective-permute-start(bf16[16,7296]{1,0:T(8,128)(2,1)S(1)} %get-tuple-element.24), channel_id=1, source_target_pairs={{0,8},{1,17},{2,10},{3,19},{4,12},{5,21},{6,14},{7,23},{8,0},{9,25... | collective-permute-start | bytes 700424 | tf_op jit(solution)/shard_map/norm/ppermute | solution.py:36
  40.1 11.5 %collective-permute-start.4 = (bf16[16,7296]{1,0:T(8,128)(2,1)S(1)}, bf16[16,7296]{1,0:T(8,128)(2,1)S(1)}, u32[]{:S(2)}, u32[]{:S(2)}) collective-permute-start(bf16[16,7296]{1,0:T(8,128)(2,1)S(1)} %get-tuple-element.24), channel_id=1, source_target_pairs={{0,4},{1,3},{2,6},{3,1},{4,0},{5,7},{6,2},{7,5},{8,12},{9,11},{10,... | collective-permute-start | bytes 700424 | tf_op jit(solution)/shard_map/norm/ppermute | solution.py:36
  51.9 7.1 %collective-permute-start.9 = (bf16[16,7296]{1,0:T(8,128)(2,1)S(1)}, bf16[16,7296]{1,0:T(8,128)(2,1)S(1)}, u32[]{:S(2)}, u32[]{:S(2)}) collective-permute-start(bf16[16,7296]{1,0:T(8,128)(2,1)S(1)} %get-tuple-element.26.refs_0_), channel_id=1, source_target_pairs={{0,18},{1,13},{2,16},{3,15},{4,22},{5,9},{6,20},{7,11},{8,26},{9,5... | collective-permute-start | bytes 700424 | tf_op jit(solution)/shard_map/spread/ppermute | solution.py:36
  53.3 8.0 %collective-permute-start.8 = (bf16[16,7296]{1,0:T(8,128)(2,1)S(1)}, bf16[16,7296]{1,0:T(8,128)(2,1)S(1)}, u32[]{:S(2)}, u32[]{:S(2)}) collective-permute-start(bf16[16,7296]{1,0:T(8,128)(2,1)S(1)} %get-tuple-element.26.refs_0_), channel_id=1, source_target_pairs={{0,16},{1,9},{2,18},{3,11},{4,20},{5,13},{6,22},{7,15},{8,24},{9,1... | collective-permute-start | bytes 700424 | tf_op jit(solution)/shard_map/spread/ppermute | solution.py:36
  54.8 7.9 %collective-permute-start.7 = (bf16[16,7296]{1,0:T(8,128)(2,1)S(1)}, bf16[16,7296]{1,0:T(8,128)(2,1)S(1)}, u32[]{:S(2)}, u32[]{:S(2)}) collective-permute-start(bf16[16,7296]{1,0:T(8,128)(2,1)S(1)} %get-tuple-element.26.refs_0_), channel_id=1, source_target_pairs={{0,2},{1,5},{2,0},{3,7},{4,6},{5,1},{6,4},{7,3},{8,10},{9,13},{10,... | collective-permute-start | bytes 700424 | tf_op jit(solution)/shard_map/spread/ppermute | solution.py:36
  55.4 7.2 %collective-permute-start.10 = (bf16[16,7296]{1,0:T(8,128)(2,1)S(1)}, bf16[16,7296]{1,0:T(8,128)(2,1)S(1)}, u32[]{:S(2)}, u32[]{:S(2)}) collective-permute-start(bf16[16,7296]{1,0:T(8,128)(2,1)S(1)} %get-tuple-element.26.refs_0_), channel_id=1, source_target_pairs={{0,1},{1,0},{2,3},{3,2},{4,5},{5,4},{6,7},{7,6},{8,9},{9,8},{10,11... | collective-permute-start | bytes 700424 | tf_op jit(solution)/shard_map/spread/ppermute | solution.py:40
  59.0 3.7 %collective-permute-start.13 = (bf16[16,7296]{1,0:T(8,128)(2,1)S(1)}, bf16[16,7296]{1,0:T(8,128)(2,1)S(1)}, u32[]{:S(2)}, u32[]{:S(2)}) collective-permute-start(bf16[16,7296]{1,0:T(8,128)(2,1)S(1)} %collective-permute-done.9.refs_3_), channel_id=1, source_target_pairs={{0,1},{1,0},{2,3},{3,2},{4,5},{5,4},{6,7},{7,6},{8,9},{9,8},{10,11... | collective-permute-start | bytes 700424 | tf_op jit(solution)/shard_map/spread/ppermute | solution.py:40
  61.4 2.4 %collective-permute-start.12 = (bf16[16,7296]{1,0:T(8,128)(2,1)S(1)}, bf16[16,7296]{1,0:T(8,128)(2,1)S(1)}, u32[]{:S(2)}, u32[]{:S(2)}) collective-permute-start(bf16[16,7296]{1,0:T(8,128)(2,1)S(1)} %collective-permute-done.8.refs_2_), channel_id=1, source_target_pairs={{0,1},{1,0},{2,3},{3,2},{4,5},{5,4},{6,7},{7,6},{8,9},{9,8},{10,11... | collective-permute-start | bytes 700424 | tf_op jit(solution)/shard_map/spread/ppermute | solution.py:40
  62.7 1.5 %collective-permute-start.11 = (bf16[16,7296]{1,0:T(8,128)(2,1)S(1)}, bf16[16,7296]{1,0:T(8,128)(2,1)S(1)}, u32[]{:S(2)}, u32[]{:S(2)}) collective-permute-start(bf16[16,7296]{1,0:T(8,128)(2,1)S(1)} %collective-permute-done.7.refs_1_), channel_id=1, source_target_pairs={{0,1},{1,0},{2,3},{3,2},{4,5},{5,4},{6,7},{7,6},{8,9},{9,8},{10,11... | collective-permute-start | bytes 700424 | tf_op jit(solution)/shard_map/spread/ppermute | solution.py:40
  67.8 2.5 %collective-permute-start.14 = (bf16[64,7168]{1,0:T(8,128)(2,1)S(1)}, bf16[64,7168]{1,0:T(8,128)(2,1)S(1)}, u32[]{:S(2)}, u32[]{:S(2)}) collective-permute-start(bf16[64,7168]{1,0:T(8,128)(2,1)S(1)} %get-tuple-element.32), channel_id=1, source_target_pairs={{0,1},{1,0},{2,3},{3,2},{4,5},{5,4},{6,7},{7,6},{8,9},{9,8},{10,11... | collective-permute-start | bytes 2752520 | tf_op jit(solution)/shard_map/collect/ppermute | solution.py:40
  70.6 7.1 %collective-permute-start.15 = (bf16[16,7168]{1,0:T(8,128)(2,1)S(1)}, bf16[16,7168]{1,0:T(8,128)(2,1)S(1)}, u32[]{:S(2)}, u32[]{:S(2)}) collective-permute-start(bf16[16,7168]{1,0:T(8,128)(2,1)S(1)} %get-tuple-element.41), channel_id=1, source_target_pairs={{0,18},{1,13},{2,16},{3,15},{4,22},{5,9},{6,20},{7,11},{8,26},{9,5... | collective-permute-start | bytes 688136 | tf_op jit(solution)/shard_map/collect/ppermute | solution.py:36
  72.0 8.1 %collective-permute-start.17 = (bf16[16,7168]{1,0:T(8,128)(2,1)S(1)}, bf16[16,7168]{1,0:T(8,128)(2,1)S(1)}, u32[]{:S(2)}, u32[]{:S(2)}) collective-permute-start(bf16[16,7168]{1,0:T(8,128)(2,1)S(1)} %get-tuple-element.42), channel_id=1, source_target_pairs={{0,2},{1,5},{2,0},{3,7},{4,6},{5,1},{6,4},{7,3},{8,10},{9,13},{10,... | collective-permute-start | bytes 688136 | tf_op jit(solution)/shard_map/collect/ppermute | solution.py:36
  73.0 7.0 %collective-permute-start.16 = (bf16[16,7168]{1,0:T(8,128)(2,1)S(1)}, bf16[16,7168]{1,0:T(8,128)(2,1)S(1)}, u32[]{:S(2)}, u32[]{:S(2)}) collective-permute-start(bf16[16,7168]{1,0:T(8,128)(2,1)S(1)} %get-tuple-element.43), channel_id=1, source_target_pairs={{0,16},{1,9},{2,18},{3,11},{4,20},{5,13},{6,22},{7,15},{8,24},{9,1... | collective-permute-start | bytes 688136 | tf_op jit(solution)/shard_map/collect/ppermute | solution.py:36
  80.2 6.1 %collective-permute-start.18 = (bf16[4,7168]{1,0:T(4,128)(2,1)S(1)}, bf16[4,7168]{1,0:T(4,128)(2,1)S(1)}, u32[]{:S(2)}, u32[]{:S(2)}) collective-permute-start(bf16[4,7168]{1,0:T(4,128)(2,1)S(1)} %get-tuple-element.47), channel_id=1, source_target_pairs={{0,12},{1,19},{2,14},{3,17},{4,8},{5,23},{6,10},{7,21},{8,4},{9,27... | collective-permute-start | bytes 172040 | tf_op jit(solution)/shard_map/collect/ppermute | solution.py:36
  82.1 5.4 %collective-permute-start.20 = (bf16[4,7168]{1,0:T(4,128)(2,1)S(1)}, bf16[4,7168]{1,0:T(4,128)(2,1)S(1)}, u32[]{:S(2)}, u32[]{:S(2)}) collective-permute-start(bf16[4,7168]{1,0:T(4,128)(2,1)S(1)} %get-tuple-element.48), channel_id=1, source_target_pairs={{0,4},{1,3},{2,6},{3,1},{4,0},{5,7},{6,2},{7,5},{8,12},{9,11},{10,... | collective-permute-start | bytes 172040 | tf_op jit(solution)/shard_map/collect/ppermute | solution.py:36
  82.1 5.4 %collective-permute-start.19 = (bf16[4,7168]{1,0:T(4,128)(2,1)S(1)}, bf16[4,7168]{1,0:T(4,128)(2,1)S(1)}, u32[]{:S(2)}, u32[]{:S(2)}) collective-permute-start(bf16[4,7168]{1,0:T(4,128)(2,1)S(1)} %get-tuple-element.49), channel_id=1, source_target_pairs={{0,8},{1,17},{2,10},{3,19},{4,12},{5,21},{6,14},{7,23},{8,0},{9,25... | collective-permute-start | bytes 172040 | tf_op jit(solution)/shard_map/collect/ppermute | solution.py:36
  (4 other events, 39.4 us)

commit v17 on v15

--- a/solution.py
+++ b/solution.py
@@ -58,18 +58,20 @@
     length = len_ref[0]
     blk = min(BLK, keys_ref.shape[1])
 
-    def block_at(i):
-        return pl.ds(pl.multiple_of(i * blk, blk), blk)
-
-    def block_copy(i):
-        return pltpu.make_async_copy(
-            keys_hbm.at[:, block_at(i)], keys_ref.at[:, block_at(i)], sem.at[i]
-        )
+    half = blk // 2
+
+    def half_at(i, part):
+        return pl.ds(pl.multiple_of(i * blk + part * half, half), half)
+
+    def half_copy(i, part):
+        here = half_at(i, part)
+        return pltpu.make_async_copy(keys_hbm.at[:, here], keys_ref.at[:, here], sem.at[i, part])
 
     def start(i):
         @pl.when(i * blk < length)
         def _():
-            block_copy(i).start()
+            half_copy(i, 0).start()
+            half_copy(i, 1).start()
 
     q_copy = pltpu.make_async_copy(q_hbm, q_ref, small_sem.at[0])
     new_copy = pltpu.make_async_copy(new_hbm, new_ref, small_sem.at[1])
@@ -101,20 +103,29 @@
 
     def update(i, masked):
         start(i + 2)
-        block_copy(i).wait()
-        keys = keys_ref[:, block_at(i)]
-        s = jnp.dot(q_ref[...], keys, preferred_element_type=F32)
-        if masked:
-            s = jnp.where(iota2(s.shape, 1) < length - i * blk, s, -1e30)
+        scores = []
+        for part in range(2):
+            half_copy(i, part).wait()
+            s = jnp.dot(q_ref[...], keys_ref[:, half_at(i, part)], preferred_element_type=F32)
+            if masked:
+                left = length - i * blk - part * half
+                s = jnp.where(iota2(s.shape, 1) < left, s, -1e30)
+            scores.append(s)
         m_old = m_ref[...]
-        m = jnp.maximum(m_old, jnp.max(s, axis=1, keepdims=True))
+        m = m_old
+        for s in scores:
+            m = jnp.maximum(m, jnp.max(s, axis=1, keepdims=True))
         factor = jnp.exp2((m_old - m) * factor_base2)
-        p = jnp.exp2((s - m) * factor_base2)
         m_ref[...] = m
-        l_ref[...] = l_ref[...] * factor + jnp.sum(p, axis=1, keepdims=True)
-        acc_ref[...] = acc_ref[...] * as_row(factor) + lax.dot_general(
-            keys[:LAT], p.astype(BF), NT, preferred_element_type=F32
-        )
+        total = l_ref[...] * factor
+        acc = acc_ref[...] * as_row(factor)
+        for part, s in enumerate(scores):
+            p = jnp.exp2((s - m) * factor_base2)
+            total += jnp.sum(p, axis=1, keepdims=True)
+            values = keys_ref[:LAT, half_at(i, part)]
+            acc += lax.dot_general(values, p.astype(BF), NT, preferred_element_type=F32)
+        l_ref[...] = total
+        acc_ref[...] = acc
 
     full = length // blk
 
@@ -148,7 +159,7 @@
             pltpu.VMEM((rows, 1), F32),
             pltpu.VMEM((LAT, rows), F32),
             pltpu.SemaphoreType.DMA((2,)),
-            pltpu.SemaphoreType.DMA((blocks,)),
+            pltpu.SemaphoreType.DMA((blocks, 2)),
         ],
         out_shape=jax.ShapeDtypeStruct((rows // STEPS, STEPS, LAT), BF),
         compiler_params=pltpu.CompilerParams(vmem_limit_bytes=56 * 1024 * 1024),

time: 88.3 us -> 88.8 us (level)
  Pallas kernels: 20 us -> 23.7 us
  starting transfers between devices: 31.9 us -> 28.9 us
    pallas_call x1, Pallas kernels: 5.9 us -> 9.65 us  [attend(): pl.pallas_call(functools.partial(attend_kernel, n), in_specs=[pl.BlockSpe...]
    all_to_all x1, starting transfers between devices: 10.3 us -> 7.28 us  [per_device(): latents = lax.all_to_all(latents, AXES, 0, 0, tiled=True)]
where the time goes in v17:
time: 88.8 us; the launch traced here: 89.1 us
  waiting for transfers between devices  34 us (38%)
  starting transfers between devices  28.9 us (33%)
  Pallas kernels  23.7 us (27%)
  other arithmetic  1.33 us (1%)
    ppermute x15, waiting for transfers between devices, swap(): lax.ppermute(x, AXES, [(d, d ^ partners(n)[d & 1][stage][i]) for d in ran...  19.9 us
    ppermute x15, starting transfers between devices, swap(): lax.ppermute(x, AXES, [(d, d ^ partners(n)[d & 1][stage][i]) for d in ran...  19.6 us
    pallas_call x1, Pallas kernels, attend(): pl.pallas_call(functools.partial(attend_kernel, n), in_specs=[pl.BlockSpe...  9.65 us
    pallas_call x2, Pallas kernels, load(): pl.pallas_call(functools.partial(load_kernel, n, ranges), in_specs=[pl.Bl...  9.08 us
    all_to_all x1, waiting for transfers between devices, per_device(): latents = lax.all_to_all(latents, AXES, 0, 0, tiled=True)  8.22 us
    all_to_all x1, starting transfers between devices, per_device(): latents = lax.all_to_all(latents, AXES, 0, 0, tiled=True)  7.28 us
    ppermute x6, waiting for transfers between devices, swap_core(): return lax.ppermute(x, AXES, [(d, d ^ 1) for d in range(n)])  5.82 us
    pallas_call x4, Pallas kernels, single(): pl.pallas_call(functools.partial(kernel, n), in_specs=[pl.BlockSpec(memor...  4.97 us
  transfers between devices with their start and end apart: 22, of which 15 were waited for; matrix products, arithmetic and copies ran while one was open for 0% of the time, Pallas kernels for 10%

profile of v17, /device:TPU:0, one launch (start us, length us, event | category | flops | bytes accessed | tf_op | source)
XLA Modules:
  0.0 89.1 jit_solution(7759385636134680241)
XLA Ops:
  0.7 9.7 %attend.1 = bf16[32,4,512]{2,1,0:T(4,128)(2,1)} custom-call(s32[1]{0:T(128)S(6)} %copy.14.len_ref, bf16[128,576]{1,0:T(8,128)(2,1)} %bitcast.30, bf16[4,576]{1,0:T(4,128)(2,1)} %bitcast.31, bf16[576,8192]{1,0:T(8,128)(2,1)} %bitcast.27), custom_call_target="tpu_custom_call" | custom-call | flops 2281701376 | bytes 9437184 | tf_op jit(solution)/shard_map/attention/attend/pallas_call | solution.py:149
  10.3 7.3 %all-to-all-start = ((bf16[32,4,512]{2,1,0:T(4,128)(2,1)}), bf16[32,4,512]{2,1,0:T(4,128)(2,1)S(1)}, u32[]{:S(2)}, u32[]{:S(2)}) async-start(bf16[32,4,512]{2,1,0:T(4,128)(2,1)} %attend.1), calls=%async_computation | async-start | bytes 262144 | tf_op jit(solution)/shard_map/heads/all_to_all | solution.py:346
  17.6 8.2 %all-to-all-done = bf16[32,4,512]{2,1,0:T(4,128)(2,1)S(1)} async-done(((bf16[32,4,512]{2,1,0:T(4,128)(2,1)}), bf16[32,4,512]{2,1,0:T(4,128)(2,1)S(1)}, u32[]{:S(2)}, u32[]{:S(2)}) %all-to-all-start) | async-done | bytes 131104 | tf_op jit(solution)/shard_map/heads/all_to_all | solution.py:346
  27.2 2.2 %collective-permute-done = bf16[64,7168]{1,0:T(8,128)(2,1)S(1)} collective-permute-done((bf16[64,7168]{1,0:T(8,128)(2,1)S(1)}, bf16[64,7168]{1,0:T(8,128)(2,1)S(1)}, u32[]{:S(2)}, u32[]{:S(2)}) %collective-permute-start) | collective-permute-done | bytes 917536 | tf_op jit(solution)/shard_map/heads/ppermute | solution.py:39
  30.2 1.5 %collective-permute-start.2 = (bf16[16,7168]{1,0:T(8,128)(2,1)S(1)}, bf16[16,7168]{1,0:T(8,128)(2,1)S(1)}, u32[]{:S(2)}, u32[]{:S(2)}) collective-permute-start(bf16[16,7168]{1,0:T(8,128)(2,1)S(1)} %get-tuple-element.45), channel_id=1, source_target_pairs={{0,16},{1,9},{2,18},{3,11},{4,20},{5,13},{6,22},{7,15},{8,24},{9,1... | collective-permute-start | bytes 688136 | tf_op jit(solution)/shard_map/heads/ppermute | solution.py:35
  31.7 1.5 %collective-permute-start.1 = (bf16[16,7168]{1,0:T(8,128)(2,1)S(1)}, bf16[16,7168]{1,0:T(8,128)(2,1)S(1)}, u32[]{:S(2)}, u32[]{:S(2)}) collective-permute-start(bf16[16,7168]{1,0:T(8,128)(2,1)S(1)} %get-tuple-element.46), channel_id=1, source_target_pairs={{0,2},{1,5},{2,0},{3,7},{4,6},{5,1},{6,4},{7,3},{8,10},{9,13},{10,... | collective-permute-start | bytes 688136 | tf_op jit(solution)/shard_map/heads/ppermute | solution.py:35
  33.4 2.3 %load.2 = (f32[16,7168]{1,0:T(8,128)S(1)}, bf16[3584,512]{1,0:T(8,128)(2,1)S(1)}) custom-call(f32[16,7168]{1,0:T(8,128)S(1)} %slice.69.refs_0_, bf16[7168,512]{1,0:T(8,128)(2,1)} %bitcast.25), custom_call_target="tpu_custom_call" | custom-call | bytes 7340032 | tf_op jit(solution)/shard_map/heads/load/pallas_call | solution.py:250
  36.7 1.4 %collective-permute-done.2.refs_2_ = bf16[16,7168]{1,0:T(8,128)(2,1)S(1)} collective-permute-done((bf16[16,7168]{1,0:T(8,128)(2,1)S(1)}, bf16[16,7168]{1,0:T(8,128)(2,1)S(1)}, u32[]{:S(2)}, u32[]{:S(2)}) %collective-permute-start.2) | collective-permute-done | bytes 229408 | tf_op jit(solution)/shard_map/heads/ppermute | solution.py:35
  39.3 1.4 %collective-permute-start.6 = (bf16[16,7296]{1,0:T(8,128)(2,1)S(1)}, bf16[16,7296]{1,0:T(8,128)(2,1)S(1)}, u32[]{:S(2)}, u32[]{:S(2)}) collective-permute-start(bf16[16,7296]{1,0:T(8,128)(2,1)S(1)} %get-tuple-element.24), channel_id=1, source_target_pairs={{0,12},{1,19},{2,14},{3,17},{4,8},{5,23},{6,10},{7,21},{8,4},{9,27... | collective-permute-start | bytes 700424 | tf_op jit(solution)/shard_map/norm/ppermute | solution.py:35
  40.9 2.8 %collective-permute-start.4 = (bf16[16,7296]{1,0:T(8,128)(2,1)S(1)}, bf16[16,7296]{1,0:T(8,128)(2,1)S(1)}, u32[]{:S(2)}, u32[]{:S(2)}) collective-permute-start(bf16[16,7296]{1,0:T(8,128)(2,1)S(1)} %get-tuple-element.24), channel_id=1, source_target_pairs={{0,4},{1,3},{2,6},{3,1},{4,0},{5,7},{6,2},{7,5},{8,12},{9,11},{10,... | collective-permute-start | bytes 700424 | tf_op jit(solution)/shard_map/norm/ppermute | solution.py:35
  43.8 6.7 %load.3 = (f32[16,7296]{1,0:T(8,128)S(1)}, bf16[3584,512]{1,0:T(8,128)(2,1)S(1)}, bf16[7168,512]{1,0:T(8,128)(2,1)S(1)}, bf16[512,7168]{1,0:T(8,128)(2,1)S(1)}) custom-call(f32[16,7296]{1,0:T(8,128)S(1)} %get-tuple-element.22.refs_0_, bf16[7168,512]{1,0:T(8,128)(2,1)} %bitcast.26, bf16[7168,512]{1,0:T(8,128)(2,1)} %bitcast.28, bf16[512,7168]{1,0:T(8,128)(2,1)} %bitcast.29), custom_call_target="tpu_custom_call" | custom-call | bytes 36700160 | tf_op jit(solution)/shard_map/norm/load/pallas_call | solution.py:250
  50.6 1.9 %collective-permute-done.5.refs_1_ = bf16[16,7296]{1,0:T(8,128)(2,1)S(1)} collective-permute-done((bf16[16,7296]{1,0:T(8,128)(2,1)S(1)}, bf16[16,7296]{1,0:T(8,128)(2,1)S(1)}, u32[]{:S(2)}, u32[]{:S(2)}) %collective-permute-start.5) | collective-permute-done | bytes 233504 | tf_op jit(solution)/shard_map/norm/ppermute | solution.py:35
  52.8 1.4 %collective-permute-start.9 = (bf16[16,7296]{1,0:T(8,128)(2,1)S(1)}, bf16[16,7296]{1,0:T(8,128)(2,1)S(1)}, u32[]{:S(2)}, u32[]{:S(2)}) collective-permute-start(bf16[16,7296]{1,0:T(8,128)(2,1)S(1)} %get-tuple-element.26.refs_0_), channel_id=1, source_target_pairs={{0,18},{1,13},{2,16},{3,15},{4,22},{5,9},{6,20},{7,11},{8,26},{9,5... | collective-permute-start | bytes 700424 | tf_op jit(solution)/shard_map/spread/ppermute | solution.py:35
  54.2 1.5 %collective-permute-start.8 = (bf16[16,7296]{1,0:T(8,128)(2,1)S(1)}, bf16[16,7296]{1,0:T(8,128)(2,1)S(1)}, u32[]{:S(2)}, u32[]{:S(2)}) collective-permute-start(bf16[16,7296]{1,0:T(8,128)(2,1)S(1)} %get-tuple-element.26.refs_0_), channel_id=1, source_target_pairs={{0,16},{1,9},{2,18},{3,11},{4,20},{5,13},{6,22},{7,15},{8,24},{9,1... | collective-permute-start | bytes 700424 | tf_op jit(solution)/shard_map/spread/ppermute | solution.py:35
  56.3 3.5 %collective-permute-done.9.refs_3_ = bf16[16,7296]{1,0:T(8,128)(2,1)S(1)} collective-permute-done((bf16[16,7296]{1,0:T(8,128)(2,1)S(1)}, bf16[16,7296]{1,0:T(8,128)(2,1)S(1)}, u32[]{:S(2)}, u32[]{:S(2)}) %collective-permute-start.9) | collective-permute-done | bytes 233504 | tf_op jit(solution)/shard_map/spread/ppermute | solution.py:35
  59.8 2.4 %collective-permute-done.8.refs_2_ = bf16[16,7296]{1,0:T(8,128)(2,1)S(1)} collective-permute-done((bf16[16,7296]{1,0:T(8,128)(2,1)S(1)}, bf16[16,7296]{1,0:T(8,128)(2,1)S(1)}, u32[]{:S(2)}, u32[]{:S(2)}) %collective-permute-start.8) | collective-permute-done | bytes 233504 | tf_op jit(solution)/shard_map/spread/ppermute | solution.py:35
  65.0 3.6 %experts.1 = (f32[64,7168]{1,0:T(8,128)S(1)}, bf16[64,7168]{1,0:T(8,128)(2,1)S(1)}) custom-call(s32[1]{0:T(128)} %bitcast.me_ref, bf16[16,7296]{1,0:T(8,128)(2,1)S(1)} %get-tuple-element.26.refs_0_, bf16[16,7296]{1,0:T(8,128)(2,1)S(1)} %collective-permute-done.7.refs_1_, bf16[16,7296]{1,0:T(8,128)(2,1)S(1)} %collective-permute-done.8.refs_2_, ...), custom_call_target="tpu_custom_call" | custom-call | flops 2818572288 | bytes 23887872 | tf_op jit(solution)/shard_map/experts/experts/pallas_call | solution.py:293
  69.0 2.1 %collective-permute-done.14 = bf16[64,7168]{1,0:T(8,128)(2,1)S(1)} collective-permute-done((bf16[64,7168]{1,0:T(8,128)(2,1)S(1)}, bf16[64,7168]{1,0:T(8,128)(2,1)S(1)}, u32[]{:S(2)}, u32[]{:S(2)}) %collective-permute-start.14) | collective-permute-done | bytes 917536 | tf_op jit(solution)/shard_map/collect/ppermute | solution.py:39
  71.5 1.4 %collective-permute-start.15 = (bf16[16,7168]{1,0:T(8,128)(2,1)S(1)}, bf16[16,7168]{1,0:T(8,128)(2,1)S(1)}, u32[]{:S(2)}, u32[]{:S(2)}) collective-permute-start(bf16[16,7168]{1,0:T(8,128)(2,1)S(1)} %get-tuple-element.41), channel_id=1, source_target_pairs={{0,18},{1,13},{2,16},{3,15},{4,22},{5,9},{6,20},{7,11},{8,26},{9,5... | collective-permute-start | bytes 688136 | tf_op jit(solution)/shard_map/collect/ppermute | solution.py:35
  75.0 3.5 %collective-permute-done.15 = bf16[16,7168]{1,0:T(8,128)(2,1)S(1)} collective-permute-done((bf16[16,7168]{1,0:T(8,128)(2,1)S(1)}, bf16[16,7168]{1,0:T(8,128)(2,1)S(1)}, u32[]{:S(2)}, u32[]{:S(2)}) %collective-permute-start.15) | collective-permute-done | bytes 229408 | tf_op jit(solution)/shard_map/collect/ppermute | solution.py:35
  78.6 2.4 %collective-permute-done.17 = bf16[16,7168]{1,0:T(8,128)(2,1)S(1)} collective-permute-done((bf16[16,7168]{1,0:T(8,128)(2,1)S(1)}, bf16[16,7168]{1,0:T(8,128)(2,1)S(1)}, u32[]{:S(2)}, u32[]{:S(2)}) %collective-permute-start.17) | collective-permute-done | bytes 229408 | tf_op jit(solution)/shard_map/collect/ppermute | solution.py:35
  81.1 1.9 %collective-permute-start.18 = (bf16[4,7168]{1,0:T(4,128)(2,1)S(1)}, bf16[4,7168]{1,0:T(4,128)(2,1)S(1)}, u32[]{:S(2)}, u32[]{:S(2)}) collective-permute-start(bf16[4,7168]{1,0:T(4,128)(2,1)S(1)} %get-tuple-element.47), channel_id=1, source_target_pairs={{0,12},{1,19},{2,14},{3,17},{4,8},{5,23},{6,10},{7,21},{8,4},{9,27... | collective-permute-start | bytes 172040 | tf_op jit(solution)/shard_map/collect/ppermute | solution.py:35
  83.0 2.6 %collective-permute-start.19 = (bf16[4,7168]{1,0:T(4,128)(2,1)S(1)}, bf16[4,7168]{1,0:T(4,128)(2,1)S(1)}, u32[]{:S(2)}, u32[]{:S(2)}) collective-permute-start(bf16[4,7168]{1,0:T(4,128)(2,1)S(1)} %get-tuple-element.49), channel_id=1, source_target_pairs={{0,8},{1,17},{2,10},{3,19},{4,12},{5,21},{6,14},{7,23},{8,0},{9,25... | collective-permute-start | bytes 172040 | tf_op jit(solution)/shard_map/collect/ppermute | solution.py:35
  85.6 1.6 %collective-permute-done.18 = bf16[4,7168]{1,0:T(4,128)(2,1)S(1)} collective-permute-done((bf16[4,7168]{1,0:T(4,128)(2,1)S(1)}, bf16[4,7168]{1,0:T(4,128)(2,1)S(1)}, u32[]{:S(2)}, u32[]{:S(2)}) %collective-permute-start.18) | collective-permute-done | bytes 57376 | tf_op jit(solution)/shard_map/collect/ppermute | solution.py:35
  (52 shorter events, 13.3 us)
Async XLA Ops:
  0.7 25.3 %copy-start = (bf16[1,128,7168]{2,1,0:T(8,128)(2,1)S(1)}, bf16[1,128,7168]{2,1,0:T(8,128)(2,1)}, u32[]{:S(2)}) copy-start(bf16[1,128,7168]{2,1,0:T(8,128)(2,1)} %param.22) | copy-start | bytes 5505028
  0.7 25.3 %copy-start.1 = (bf16[1,512,128]{2,1,0:T(8,128)(2,1)S(1)}, bf16[1,512,128]{2,1,0:T(8,128)(2,1)}, u32[]{:S(2)}) copy-start(bf16[1,512,128]{2,1,0:T(8,128)(2,1)} %param.21) | copy-start | bytes 393220
  10.3 15.5 %all-to-all-start = ((bf16[32,4,512]{2,1,0:T(4,128)(2,1)}), bf16[32,4,512]{2,1,0:T(4,128)(2,1)S(1)}, u32[]{:S(2)}, u32[]{:S(2)}) async-start(bf16[32,4,512]{2,1,0:T(4,128)(2,1)} %attend.1), calls=%async_computation | async-start | bytes 262144 | tf_op jit(solution)/shard_map/heads/all_to_all | solution.py:346
  26.8 2.5 %collective-permute-start = (bf16[64,7168]{1,0:T(8,128)(2,1)S(1)}, bf16[64,7168]{1,0:T(8,128)(2,1)S(1)}, u32[]{:S(2)}, u32[]{:S(2)}) collective-permute-start(bf16[64,7168]{1,0:T(8,128)(2,1)S(1)} %get-tuple-element.20), channel_id=1, source_target_pairs={{0,1},{1,0},{2,3},{3,2},{4,5},{5,4},{6,7},{7,6},{8,9},{9,8},{10,11... | collective-permute-start | bytes 2752520 | tf_op jit(solution)/shard_map/heads/ppermute | solution.py:39
  29.7 7.1 %collective-permute-start.3 = (bf16[16,7168]{1,0:T(8,128)(2,1)S(1)}, bf16[16,7168]{1,0:T(8,128)(2,1)S(1)}, u32[]{:S(2)}, u32[]{:S(2)}) collective-permute-start(bf16[16,7168]{1,0:T(8,128)(2,1)S(1)} %get-tuple-element.44), channel_id=1, source_target_pairs={{0,18},{1,13},{2,16},{3,15},{4,22},{5,9},{6,20},{7,11},{8,26},{9,5... | collective-permute-start | bytes 688136 | tf_op jit(solution)/shard_map/heads/ppermute | solution.py:35
  30.2 7.9 %collective-permute-start.2 = (bf16[16,7168]{1,0:T(8,128)(2,1)S(1)}, bf16[16,7168]{1,0:T(8,128)(2,1)S(1)}, u32[]{:S(2)}, u32[]{:S(2)}) collective-permute-start(bf16[16,7168]{1,0:T(8,128)(2,1)S(1)} %get-tuple-element.45), channel_id=1, source_target_pairs={{0,16},{1,9},{2,18},{3,11},{4,20},{5,13},{6,22},{7,15},{8,24},{9,1... | collective-permute-start | bytes 688136 | tf_op jit(solution)/shard_map/heads/ppermute | solution.py:35
  31.7 7.4 %collective-permute-start.1 = (bf16[16,7168]{1,0:T(8,128)(2,1)S(1)}, bf16[16,7168]{1,0:T(8,128)(2,1)S(1)}, u32[]{:S(2)}, u32[]{:S(2)}) collective-permute-start(bf16[16,7168]{1,0:T(8,128)(2,1)S(1)} %get-tuple-element.46), channel_id=1, source_target_pairs={{0,2},{1,5},{2,0},{3,7},{4,6},{5,1},{6,4},{7,3},{8,10},{9,13},{10,... | collective-permute-start | bytes 688136 | tf_op jit(solution)/shard_map/heads/ppermute | solution.py:35
  39.3 11.2 %collective-permute-start.6 = (bf16[16,7296]{1,0:T(8,128)(2,1)S(1)}, bf16[16,7296]{1,0:T(8,128)(2,1)S(1)}, u32[]{:S(2)}, u32[]{:S(2)}) collective-permute-start(bf16[16,7296]{1,0:T(8,128)(2,1)S(1)} %get-tuple-element.24), channel_id=1, source_target_pairs={{0,12},{1,19},{2,14},{3,17},{4,8},{5,23},{6,10},{7,21},{8,4},{9,27... | collective-permute-start | bytes 700424 | tf_op jit(solution)/shard_map/norm/ppermute | solution.py:35
  40.7 11.7 %collective-permute-start.5 = (bf16[16,7296]{1,0:T(8,128)(2,1)S(1)}, bf16[16,7296]{1,0:T(8,128)(2,1)S(1)}, u32[]{:S(2)}, u32[]{:S(2)}) collective-permute-start(bf16[16,7296]{1,0:T(8,128)(2,1)S(1)} %get-tuple-element.24), channel_id=1, source_target_pairs={{0,8},{1,17},{2,10},{3,19},{4,12},{5,21},{6,14},{7,23},{8,0},{9,25... | collective-permute-start | bytes 700424 | tf_op jit(solution)/shard_map/norm/ppermute | solution.py:35
  40.9 11.5 %collective-permute-start.4 = (bf16[16,7296]{1,0:T(8,128)(2,1)S(1)}, bf16[16,7296]{1,0:T(8,128)(2,1)S(1)}, u32[]{:S(2)}, u32[]{:S(2)}) collective-permute-start(bf16[16,7296]{1,0:T(8,128)(2,1)S(1)} %get-tuple-element.24), channel_id=1, source_target_pairs={{0,4},{1,3},{2,6},{3,1},{4,0},{5,7},{6,2},{7,5},{8,12},{9,11},{10,... | collective-permute-start | bytes 700424 | tf_op jit(solution)/shard_map/norm/ppermute | solution.py:35
  52.8 7.1 %collective-permute-start.9 = (bf16[16,7296]{1,0:T(8,128)(2,1)S(1)}, bf16[16,7296]{1,0:T(8,128)(2,1)S(1)}, u32[]{:S(2)}, u32[]{:S(2)}) collective-permute-start(bf16[16,7296]{1,0:T(8,128)(2,1)S(1)} %get-tuple-element.26.refs_0_), channel_id=1, source_target_pairs={{0,18},{1,13},{2,16},{3,15},{4,22},{5,9},{6,20},{7,11},{8,26},{9,5... | collective-permute-start | bytes 700424 | tf_op jit(solution)/shard_map/spread/ppermute | solution.py:35
  54.2 8.0 %collective-permute-start.8 = (bf16[16,7296]{1,0:T(8,128)(2,1)S(1)}, bf16[16,7296]{1,0:T(8,128)(2,1)S(1)}, u32[]{:S(2)}, u32[]{:S(2)}) collective-permute-start(bf16[16,7296]{1,0:T(8,128)(2,1)S(1)} %get-tuple-element.26.refs_0_), channel_id=1, source_target_pairs={{0,16},{1,9},{2,18},{3,11},{4,20},{5,13},{6,22},{7,15},{8,24},{9,1... | collective-permute-start | bytes 700424 | tf_op jit(solution)/shard_map/spread/ppermute | solution.py:35
  55.7 7.9 %collective-permute-start.7 = (bf16[16,7296]{1,0:T(8,128)(2,1)S(1)}, bf16[16,7296]{1,0:T(8,128)(2,1)S(1)}, u32[]{:S(2)}, u32[]{:S(2)}) collective-permute-start(bf16[16,7296]{1,0:T(8,128)(2,1)S(1)} %get-tuple-element.26.refs_0_), channel_id=1, source_target_pairs={{0,2},{1,5},{2,0},{3,7},{4,6},{5,1},{6,4},{7,3},{8,10},{9,13},{10,... | collective-permute-start | bytes 700424 | tf_op jit(solution)/shard_map/spread/ppermute | solution.py:35
  56.3 7.2 %collective-permute-start.10 = (bf16[16,7296]{1,0:T(8,128)(2,1)S(1)}, bf16[16,7296]{1,0:T(8,128)(2,1)S(1)}, u32[]{:S(2)}, u32[]{:S(2)}) collective-permute-start(bf16[16,7296]{1,0:T(8,128)(2,1)S(1)} %get-tuple-element.26.refs_0_), channel_id=1, source_target_pairs={{0,1},{1,0},{2,3},{3,2},{4,5},{5,4},{6,7},{7,6},{8,9},{9,8},{10,11... | collective-permute-start | bytes 700424 | tf_op jit(solution)/shard_map/spread/ppermute | solution.py:39
  59.8 3.7 %collective-permute-start.13 = (bf16[16,7296]{1,0:T(8,128)(2,1)S(1)}, bf16[16,7296]{1,0:T(8,128)(2,1)S(1)}, u32[]{:S(2)}, u32[]{:S(2)}) collective-permute-start(bf16[16,7296]{1,0:T(8,128)(2,1)S(1)} %collective-permute-done.9.refs_3_), channel_id=1, source_target_pairs={{0,1},{1,0},{2,3},{3,2},{4,5},{5,4},{6,7},{7,6},{8,9},{9,8},{10,11... | collective-permute-start | bytes 700424 | tf_op jit(solution)/shard_map/spread/ppermute | solution.py:39
  62.2 2.5 %collective-permute-start.12 = (bf16[16,7296]{1,0:T(8,128)(2,1)S(1)}, bf16[16,7296]{1,0:T(8,128)(2,1)S(1)}, u32[]{:S(2)}, u32[]{:S(2)}) collective-permute-start(bf16[16,7296]{1,0:T(8,128)(2,1)S(1)} %collective-permute-done.8.refs_2_), channel_id=1, source_target_pairs={{0,1},{1,0},{2,3},{3,2},{4,5},{5,4},{6,7},{7,6},{8,9},{9,8},{10,11... | collective-permute-start | bytes 700424 | tf_op jit(solution)/shard_map/spread/ppermute | solution.py:39
  63.6 1.5 %collective-permute-start.11 = (bf16[16,7296]{1,0:T(8,128)(2,1)S(1)}, bf16[16,7296]{1,0:T(8,128)(2,1)S(1)}, u32[]{:S(2)}, u32[]{:S(2)}) collective-permute-start(bf16[16,7296]{1,0:T(8,128)(2,1)S(1)} %collective-permute-done.7.refs_1_), channel_id=1, source_target_pairs={{0,1},{1,0},{2,3},{3,2},{4,5},{5,4},{6,7},{7,6},{8,9},{9,8},{10,11... | collective-permute-start | bytes 700424 | tf_op jit(solution)/shard_map/spread/ppermute | solution.py:39
  68.6 2.5 %collective-permute-start.14 = (bf16[64,7168]{1,0:T(8,128)(2,1)S(1)}, bf16[64,7168]{1,0:T(8,128)(2,1)S(1)}, u32[]{:S(2)}, u32[]{:S(2)}) collective-permute-start(bf16[64,7168]{1,0:T(8,128)(2,1)S(1)} %get-tuple-element.32), channel_id=1, source_target_pairs={{0,1},{1,0},{2,3},{3,2},{4,5},{5,4},{6,7},{7,6},{8,9},{9,8},{10,11... | collective-permute-start | bytes 2752520 | tf_op jit(solution)/shard_map/collect/ppermute | solution.py:39
  71.5 7.1 %collective-permute-start.15 = (bf16[16,7168]{1,0:T(8,128)(2,1)S(1)}, bf16[16,7168]{1,0:T(8,128)(2,1)S(1)}, u32[]{:S(2)}, u32[]{:S(2)}) collective-permute-start(bf16[16,7168]{1,0:T(8,128)(2,1)S(1)} %get-tuple-element.41), channel_id=1, source_target_pairs={{0,18},{1,13},{2,16},{3,15},{4,22},{5,9},{6,20},{7,11},{8,26},{9,5... | collective-permute-start | bytes 688136 | tf_op jit(solution)/shard_map/collect/ppermute | solution.py:35
  72.8 8.1 %collective-permute-start.17 = (bf16[16,7168]{1,0:T(8,128)(2,1)S(1)}, bf16[16,7168]{1,0:T(8,128)(2,1)S(1)}, u32[]{:S(2)}, u32[]{:S(2)}) collective-permute-start(bf16[16,7168]{1,0:T(8,128)(2,1)S(1)} %get-tuple-element.42), channel_id=1, source_target_pairs={{0,2},{1,5},{2,0},{3,7},{4,6},{5,1},{6,4},{7,3},{8,10},{9,13},{10,... | collective-permute-start | bytes 688136 | tf_op jit(solution)/shard_map/collect/ppermute | solution.py:35
  73.8 7.1 %collective-permute-start.16 = (bf16[16,7168]{1,0:T(8,128)(2,1)S(1)}, bf16[16,7168]{1,0:T(8,128)(2,1)S(1)}, u32[]{:S(2)}, u32[]{:S(2)}) collective-permute-start(bf16[16,7168]{1,0:T(8,128)(2,1)S(1)} %get-tuple-element.43), channel_id=1, source_target_pairs={{0,16},{1,9},{2,18},{3,11},{4,20},{5,13},{6,22},{7,15},{8,24},{9,1... | collective-permute-start | bytes 688136 | tf_op jit(solution)/shard_map/collect/ppermute | solution.py:35
  81.1 6.1 %collective-permute-start.18 = (bf16[4,7168]{1,0:T(4,128)(2,1)S(1)}, bf16[4,7168]{1,0:T(4,128)(2,1)S(1)}, u32[]{:S(2)}, u32[]{:S(2)}) collective-permute-start(bf16[4,7168]{1,0:T(4,128)(2,1)S(1)} %get-tuple-element.47), channel_id=1, source_target_pairs={{0,12},{1,19},{2,14},{3,17},{4,8},{5,23},{6,10},{7,21},{8,4},{9,27... | collective-permute-start | bytes 172040 | tf_op jit(solution)/shard_map/collect/ppermute | solution.py:35
  83.0 5.4 %collective-permute-start.20 = (bf16[4,7168]{1,0:T(4,128)(2,1)S(1)}, bf16[4,7168]{1,0:T(4,128)(2,1)S(1)}, u32[]{:S(2)}, u32[]{:S(2)}) collective-permute-start(bf16[4,7168]{1,0:T(4,128)(2,1)S(1)} %get-tuple-element.48), channel_id=1, source_target_pairs={{0,4},{1,3},{2,6},{3,1},{4,0},{5,7},{6,2},{7,5},{8,12},{9,11},{10,... | collective-permute-start | bytes 172040 | tf_op jit(solution)/shard_map/collect/ppermute | solution.py:35
  83.0 5.4 %collective-permute-start.19 = (bf16[4,7168]{1,0:T(4,128)(2,1)S(1)}, bf16[4,7168]{1,0:T(4,128)(2,1)S(1)}, u32[]{:S(2)}, u32[]{:S(2)}) collective-permute-start(bf16[4,7168]{1,0:T(4,128)(2,1)S(1)} %get-tuple-element.49), channel_id=1, source_target_pairs={{0,8},{1,17},{2,10},{3,19},{4,12},{5,21},{6,14},{7,23},{8,0},{9,25... | collective-permute-start | bytes 172040 | tf_op jit(solution)/shard_map/collect/ppermute | solution.py:35
  (4 other events, 36.9 us)
